TPU v7x, 32 devices: a whole 2x2x4 slice. The times are simulated.
32 devices in a mesh: dp: 16 (over z, y, core), opt: 2 (over x).
Axes of the slice: x: 2, y: 2, z: 4, core: 2. Of those that a mesh axis runs over, the one named last changes fastest.
Arguments:
- tokens: bfloat16 [32768, 768], P(('dp', 'opt')), may hold values from -6 to 6
- cotangent: bfloat16 [32768, 768], P(('dp', 'opt')), may hold values from -6 to 6
- lengths: int32 [128], P(('dp', 'opt')), may hold values from 1 to 256, 16384 in all
- key_mask: int32 [32768], P(('dp', 'opt')), may hold values 0 or 1
- type_ids: int32 [32768], P(('dp', 'opt')), may hold values from 0 to 1
- weights: bfloat16 [768, 9216], P(None, 'dp')
- vectors: bfloat16 [10752], P('dp')
- master: float32 [768, 9216], P(None, ('dp', 'opt')), may hold values from -0.21875 to 0.21875
- slow_weights: float32 [768, 9216], P(None, ('dp', 'opt')), may hold values from -0.21875 to 0.21875
- left_stats: float32 [24576, 768], P(('dp', 'opt')), as said below
- right_stats: float32 [9216, 288], P(('dp', 'opt')), as said below
- left_root: float32 [24576, 768], P(('dp', 'opt')), as said below
- right_root: float32 [9216, 288], P(('dp', 'opt')), as said below
- vector_master: float32 [10752], P(('dp', 'opt'))
- vector_moment: float32 [10752], P(('dp', 'opt')), as said below
- slow_vectors: float32 [10752], P(('dp', 'opt'))
Outputs:
- layer_out: bfloat16 [32768, 768], P(('dp', 'opt'))
- input_grad: float32 [32768, 768], P(('dp', 'opt'))
- weight_grad: float32 [768, 9216], P(None, ('dp', 'opt'))
- left_new: float32 [24576, 768], P(('dp', 'opt'))
- right_new: float32 [9216, 288], P(('dp', 'opt'))
- master_new: float32 [768, 9216], P(None, ('dp', 'opt'))
- slow_new: float32 [768, 9216], P(None, ('dp', 'opt'))
- weights_new: bfloat16 [768, 9216], P(None, ('dp', 'opt'))
- vector_grad: float32 [10752], P(('dp', 'opt'))
- moment_new: float32 [10752], P(('dp', 'opt'))
- vector_master_new: float32 [10752], P(('dp', 'opt'))
- slow_vectors_new: float32 [10752], P(('dp', 'opt'))
- vectors_new: bfloat16 [10752], P(('dp', 'opt'))
Inputs may be any that keep to these rules, and one draw needn't show every extreme that they name: Each block of left_stats and right_stats is symmetric positive definite. Each block of right_stats is symmetric positive definite. `left_root`: each block is symmetric. `right_root`: each block is symmetric. `vector_moment`: positive.
All inputs are finite; a program needn't handle non-finite values. No bound on the sum of `lengths` or of `key_mask` on one device may be relied on, other than what follows from the above.
Results may differ from a plain program's by a relative error of at most 0.012.
The roundings to bfloat16 on the way count: a program that leaves them out, or rounds other values in their place, can miss the bound.
Values may be sent and summed in bfloat16 or wider, within the bound.
No kernel may reach another device: no remote copies, remote signals or barrier semaphores. Data moves between devices by JAX's collectives and lax.ppermute only.
A program may use at most 256 MiB of HBM per device.

v0:
```python
import math

import jax
import jax.numpy as jnp
from jax import lax
from jax.sharding import PartitionSpec as P

D = 768
H = 12
HD = 64
FF = 3072


highest = lax.Precision.HIGHEST
norm_eps = 1e-12
learning_rate = 0.03
vector_rate = 0.2
stat_decay = 0.5
slow_decay = 0.9


def layer_norm(inputs, norm_gain, norm_shift):
    centre = jnp.mean(inputs, axis=-1, keepdims=True)
    offset = inputs - centre
    spread = lax.rsqrt(jnp.mean(offset * offset, axis=-1, keepdims=True) + norm_eps)
    normed = offset * spread
    return (normed * norm_gain + norm_shift, normed, spread)


def norm_back(upstream, normed, spread, norm_gain):
    scaled = upstream * norm_gain
    within = (
        scaled
        - jnp.mean(scaled, axis=-1, keepdims=True)
        - normed * jnp.mean(scaled * normed, axis=-1, keepdims=True)
    )
    return (within * spread, jnp.sum(upstream * normed, 0), jnp.sum(upstream, 0))


def gelu_parts(pre_active):
    cumulative = 0.5 * (1.0 + lax.erf(pre_active * (1.0 / math.sqrt(2.0))))
    density = jnp.exp(-0.5 * pre_active * pre_active) * (1.0 / math.sqrt(2.0 * math.pi))
    return (pre_active * cumulative, cumulative + pre_active * density)


def contract_rows(left_side, right_side):
    return lax.dot_general(
        left_side, right_side, (((0,), (0,)), ((), ())), preferred_element_type=jnp.float32
    )


def contract_cols(left_side, right_side):
    return lax.dot_general(
        left_side, right_side, (((1,), (1,)), ((), ())), preferred_element_type=jnp.float32
    )


def token_sum(values_low):
    return jnp.sum(values_low, axis=0, dtype=jnp.float32)


def per_device(
    tokens,
    cotangent,
    lengths,
    key_mask,
    type_ids,
    weights,
    vectors,
    master,
    slow_weights,
    left_stats,
    right_stats,
    left_root,
    right_root,
    vector_master,
    vector_moment,
    slow_vectors,
):
    row_count = tokens.shape[0]
    seq_count = lengths.shape[0]
    seq_span = row_count // seq_count
    score_scale = HD ** (-0.5)
    full_weights, full_vectors = (
        lax.all_gather(weights, "dp", axis=1, tiled=True),
        lax.all_gather(vectors, "dp", axis=0, tiled=True),
    )
    vector_table = full_vectors.astype(jnp.float32)

    def segment(slot_index):
        return vector_table[slot_index * D : (slot_index + 1) * D]

    type_zero, type_one = (segment(0), segment(1))
    gain_one, shift_one = (segment(2), segment(3))
    query_bias, value_bias, out_bias = (segment(4), segment(5), segment(6))
    gain_two, shift_two, down_bias = (segment(7), segment(8), segment(9))
    up_bias = vector_table[10 * D : 10 * D + FF]
    is_region = (type_ids == 1)[:, None]
    embedded = tokens.astype(jnp.float32) + jnp.where(is_region, type_one, type_zero)
    embedded_low = embedded.astype(jnp.bfloat16)
    qkv_bias = jnp.concatenate([query_bias, jnp.zeros((D,), jnp.float32), value_bias])
    qkv_low = (
        jnp.dot(embedded_low, full_weights[:, : 3 * D], preferred_element_type=jnp.float32)
        + qkv_bias
    ).astype(jnp.bfloat16)
    query_heads = qkv_low[:, :D].reshape(seq_count, seq_span, H, HD)
    key_heads = qkv_low[:, D : 2 * D].reshape(seq_count, seq_span, H, HD)
    value_heads = qkv_low[:, 2 * D :].reshape(seq_count, seq_span, H, HD)
    position = jnp.arange(seq_span)
    allowed = (position[None, :] < lengths[:, None]) & (
        (key_mask.reshape(seq_count, seq_span) == 1) | (position[None, :] == 0)
    )
    key_keep = allowed[:, None, None, :]

    def score_block():
        raw_scores = (
            jnp.einsum(
                "sqhd,skhd->shqk", query_heads, key_heads, preferred_element_type=jnp.float32
            )
            * score_scale
        )
        return jnp.where(key_keep, raw_scores, -1e30)

    scores = score_block()
    peak_score = jnp.max(scores, axis=-1, keepdims=True)
    powers = jnp.exp(scores - peak_score)
    totals = jnp.sum(powers, axis=-1, keepdims=True)
    log_total = peak_score + jnp.log(totals)
    attn_probs = (powers / totals).astype(jnp.bfloat16)
    context = jnp.einsum(
        "shqk,skhd->sqhd", attn_probs, value_heads, preferred_element_type=jnp.float32
    )
    context = context.reshape(row_count, D).astype(jnp.bfloat16)
    branch = (
        jnp.dot(context, full_weights[:, 3 * D : 4 * D], preferred_element_type=jnp.float32)
        + out_bias
    )
    normed_one, unit_one, spread_one = layer_norm(embedded + branch, gain_one, shift_one)
    normed_low = normed_one.astype(jnp.bfloat16)
    pre_active = (
        jnp.dot(normed_low, full_weights[:, 4 * D : 4 * D + FF], preferred_element_type=jnp.float32)
        + up_bias
    )
    active, slope_gelu = gelu_parts(pre_active)
    active_low = active.astype(jnp.bfloat16)
    feed_out = contract_cols(active_low, full_weights[:, 4 * D + FF :]) + down_bias
    final_norm, unit_two, spread_two = layer_norm(normed_one + feed_out, gain_two, shift_two)
    layer_out = final_norm.astype(jnp.bfloat16)
    back_weights = lax.all_gather(weights, "dp", axis=1, tiled=True)
    upstream = cotangent.astype(jnp.float32)
    grad_second, grad_gain_two, grad_shift_two = norm_back(upstream, unit_two, spread_two, gain_two)
    feed_low = grad_second.astype(jnp.bfloat16)
    grad_down_bias = token_sum(feed_low)
    grad_down = contract_rows(feed_low, active_low)
    grad_active = jnp.dot(
        feed_low, back_weights[:, 4 * D + FF :], preferred_element_type=jnp.float32
    )
    grad_pre = (grad_active * slope_gelu).astype(jnp.bfloat16)
    grad_up_bias = token_sum(grad_pre)
    grad_up = contract_rows(normed_low, grad_pre)
    grad_normed = grad_second + contract_cols(grad_pre, back_weights[:, 4 * D : 4 * D + FF])
    grad_first, grad_gain_one, grad_shift_one = norm_back(
        grad_normed, unit_one, spread_one, gain_one
    )
    branch_low = grad_first.astype(jnp.bfloat16)
    grad_out_bias = token_sum(branch_low)
    grad_out = contract_rows(context, branch_low)
    grad_context = contract_cols(branch_low, back_weights[:, 3 * D : 4 * D]).astype(jnp.bfloat16)
    grad_context = grad_context.reshape(seq_count, seq_span, H, HD)
    probs_full = jnp.exp(score_block() - log_total)
    grad_probs = jnp.einsum(
        "sqhd,skhd->shqk", grad_context, value_heads, preferred_element_type=jnp.float32
    )
    row_inner = jnp.sum(probs_full * grad_probs, axis=-1, keepdims=True)
    grad_scores = (probs_full * (grad_probs - row_inner)).astype(jnp.bfloat16)
    grad_query = (
        jnp.einsum("shqk,skhd->sqhd", grad_scores, key_heads, preferred_element_type=jnp.float32)
        * score_scale
    )
    grad_key = (
        jnp.einsum("shqk,sqhd->skhd", grad_scores, query_heads, preferred_element_type=jnp.float32)
        * score_scale
    )
    grad_value = jnp.einsum(
        "shqk,sqhd->skhd", attn_probs, grad_context, preferred_element_type=jnp.float32
    )
    grad_mixed = jnp.concatenate(
        [
            grad_query.reshape(row_count, D),
            grad_key.reshape(row_count, D),
            grad_value.reshape(row_count, D),
        ],
        axis=1,
    ).astype(jnp.bfloat16)
    grad_query_bias = token_sum(grad_mixed[:, :D])
    grad_value_bias = token_sum(grad_mixed[:, 2 * D :])
    grad_qkv = contract_rows(embedded_low, grad_mixed)
    input_grad = grad_first + contract_cols(grad_mixed, back_weights[:, : 3 * D])
    grad_type_one = jnp.sum(jnp.where(is_region, input_grad, 0.0), 0)
    grad_type_zero = jnp.sum(jnp.where(is_region, 0.0, input_grad), 0)
    weight_sums = jnp.concatenate([grad_qkv, grad_out, grad_up, grad_down], axis=1)
    vector_sums = jnp.concatenate(
        [
            grad_type_zero,
            grad_type_one,
            grad_gain_one,
            grad_shift_one,
            grad_query_bias,
            grad_value_bias,
            grad_out_bias,
            grad_gain_two,
            grad_shift_two,
            grad_down_bias,
            grad_up_bias,
        ]
    )
    owned_grad, owned_vector = (
        lax.psum_scatter(weight_sums, ("dp", "opt"), scatter_dimension=1, tiled=True),
        lax.psum_scatter(vector_sums, ("dp", "opt"), scatter_dimension=0, tiled=True),
    )
    left_new = stat_decay * left_stats + (1.0 - stat_decay) * jnp.dot(
        owned_grad, owned_grad.T, precision=highest
    )
    right_new = stat_decay * right_stats + (1.0 - stat_decay) * jnp.dot(
        owned_grad.T, owned_grad, precision=highest
    )
    steered = jnp.dot(
        jnp.dot(left_root, owned_grad, precision=highest), right_root, precision=highest
    )
    master_new = master - learning_rate * steered
    slow_new = slow_decay * slow_weights + (1.0 - slow_decay) * master_new
    weights_new = master_new.astype(jnp.bfloat16)
    moment_new = stat_decay * vector_moment + (1.0 - stat_decay) * owned_vector * owned_vector
    vector_master_new = vector_master - vector_rate * owned_vector / (jnp.sqrt(moment_new) + 1e-08)
    slow_vectors_new = slow_decay * slow_vectors + (1.0 - slow_decay) * vector_master_new
    vectors_new = vector_master_new.astype(jnp.bfloat16)
    return (
        layer_out,
        input_grad,
        owned_grad,
        left_new,
        right_new,
        master_new,
        slow_new,
        weights_new,
        owned_vector,
        moment_new,
        vector_master_new,
        slow_vectors_new,
        vectors_new,
    )


def solution(mesh):
    in_specs = (
        P(("dp", "opt"), None),
        P(("dp", "opt"), None),
        P(("dp", "opt")),
        P(("dp", "opt")),
        P(("dp", "opt")),
        P(None, "dp"),
        P("dp"),
        P(None, ("dp", "opt")),
        P(None, ("dp", "opt")),
        P(("dp", "opt"), None),
        P(("dp", "opt"), None),
        P(("dp", "opt"), None),
        P(("dp", "opt"), None),
        P(("dp", "opt")),
        P(("dp", "opt")),
        P(("dp", "opt")),
    )
    out_specs = (
        P(("dp", "opt"), None),
        P(("dp", "opt"), None),
        P(None, ("dp", "opt")),
        P(("dp", "opt"), None),
        P(("dp", "opt"), None),
        P(None, ("dp", "opt")),
        P(None, ("dp", "opt")),
        P(None, ("dp", "opt")),
        P(("dp", "opt")),
        P(("dp", "opt")),
        P(("dp", "opt")),
        P(("dp", "opt")),
        P(("dp", "opt")),
    )
    return jax.shard_map(
        per_device, mesh=mesh, in_specs=in_specs, out_specs=out_specs, check_vma=False
    )
```

profile of v0, /device:TPU:0, one launch (start us, length us, event | category | flops | bytes accessed | tf_op | source)
XLA Modules:
  0.0 636.4 jit_solution(1807470500207263623)
XLA Ops:
  7.2 0.7 all-gather.2.cloned.1.call-update
  8.0 0.7 broadcast_compare_fusion
  8.7 1.2 dynamic-slice
  10.6 0.9 dynamic-update-slice
  11.5 65.3 %all-reduce = bf16[10752]{0:T(1024)(128)(2,1)S(1)} all-reduce(bf16[10752]{0:T(1024)(128)(2,1)S(1)} %dynamic-update-slice), channel_id=1, replica_groups=mesh['dp'=16,'opt'=2] {'dp'}, use_global_device_ids=true, to_apply=%add | all-reduce | flops 10752 | bytes 43008
  76.8 0.7 fusion.56
  77.6 0.7 broadcast_compare_fusion.1
  78.3 45.8 %all-gather.2.cloned.1.call-done = bf16[768,9216]{0,1:T(8,128)(2,1)} async-done(((bf16[768,576]{0,1:T(8,128)(2,1)}), bf16[768,9216]{0,1:T(8,128)(2,1)}) %all-gather.2.cloned.1.call-update) | async-done | bytes 14155792 | tf_op jit(solution)/shard_map/all_gather | solution.py:85
  124.1 6.5 %add_convert_fusion = bf16[1024,2304]{1,0:T(8,128)(2,1)S(1)} fusion(f32[2304]{0:T(1024)S(1)} %pad_maximum_fusion.1, bf16[768,9216]{0,1:T(8,128)(2,1)} %all-gather.2.cloned.1.call-done, bf16[1024,768]{1,0:T(8,128)(2,1)} %param.16, f32[768]{0:T(1024)S(1)} %get-tuple-element.83, f32[768]{0:T(1024)S(1)} %get-tuple-element.82, ...), kind=kOutput, calls=%fused_computation.18 | convolution fusion | flops 3631742976 | bytes 9846784 | tf_op jit(solution)/shard_map/dot_general | solution.py:103
  130.5 2.3 fusion.70
  132.8 2.6 copy.66
  135.4 3.9 reshape.156
  139.3 2.6 copy.67
  141.9 3.9 reshape.157
  145.7 4.8 fusion.7
  150.6 3.9 fusion.6
  154.5 0.7 copy-done.1
  155.1 5.3 divide_convert_fusion
  160.4 2.6 copy.65
  163.0 4.1 reshape.155
  167.1 4.3 fusion.35
  171.4 1.2 copy.72
  173.0 4.0 fusion.73
  177.0 0.5 multiply_reduce_fusion.4
  177.6 11.6 %multiply_convert_fusion.1 = (bf16[1024,3072]{1,0:T(8,128)(2,1)S(1)}, f32[1024,3072]{1,0:T(8,128)}) fusion(f32[3072]{0:T(1024)S(1)} %slice.91, bf16[768,9216]{0,1:T(8,128)(2,1)} %all-gather.2.cloned.1.call-done, f32[1024,768]{1,0:T(8,128)S(1)} %get-tuple-element.89, f32[768]{0:T(1024)S(1)} %get-tuple-element.80, f32[768]{0:T(1024)S(1)} %get-tuple-element.79, ...), kind=kOutput, calls=%fused_computation.12 | convolution fusion | flops 4854644736 | bytes 26765312 | tf_op jit(solution)/shard_map/dot_general | solution.py:141
  189.1 10.1 %fusion.74 = (f32[1024]{0:T(1024)S(1)}, f32[1024,768]{1,0:T(8,128)S(1)}) fusion(f32[768]{0:T(1024)S(1)} %get-tuple-element.78, bf16[1024,3072]{1,0:T(8,128)(2,1)S(1)} %get-tuple-element.90, bf16[768,9216]{0,1:T(8,128)(2,1)} %all-gather.2.cloned.1.call-done, f32[768]{0:T(1024)S(1)} %get-tuple-element.80, f32[768]{0:T(1024)S(1)} %get-tuple-element.79, ...), kind=kOutput, calls=%fused_computation.136 | convolution fusion | flops 4837342208 | bytes 17323008 | tf_op jit(solution)/shard_map/dot_general | solution.py:53
  199.3 0.5 multiply_reduce_fusion.3
  199.8 0.9 copy-done.14
  200.6 1.7 fusion.21
  202.4 2.7 convert_reduce_fusion.2
  205.1 0.7 copy-done.34
  205.8 10.9 %convert_reduce_fusion = (f32[3072]{0:T(1024)S(1)}, bf16[1024,3072]{1,0:T(8,128)(2,1)S(1)}) fusion(f32[1024,3072]{1,0:T(8,128)S(1)} %copy-done.34, f32[3072]{0:T(1024)S(1)} %slice.91, bf16[768,9216]{0,1:T(8,128)(2,1)} %all-gather.2.cloned.1.call-done, f32[1024,768]{1,0:T(8,128)S(1)} %get-tuple-element.67), kind=kOutput, calls=%fused_computation.8 | convolution fusion | flops 4873516032 | bytes 26763264 | tf_op jit(solution)/shard_map/dot_general | solution.py:155
  216.7 10.6 %multiply_reduce_fusion.1 = (f32[768]{0:T(1024)S(1)}, f32[1024]{0:T(1024)S(1)}, f32[1024]{0:T(1024)S(1)}, f32[768]{0:T(1024)S(1)}, f32[1024,768]{1,0:T(8,128)S(1)}) fusion(f32[1024,768]{1,0:T(8,128)S(1)} %get-tuple-element.89, f32[1024]{0:T(1024)S(1)} %add_rsqrt_fusion.1, f32[1024]{0:T(1024)S(1)} %broadcast_multiply_fusion.5, ...), kind=kOutput, calls=%fused_computation.41 | convolution fusion | flops 4839698432 | bytes 20472832 | tf_op jit(solution)/shard_map/dot_general | solution.py:53
  227.4 1.2 convert_reduce_fusion.3
  228.6 1.7 copy-done.17
  230.3 3.9 convolution_convert_fusion.2
  234.2 2.6 copy.73
  236.7 3.8 reshape.158
  240.6 5.4 fusion.36
  246.0 10.2 %multiply_reduce_fusion = (f32[4,12,256]{2,1,0:T(8,128)S(1)}, f32[4,12,256,256]{2,3,1,0:T(8,128)}) fusion(f32[4,12,256,256]{2,3,1,0:T(8,128)} %copy-done.1, f32[4,12,256]{2,1,0:T(8,128)S(1)} %log_add_fusion, pred[4,256]{1,0:T(4,128)(4,1)S(1)} %fusion.56, bf16[4,256,12,64]{1,0,3,2:T(4,128)(2,1)S(1)} %copy-done.6, bf16[4,256,12,64]{1,0,3,2:T(4,128)(2,1)S(1)} %copy-done.4), kind=kOutput, calls=%fused_computation.10 | convolution fusion | flops 418369536 | bytes 28410880 | tf_op jit(solution)/shard_map/sqhd,skhd->shqk/dot_general | solution.py:171
  256.3 8.3 %multiply_convert_fusion = bf16[4,12,256,256]{2,3,1,0:T(8,128)(2,1)S(1)} fusion(f32[4,12,256,256]{2,3,1,0:T(8,128)} %get-tuple-element.96, f32[4,12,256,256]{2,3,1,0:T(8,128)S(1)} %bitcast.60, f32[4,12,256]{2,1,0:T(8,128)S(1)} %get-tuple-element.95, f32[4,12,256]{2,1,0:T(8,128)S(1)} %log_add_fusion, pred[4,256]{1,0:T(4,128)(4,1)S(1)} %fusion.56), kind=kLoop, calls=%fused_computation.9 | loop fusion | flops 18874368 | bytes 31556608 | tf_op jit(solution)/shard_map/convert_element_type | solution.py:175
  264.6 2.0 fusion.38
  266.6 1.0 fusion.37
  267.6 0.9 copy-done.3
  268.5 11.2 %fusion.64 = f32[768,3072]{1,0:T(8,128)} fusion(bf16[1024,3072]{1,0:T(8,128)(2,1)} %copy-done.13, f32[1024,768]{1,0:T(8,128)S(1)} %copy-done.3, f32[768]{0:T(1024)S(1)} %get-tuple-element.80, f32[768]{0:T(1024)S(1)} %get-tuple-element.79, f32[1024]{0:T(1024)S(1)} %add_rsqrt_fusion.1, f32[1024]{0:T(1024)S(1)} %broadcast_multiply_fusion.5), kind=kOutput, calls=%fused_computation.130 | convolution fusion | flops 4835770368 | bytes 18888704 | tf_op jit(solution)/shard_map/dot_general | solution.py:47
  279.7 8.2 %fusion.61 = f32[768,3072]{1,0:T(8,128)} fusion(bf16[1024,3072]{1,0:T(8,128)(2,1)S(1)} %bitcast.78, f32[1024,768]{1,0:T(8,128)S(1)} %copy-done.16), kind=kOutput, calls=%fused_computation.127 | convolution fusion | flops 4832624640 | bytes 18874368 | tf_op jit(solution)/shard_map/dot_general | solution.py:47
  287.9 2.8 fusion.58
  290.7 1.2 copy.84
  292.3 1.2 copy.81
  293.9 1.2 copy.78
  295.8 0.9 copy-done.11
  296.8 2.1 copy-done.24
  298.8 6.5 %fusion.53 = f32[768,2304]{1,0:T(8,128)} fusion(bf16[1024,2304]{0,1:T(8,128)(2,1)S(1)} %constant_dynamic-update-slice_fusion, bf16[1024,768]{1,0:T(8,128)(2,1)S(1)} %copy-done.32, f32[768]{0:T(1024)S(1)} %get-tuple-element.83, f32[768]{0:T(1024)S(1)} %get-tuple-element.82, pred[1024]{0:T(1024)(128)(4,1)S(1)} %broadcast_compare_fusion.1), kind=kOutput, calls=%fused_computation.90 | convolution fusion | flops 3627024384 | bytes 13376512 | tf_op jit(solution)/shard_map/dot_general | solution.py:47
  305.3 19.2 %pad_maximum_fusion = f32[768,9216]{1,0:T(8,128)} fusion(f32[768,3072]{1,0:T(8,128)} %fusion.61, f32[768,3072]{1,0:T(8,128)} %fusion.64, f32[768,768]{1,0:T(8,128)} %fusion.58, f32[768,2304]{1,0:T(8,128)} %fusion.53), kind=kLoop, calls=%fused_computation | loop fusion | flops 21233664 | bytes 56623104 | tf_op jit(solution)/shard_map/concatenate | solution.py:201
  324.5 27.8 %copy.92 = f32[768,9216]{0,1:T(8,128)} copy(f32[768,9216]{1,0:T(8,128)} %pad_maximum_fusion) | data formatting | bytes 56623104
  352.3 10.8 %select_reduce_fusion = (f32[768]{0:T(1024)S(1)}, f32[768]{0:T(1024)S(1)}, f32[1024,768]{1,0:T(8,128)}) fusion(pred[1024]{0:T(1024)(128)(4,1)S(1)} %broadcast_compare_fusion.1, f32[1024,768]{1,0:T(8,128)} %copy-done.17, bf16[1024,2304]{0,1:T(8,128)(2,1)} %copy-done.24, bf16[768,9216]{0,1:T(8,128)(2,1)} %all-gather.2.cloned.1.call-done), kind=kOutput, calls=%fused_computation.42 | convolution fusion | flops 3627809280 | bytes 14556160 | tf_op jit(solution)/shard_map/dot_general | solution.py:53
  363.8 38.8 %all-reduce.1 = f32[10752]{0:T(1024)S(1)} all-reduce(f32[10752]{0:T(1024)S(1)} %constant_dynamic-update-slice_fusion.6), channel_id=3, replica_groups=mesh['dp'=16,'opt'=2] {'dp','opt'}, use_global_device_ids=true, to_apply=%region_23.24.clone | all-reduce | flops 10752 | bytes 86016
  402.6 0.7 fusion.67
  403.3 0.6 multiply_add_fusion.2
  403.9 210.6 %reduce-scatter.4.cloned.1.call-done = f32[288,768]{1,0:T(8,128)} async-done(((f32[9216,768]{1,0:T(8,128)}), f32[288,768]{1,0:T(8,128)}) %reduce-scatter.4.cloned.1.call-update) | async-done | bytes 884752
  614.5 3.7 fusion.75
  618.3 5.6 add_multiply_fusion.1
  623.9 2.3 fusion.50
  626.2 3.2 fusion.71
  (114 shorter events, 2.7 us)
Async XLA Ops:
  7.2 607.3 %copy-start = (f32[768,768]{1,0:T(8,128)S(1)}, f32[768,768]{1,0:T(8,128)}, u32[]{:S(2)}) copy-start(f32[768,768]{1,0:T(8,128)} %param.27) | copy-start | bytes 7077892
  7.2 116.9 %all-gather.2.cloned.1.call-start = ((), (), s32[]{:S(2)}) async-start(), calls=%async_computation.1 | async-start | bytes 15040512 | tf_op jit(solution)/shard_map/all_gather | solution.py:85
  7.9 606.6 %reduce-scatter.4.cloned.1.call-start = ((), (), s32[]{:S(2)}) async-start(), calls=%async_computation.2 | async-start | bytes 29196288
  150.6 4.6 copy-start.1
  171.3 1.6 copy-start.31
  172.9 4.1 copy-start.20
  177.0 50.3 %copy-start.2 = (f32[1024,768]{1,0:T(8,128)}, f32[1024,768]{1,0:T(8,128)S(1)}, u32[]{:S(2)}) copy-start(f32[1024,768]{1,0:T(8,128)S(1)} %get-tuple-element.89) | copy-start | bytes 9437188
  189.1 10.1 %copy-start.33 = (bf16[1024,3072]{1,0:T(8,128)(2,1)}, bf16[1024,3072]{1,0:T(8,128)(2,1)S(1)}, u32[]{:S(2)}) copy-start(bf16[1024,3072]{1,0:T(8,128)(2,1)S(1)} %get-tuple-element.90) | copy-start | bytes 18874372
  199.2 1.4 copy-start.14
  200.6 5.1 copy-start.34
  205.1 11.6 %copy-start.15 = (f32[1024,768]{1,0:T(8,128)}, f32[1024,768]{1,0:T(8,128)S(1)}, u32[]{:S(2)}) copy-start(f32[1024,768]{1,0:T(8,128)S(1)} %get-tuple-element.67) | copy-start | bytes 9437188
  216.7 10.7 %copy-start.13 = (bf16[1024,3072]{1,0:T(8,128)(2,1)}, bf16[1024,3072]{1,0:T(8,128)(2,1)S(1)}, u32[]{:S(2)}) copy-start(bf16[1024,3072]{1,0:T(8,128)(2,1)S(1)} %get-tuple-element.100) | copy-start | bytes 18874372
  228.6 1.7 copy-start.17
  240.6 5.4 copy-start.4
  240.6 5.4 copy-start.6
  240.6 15.7 %slice-start = ((s8[12582912]{0:T(1024)(128)(4,1)}), s8[4194304]{0:T(1024)(128)(4,1)S(1)}, s32[]{:S(2)}) async-start(s8[12582912]{0:T(1024)(128)(4,1)} %bitcast.59), calls=%async_computation.3 | async-start | bytes 8388608
  246.0 10.2 %slice-start.1 = ((s8[12582912]{0:T(1024)(128)(4,1)}), s8[4194304]{0:T(1024)(128)(4,1)S(1)}, s32[]{:S(2)}) async-start(s8[12582912]{0:T(1024)(128)(4,1)} %bitcast.59), calls=%async_computation.4 | async-start | bytes 8388608
  246.0 10.2 %slice-start.2 = ((s8[12582912]{0:T(1024)(128)(4,1)}), s8[4194304]{0:T(1024)(128)(4,1)S(1)}, s32[]{:S(2)}) async-start(s8[12582912]{0:T(1024)(128)(4,1)} %bitcast.59), calls=%async_computation.5 | async-start | bytes 8388608
  256.3 8.3 %copy-start.7 = (bf16[4,256,12,64]{1,0,3,2:T(4,128)(2,1)S(1)}, bf16[4,256,12,64]{1,0,3,2:T(4,128)(2,1)}, u32[]{:S(2)}) copy-start(bf16[4,256,12,64]{1,0,3,2:T(4,128)(2,1)} %reshape.156) | copy-start | bytes 4718596
  264.6 2.0 copy-start.8
  266.6 1.9 copy-start.3
  266.6 13.1 %slice-start.3 = ((s8[6291456]{0:T(1024)(128)(4,1)}), s8[4194304]{0:T(1024)(128)(4,1)S(1)}, s32[]{:S(2)}) async-start(s8[6291456]{0:T(1024)(128)(4,1)} %bitcast.77), calls=%async_computation.6 | async-start | bytes 8388608
  268.5 11.2 %copy-start.16 = (f32[1024,768]{1,0:T(8,128)S(1)}, f32[1024,768]{1,0:T(8,128)}, u32[]{:S(2)}) copy-start(f32[1024,768]{1,0:T(8,128)} %copy-done.15) | copy-start | bytes 9437188
  268.5 11.2 %slice-start.4 = ((s8[6291456]{0:T(1024)(128)(4,1)}), s8[2097152]{0:T(1024)(128)(4,1)S(1)}, s32[]{:S(2)}) async-start(s8[6291456]{0:T(1024)(128)(4,1)} %bitcast.77), calls=%async_computation.7 | async-start | bytes 4194304
  279.7 8.2 %copy-start.18 = (f32[1024,768]{1,0:T(8,128)S(1)}, f32[1024,768]{1,0:T(8,128)}, u32[]{:S(2)}) copy-start(f32[1024,768]{1,0:T(8,128)} %copy-done.17) | copy-start | bytes 9437188
  279.7 8.2 %copy-start.21 = (bf16[96,8,4,256]{3,1,2,0:T(8,128)(2,1)S(1)}, bf16[96,8,4,256]{3,1,2,0:T(8,128)(2,1)}, u32[]{:S(2)}) copy-start(bf16[96,8,4,256]{3,1,2,0:T(8,128)(2,1)} %copy-done.20) | copy-start | bytes 4718596
  292.3 4.3 copy-start.9
  295.5 1.1 copy-start.11
  295.6 3.2 copy-start.32
  296.7 2.1 copy-start.24
  352.3 10.9 %copy-start.12 = (bf16[96,8,4,256]{3,1,2,0:T(8,128)(2,1)S(1)}, bf16[96,8,4,256]{3,1,2,0:T(8,128)(2,1)}, u32[]{:S(2)}) copy-start(bf16[96,8,4,256]{3,1,2,0:T(8,128)(2,1)} %copy-done.11) | copy-start | bytes 4718596
  352.3 11.1 %copy-start.10 = (bf16[96,8,4,256]{3,1,2,0:T(8,128)(2,1)S(1)}, bf16[96,8,4,256]{3,1,2,0:T(8,128)(2,1)}, u32[]{:S(2)}) copy-start(bf16[96,8,4,256]{3,1,2,0:T(8,128)(2,1)} %copy-done.9) | copy-start | bytes 4718596
  363.1 39.5 %copy-start.28 = (f32[336]{0:T(512)S(1)}, f32[336]{0:T(512)}, u32[]{:S(2)}) copy-start(f32[336]{0:T(512)} %param.29) | copy-start | bytes 4036
  363.1 39.5 %copy-start.29 = (f32[336]{0:T(512)S(1)}, f32[336]{0:T(512)}, u32[]{:S(2)}) copy-start(f32[336]{0:T(512)} %param.30) | copy-start | bytes 4036
  363.1 40.2 %copy-start.30 = (f32[336]{0:T(512)S(1)}, f32[336]{0:T(512)}, u32[]{:S(2)}) copy-start(f32[336]{0:T(512)} %param.31) | copy-start | bytes 4036
  403.3 220.6 %copy-start.27 = (f32[336]{0:T(512)}, f32[336]{0:T(512)S(1)}, u32[]{:S(2)}) copy-start(f32[336]{0:T(512)S(1)} %get-tuple-element.63) | copy-start | bytes 4036
  614.5 3.7 copy-start.5
  614.5 3.7 copy-start.19
  618.2 5.7 copy-start.25
  618.2 8.0 %copy-start.22 = (f32[768,288]{0,1:T(8,128)S(1)}, f32[768,288]{0,1:T(8,128)}, u32[]{:S(2)}) copy-start(f32[768,288]{0,1:T(8,128)} %param.24) | copy-start | bytes 2654212
  618.3 8.0 %copy-start.23 = (f32[768,288]{0,1:T(8,128)S(1)}, f32[768,288]{0,1:T(8,128)}, u32[]{:S(2)}) copy-start(f32[768,288]{0,1:T(8,128)} %param.23) | copy-start | bytes 2654212
  618.3 8.0 %copy-start.26 = (f32[288,288]{1,0:T(8,128)S(1)}, f32[288,288]{1,0:T(8,128)}, u32[]{:S(2)}) copy-start(f32[288,288]{1,0:T(8,128)} %param.28) | copy-start | bytes 995332
Sparse Core Ops, SparseCore 0:
  10.3 113.6 all-gather.1
  352.4 262.0 reduce-scatter.3
where the time goes:
time: 646 us; the launch traced here: 636 us
  waiting for transfers between devices  257 us (40%)
  matrix products  140 us (22%)
  blocking collectives  104 us (16%)
  local copies, waits for them, and re-layouts  72.7 us (11%)
  other arithmetic  47.3 us (7%)
  between operations  15.7 us (2%)
    unnamed x3, waiting for transfers between devices  211 us
    unnamed x2, blocking collectives  104 us
    all_gather x1, waiting for transfers between devices, per_device(): lax.all_gather(weights, 'dp', axis=1, tiled=True)  45.8 us
    unnamed x100, local copies, waits for them, and re-layouts  39.4 us
    dot_general x4, matrix products, contract_cols(): lax.dot_general(left_side, right_side, (((1,), (1,)), ((), ())), preferre...  35.4 us
    dot_general x4, matrix products, contract_rows(): lax.dot_general(left_side, right_side, (((0,), (0,)), ((), ())), preferre...  28.6 us
    concatenate x1, other arithmetic, per_device(): jnp.concatenate([grad_qkv, grad_out, grad_up, grad_down], axis=1)  19.2 us
  transfers between devices with their start and end apart: 2, of which 2 were waited for; matrix products, arithmetic and copies ran while one was open for 3% of the time, Pallas kernels for 0%

commit v1 on v0

v1 whole, which is shorter than its diff:
```python
import functools
import math

import jax
import jax.numpy as jnp
import numpy as np
from jax import lax
from jax.experimental import pallas as pl
from jax.experimental.pallas import tpu as pltpu
from jax.sharding import PartitionSpec as P

D = 768
H = 12
HD = 64
FF = 3072
WCOLS = 4 * D + 2 * FF
NVEC = 10 * D + FF

highest = lax.Precision.HIGHEST
norm_eps = 1e-12
learning_rate = 0.03
vector_rate = 0.2
stat_decay = 0.5
slow_decay = 0.9
f32 = jnp.float32
bf16 = jnp.bfloat16
AXES = ("dp", "opt")


def contract(left_side, right_side, left_dim, right_dim):
    return lax.dot_general(
        left_side, right_side, (((left_dim,), (right_dim,)), ((), ())), preferred_element_type=f32
    )


def block_index(z, y, c, x):
    return z * 8 + y * 4 + c * 2 + x


def permutation(move):
    pairs = []
    for b in range(32):
        z, y, c, x = b // 8, (b // 4) % 2, (b // 2) % 2, b % 2
        pairs.append((b, block_index(*move(z, y, c, x))))
    return pairs


Z_CYCLE = permutation(lambda z, y, c, x: ((2, 0, 3, 1)[z], y, c, x))
Z_CYCLE_BACK = permutation(lambda z, y, c, x: ((1, 3, 0, 2)[z], y, c, x))
Z_NEAR = permutation(lambda z, y, c, x: (z ^ 1, y, c, x))
Z_FAR = permutation(lambda z, y, c, x: (z ^ 2, y, c, x))
Z_MIDDLE = permutation(lambda z, y, c, x: ((0, 2, 1, 3)[z], y, c, x))
PLANE_A = permutation(lambda z, y, c, x: (z, 1 - y, c, x) if c == 0 else (z, y, c, 1 - x))
PLANE_B = permutation(lambda z, y, c, x: (z, y, c, 1 - x) if c == 0 else (z, 1 - y, c, x))
CORES = permutation(lambda z, y, c, x: (z, y, 1 - c, x))


def send(values, pairs):
    return lax.ppermute(values, AXES, pairs)


QUARTER_SLOT = np.array([[0, 1, 3, 2], [1, 0, 3, 2], [1, 3, 0, 2], [1, 3, 2, 0]])


def unit_of(flag):
    return flag[0, 0]


class Ring:
    def __init__(self):
        dp = lax.axis_index("dp")
        self.z, self.y, self.c = dp // 4, (dp // 2) % 2, dp % 2
        self.x = lax.axis_index("opt")
        slots = [self.number([int(v) for v in QUARTER_SLOT[:, q]]) for q in range(4)]
        self.place = jnp.stack([self.y, self.c, self.x, self.z] + slots).astype(jnp.int32)

    def number(self, values):
        out = values[3]
        for z in (2, 1, 0):
            out = jnp.where(self.z == z, values[z], out)
        return out

    def pick(self, table, *choices):
        return self.number([choices[k] for k in table])

    def gather_early(self, weights, vectors):
        rows, entries = weights.shape[1] // 2, vectors.shape[0] // 2
        own = lax.dynamic_slice_in_dim(weights, self.x * rows, rows, 1).T
        few = lax.dynamic_slice_in_dim(vectors, self.x * entries, entries, 0)
        few = jnp.pad(few, (0, D - entries))[None, :]
        slab = jnp.where(jnp.arange(16)[:, None] == self.z, few, 0).astype(bf16)

        def merge(old, new):
            return jnp.where(old == 0, new, old)

        got = send(jnp.concatenate([own, slab]), Z_CYCLE)
        side = send(own, PLANE_A)
        pair = jnp.stack([own, side])
        across = send(pair, PLANE_B)
        half = jnp.concatenate([pair, across])
        slot_a = [half, send(half, CORES)]
        one, slab = got[:rows], merge(slab, got[rows:])
        got = send(jnp.concatenate([self.pick((0, 1, 1, 0), own, one), slab]), Z_NEAR)
        far = send(slab, Z_FAR)
        middle = send(own, Z_MIDDLE)
        two, slab = got[:rows], merge(merge(slab, got[rows:]), far)
        block = jnp.concatenate([self.pick((0, 1, 0, 1), one, two), slab])
        pair = jnp.stack([block, send(block, PLANE_A)])
        three = send(middle, Z_NEAR)
        slot_c = self.pick((1, 0, 1, 0), one, two)
        slot_d = self.pick((1, 0, 0, 1), middle, three)
        across = send(pair, PLANE_B)
        slot_b = [pair, across, send(pair, CORES), send(across, CORES)]
        own = jnp.stack([slot_c, slot_d])
        self.late = jnp.stack([own, send(own, PLANE_A)])
        slabs = jnp.stack([v[k, rows : rows + 4, :entries] for v, k in self.eight(slot_b)])
        owned = jnp.swapaxes(self.ordered(slabs.astype(f32)), 0, 1)
        return slot_a, slot_b, owned.reshape(-1)

    @staticmethod
    def eight(slot):
        return [(slot[0], 0), (slot[0], 1), (slot[1], 0), (slot[1], 1), (slot[2], 0), (slot[2], 1), (slot[3], 0), (slot[3], 1)]

    def gather_late(self, flag):
        across = send(self.late, PLANE_B)
        swapped = send(self.late, CORES)
        across = across * unit_of(flag).astype(bf16)
        return [self.late, across, swapped, send(across, CORES)]

    def hits(self):
        return jnp.stack([block_place((self.y, self.c, self.x), who, k) for who in (0, 1) for k in range(4)])

    def ordered(self, pieces):
        hit = (jnp.arange(8)[:, None] == self.hits()[None, :]).reshape((8, 8) + (1,) * (pieces.ndim - 1))
        return jnp.sum(jnp.where(hit, pieces[None], 0.0), axis=1)

    def disordered(self, blocks):
        hit = (jnp.arange(8)[None, :] == self.hits()[:, None]).reshape((8, 8) + (1,) * (blocks.ndim - 1))
        return jnp.sum(jnp.where(hit, blocks[None], 0.0), axis=1)

    def reduction(self, keep, give):
        return Reduction(keep, give)

    def vector_reduction(self, vector_sums):
        pieces = self.disordered(jnp.swapaxes(vector_sums.reshape(4, 8, -1), 0, 1))
        kept, more = pieces[:4], pieces[4:]
        for pairs, count in ((CORES, 4), (PLANE_B, 2), (PLANE_A, 1)):
            if count < 4:
                kept, more = kept[:count], kept[count : 2 * count]
            kept = kept + unpack(send(pack(more), pairs), kept.shape[-1])
        kept = kept[0]
        for pairs in (Z_NEAR, Z_FAR):
            kept = kept + unpack(send(pack(kept), pairs), kept.shape[-1])
        return lax.dynamic_index_in_dim(kept, self.z, 0, False)

    def reduce_far(self, sum_one, sum_two):
        far = send(self.pick((1, 1, 0, 0), sum_one, sum_two).astype(bf16), Z_FAR).astype(f32)
        return sum_one + far, sum_two + far

    def reduce_tail(self, sum_zero, sum_one, sum_two, sum_three):
        rows = sum_zero.shape[0]
        done = []
        for here in (slice(0, rows // 2), slice(rows // 2, rows)):
            near = send(self.pick((1, 0, 1, 0), sum_zero[here], sum_three[here]).astype(bf16), Z_NEAR).astype(f32)
            zero, three = sum_zero[here] + near, sum_three[here] + near
            give = self.pick((0, 1, 2, 3), sum_one[here], three, zero, sum_two[here]).astype(bf16)
            last = send(give, Z_CYCLE_BACK).astype(f32)
            done.append(self.pick((0, 1, 2, 3), zero, sum_one[here], sum_two[here], three) + last)
        return jnp.concatenate(done)


class Reduction:
    def __init__(self, keep, give):
        self.keep = keep
        self.got = [send(give, CORES)]

    def have(self, here):
        total = self.keep[here].astype(f32)
        for got in self.got:
            total = total + got[here].astype(f32)
        return total

    def across(self, flag=None):
        give = self.have(slice(2, 4))
        if flag is not None:
            give = give * unit_of(flag)
        self.got.append(send(give.astype(bf16), PLANE_B))

    def side(self, flag=None):
        give = self.have(slice(1, 2))
        if flag is not None:
            give = give * unit_of(flag)
        self.got.append(send(give.astype(bf16), PLANE_A))

    def total(self):
        return self.have(0)

    def keep_after(self):
        return self.got[0]


class Plain:
    def __init__(self):
        self.place = jnp.asarray(np.array([0, 0, 0, 0, 0, 1, 2, 3]), jnp.int32)

    def gather_early(self, weights, vectors):
        turned = lax.all_gather(weights, "dp", axis=1, tiled=True).T
        blocks = turned.reshape(4, 8, -1, D)
        self.mine, self.theirs = (blocks[:, np.array(k)] for k in ([0, 4, 1, 5], [2, 3, 6, 7]))
        entries = vectors.shape[0]
        tiles = -(-entries // 2048)
        padded = jnp.pad(vectors, (0, tiles * 2048 - entries)).reshape(tiles * 16, 128)
        gathered = lax.all_gather(padded, "dp", axis=0, tiled=True)
        gathered = gathered.reshape(-1, tiles * 2048)[:, :entries].reshape(-1).astype(f32)
        slot_b = [jnp.pad(v, ((0, 0), (0, 16), (0, 0))) for v in self.halves(1)]
        return [self.mine[0], self.theirs[0]], slot_b, gathered

    def halves(self, q):
        return [self.mine[q, :2], self.mine[q, 2:], self.theirs[q, :2], self.theirs[q, 2:]]

    def gather_late(self, flag):
        return [jnp.stack(both, axis=1) for both in zip(self.halves(2), self.halves(3))]

    def reduction(self, keep, give):
        return PlainReduction(keep, give)

    def vector_reduction(self, vector_sums):
        return lax.psum_scatter(vector_sums, AXES, scatter_dimension=0, tiled=True)

    def reduce_far(self, sum_one, sum_two):
        return sum_one, sum_two

    def reduce_tail(self, sum_zero, sum_one, sum_two, sum_three):
        sums = jnp.concatenate([sum_zero, sum_one, sum_two, sum_three])
        return lax.psum_scatter(sums, AXES, scatter_dimension=0, tiled=True).astype(f32)


class PlainReduction:
    def __init__(self, keep, give):
        self.pieces = jnp.concatenate([keep, give])

    def across(self, flag=None):
        pass

    def side(self, flag=None):
        pass

    def total(self):
        order = np.argsort(np.array([0, 4, 1, 5, 2, 3, 6, 7]))
        pieces = jnp.swapaxes(self.pieces[order], 0, 1)
        return pieces.reshape(pieces.shape[0], -1, D)

    def keep_after(self):
        return self.pieces


def pack(values):
    high = lax.reduce_precision(values, 8, 7)
    both = jnp.concatenate([high, values - high], axis=-1).astype(bf16)
    gaps = [(0, 0)] * (both.ndim - 2) + [(0, 12), (0, D - both.shape[-1])]
    return jnp.pad(both, gaps)


def unpack(packed, count):
    wide = packed[..., :4, :].astype(f32)
    return wide[..., :count] + wide[..., count : 2 * count]


VMEM_LIMIT = 60 * 1024 * 1024
whole = pl.BlockSpec(memory_space=pltpu.VMEM)
scalars = pl.BlockSpec(memory_space=pltpu.SMEM)
anywhere = pl.BlockSpec(memory_space=pl.ANY)
shape = jax.ShapeDtypeStruct
CHUNK = 256
CHUNKS = FF // CHUNK
Q = 3 * D
SPAN = 256
PART = 256
flag_shape = jax.ShapeDtypeStruct((8, 128), jnp.float32)


def call(kernel, outs, out_specs, scratch, flops, moved, *args, specs, name):
    return pl.pallas_call(
        kernel,
        out_shape=outs,
        in_specs=specs,
        out_specs=out_specs,
        scratch_shapes=scratch,
        compiler_params=pltpu.CompilerParams(vmem_limit_bytes=VMEM_LIMIT),
        cost_estimate=pl.CostEstimate(flops=flops, bytes_accessed=moved, transcendentals=0),
        name=name,
    )(*args)


def block_place(place, who, k):
    y, c, x = place[0], place[1], place[2]
    core = c if who == 0 else 1 - c
    first, second = k & 1, k >> 1
    to_y = jnp.where(core == 0, y ^ first, y ^ second)
    to_x = jnp.where(core == 0, x ^ second, x ^ first)
    return to_y * 4 + core * 2 + to_x


def block_rows(place, who, k, rows):
    return pl.ds(pl.multiple_of(block_place(place, who, k) * rows, math.gcd(rows, 16)), rows)


def begin(source, target, sem):
    copy = pltpu.make_async_copy(source, target, sem)
    copy.start()
    return copy


def slot_pieces(slots):
    out = []
    for slot, refs in enumerate(slots):
        if len(refs) == 2:
            out.append([(refs[k // 4], (k % 4,)) for k in range(8)])
        else:
            more = () if len(slots) == 2 or slot < 2 else (slot - 2,)
            out.append([(refs[k // 2], (k % 2,) + more) for k in range(8)])
    return out


def ingest(place, quarter, slots, into, sems):
    rows = into.shape[0] // 8
    targets = [into.at[block_rows(place, k // 4, k % 4, rows)] for k in range(8)]
    all_pieces = slot_pieces(slots)
    for slot, pieces in enumerate(all_pieces):

        @pl.when(place[4 + quarter] == slot)
        def _():
            for k, (ref, index) in enumerate(pieces):
                pltpu.make_async_copy(ref.at[(*index, pl.ds(0, rows))], targets[k], sems.at[k]).start()

    return [
        pltpu.make_async_copy(ref.at[(*index, pl.ds(0, rows))], targets[k], sems.at[k])
        for k, (ref, index) in enumerate(all_pieces[0])
    ]


def hand_out(place, source, keep, give, part, sems):
    rows = source.shape[0] // 8
    return [
        begin(source.at[block_rows(place, who, k, rows)], target.at[k, part], sems.at[4 * who + k])
        for who, target in ((1, give), (0, keep))
        for k in range(4)
    ]


def finish(*copies):
    for copy in copies:
        if isinstance(copy, (list, tuple)):
            finish(*copy)
        else:
            copy.wait()


def rows_of(i, step):
    return pl.ds(pl.multiple_of(i * step, step), step)


def loop(count, body):
    def step(i, carry):
        body(i)
        return carry

    lax.fori_loop(0, count, step, 0)


def column(row, width):
    return jnp.broadcast_to(row, (width, row.shape[1])).T


def embed(tokens, region, table):
    is_region = column(region, 128)[:, 0:1] > 0.5
    return tokens.astype(f32) + jnp.where(is_region, table[1:2, :], table[0:1, :])


def attend_kernel(
    place, a0, a1, b0, b1, b2, b3, tokens, region, allowed, table, bias,
    turned_out, context_out, spreads, flag,
    weights, low, turned, context_turned, context, mask, sems,
):
    copies = ingest(place, 0, ((a0, a1), (b0, b1, b2, b3)), weights, sems)
    flag[...] = jnp.ones_like(flag)
    rows = tokens.shape[0]

    def prepare(i):
        here = rows_of(i, PART)
        low[here, :] = embed(tokens[here, :], region[:, here], table[...]).astype(bf16)
        mask[here, :] = column(allowed[:, here], SPAN)

    loop(rows // PART, prepare)
    finish(copies)
    step = 384

    def project(i):
        here = rows_of(i, step)
        made = contract(weights[here, :], low[...], 1, 1) + column(bias[:, here], 128)[:, 0:1]
        made = made * jnp.where(i < D // step, HD ** (-0.5), 1.0)
        turned[here, :] = made.astype(bf16)

    loop(Q // step, project)
    sent = begin(turned, turned_out, sems.at[8])

    together = 8

    def units(i):
        places = []
        for j in range(together):
            u = i * together + j
            places.append((u % H, pl.multiple_of((u % H) * HD, HD), rows_of(u // H, SPAN)))
        scores = [
            contract(turned[pl.ds(D + at, HD), cols], turned[pl.ds(at, HD), cols], 0, 0)
            for _, at, cols in places
        ]
        probs = []
        for (h, at, cols), score in zip(places, scores):
            score = jnp.minimum(score, mask[cols, :])
            peak = jnp.max(score, axis=0, keepdims=True)
            powers = jnp.exp(score - peak)
            total = jnp.sum(powers, axis=0, keepdims=True)
            probs.append((powers * (1.0 / total)).astype(bf16))
            spreads[pl.ds(h, 1), cols] = peak + jnp.log(total)
        for (h, at, cols), prob in zip(places, probs):
            context_turned[pl.ds(at, HD), cols] = contract(turned[pl.ds(2 * D + at, HD), cols], prob, 1, 0).astype(bf16)

    loop(H * (rows // SPAN) // together, units)

    def turn(i):
        here = rows_of(i, 128)
        context[here, :] = context_turned[:, here].T

    loop(rows // 128, turn)
    finish(begin(context, context_out, sems.at[9]), sent)


def attend(place, pieces, tokens, region, allowed, table, bias):
    rows = tokens.shape[0]
    return call(
        attend_kernel,
        [shape((Q, rows), bf16), shape((rows, D), bf16), shape((H, rows), f32), flag_shape],
        [anywhere, anywhere, whole, whole],
        [
            pltpu.VMEM((Q, D), bf16),
            pltpu.VMEM((rows, D), bf16),
            pltpu.VMEM((Q, rows), bf16),
            pltpu.VMEM((D, rows), bf16),
            pltpu.VMEM((rows, D), bf16),
            pltpu.VMEM((rows, SPAN), f32),
            pltpu.SemaphoreType.DMA((10,)),
        ],
        2 * rows * Q * D + 4 * rows * 256 * D,
        20 << 20,
        place, *pieces, tokens, region, allowed, table, bias,
        specs=[scalars] + [anywhere] * 6 + [whole] * 5,
        name="attend",
    )


def normalise(inputs):
    centre = jnp.mean(inputs, axis=-1, keepdims=True)
    offset = inputs - centre
    spread = lax.rsqrt(jnp.mean(offset * offset, axis=-1, keepdims=True) + norm_eps)
    return offset * spread, spread


def normalise_back(scaled, unit, spread):
    return spread * (
        scaled
        - jnp.mean(scaled, axis=-1, keepdims=True)
        - unit * jnp.mean(scaled * unit, axis=-1, keepdims=True)
    )


def gelu_both(v):
    cumulative = 0.5 * (1.0 + lax.erf(v * math.sqrt(0.5)))
    density = jnp.exp(-0.5 * v * v) * (1.0 / math.sqrt(2.0 * math.pi))
    return v * cumulative, cumulative + v * density


def weight_chunk(weights, offset, i):
    return weights[pl.ds(pl.multiple_of(offset + i * CHUNK, CHUNK), CHUNK), :]


def three_sums(count, body, sums):
    zero = jnp.zeros((8, D), f32)

    def step(i, carry):
        made = body(i)
        return tuple(
            have + jnp.sum(more.reshape(-1, 8, D), axis=0) for have, more in zip(carry, made)
        )

    made = lax.fori_loop(0, count, step, (zero, zero, zero))
    for i in range(3):
        sums[i : i + 1, :] = jnp.sum(made[i], axis=0, keepdims=True)


STEP = 512


def feed_kernel(
    place, a0, a1, b0, b1, b2, b3, c0, c1, c2, c3, tokens_in, context_in, cotangent_in, region, table, up_bias,
    layer_out_to, slope_to, unit_one_to, spread_one, normed_low_to, grad_second_to, feed_low_to, sums, keep, give, rest, flag,
    weights, pre_a, pre_b, total, tokens, context, cotangent, active, slope, unit_one, normed_low, made, sems, more,
):
    rows = tokens.shape[0]
    early = [begin(context_in, context, more.at[0]), begin(tokens_in, tokens, more.at[1])]
    slots = ((a0, a1), (b0, b1, b2, b3), (c0, c1, c2, c3), (c0, c1, c2, c3))
    batches = [ingest(place, 1, slots, weights.at[pl.ds(0, Q)], sems.at[0])]
    flag[...] = jnp.ones_like(flag)
    up, down = D, D + FF
    finish(early, batches[0])
    batches.append(ingest(place, 2, slots, weights.at[pl.ds(Q, Q)], sems.at[1]))
    batches.append(ingest(place, 3, slots, weights.at[pl.ds(2 * Q, Q)], sems.at[2]))
    late = begin(cotangent_in, cotangent, more.at[2])

    def branch(i):
        here = rows_of(i, SPAN)
        total[here, :] = contract(context[here, :], weights[0:D, :], 1, 1)

    loop(rows // SPAN, branch)

    def first(i):
        here = rows_of(i, PART)
        unit, spread = normalise(embed(tokens[here, :], region[:, here], table[...]) + (total[here, :] + table[6:7, :]))
        unit_one[here, :] = unit
        spread_one[here, :] = jnp.broadcast_to(spread, (PART, 128))
        normed_low[here, :] = (unit * table[2:3, :] + table[3:4, :]).astype(bf16)

    loop(rows // PART, first)
    sent = [begin(unit_one, unit_one_to, more.at[3]), begin(normed_low, normed_low_to, more.at[4])]
    finish(batches[1])

    def gelu(pre, i, here):
        cols = rows_of(i, CHUNK)
        return gelu_both(pre[here, :] + up_bias[:, cols])

    def keep_gelu(made, i, here):
        cols = rows_of(i, CHUNK)
        active[here, cols] = made[0].astype(bf16)
        slope[here, cols] = made[1]

    everything = slice(None)

    def middle(t):
        before = jnp.maximum(2 * t - 1, 0)
        both = gelu(pre_b, before, everything)
        pre_a[...] = contract(normed_low[...], weight_chunk(weights, up, 2 * t), 1, 1)
        keep_gelu(both, before, everything)
        both = gelu(pre_a, 2 * t, everything)
        pre_b[...] = contract(normed_low[...], weight_chunk(weights, up, 2 * t + 1), 1, 1)
        keep_gelu(both, 2 * t, everything)

    loop(CHUNKS // 2, middle)

    def final(i):
        here = rows_of(i, PART)
        keep_gelu(gelu(pre_b, CHUNKS - 1, here), CHUNKS - 1, here)

    loop(rows // PART, final)
    sent.append(begin(slope, slope_to, more.at[6]))
    finish(batches[2])

    def add_down(i):
        here = rows_of(i, SPAN)
        total[here, :] = contract(active[here, :], weights[down : down + FF, :], 1, 0)

    loop(rows // SPAN, add_down)
    finish(late)

    def last(i):
        here = rows_of(i, PART)
        normed_one = unit_one[here, :] * table[2:3, :] + table[3:4, :]
        unit, spread = normalise(normed_one + (total[here, :] + table[9:10, :]))
        context[here, :] = (unit * table[7:8, :] + table[8:9, :]).astype(bf16)
        upstream = cotangent[here, :].astype(f32)
        grad = normalise_back(upstream * table[7:8, :], unit, spread)
        total[here, :] = grad
        low = grad.astype(bf16)
        tokens[here, :] = low
        return upstream * unit, upstream, low.astype(f32)

    three_sums(rows // PART, last, sums)
    sent += [
        begin(context, layer_out_to, more.at[7]),
        begin(total, grad_second_to, more.at[8]),
        begin(tokens, feed_low_to, more.at[9]),
    ]

    def weigh(i):
        here = rows_of(i, STEP)
        made[here, :] = contract(active[:, here], tokens[...], 0, 0).astype(bf16)

    loop(FF // STEP, weigh)
    finish(
        hand_out(place, made.at[pl.ds(D, Q)], keep, give, 0, sems.at[0]),
        begin(made.at[pl.ds(0, D)], rest, more.at[5]),
        sent,
    )


def feed(place, pieces, tokens, region, context, cotangent, table, up_bias):
    rows = tokens.shape[0]
    return call(
        feed_kernel,
        [
            shape((rows, D), bf16),
            shape((rows, FF), f32),
            shape((rows, D), f32),
            shape((rows, 128), f32),
            shape((rows, D), bf16),
            shape((rows, D), f32),
            shape((rows, D), bf16),
            shape((3, D), f32),
            shape((4, 1, Q // 8, D), bf16),
            shape((4, 1, Q // 8, D), bf16),
            shape((D, D), bf16),
            flag_shape,
        ],
        [anywhere] * 3 + [whole] + [anywhere] * 3 + [whole] + [anywhere] * 3 + [whole],
        [
            pltpu.VMEM((3 * Q, D), bf16),
            pltpu.VMEM((rows, CHUNK), f32),
            pltpu.VMEM((rows, CHUNK), f32),
            pltpu.VMEM((rows, D), f32),
            pltpu.VMEM((rows, D), bf16),
            pltpu.VMEM((rows, D), bf16),
            pltpu.VMEM((rows, D), bf16),
            pltpu.VMEM((rows, FF), bf16),
            pltpu.VMEM((rows, FF), f32),
            pltpu.VMEM((rows, D), f32),
            pltpu.VMEM((rows, D), bf16),
            pltpu.VMEM((FF, D), bf16),
            pltpu.SemaphoreType.DMA((3, 8)),
            pltpu.SemaphoreType.DMA((10,)),
        ],
        2 * rows * (3 * Q + FF) * D,
        50 << 20,
        place, *pieces, tokens, context, cotangent, region, table, up_bias,
        specs=[scalars] + [anywhere] * 13 + [whole] * 3,
        name="feed",
    )


def back_kernel(
    place, a0, a1, b0, b1, b2, b3, c0, c1, c2, c3, slope_in, grad_second_in, unit_one_in, feed_low_in, spread_one, table,
    grad_pre_to, grad_first_to, branch_low_to, grad_context_to, sums, flag,
    weights, pre_a, pre_b, total, slope, grad_pre, unit_one, feed_low, branch_low, grad_context, sems, more, arrived,
):
    rows = feed_low.shape[0]
    slots = ((a0, a1), (b0, b1, b2, b3), (c0, c1, c2, c3), (c0, c1, c2, c3))
    begin_low = begin(feed_low_in, feed_low, more.at[7])
    batches = [None] * 3
    batches[2] = ingest(place, 3, slots, weights.at[pl.ds(2 * Q, Q)], sems.at[2])
    batches[1] = ingest(place, 2, slots, weights.at[pl.ds(Q, Q)], sems.at[1])
    flag[...] = jnp.ones_like(flag)
    finish(begin_low, batches[1], batches[2])
    for i in range(CHUNKS):
        begin(slope_in.at[:, pl.ds(i * CHUNK, CHUNK)], slope.at[:, pl.ds(i * CHUNK, CHUNK)], arrived.at[i])
    loads = [begin(grad_second_in, total, more.at[1])]
    batches[0] = ingest(place, 1, slots, weights.at[pl.ds(0, Q)], sems.at[0])
    loads.append(begin(unit_one_in, unit_one, more.at[2]))
    up, down = D, D + FF

    def through(pre, i, here):
        cols = rows_of(i, CHUNK)
        return (pre[here, :] * slope[here, cols]).astype(bf16)

    def slope_here(i):
        cols = rows_of(i, CHUNK)
        pltpu.make_async_copy(slope_in.at[:, cols], slope.at[:, cols], arrived.at[i]).wait()

    everything = slice(None)

    def middle(t):
        before = jnp.maximum(2 * t - 1, 0)
        slope_here(2 * t)
        slope_here(2 * t + 1)
        low = through(pre_b, before, everything)
        pre_a[...] = contract(feed_low[...], weight_chunk(weights, down, 2 * t), 1, 1)
        grad_pre[:, rows_of(before, CHUNK)] = low
        low = through(pre_a, 2 * t, everything)
        pre_b[...] = contract(feed_low[...], weight_chunk(weights, down, 2 * t + 1), 1, 1)
        grad_pre[:, rows_of(2 * t, CHUNK)] = low

    loop(CHUNKS // 2, middle)

    def final(i):
        here = rows_of(i, PART)
        grad_pre[here, rows_of(CHUNKS - 1, CHUNK)] = through(pre_b, CHUNKS - 1, here)

    loop(rows // PART, final)
    sent = [begin(grad_pre, grad_pre_to, more.at[3])]
    finish(batches[0], loads)

    def add_up(i):
        here = rows_of(i, SPAN)
        total[here, :] += contract(grad_pre[here, :], weights[up : up + FF, :], 1, 0)

    loop(rows // SPAN, add_up)

    def last(i):
        here = rows_of(i, PART)
        upstream = total[here, :]
        unit = unit_one[here, :]
        grad = normalise_back(upstream * table[2:3, :], unit, spread_one[here, 0:1])
        total[here, :] = grad
        low = grad.astype(bf16)
        branch_low[here, :] = low
        return upstream * unit, upstream, low.astype(f32)

    three_sums(rows // PART, last, sums)
    sent += [begin(total, grad_first_to, more.at[4]), begin(branch_low, branch_low_to, more.at[5])]

    def through_out(i):
        here = rows_of(i, SPAN)
        grad_context[:, here] = contract(branch_low[here, :], weights[0:D, :], 1, 0).T.astype(bf16)

    loop(rows // SPAN, through_out)
    finish(begin(grad_context, grad_context_to, more.at[6]), sent)


def back(place, pieces, slope, grad_second, unit_one, feed_low, spread_one, table):
    rows = feed_low.shape[0]
    return call(
        back_kernel,
        [
            shape((rows, FF), bf16),
            shape((rows, D), f32),
            shape((rows, D), bf16),
            shape((D, rows), bf16),
            shape((3, D), f32),
            flag_shape,
        ],
        [anywhere] * 4 + [whole] * 2,
        [
            pltpu.VMEM((3 * Q, D), bf16),
            pltpu.VMEM((rows, CHUNK), f32),
            pltpu.VMEM((rows, CHUNK), f32),
            pltpu.VMEM((rows, D), f32),
            pltpu.VMEM((rows, FF), f32),
            pltpu.VMEM((rows, FF), bf16),
            pltpu.VMEM((rows, D), f32),
            pltpu.VMEM((rows, D), bf16),
            pltpu.VMEM((rows, D), bf16),
            pltpu.VMEM((D, rows), bf16),
            pltpu.SemaphoreType.DMA((3, 8)),
            pltpu.SemaphoreType.DMA((8,)),
            pltpu.SemaphoreType.DMA((CHUNKS,)),
        ],
        2 * rows * 3 * Q * D,
        45 << 20,
        place, *pieces, slope, grad_second, unit_one, feed_low, spread_one, table,
        specs=[scalars] + [anywhere] * 14 + [whole] * 2,
        name="back",
    )


def up_grad_kernel(
    place, rest, grad_pre_in, normed_low, branch_low, context,
    keep, give, up_sums, flag,
    grad_pre, made, sems, more,
):
    count = FF // STEP
    flag[...] = jnp.ones_like(flag)
    other = begin(rest, made.at[pl.ds(D + FF, D)], sems.at[2, 0])
    for i in [*range(count // 2, count), *range(count // 2)]:
        here = pl.ds(i * STEP, STEP)
        begin(grad_pre_in.at[:, here], grad_pre.at[:, here], more.at[i])

    def weigh(i):
        here = rows_of(i, STEP)
        pltpu.make_async_copy(grad_pre_in.at[:, here], grad_pre.at[:, here], more.at[i]).wait()
        made[pl.ds(pl.multiple_of(D + i * STEP, 256), STEP), :] = contract(grad_pre[:, here], normed_low[...], 0, 0).astype(bf16)
        up_sums[:, here] = jnp.sum(grad_pre[:, here].astype(f32), 0, keepdims=True)

    loop(count // 2, lambda i: weigh(count // 2 + i))
    finish(other)
    copies = hand_out(place, made.at[pl.ds(Q, Q)], keep, give, 1, sems.at[1])
    loop(count // 2, weigh)

    def weigh_out(i):
        here = rows_of(i, 384)
        made[here, :] = contract(branch_low[:, here], context[...], 0, 0).astype(bf16)

    loop(2, weigh_out)
    finish(copies, hand_out(place, made.at[pl.ds(0, Q)], keep, give, 0, sems.at[0]))


def up_grad(place, rest, grad_pre, normed_low, branch_low, context):
    rows = grad_pre.shape[0]
    return call(
        up_grad_kernel,
        [shape((4, 2, Q // 8, D), bf16)] * 2 + [shape((1, FF), f32), flag_shape],
        [anywhere] * 2 + [whole] * 2,
        [
            pltpu.VMEM((rows, FF), bf16),
            pltpu.VMEM((2 * Q, D), bf16),
            pltpu.SemaphoreType.DMA((3, 8)),
            pltpu.SemaphoreType.DMA((FF // STEP,)),
        ],
        2 * rows * (FF + D) * D,
        20 << 20,
        place, rest, grad_pre, normed_low, branch_low, context,
        specs=[scalars, anywhere, anywhere] + [whole] * 3,
        name="up_grad",
    )


def attend_back_kernel(
    place, turned, grad_context, spreads, allowed, tokens, region, table, after,
    mixed_to, keep, give, bias_sums, flag,
    low, mixed, made, mask, sems,
):
    rows = turned.shape[1]
    flag[...] = jnp.ones_like(flag)

    def prepare(i):
        here = rows_of(i, PART)
        low[here, :] = embed(tokens[here, :], region[:, here], table[...]).astype(bf16)
        mask[here, :] = column(allowed[:, here], SPAN)

    loop(rows // PART, prepare)

    together = 6

    def units(i):
        places = []
        for j in range(together):
            u = i * together + j
            places.append((u % H, pl.multiple_of((u % H) * HD, HD), rows_of(u // H, SPAN)))
        query = [turned[pl.ds(at, HD), cols] for _, at, cols in places]
        key = [turned[pl.ds(D + at, HD), cols] for _, at, cols in places]
        grad = [grad_context[pl.ds(at, HD), cols] for _, at, cols in places]
        scores = [contract(k, q, 0, 0) for k, q in zip(key, query)]
        grad_probs = [
            contract(turned[pl.ds(2 * D + at, HD), cols], g, 0, 0) for (_, at, cols), g in zip(places, grad)
        ]
        made = []
        for (h, at, cols), score, grad_prob in zip(places, scores, grad_probs):
            probs = jnp.exp(jnp.minimum(score, mask[cols, :]) - spreads[pl.ds(h, 1), cols])
            inner = jnp.sum(probs * grad_prob, axis=0, keepdims=True)
            made.append(((probs * (grad_prob - inner)).astype(bf16), probs.astype(bf16)))
        for (h, at, cols), q, k, g, (grad_score, prob) in zip(places, query, key, grad, made):
            mixed[pl.ds(at, HD), cols] = (contract(k, grad_score, 1, 0) * HD ** (-0.5)).astype(bf16)
            mixed[pl.ds(D + at, HD), cols] = contract(q, grad_score, 1, 1).astype(bf16)
            mixed[pl.ds(2 * D + at, HD), cols] = contract(g, prob, 1, 1).astype(bf16)

    loop(H * (rows // SPAN) // together, units)
    sent = begin(mixed, mixed_to, sems.at[8])
    ones = jnp.ones((rows, 128), bf16)

    def weigh(i):
        here = rows_of(i, 768)
        made[here, :] = contract(mixed[here, :], low[...], 1, 0).astype(bf16)
        bias_sums[:, here] = contract(mixed[here, :], ones, 1, 0).T[0:8, :]

    loop(3, weigh)
    finish(hand_out(place, made, keep, give, 0, sems), sent)


def attend_back(place, turned, grad_context, spreads, allowed, tokens, region, table, after):
    rows = turned.shape[1]
    return call(
        attend_back_kernel,
        [
            shape((Q, rows), bf16),
            shape((4, 1, Q // 8, D), bf16),
            shape((4, 1, Q // 8, D), bf16),
            shape((8, Q), f32),
            flag_shape,
        ],
        [anywhere, anywhere, anywhere, whole, whole],
        [
            pltpu.VMEM((rows, D), bf16),
            pltpu.VMEM((Q, rows), bf16),
            pltpu.VMEM((Q, D), bf16),
            pltpu.VMEM((rows, SPAN), f32),
            pltpu.SemaphoreType.DMA((9,)),
        ],
        2 * rows * Q * D + 10 * rows * 256 * D,
        25 << 20,
        place, turned, grad_context, spreads, allowed, tokens, region, table, after,
        specs=[scalars] + [whole] * 7 + [anywhere],
        name="attend_back",
    )


def input_kernel(place, a0, a1, b0, b1, b2, b3, mixed, grad_first, region, after, input_grad_to, sums, weights, made, sems):
    finish(ingest(place, 0, ((a0, a1), (b0, b1, b2, b3)), weights, sems))
    rows = grad_first.shape[0]

    def through(i):
        here = rows_of(i, SPAN)
        made[here, :] = grad_first[here, :] + contract(mixed[:, here], weights[...], 0, 0)
        begin(made.at[here], input_grad_to.at[here], sems.at[i])

    loop(rows // SPAN, through)
    zero = jnp.zeros((8, D), f32)

    def count(i, have):
        here = rows_of(i, PART)
        is_region = column(region[:, here], 128)[:, 0:1] > 0.5
        grad = made[here, :]
        return (
            have[0] + jnp.sum(jnp.where(is_region, 0.0, grad).reshape(-1, 8, D), 0),
            have[1] + jnp.sum(jnp.where(is_region, grad, 0.0).reshape(-1, 8, D), 0),
        )

    both = lax.fori_loop(0, rows // PART, count, (zero, zero))
    for i in range(2):
        sums[i : i + 1, :] = jnp.sum(both[i], 0, keepdims=True)
    for i in range(rows // SPAN):
        here = pl.ds(i * SPAN, SPAN)
        pltpu.make_async_copy(made.at[here], input_grad_to.at[here], sems.at[i]).wait()


def input_back(place, pieces, mixed, grad_first, region, after):
    rows = grad_first.shape[0]
    return call(
        input_kernel,
        [shape((rows, D), f32), shape((2, D), f32)],
        [anywhere, whole],
        [pltpu.VMEM((Q, D), bf16), pltpu.VMEM((rows, D), f32), pltpu.SemaphoreType.DMA((8,))],
        2 * rows * Q * D,
        15 << 20,
        place, *pieces, mixed, grad_first, region, after,
        specs=[scalars] + [anywhere] * 6 + [whole] * 3 + [anywhere],
        name="input_back",
    )


def per_device(
    ring,
    tokens,
    cotangent,
    lengths,
    key_mask,
    type_ids,
    weights,
    vectors,
    master,
    slow_weights,
    left_stats,
    right_stats,
    left_root,
    right_root,
    vector_master,
    vector_moment,
    slow_vectors,
):
    row_count = tokens.shape[0]
    seq_count = lengths.shape[0]
    seq_span = row_count // seq_count
    ring = ring()
    place = ring.place
    slot_a, slot_b, vector_table = ring.gather_early(weights, vectors)
    table = vector_table[: 10 * D].reshape(10, D)
    up_bias = vector_table[10 * D :].reshape(1, FF)
    qkv_bias = jnp.concatenate([table[4:5], jnp.zeros((1, D), f32), table[5:6]], axis=1)
    region = (type_ids == 1).astype(f32)[None, :]
    position = jnp.arange(seq_span)
    allowed = (position[None, :] < lengths[:, None]) & (
        (key_mask.reshape(seq_count, seq_span) == 1) | (position[None, :] == 0)
    )
    allowed = jnp.where(allowed, 3e38, -1e30).astype(f32).reshape(1, row_count)

    early = [*slot_a, *slot_b]
    turned, context, spreads, flag = attend(place, early, tokens, region, allowed, table, qkv_bias)
    pieces = early + ring.gather_late(flag)
    (
        layer_out, slope, unit_one, spread_one, normed_low, grad_second, feed_low, second_sums, keep, give, rest, flag
    ) = feed(place, pieces, tokens, region, context, cotangent, table, up_bias)
    reduce_three = ring.reduction(keep, give)
    grad_pre, grad_first, branch_low, grad_context, first_sums, flag = back(
        place, pieces, slope, grad_second, unit_one, feed_low, spread_one, table
    )
    reduce_three.across(flag)
    keep, give, up_sums, flag = up_grad(place, rest, grad_pre, normed_low, branch_low, context)
    reduce_three.side(flag)
    reduce_both = ring.reduction(keep, give)
    reduce_both.across()
    mixed, keep, give, bias_sums, flag = attend_back(
        place, turned, grad_context, spreads, allowed, tokens, region, table, reduce_both.keep_after()
    )
    reduce_zero = ring.reduction(keep, give)
    reduce_zero.across()
    reduce_both.side(flag)
    input_grad, type_sums = input_back(place, early, mixed, grad_first, region, reduce_zero.keep_after())
    reduce_zero.side()
    vector_sums = jnp.concatenate(
        [
            type_sums.reshape(-1),
            first_sums[:2].reshape(-1),
            bias_sums[0, :D],
            bias_sums[0, 2 * D :],
            first_sums[2],
            second_sums.reshape(-1),
            up_sums.reshape(-1),
        ]
    )
    owned_vector = ring.vector_reduction(vector_sums)
    both = reduce_both.total()
    sum_one, sum_two = ring.reduce_far(both[0], both[1])
    owned_turned = ring.reduce_tail(reduce_zero.total()[0], sum_one, sum_two, reduce_three.total()[0])
    owned_grad = owned_turned.T
    left_new = stat_decay * left_stats + (1.0 - stat_decay) * jnp.dot(
        owned_grad, owned_grad.T, precision=highest
    )
    right_new = stat_decay * right_stats + (1.0 - stat_decay) * jnp.dot(
        owned_grad.T, owned_grad, precision=highest
    )
    steered = jnp.dot(
        jnp.dot(left_root, owned_grad, precision=highest), right_root, precision=highest
    )
    master_new = master - learning_rate * steered
    slow_new = slow_decay * slow_weights + (1.0 - slow_decay) * master_new
    weights_new = master_new.astype(bf16)
    moment_new = stat_decay * vector_moment + (1.0 - stat_decay) * owned_vector * owned_vector
    vector_master_new = vector_master - vector_rate * owned_vector / (jnp.sqrt(moment_new) + 1e-08)
    slow_vectors_new = slow_decay * slow_vectors + (1.0 - slow_decay) * vector_master_new
    vectors_new = vector_master_new.astype(bf16)
    return (
        layer_out,
        input_grad,
        owned_grad,
        left_new,
        right_new,
        master_new,
        slow_new,
        weights_new,
        owned_vector,
        moment_new,
        vector_master_new,
        slow_vectors_new,
        vectors_new,
    )


def solution(mesh):
    in_specs = (
        P(("dp", "opt"), None),
        P(("dp", "opt"), None),
        P(("dp", "opt")),
        P(("dp", "opt")),
        P(("dp", "opt")),
        P(None, "dp"),
        P("dp"),
        P(None, ("dp", "opt")),
        P(None, ("dp", "opt")),
        P(("dp", "opt"), None),
        P(("dp", "opt"), None),
        P(("dp", "opt"), None),
        P(("dp", "opt"), None),
        P(("dp", "opt")),
        P(("dp", "opt")),
        P(("dp", "opt")),
    )
    out_specs = (
        P(("dp", "opt"), None),
        P(("dp", "opt"), None),
        P(None, ("dp", "opt")),
        P(("dp", "opt"), None),
        P(("dp", "opt"), None),
        P(None, ("dp", "opt")),
        P(None, ("dp", "opt")),
        P(None, ("dp", "opt")),
        P(("dp", "opt")),
        P(("dp", "opt")),
        P(("dp", "opt")),
        P(("dp", "opt")),
        P(("dp", "opt")),
    )
    ring = Ring if dict(mesh.shape) == {"dp": 16, "opt": 2} else Plain
    return jax.shard_map(
        functools.partial(per_device, ring),
        mesh=mesh,
        in_specs=in_specs,
        out_specs=out_specs,
        check_vma=False,
    )
```

time: 646 us -> 353 us (0.55)
  waiting for transfers between devices: 257 us -> 108 us
  Pallas kernels: 0 us -> 130 us
  matrix products: 140 us -> 13.6 us
  blocking collectives: 104 us -> 0 us
  local copies, waits for them, and re-layouts: 72.7 us -> 15.2 us
  starting transfers between devices: 0.08 us -> 38 us
  between operations: 15.7 us -> 1.64 us
    unnamed x3 -> x0, waiting for transfers between devices: 211 us -> none
    pallas_call x0 -> x6, Pallas kernels: none -> 130 us  [call(): pl.pallas_call(kernel, out_shape=outs, in_specs=specs, out_specs=out_spec...]
    dot_general x18 -> x0, matrix products: 125 us -> none  [the longest x4 35.4 us: contract_cols(): lax.dot_general(left_side, right_side, (((1,), (1,)), ((), ())), preferre...]
    ppermute x0 -> x35, waiting for transfers between devices: none -> 108 us  [send(): return lax.ppermute(values, AXES, pairs)]
    unnamed x2 -> x0, blocking collectives: 104 us -> none
    all_gather x1 -> x0, waiting for transfers between devices: 45.8 us -> none  [per_device(): lax.all_gather(weights, 'dp', axis=1, tiled=True)]
    ppermute x0 -> x35, starting transfers between devices: none -> 38 us  [send(): return lax.ppermute(values, AXES, pairs)]
    unnamed x100 -> x66, local copies, waits for them, and re-layouts: 39.4 us -> 4.45 us
  transfers between devices with their start and end apart: 2 -> 35, of which waited for: 2 -> 16; matrix products, arithmetic and copies ran while one was open for 3% -> 14% of each run, Pallas kernels for 0% -> 15%
where the time goes in v1:
time: 353 us; the launch traced here: 349 us
  Pallas kernels  130 us (37%)
  waiting for transfers between devices  108 us (31%)
  other arithmetic  42.2 us (12%)
  starting transfers between devices  38 us (11%)
  local copies, waits for them, and re-layouts  15.2 us (4%)
  matrix products  13.6 us (4%)
    pallas_call x6, Pallas kernels, call(): pl.pallas_call(kernel, out_shape=outs, in_specs=specs, out_specs=out_spec...  130 us
    ppermute x35, waiting for transfers between devices, send(): return lax.ppermute(values, AXES, pairs)  108 us
    ppermute x35, starting transfers between devices, send(): return lax.ppermute(values, AXES, pairs)  38 us
  transfers between devices with their start and end apart: 35, of which 16 were waited for; matrix products, arithmetic and copies ran while one was open for 14% of the time, Pallas kernels for 15%

profile of v1, /device:TPU:0, one launch (start us, length us, event | category | flops | bytes accessed | tf_op | source)
XLA Modules:
  0.0 348.8 jit_solution(12607354192718865723)
XLA Ops:
  3.6 4.0 %collective-permute-start.3 = (bf16[304,768]{1,0:T(8,128)(2,1)}, bf16[304,768]{1,0:T(8,128)(2,1)}, u32[]{:S(2)}, u32[]{:S(2)}) collective-permute-start(bf16[304,768]{1,0:T(8,128)(2,1)} %pad_maximum_fusion.6), channel_id=1, source_target_pairs={{0,16},{1,17},{2,18},{3,19},{4,20},{5,21},{6,22},{7,23},{8,0},{9,1... | collective-permute-start | bytes 1400840 | tf_op jit(solution)/shard_map/ppermute | solution.py:59
  7.6 10.3 %collective-permute-done.3 = bf16[304,768]{1,0:T(8,128)(2,1)} collective-permute-done((bf16[304,768]{1,0:T(8,128)(2,1)}, bf16[304,768]{1,0:T(8,128)(2,1)}, u32[]{:S(2)}, u32[]{:S(2)}) %collective-permute-start.3) | collective-permute-done | bytes 466976 | tf_op jit(solution)/shard_map/ppermute | solution.py:59
  20.6 2.4 collective-permute-start.4
  22.9 1.5 collective-permute-start
  24.4 1.4 collective-permute-start.10
  26.0 2.3 collective-permute-start.5
  28.2 4.8 %collective-permute-done.4 = bf16[304,768]{1,0:T(8,128)(2,1)} collective-permute-done((bf16[304,768]{1,0:T(8,128)(2,1)}, bf16[304,768]{1,0:T(8,128)(2,1)}, u32[]{:S(2)}, u32[]{:S(2)}) %collective-permute-start.4) | collective-permute-done | bytes 466976 | tf_op jit(solution)/shard_map/ppermute | solution.py:59
  33.1 1.2 fusion.9
  34.3 3.5 collective-permute-done.5
  38.7 1.6 collective-permute-start.6
  41.5 2.0 pad_maximum_fusion.3
  44.1 7.5 %collective-permute-done.6 = bf16[304,768]{1,0:T(8,128)(2,1)S(1)} collective-permute-done((bf16[304,768]{1,0:T(8,128)(2,1)S(1)}, bf16[304,768]{1,0:T(8,128)(2,1)S(1)}, u32[]{:S(2)}, u32[]{:S(2)}) %collective-permute-start.6) | collective-permute-done | bytes 466976 | tf_op jit(solution)/shard_map/ppermute | solution.py:59
  51.6 1.1 pad_maximum_fusion.2.b0
  53.8 1.3 fusion.61
  55.2 1.3 collective-permute-start.12
  57.7 3.4 collective-permute-done.1
  61.1 2.7 pad_maximum_fusion.a0
  63.7 12.7 %collective-permute-done.7.b1 = bf16[2,304,768]{2,1,0:T(8,128)(2,1)} collective-permute-done((bf16[2,304,768]{2,1,0:T(8,128)(2,1)}, bf16[2,304,768]{2,1,0:T(8,128)(2,1)}, u32[]{:S(2)}, u32[]{:S(2)}) %collective-permute-start.7) | collective-permute-done | bytes 933920 | tf_op jit(solution)/shard_map/ppermute | solution.py:59
  77.8 2.6 pad_maximum_fusion.1.c0
  84.5 17.5 %attend.1 = (bf16[2304,1024]{1,0:T(8,128)(2,1)}, bf16[1024,768]{1,0:T(8,128)(2,1)}, f32[12,1024]{1,0:T(8,128)}, f32[8,128]{1,0:T(8,128)}) custom-call(s32[8]{0:T(128)} %stack.111.place, bf16[4,288,768]{2,1,0:T(8,128)(2,1)} %pad_maximum_fusion.a0, bf16[4,288,768]{2,1,0:T(8,128)(2,1)} %collective-permute-done.2.a1, bf16[2,304,768]{2,1,0:T(8,128)(2,1)} %pad_maximum_fusion.2.b0, ...), custom_call_target="tpu_custom_call" | custom-call | flops 4429185024 | bytes 20971520 | tf_op jit(solution)/shard_map/attend/pallas_call | solution.py:283
  103.3 2.2 broadcast_multiply_fusion.c1
  105.9 1.4 slice.363
  107.3 2.0 collective-permute-done.15.c3
  109.3 1.2 copy-done.26
  110.5 37.3 %feed.1 = (bf16[1024,768]{1,0:T(8,128)(2,1)}, f32[1024,3072]{1,0:T(8,128)}, f32[1024,768]{1,0:T(8,128)}, f32[1024,128]{1,0:T(8,128)}, bf16[1024,768]{1,0:T(8,128...) custom-call(s32[8]{0:T(128)} %stack.111.place, ...), custom_call_target="tpu_custom_call" | custom-call | flops 15703474176 | bytes 52428800 | tf_op jit(solution)/shard_map/feed/pallas_call | solution.py:283
  147.9 25.5 %back.1 = (bf16[1024,3072]{1,0:T(8,128)(2,1)}, f32[1024,768]{1,0:T(8,128)}, bf16[1024,768]{1,0:T(8,128)(2,1)}, bf16[768,1024]{1,0:T(8,128)(2,1)}, f32[3,768]{1,0:T(4,128)}, /*index=5*/f32[8,128]{1,0:T(8,128)}) custom-call(s32[8]{0:T(128)} %stack.111.place, bf16[4,288,768]{2,1,0:T(8,128)(2,1)} %pad_maximum_fusion.a0, ...), custom_call_target="tpu_custom_call" | custom-call | flops 10871635968 | bytes 47185920 | tf_op jit(solution)/shard_map/back/pallas_call | solution.py:283
  173.3 15.3 %up_grad.1 = (bf16[4,2,288,768]{3,2,1,0:T(8,128)(2,1)}, bf16[4,2,288,768]{3,2,1,0:T(8,128)(2,1)}, f32[1,3072]{1,0:T(1,128)}, f32[8,128]{1,0:T(8,128)}) custom-call(s32[8]{0:T(128)} %stack.111.place, bf16[768,768]{1,0:T(8,128)(2,1)} %get-tuple-element.56.rest, bf16[1024,3072]{1,0:T(8,128)(2,1)} %get-tuple-element.57.grad_pre_in, ...), custom_call_target="tpu_custom_call" | custom-call | flops 6039797760 | bytes 20971520 | tf_op jit(solution)/shard_map/up_grad/pallas_call | solution.py:283
  189.2 6.1 %collective-permute-done.16.after = bf16[4,2,288,768]{3,2,1,0:T(8,128)(2,1)} collective-permute-done((bf16[4,2,288,768]{3,2,1,0:T(8,128)(2,1)}, bf16[4,2,288,768]{3,2,1,0:T(8,128)(2,1)}, u32[]{:S(2)}, u32[]{:S(2)}) %collective-permute-start.16) | collective-permute-done | bytes 3538976 | tf_op jit(solution)/shard_map/ppermute | solution.py:59
  195.3 22.6 %attend_back.1 = (bf16[2304,1024]{1,0:T(8,128)(2,1)}, bf16[4,1,288,768]{3,2,1,0:T(8,128)(2,1)}, bf16[4,1,288,768]{3,2,1,0:T(8,128)(2,1)}, f32[8,2304]{1,0:T(8,128)}, f32[8,128]{1,0:T(8,128)}) custom-call(s32[8]{0:T(128)} %stack.111.place, bf16[2304,1024]{1,0:T(8,128)(2,1)} %get-tuple-element.48.turned, bf16[768,1024]{1,0:T(8,128)(2,1)} %get-tuple-element.54.grad_context, ...), custom_call_target="tpu_custom_call" | custom-call | flops 5637144576 | bytes 26214400 | tf_op jit(solution)/shard_map/attend_back/pallas_call | solution.py:283
  218.3 1.2 slice.299
  219.5 1.2 slice.304
  220.7 2.3 multiply_convert_fusion.1
  223.1 1.6 collective-permute-start.21
  225.4 11.7 %input_back.1 = (f32[1024,768]{1,0:T(8,128)}, f32[2,768]{1,0:T(2,128)}) custom-call(s32[8]{0:T(128)} %stack.111.place, bf16[4,288,768]{2,1,0:T(8,128)(2,1)} %pad_maximum_fusion.a0, bf16[4,288,768]{2,1,0:T(8,128)(2,1)} %collective-permute-done.2.a1, bf16[2,304,768]{2,1,0:T(8,128)(2,1)} %pad_maximum_fusion.2.b0, ...), custom_call_target="tpu_custom_call" | custom-call | flops 3623878656 | bytes 15728640 | tf_op jit(solution)/shard_map/input_back/pallas_call | solution.py:283
  238.4 2.4 multiply_convert_fusion.2
  241.6 1.4 collective-permute-start.31
  243.0 6.7 %collective-permute-done.22 = bf16[1,1,288,768]{3,2,1,0:T(8,128)(2,1)S(1)} collective-permute-done((bf16[1,1,288,768]{3,2,1,0:T(8,128)(2,1)S(1)}, bf16[1,1,288,768]{3,2,1,0:T(8,128)(2,1)S(1)}, u32[]{:S(2)}, u32[]{:S(2)}) %collective-permute-start.22) | collective-permute-done | bytes 442400 | tf_op jit(solution)/shard_map/ppermute | solution.py:59
  249.7 1.5 add_bitcast_fusion
  251.9 2.1 add_convert_fusion
  254.0 1.4 collective-permute-start.24
  255.4 1.2 slice.315
  256.8 2.0 collective-permute-start.33
  258.8 1.4 add_convert_fusion.1
  261.2 2.0 collective-permute-start.34
  263.2 13.4 %collective-permute-done.24 = bf16[2,2,288,768]{3,2,1,0:T(8,128)(2,1)S(1)} collective-permute-done((bf16[2,2,288,768]{3,2,1,0:T(8,128)(2,1)S(1)}, bf16[2,2,288,768]{3,2,1,0:T(8,128)(2,1)S(1)}, u32[]{:S(2)}, u32[]{:S(2)}) %collective-permute-start.24) | collective-permute-done | bytes 1769504 | tf_op jit(solution)/shard_map/ppermute | solution.py:59
  276.6 2.2 multiply_convert_fusion
  278.8 1.6 collective-permute-start.25
  281.1 10.9 %collective-permute-done.18 = bf16[2,1,288,768]{3,2,1,0:T(8,128)(2,1)S(1)} collective-permute-done((bf16[2,1,288,768]{3,2,1,0:T(8,128)(2,1)S(1)}, bf16[2,1,288,768]{3,2,1,0:T(8,128)(2,1)S(1)}, u32[]{:S(2)}, u32[]{:S(2)}) %collective-permute-start.18) | collective-permute-done | bytes 884768 | tf_op jit(solution)/shard_map/ppermute | solution.py:59
  292.0 1.2 add_convert_fusion.2
  293.2 1.7 collective-permute-start.19
  295.0 1.6 convert_add_fusion
  296.7 2.3 collective-permute-start.26
  299.0 2.6 collective-permute-done.19
  301.6 1.2 add_bitcast_fusion.1
  302.9 2.2 collective-permute-start.23
  305.2 14.4 %collective-permute-done.26 = bf16[288,768]{1,0:T(8,128)(2,1)S(1)} collective-permute-done((bf16[288,768]{1,0:T(8,128)(2,1)S(1)}, bf16[288,768]{1,0:T(8,128)(2,1)S(1)}, u32[]{:S(2)}, u32[]{:S(2)}) %collective-permute-start.26) | collective-permute-done | bytes 442400 | tf_op jit(solution)/shard_map/ppermute | solution.py:59
  319.9 2.2 collective-permute-done.28
  322.4 2.6 collective-permute-start.29
  325.6 5.5 %collective-permute-done.27 = bf16[144,768]{1,0:T(8,128)(2,1)S(1)} collective-permute-done((bf16[144,768]{1,0:T(8,128)(2,1)S(1)}, bf16[144,768]{1,0:T(8,128)(2,1)S(1)}, u32[]{:S(2)}, u32[]{:S(2)}) %collective-permute-start.27) | collective-permute-done | bytes 221216 | tf_op jit(solution)/shard_map/ppermute | solution.py:59
  331.1 2.4 collective-permute-done.29
  334.8 2.4 fusion.13
  337.2 2.3 fusion.1
  339.6 5.7 %add_multiply_fusion = f32[768,768]{1,0:T(8,128)} fusion(f32[768,768]{1,0:T(8,128)S(1)} %copy-done.3, f32[144,768]{1,0:T(8,128)S(1)} %get-tuple-element.87, f32[144,768]{1,0:T(8,128)S(1)} %get-tuple-element.86), kind=kOutput, calls=%fused_computation.1 | convolution fusion | flops 2039832576 | bytes 5603328 | tf_op jit(solution)/shard_map/dot_general | solution.py:1010
  345.2 3.2 fusion.66
  (177 shorter events, 26.9 us)
Async XLA Ops:
  0.6 334.1 %copy-start = (f32[768,768]{1,0:T(8,128)S(1)}, f32[768,768]{1,0:T(8,128)}, u32[]{:S(2)}) copy-start(f32[768,768]{1,0:T(8,128)} %param.27) | copy-start | bytes 7077892
  3.6 14.3 %collective-permute-start.3 = (bf16[304,768]{1,0:T(8,128)(2,1)}, bf16[304,768]{1,0:T(8,128)(2,1)}, u32[]{:S(2)}, u32[]{:S(2)}) collective-permute-start(bf16[304,768]{1,0:T(8,128)(2,1)} %pad_maximum_fusion.6), channel_id=1, source_target_pairs={{0,16},{1,17},{2,18},{3,19},{4,20},{5,21},{6,22},{7,23},{8,0},{9,1... | collective-permute-start | bytes 1400840 | tf_op jit(solution)/shard_map/ppermute | solution.py:59
  20.6 20.4 %copy-start.21 = (s32[1024]{0:T(1024)S(1)}, s32[1024]{0:T(1024)}, u32[]{:S(2)}) copy-start(s32[1024]{0:T(1024)} %param.20) | copy-start | bytes 12292
  20.6 12.5 %collective-permute-start.4 = (bf16[304,768]{1,0:T(8,128)(2,1)}, bf16[304,768]{1,0:T(8,128)(2,1)}, u32[]{:S(2)}, u32[]{:S(2)}) collective-permute-start(bf16[304,768]{1,0:T(8,128)(2,1)} %pad_maximum_fusion.7), channel_id=1, source_target_pairs={{0,8},{1,9},{2,10},{3,11},{4,12},{5,13},{6,14},{7,15},{8,0},{9,1},... | collective-permute-start | bytes 1400840 | tf_op jit(solution)/shard_map/ppermute | solution.py:59
  22.9 18.6 %collective-permute-start = (bf16[288,768]{1,0:T(8,128)(2,1)S(1)}, bf16[288,768]{1,0:T(8,128)(2,1)}, u32[]{:S(2)}, u32[]{:S(2)}) collective-permute-start(bf16[288,768]{1,0:T(8,128)(2,1)S(1)} %get-tuple-element.101), channel_id=1, source_target_pairs={{0,4},{1,5},{2,3},{3,2},{4,0},{5,1},{6,7},{7,6},{8,12},{9,13},{10,... | collective-permute-start | bytes 1327112 | tf_op jit(solution)/shard_map/ppermute | solution.py:59
  24.4 17.1 %collective-permute-start.10 = (bf16[288,768]{1,0:T(8,128)(2,1)S(1)}, bf16[288,768]{1,0:T(8,128)(2,1)}, u32[]{:S(2)}, u32[]{:S(2)}) collective-permute-start(bf16[288,768]{1,0:T(8,128)(2,1)S(1)} %get-tuple-element.101), channel_id=1, source_target_pairs={{0,0},{1,1},{2,2},{3,3},{4,4},{5,5},{6,6},{7,7},{8,16},{9,17},{10,... | collective-permute-start | bytes 1327112 | tf_op jit(solution)/shard_map/ppermute | solution.py:59
  26.0 11.8 %collective-permute-start.5 = (bf16[16,768]{1,0:T(8,128)(2,1)S(1)}, bf16[16,768]{1,0:T(8,128)(2,1)S(1)}, u32[]{:S(2)}, u32[]{:S(2)}) collective-permute-start(bf16[16,768]{1,0:T(8,128)(2,1)S(1)} %compare_select_fusion.2), channel_id=1, source_target_pairs={{0,16},{1,17},{2,18},{3,19},{4,20},{5,21},{6,22},{7,23},{8,24},{9,... | collective-permute-start | bytes 73736 | tf_op jit(solution)/shard_map/ppermute | solution.py:59
  38.7 14.0 %copy-start.4 = (bf16[1,304,768]{2,1,0:T(8,128)(2,1)}, bf16[1,304,768]{2,1,0:T(8,128)(2,1)S(1)}, u32[]{:S(2)}) copy-start(bf16[1,304,768]{2,1,0:T(8,128)(2,1)S(1)} %get-tuple-element.102) | copy-start | bytes 1400836
  38.7 12.9 %collective-permute-start.6 = (bf16[304,768]{1,0:T(8,128)(2,1)S(1)}, bf16[304,768]{1,0:T(8,128)(2,1)S(1)}, u32[]{:S(2)}, u32[]{:S(2)}) collective-permute-start(bf16[304,768]{1,0:T(8,128)(2,1)S(1)} %get-tuple-element.103), channel_id=1, source_target_pairs={{0,4},{1,5},{2,3},{3,2},{4,0},{5,1},{6,7},{7,6},{8,12},{9,13},{10,... | collective-permute-start | bytes 1400840 | tf_op jit(solution)/shard_map/ppermute | solution.py:59
  41.5 11.2 %collective-permute-start.11 = (bf16[288,768]{1,0:T(8,128)(2,1)}, bf16[288,768]{1,0:T(8,128)(2,1)S(1)}, u32[]{:S(2)}, u32[]{:S(2)}) collective-permute-start(bf16[288,768]{1,0:T(8,128)(2,1)} %collective-permute-done.10), channel_id=1, source_target_pairs={{0,8},{1,9},{2,10},{3,11},{4,12},{5,13},{6,14},{7,15},{8,0},{9,1},... | collective-permute-start | bytes 1327112 | tf_op jit(solution)/shard_map/ppermute | solution.py:59
  41.5 11.2 %copy-start.27 = (s32[4]{0:T(128)S(1)}, s32[4]{0:T(128)}, u32[]{:S(2)}) copy-start(s32[4]{0:T(128)} %param.18) | copy-start | bytes 52
  43.6 17.5 %collective-permute-start.1 = (bf16[2,288,768]{2,1,0:T(8,128)(2,1)}, bf16[2,288,768]{2,1,0:T(8,128)(2,1)}, u32[]{:S(2)}, u32[]{:S(2)}) collective-permute-start(bf16[2,288,768]{2,1,0:T(8,128)(2,1)} %pad_maximum_fusion.3), channel_id=1, source_target_pairs={{0,1},{1,0},{2,6},{3,7},{4,5},{5,4},{6,2},{7,3},{8,9},{9,8},{10,14... | collective-permute-start | bytes 2654216 | tf_op jit(solution)/shard_map/ppermute | solution.py:59
  51.6 1.2 copy-start.11
  52.7 23.7 %collective-permute-start.7 = (bf16[2,304,768]{2,1,0:T(8,128)(2,1)}, bf16[2,304,768]{2,1,0:T(8,128)(2,1)}, u32[]{:S(2)}, u32[]{:S(2)}) collective-permute-start(bf16[2,304,768]{2,1,0:T(8,128)(2,1)} %pad_maximum_fusion.2.b0), channel_id=1, source_target_pairs={{0,1},{1,0},{2,6},{3,7},{4,5},{5,4},{6,2},{7,3},{8,9},{9,8},{10,14... | collective-permute-start | bytes 2801672 | tf_op jit(solution)/shard_map/ppermute | solution.py:59
  52.8 4.3 %copy-start.22 = (s32[1024]{0:T(1024)S(1)}, s32[1024]{0:T(1024)}, u32[]{:S(2)}) copy-start(s32[1024]{0:T(1024)} %param.19) | copy-start | bytes 12292
  55.2 22.6 %collective-permute-start.12 = (bf16[2,288,768]{2,1,0:T(8,128)(2,1)}, bf16[2,288,768]{2,1,0:T(8,128)(2,1)}, u32[]{:S(2)}, u32[]{:S(2)}) collective-permute-start(bf16[2,288,768]{2,1,0:T(8,128)(2,1)} %get-tuple-element.99), channel_id=1, source_target_pairs={{0,4},{1,5},{2,3},{3,2},{4,0},{5,1},{6,7},{7,6},{8,12},{9,13},{10,... | collective-permute-start | bytes 2654216 | tf_op jit(solution)/shard_map/ppermute | solution.py:59
  57.7 20.1 %copy-start.1 = (bf16[1,2,288,768]{3,2,1,0:T(8,128)(2,1)S(1)}, bf16[1,2,288,768]{3,2,1,0:T(8,128)(2,1)}, u32[]{:S(2)}) copy-start(bf16[1,2,288,768]{3,2,1,0:T(8,128)(2,1)} %get-tuple-element.98) | copy-start | bytes 2654212
  57.7 24.2 %collective-permute-start.8 = (bf16[2,304,768]{2,1,0:T(8,128)(2,1)}, bf16[2,304,768]{2,1,0:T(8,128)(2,1)S(1)}, u32[]{:S(2)}, u32[]{:S(2)}) collective-permute-start(bf16[2,304,768]{2,1,0:T(8,128)(2,1)} %pad_maximum_fusion.2.b0), channel_id=1, source_target_pairs={{0,2},{1,3},{2,0},{3,1},{4,6},{5,7},{6,4},{7,5},{8,10},{9,11},{10,... | collective-permute-start | bytes 2801672 | tf_op jit(solution)/shard_map/ppermute | solution.py:59
  63.7 20.8 %collective-permute-start.2 = (bf16[4,288,768]{2,1,0:T(8,128)(2,1)}, bf16[4,288,768]{2,1,0:T(8,128)(2,1)}, u32[]{:S(2)}, u32[]{:S(2)}) collective-permute-start(bf16[4,288,768]{2,1,0:T(8,128)(2,1)} %pad_maximum_fusion.a0), channel_id=1, source_target_pairs={{0,2},{1,3},{2,0},{3,1},{4,6},{5,7},{6,4},{7,5},{8,10},{9,11},{10,... | collective-permute-start | bytes 5308424 | tf_op jit(solution)/shard_map/ppermute | solution.py:59
  76.4 6.4 %collective-permute-start.9 = (bf16[2,304,768]{2,1,0:T(8,128)(2,1)}, bf16[2,304,768]{2,1,0:T(8,128)(2,1)S(1)}, u32[]{:S(2)}, u32[]{:S(2)}) collective-permute-start(bf16[2,304,768]{2,1,0:T(8,128)(2,1)} %collective-permute-done.7.b1), channel_id=1, source_target_pairs={{0,2},{1,3},{2,0},{3,1},{4,6},{5,7},{6,4},{7,5},{8,10},{9,11},{10,... | collective-permute-start | bytes 2801672 | tf_op jit(solution)/shard_map/ppermute | solution.py:59
  80.4 22.9 %collective-permute-start.13 = (bf16[2,2,288,768]{3,2,1,0:T(8,128)(2,1)}, bf16[2,2,288,768]{3,2,1,0:T(8,128)(2,1)}, u32[]{:S(2)}, u32[]{:S(2)}) collective-permute-start(bf16[2,2,288,768]{3,2,1,0:T(8,128)(2,1)} %pad_maximum_fusion.1.c0), channel_id=1, source_target_pairs={{0,1},{1,0},{2,6},{3,7},{4,5},{5,4},{6,2},{7,3},{8,9},{9,8},{10,14... | collective-permute-start | bytes 5308424 | tf_op jit(solution)/shard_map/ppermute | solution.py:59
  80.9 26.3 %collective-permute-start.14 = (bf16[2,2,288,768]{3,2,1,0:T(8,128)(2,1)}, bf16[2,2,288,768]{3,2,1,0:T(8,128)(2,1)}, u32[]{:S(2)}, u32[]{:S(2)}) collective-permute-start(bf16[2,2,288,768]{3,2,1,0:T(8,128)(2,1)} %pad_maximum_fusion.1.c0), channel_id=1, source_target_pairs={{0,2},{1,3},{2,0},{3,1},{4,6},{5,7},{6,4},{7,5},{8,10},{9,11},{10,... | collective-permute-start | bytes 5308424 | tf_op jit(solution)/shard_map/ppermute | solution.py:59
  81.9 0.9 copy-start.7
  82.8 1.7 copy-start.8
  83.2 18.9 %copy-start.14 = (f32[10752]{0:T(1024)}, f32[10752]{0:T(1024)S(1)}, u32[]{:S(2)}) copy-start(f32[10752]{0:T(1024)S(1)} %reshape.341) | copy-start | bytes 129028
  105.5 5.0 %copy-start.6 = (bf16[2,2,288,768]{3,2,1,0:T(8,128)(2,1)}, bf16[2,2,288,768]{3,2,1,0:T(8,128)(2,1)S(1)}, u32[]{:S(2)}) copy-start(bf16[2,2,288,768]{3,2,1,0:T(8,128)(2,1)S(1)} %broadcast_multiply_fusion.c1) | copy-start | bytes 5308420
  105.5 3.8 %collective-permute-start.15 = (bf16[2,2,288,768]{3,2,1,0:T(8,128)(2,1)S(1)}, bf16[2,2,288,768]{3,2,1,0:T(8,128)(2,1)S(1)}, u32[]{:S(2)}, u32[]{:S(2)}) collective-permute-start(bf16[2,2,288,768]{3,2,1,0:T(8,128)(2,1)S(1)} %broadcast_multiply_fusion.c1), channel_id=1, source_target_pairs={{0,2},{1,3},{2,0},{3,1},{4,6},{5,7},{6,4},{7,5},{8,10},{9,11},{10,... | collective-permute-start | bytes 5308424 | tf_op jit(solution)/shard_map/ppermute | solution.py:59
  109.3 1.2 copy-start.26
  188.6 6.6 %collective-permute-start.16 = (bf16[4,2,288,768]{3,2,1,0:T(8,128)(2,1)}, bf16[4,2,288,768]{3,2,1,0:T(8,128)(2,1)}, u32[]{:S(2)}, u32[]{:S(2)}) collective-permute-start(bf16[4,2,288,768]{3,2,1,0:T(8,128)(2,1)} %get-tuple-element.60), channel_id=1, source_target_pairs={{0,2},{1,3},{2,0},{3,1},{4,6},{5,7},{6,4},{7,5},{8,10},{9,11},{10,... | collective-permute-start | bytes 10616840 | tf_op jit(solution)/shard_map/ppermute | solution.py:59
  189.0 31.7 %collective-permute-start.20 = (bf16[4,1,288,768]{3,2,1,0:T(8,128)(2,1)}, bf16[4,1,288,768]{3,2,1,0:T(8,128)(2,1)}, u32[]{:S(2)}, u32[]{:S(2)}) collective-permute-start(bf16[4,1,288,768]{3,2,1,0:T(8,128)(2,1)} %get-tuple-element.67), channel_id=1, source_target_pairs={{0,2},{1,3},{2,0},{3,1},{4,6},{5,7},{6,4},{7,5},{8,10},{9,11},{10,... | collective-permute-start | bytes 5308424 | tf_op jit(solution)/shard_map/ppermute | solution.py:59
  195.3 23.0 %copy-start.19 = (f32[3,768]{1,0:T(4,128)S(1)}, f32[3,768]{1,0:T(4,128)}, u32[]{:S(2)}) copy-start(f32[3,768]{1,0:T(4,128)} %get-tuple-element.73) | copy-start | bytes 27652
  195.3 23.0 %copy-start.16 = (f32[3,768]{1,0:T(4,128)S(1)}, f32[3,768]{1,0:T(4,128)}, u32[]{:S(2)}) copy-start(f32[3,768]{1,0:T(4,128)} %get-tuple-element.75) | copy-start | bytes 27652
  217.9 7.5 %collective-permute-start.17 = (bf16[4,1,288,768]{3,2,1,0:T(8,128)(2,1)}, bf16[4,1,288,768]{3,2,1,0:T(8,128)(2,1)}, u32[]{:S(2)}, u32[]{:S(2)}) collective-permute-start(bf16[4,1,288,768]{3,2,1,0:T(8,128)(2,1)} %get-tuple-element.63), channel_id=1, source_target_pairs={{0,2},{1,3},{2,0},{3,1},{4,6},{5,7},{6,4},{7,5},{8,10},{9,11},{10,... | collective-permute-start | bytes 5308424 | tf_op jit(solution)/shard_map/ppermute | solution.py:59
  223.1 15.3 %collective-permute-start.21 = (bf16[2,1,288,768]{3,2,1,0:T(8,128)(2,1)S(1)}, bf16[2,1,288,768]{3,2,1,0:T(8,128)(2,1)}, u32[]{:S(2)}, u32[]{:S(2)}) collective-permute-start(bf16[2,1,288,768]{3,2,1,0:T(8,128)(2,1)S(1)} %multiply_convert_fusion.1), channel_id=1, source_target_pairs={{0,1},{1,0},{2,6},{3,7},{4,5},{5,4},{6,2},{7,3},{8,9},{9,8},{10,14... | collective-permute-start | bytes 2654216 | tf_op jit(solution)/shard_map/ppermute | solution.py:59
  225.4 12.5 %copy-start.15 = (f32[1,3072]{1,0:T(1,128)S(1)}, f32[1,3072]{1,0:T(1,128)}, u32[]{:S(2)}) copy-start(f32[1,3072]{1,0:T(1,128)} %get-tuple-element.76) | copy-start | bytes 36868
  225.4 12.6 %copy-start.20 = (pred[8,8]{1,0:T(8,128)(4,1)S(1)}, pred[8,8]{1,0:T(8,128)(4,1)}, u32[]{:S(2)}) copy-start(pred[8,8]{1,0:T(8,128)(4,1)} %get-tuple-element.114) | copy-start | bytes 196
  238.3 3.1 collective-permute-start.30
  238.4 13.5 %copy-start.2 = (bf16[4,2,288,768]{3,2,1,0:T(8,128)(2,1)S(1)}, bf16[4,2,288,768]{3,2,1,0:T(8,128)(2,1)}, u32[]{:S(2)}) copy-start(bf16[4,2,288,768]{3,2,1,0:T(8,128)(2,1)} %get-tuple-element.70) | copy-start | bytes 10616836
  240.8 8.9 %collective-permute-start.22 = (bf16[1,1,288,768]{3,2,1,0:T(8,128)(2,1)S(1)}, bf16[1,1,288,768]{3,2,1,0:T(8,128)(2,1)S(1)}, u32[]{:S(2)}, u32[]{:S(2)}) collective-permute-start(bf16[1,1,288,768]{3,2,1,0:T(8,128)(2,1)S(1)} %multiply_convert_fusion.2), channel_id=1, source_target_pairs={{0,4},{1,5},{2,3},{3,2},{4,0},{5,1},{6,7},{7,6},{8,12},{9,13},{10,... | collective-permute-start | bytes 1327112 | tf_op jit(solution)/shard_map/ppermute | solution.py:59
  241.6 9.6 %collective-permute-start.31 = (bf16[2,16,768]{2,1,0:T(8,128)(2,1)S(1)}, bf16[2,16,768]{2,1,0:T(8,128)(2,1)S(1)}, u32[]{:S(2)}, u32[]{:S(2)}) collective-permute-start(bf16[2,16,768]{2,1,0:T(8,128)(2,1)S(1)} %fusion.26), channel_id=1, source_target_pairs={{0,1},{1,0},{2,6},{3,7},{4,5},{5,4},{6,2},{7,3},{8,9},{9,8},{10,14... | collective-permute-start | bytes 147464 | tf_op jit(solution)/shard_map/ppermute | solution.py:59
  251.4 5.2 %collective-permute-start.32 = (bf16[1,16,768]{2,1,0:T(8,128)(2,1)S(1)}, bf16[1,16,768]{2,1,0:T(8,128)(2,1)S(1)}, u32[]{:S(2)}, u32[]{:S(2)}) collective-permute-start(bf16[1,16,768]{2,1,0:T(8,128)(2,1)S(1)} %fusion.38), channel_id=1, source_target_pairs={{0,4},{1,5},{2,3},{3,2},{4,0},{5,1},{6,7},{7,6},{8,12},{9,13},{10,... | collective-permute-start | bytes 73736 | tf_op jit(solution)/shard_map/ppermute | solution.py:59
  251.9 6.9 %copy-start.5 = (bf16[4,1,288,768]{3,2,1,0:T(8,128)(2,1)S(1)}, bf16[4,1,288,768]{3,2,1,0:T(8,128)(2,1)}, u32[]{:S(2)}) copy-start(bf16[4,1,288,768]{3,2,1,0:T(8,128)(2,1)} %get-tuple-element.65) | copy-start | bytes 5308420
  254.0 22.6 %collective-permute-start.24 = (bf16[2,2,288,768]{3,2,1,0:T(8,128)(2,1)S(1)}, bf16[2,2,288,768]{3,2,1,0:T(8,128)(2,1)S(1)}, u32[]{:S(2)}, u32[]{:S(2)}) collective-permute-start(bf16[2,2,288,768]{3,2,1,0:T(8,128)(2,1)S(1)} %add_convert_fusion), channel_id=1, source_target_pairs={{0,1},{1,0},{2,6},{3,7},{4,5},{5,4},{6,2},{7,3},{8,9},{9,8},{10,14... | collective-permute-start | bytes 5308424 | tf_op jit(solution)/shard_map/ppermute | solution.py:59
  256.8 4.2 %collective-permute-start.33 = (bf16[16,768]{1,0:T(8,128)(2,1)S(1)}, bf16[16,768]{1,0:T(8,128)(2,1)S(1)}, u32[]{:S(2)}, u32[]{:S(2)}) collective-permute-start(bf16[16,768]{1,0:T(8,128)(2,1)S(1)} %fusion.40), channel_id=1, source_target_pairs={{0,8},{1,9},{2,10},{3,11},{4,12},{5,13},{6,14},{7,15},{8,0},{9,1},... | collective-permute-start | bytes 73736 | tf_op jit(solution)/shard_map/ppermute | solution.py:59
  260.2 31.8 %collective-permute-start.18 = (bf16[2,1,288,768]{3,2,1,0:T(8,128)(2,1)S(1)}, bf16[2,1,288,768]{3,2,1,0:T(8,128)(2,1)S(1)}, u32[]{:S(2)}, u32[]{:S(2)}) collective-permute-start(bf16[2,1,288,768]{3,2,1,0:T(8,128)(2,1)S(1)} %add_convert_fusion.1), channel_id=1, source_target_pairs={{0,1},{1,0},{2,6},{3,7},{4,5},{5,4},{6,2},{7,3},{8,9},{9,8},{10,14... | collective-permute-start | bytes 2654216 | tf_op jit(solution)/shard_map/ppermute | solution.py:59
  261.2 19.2 %collective-permute-start.34 = (bf16[16,768]{1,0:T(8,128)(2,1)S(1)}, bf16[16,768]{1,0:T(8,128)(2,1)S(1)}, u32[]{:S(2)}, u32[]{:S(2)}) collective-permute-start(bf16[16,768]{1,0:T(8,128)(2,1)S(1)} %fusion.44), channel_id=1, source_target_pairs={{0,16},{1,17},{2,18},{3,19},{4,20},{5,21},{6,22},{7,23},{8,24},{9,... | collective-permute-start | bytes 73736 | tf_op jit(solution)/shard_map/ppermute | solution.py:59
  276.6 3.9 %copy-start.24 = (f32[336]{0:T(512)S(1)}, f32[336]{0:T(512)}, u32[]{:S(2)}) copy-start(f32[336]{0:T(512)} %param.29) | copy-start | bytes 4036
  276.6 4.0 %copy-start.25 = (f32[336]{0:T(512)S(1)}, f32[336]{0:T(512)}, u32[]{:S(2)}) copy-start(f32[336]{0:T(512)} %param.30) | copy-start | bytes 4036
  278.8 16.1 %collective-permute-start.25 = (bf16[1,2,288,768]{3,2,1,0:T(8,128)(2,1)S(1)}, bf16[1,2,288,768]{3,2,1,0:T(8,128)(2,1)S(1)}, u32[]{:S(2)}, u32[]{:S(2)}) collective-permute-start(bf16[1,2,288,768]{3,2,1,0:T(8,128)(2,1)S(1)} %multiply_convert_fusion), channel_id=1, source_target_pairs={{0,4},{1,5},{2,3},{3,2},{4,0},{5,1},{6,7},{7,6},{8,12},{9,13},{10,... | collective-permute-start | bytes 2654216 | tf_op jit(solution)/shard_map/ppermute | solution.py:59
  280.5 16.0 %copy-start.17 = (f32[336]{0:T(512)}, f32[336]{0:T(512)S(1)}, u32[]{:S(2)}) copy-start(f32[336]{0:T(512)S(1)} %fusion.56) | copy-start | bytes 4036
  281.1 43.9 %copy-start.18 = (f32[336]{0:T(512)}, f32[336]{0:T(512)S(1)}, u32[]{:S(2)}) copy-start(f32[336]{0:T(512)S(1)} %get-tuple-element.80) | copy-start | bytes 4036
  293.2 8.4 %collective-permute-start.19 = (bf16[1,1,288,768]{3,2,1,0:T(8,128)(2,1)S(1)}, bf16[1,1,288,768]{3,2,1,0:T(8,128)(2,1)S(1)}, u32[]{:S(2)}, u32[]{:S(2)}) collective-permute-start(bf16[1,1,288,768]{3,2,1,0:T(8,128)(2,1)S(1)} %add_convert_fusion.2), channel_id=1, source_target_pairs={{0,4},{1,5},{2,3},{3,2},{4,0},{5,1},{6,7},{7,6},{8,12},{9,13},{10,... | collective-permute-start | bytes 1327112 | tf_op jit(solution)/shard_map/ppermute | solution.py:59
  296.7 23.0 %collective-permute-start.26 = (bf16[288,768]{1,0:T(8,128)(2,1)S(1)}, bf16[288,768]{1,0:T(8,128)(2,1)S(1)}, u32[]{:S(2)}, u32[]{:S(2)}) collective-permute-start(bf16[288,768]{1,0:T(8,128)(2,1)S(1)} %fusion.2), channel_id=1, source_target_pairs={{0,16},{1,17},{2,18},{3,19},{4,20},{5,21},{6,22},{7,23},{8,24},{9,... | collective-permute-start | bytes 1327112 | tf_op jit(solution)/shard_map/ppermute | solution.py:59
  302.9 16.9 %collective-permute-start.23 = (bf16[144,768]{1,0:T(8,128)(2,1)S(1)}, bf16[144,768]{1,0:T(8,128)(2,1)S(1)}, u32[]{:S(2)}, u32[]{:S(2)}) collective-permute-start(bf16[144,768]{1,0:T(8,128)(2,1)S(1)} %get-tuple-element.92), channel_id=1, source_target_pairs={{0,8},{1,9},{2,10},{3,11},{4,12},{5,13},{6,14},{7,15},{8,0},{9,1},... | collective-permute-start | bytes 663560 | tf_op jit(solution)/shard_map/ppermute | solution.py:59
  305.1 16.9 %collective-permute-start.28 = (bf16[144,768]{1,0:T(8,128)(2,1)S(1)}, bf16[144,768]{1,0:T(8,128)(2,1)S(1)}, u32[]{:S(2)}, u32[]{:S(2)}) collective-permute-start(bf16[144,768]{1,0:T(8,128)(2,1)S(1)} %get-tuple-element.93), channel_id=1, source_target_pairs={{0,8},{1,9},{2,10},{3,11},{4,12},{5,13},{6,14},{7,15},{8,0},{9,1},... | collective-permute-start | bytes 663560 | tf_op jit(solution)/shard_map/ppermute | solution.py:59
  322.1 3.0 copy-start.23
  322.4 8.8 %collective-permute-start.27 = (bf16[144,768]{1,0:T(8,128)(2,1)S(1)}, bf16[144,768]{1,0:T(8,128)(2,1)S(1)}, u32[]{:S(2)}, u32[]{:S(2)}) collective-permute-start(bf16[144,768]{1,0:T(8,128)(2,1)S(1)} %get-tuple-element.88), channel_id=1, source_target_pairs={{0,8},{1,9},{2,10},{3,11},{4,12},{5,13},{6,14},{7,15},{8,24},{9,25... | collective-permute-start | bytes 663560 | tf_op jit(solution)/shard_map/ppermute | solution.py:59
  322.4 11.1 %collective-permute-start.29 = (bf16[144,768]{1,0:T(8,128)(2,1)S(1)}, bf16[144,768]{1,0:T(8,128)(2,1)S(1)}, u32[]{:S(2)}, u32[]{:S(2)}) collective-permute-start(bf16[144,768]{1,0:T(8,128)(2,1)S(1)} %get-tuple-element.89), channel_id=1, source_target_pairs={{0,8},{1,9},{2,10},{3,11},{4,12},{5,13},{6,14},{7,15},{8,24},{9,25... | collective-permute-start | bytes 663560 | tf_op jit(solution)/shard_map/ppermute | solution.py:59
  334.8 2.4 copy-start.12
  334.8 4.8 %copy-start.3 = (f32[768,768]{1,0:T(8,128)S(1)}, f32[768,768]{1,0:T(8,128)}, u32[]{:S(2)}) copy-start(f32[768,768]{1,0:T(8,128)} %param.25) | copy-start | bytes 7077892
  339.5 5.7 %copy-start.9 = (f32[768,288]{0,1:T(8,128)S(1)}, f32[768,288]{0,1:T(8,128)}, u32[]{:S(2)}) copy-start(f32[768,288]{0,1:T(8,128)} %param.24) | copy-start | bytes 2654212
  339.5 5.7 %copy-start.10 = (f32[768,288]{0,1:T(8,128)S(1)}, f32[768,288]{0,1:T(8,128)}, u32[]{:S(2)}) copy-start(f32[768,288]{0,1:T(8,128)} %param.23) | copy-start | bytes 2654212
  339.5 5.7 %copy-start.13 = (f32[288,288]{1,0:T(8,128)S(1)}, f32[288,288]{1,0:T(8,128)}, u32[]{:S(2)}) copy-start(f32[288,288]{1,0:T(8,128)} %param.28) | copy-start | bytes 995332

commit v2 on v1

v2 whole, which is shorter than its diff:
```python
import functools
import math

import jax
import jax.numpy as jnp
import numpy as np
from jax import lax
from jax.experimental import pallas as pl
from jax.experimental.pallas import tpu as pltpu
from jax.sharding import PartitionSpec as P

D = 768
H = 12
HD = 64
FF = 3072
WCOLS = 4 * D + 2 * FF
NVEC = 10 * D + FF

highest = lax.Precision.HIGHEST
norm_eps = 1e-12
learning_rate = 0.03
vector_rate = 0.2
stat_decay = 0.5
slow_decay = 0.9
f32 = jnp.float32
bf16 = jnp.bfloat16
AXES = ("dp", "opt")


def contract(left_side, right_side, left_dim, right_dim):
    return lax.dot_general(
        left_side, right_side, (((left_dim,), (right_dim,)), ((), ())), preferred_element_type=f32
    )


def block_index(z, y, c, x):
    return z * 8 + y * 4 + c * 2 + x


def permutation(move):
    pairs = []
    for b in range(32):
        z, y, c, x = b // 8, (b // 4) % 2, (b // 2) % 2, b % 2
        pairs.append((b, block_index(*move(z, y, c, x))))
    return pairs


Z_CYCLE = permutation(lambda z, y, c, x: ((2, 0, 3, 1)[z], y, c, x))
Z_CYCLE_BACK = permutation(lambda z, y, c, x: ((1, 3, 0, 2)[z], y, c, x))
Z_NEAR = permutation(lambda z, y, c, x: (z ^ 1, y, c, x))
Z_FAR = permutation(lambda z, y, c, x: (z ^ 2, y, c, x))
Z_MIDDLE = permutation(lambda z, y, c, x: ((0, 2, 1, 3)[z], y, c, x))
PLANE_A = permutation(lambda z, y, c, x: (z, 1 - y, c, x) if c == 0 else (z, y, c, 1 - x))
PLANE_B = permutation(lambda z, y, c, x: (z, y, c, 1 - x) if c == 0 else (z, 1 - y, c, x))
CORES = permutation(lambda z, y, c, x: (z, y, 1 - c, x))


def send(values, pairs):
    return lax.ppermute(values, AXES, pairs)


QUARTER_SLOT = np.array([[0, 1, 3, 2], [1, 0, 3, 2], [1, 3, 0, 2], [1, 3, 2, 0]])


class Ring:
    def __init__(self):
        dp = lax.axis_index("dp")
        self.z, self.y, self.c = dp // 4, (dp // 2) % 2, dp % 2
        self.x = lax.axis_index("opt")
        slots = [self.number([int(v) for v in QUARTER_SLOT[:, q]]) for q in range(4)]
        self.place = jnp.stack([self.y, self.c, self.x, self.z] + slots).astype(jnp.int32)

    def number(self, values):
        out = values[3]
        for z in (2, 1, 0):
            out = jnp.where(self.z == z, values[z], out)
        return out

    def gather_early(self, weights, vectors):
        place, rows = self.place, weights.shape[1] // 2
        own = prepare_own(place, weights.T, vectors[None, :])
        one = send(own, Z_CYCLE)
        side = send(own, PLANE_A)
        pass_on, slab, pair_a = after_one(place, own, one, side)
        two = send(pass_on, Z_NEAR)
        across_a = send(pair_a, PLANE_B)
        far = send(slab, Z_FAR)
        middle = send(own, Z_MIDDLE)
        swap_a = send(pair_a, CORES)
        block_b, slot_c = after_two(place, pass_on, one, two, far, after=[across_a, swap_a])
        side_b = send(block_b, PLANE_A)
        side_c = send(slot_c, PLANE_A)
        three = send(middle, Z_NEAR)
        swap_aa = send(across_a, CORES)
        pair_b, slot_d = after_three(place, block_b, side_b, middle, three, after=[side_c, swap_aa])
        across_b = send(pair_b, PLANE_B)
        swap_b = send(pair_b, CORES)
        side_d = send(slot_d, PLANE_A)
        self.late = after_four(slot_c, side_c, slot_d, side_d, after=[across_b, swap_b])
        swap_bb = send(across_b, CORES)
        slot_b = [pair_b, across_b, swap_b, swap_bb]
        table = read_vectors(place, slot_b, vectors.shape[0] // 2)
        return [pair_a, across_a, swap_a, swap_aa], slot_b, table.reshape(-1, D)

    def gather_late(self):
        self.across = send(self.late, PLANE_B)
        self.swapped = send(self.late, CORES)
        return [self.late]

    def gather_last(self, context):
        across = hold(self.across, context)
        return [self.late, across, self.swapped, send(across, CORES)]

    def disordered(self, blocks):
        hits = jnp.stack([block_place((self.y, self.c, self.x), who, k) for who in (0, 1) for k in range(4)])
        hit = (jnp.arange(8)[None, :] == hits[:, None]).reshape((8, 8) + (1,) * (blocks.ndim - 1))
        return jnp.sum(jnp.where(hit, blocks[None], 0.0), axis=1)

    def reduction(self, pieces, after=()):
        return Reduction(pieces, after)

    def vectors_begin(self, vector_sums):
        pieces = self.disordered(jnp.swapaxes(vector_sums.reshape(4, 8, -1), 0, 1))
        self.kept = pieces[:4]
        return self.cross_vectors(pieces[4:], CORES)

    def vectors_next(self, pairs):
        if pairs in (PLANE_B, PLANE_A):
            count = self.kept.shape[0] // 2
            more, self.kept = self.kept[count:], self.kept[:count]
            return self.cross_vectors(more, pairs)
        return self.cross_vectors(self.kept, pairs)

    def cross_vectors(self, more, pairs):
        arrived = send(pack(more), pairs)
        self.kept = self.kept + unpack(arrived, self.kept.shape[-1])
        return [arrived]

    def vectors_end(self):
        return lax.dynamic_index_in_dim(self.kept[0], self.z, 0, False)

    def reduce_far(self, rest, after=()):
        self.kept_far, give = far_sums(self.place, rest.parts(), after)
        self.far = send(give, Z_FAR)

    def reduce_near(self, zero, rest, after=()):
        self.kept_near, give = near_sums(self.place, zero.parts(), rest.parts(), after)
        self.near = send(give, Z_NEAR)

    def reduce_last(self, after=()):
        base, give = last_sums(self.place, self.kept_near, self.kept_far, self.near, self.far, after=after)
        return base, send(give, Z_CYCLE_BACK)


class Reduction:
    def __init__(self, pieces, after=()):
        self.keep_lo, self.keep_hi, give_lo, give_hi = pieces
        if after:
            give_hi = hold(give_hi, *after)
        self.got_hi = send(give_hi, CORES)
        self.got_lo = send(give_lo, CORES)
        self.more = []

    def across(self, after=()):
        self.give = [add_pieces([self.keep_hi, self.got_hi], 0, 2, after)]
        self.more.append(send(*self.give, PLANE_B))

    def side(self, after=()):
        self.give = [add_pieces(self.parts(), 1, 1, after)]
        self.more.append(send(*self.give, PLANE_A))

    def parts(self):
        return [self.keep_lo, self.got_lo, *self.more]

    def first(self):
        return [self.got_hi]

    def last(self):
        return self.more[-1:]


class Plain:
    def __init__(self):
        self.place = jnp.asarray(np.array([0, 0, 0, 0, 0, 1, 2, 3]), jnp.int32)

    def gather_early(self, weights, vectors):
        turned = lax.all_gather(weights, "dp", axis=1, tiled=True).T
        blocks = turned.reshape(4, 8, -1, D)
        self.mine, self.theirs = (blocks[:, np.array(k)] for k in ([0, 4, 1, 5], [2, 3, 6, 7]))
        entries = vectors.shape[0]
        tiles = -(-entries // 2048)
        padded = jnp.pad(vectors, (0, tiles * 2048 - entries)).reshape(tiles * 16, 128)
        gathered = lax.all_gather(padded, "dp", axis=0, tiled=True)
        gathered = gathered.reshape(-1, tiles * 2048)[:, :entries].reshape(-1, D).astype(f32)
        slots = [[jnp.pad(v, ((0, 0), (0, 16), (0, 0))) for v in self.halves(q)] for q in (0, 1)]
        return *slots, gathered

    def halves(self, q):
        return [self.mine[q, :2], self.mine[q, 2:], self.theirs[q, :2], self.theirs[q, 2:]]

    def gather_late(self):
        return []

    def gather_last(self, context):
        return [jnp.stack(both, axis=1) for both in zip(self.halves(2), self.halves(3))]

    def reduction(self, pieces, after=()):
        return PlainReduction(pieces)

    def vectors_begin(self, vector_sums):
        self.vector_sums = vector_sums.reshape(-1)
        return []

    def vectors_next(self, pairs):
        return []

    def vectors_end(self):
        return lax.psum_scatter(self.vector_sums, AXES, scatter_dimension=0, tiled=True)

    def reduce_far(self, rest, after=()):
        self.rest = rest

    def reduce_near(self, zero, rest, after=()):
        self.zero = zero

    def reduce_last(self, after=()):
        sums = jnp.concatenate([self.zero.whole(), self.rest.whole()])
        owned = lax.psum_scatter(sums, AXES, scatter_dimension=0, tiled=True)
        return owned.astype(f32), jnp.zeros_like(owned)


class PlainReduction:
    def __init__(self, pieces):
        self.pieces = jnp.concatenate(pieces)
        self.give = []

    def across(self, after=()):
        pass

    def side(self, after=()):
        pass

    def first(self):
        return []

    def last(self):
        return []

    def whole(self):
        order = np.argsort(np.array([0, 4, 1, 5, 2, 3, 6, 7]))
        return jnp.swapaxes(self.pieces[order], 0, 1).reshape(-1, D)


def pack(values):
    high = lax.reduce_precision(values, 8, 7)
    both = jnp.concatenate([high, values - high], axis=-1).astype(bf16)
    gaps = [(0, 0)] * (both.ndim - 2) + [(0, 12), (0, D - both.shape[-1])]
    return jnp.pad(both, gaps)


def unpack(packed, count):
    wide = packed[..., :4, :].astype(f32)
    return wide[..., :count] + wide[..., count : 2 * count]


VMEM_LIMIT = 60 * 1024 * 1024
whole = pl.BlockSpec(memory_space=pltpu.VMEM)
scalars = pl.BlockSpec(memory_space=pltpu.SMEM)
anywhere = pl.BlockSpec(memory_space=pl.ANY)
shape = jax.ShapeDtypeStruct
CHUNK = 256
CHUNKS = FF // CHUNK
Q = 3 * D
SPAN = 256
PART = 256


def call(kernel, outs, out_specs, scratch, flops, moved, *args, specs, name, after=(), limit=VMEM_LIMIT):
    count, skip = len(specs), len(after)

    def body(*refs):
        kernel(*refs[:count], *refs[count + skip :])

    return pl.pallas_call(
        body,
        out_shape=outs,
        in_specs=[*specs, *[anywhere] * skip],
        out_specs=out_specs,
        scratch_shapes=scratch,
        compiler_params=pltpu.CompilerParams(vmem_limit_bytes=limit),
        cost_estimate=pl.CostEstimate(flops=flops, bytes_accessed=moved, transcendentals=0),
        name=name,
    )(*args, *after)


def block_place(place, who, k):
    y, c, x = place[0], place[1], place[2]
    core = c if who == 0 else 1 - c
    first, second = k & 1, k >> 1
    to_y = jnp.where(core == 0, y ^ first, y ^ second)
    to_x = jnp.where(core == 0, x ^ second, x ^ first)
    return to_y * 4 + core * 2 + to_x


def block_rows(place, who, k, rows):
    return pl.ds(pl.multiple_of(block_place(place, who, k) * rows, math.gcd(rows, 16)), rows)


def begin(source, target, sem):
    copy = pltpu.make_async_copy(source, target, sem)
    copy.start()
    return copy


def slot_pieces(slots):
    return [
        [(refs[k // 2], (k % 2,) + ((slot - 2,) if slot > 1 else ())) for k in range(8)]
        for slot, refs in enumerate(slots)
    ]


def ingest(place, quarter, slots, into, sems):
    rows = into.shape[0] // 8
    targets = [into.at[block_rows(place, k // 4, k % 4, rows)] for k in range(8)]
    all_pieces = slot_pieces(slots)
    for slot, pieces in enumerate(all_pieces):

        @pl.when(place[4 + quarter] == slot)
        def _():
            for k, (ref, index) in enumerate(pieces):
                pltpu.make_async_copy(ref.at[(*index, pl.ds(0, rows))], targets[k], sems.at[k]).start()

    return [
        pltpu.make_async_copy(ref.at[(*index, pl.ds(0, rows))], targets[k], sems.at[k])
        for k, (ref, index) in enumerate(all_pieces[0])
    ]


def hand_block(place, source, at, targets, part, sem):
    rows = source.shape[0] // 8
    y, c, x = place[0], place[1], place[2]
    core = (at >> 1) & 1
    flip_y, flip_x = (at >> 2) ^ y, (at & 1) ^ x
    first = jnp.where(core == 0, flip_y, flip_x)
    second = jnp.where(core == 0, flip_x, flip_y)
    which = jnp.where(core == c, 0, 2) + second
    for k, target in enumerate(targets):

        @pl.when(which == k)
        def _():
            pltpu.make_async_copy(source.at[rows_of(at, rows)], target.at[first, part], sem).start()


def hand_wait(source, targets, part, sems):
    rows = source.shape[0] // 8
    for k in range(8):
        pltpu.make_async_copy(source.at[pl.ds(0, rows)], targets[0].at[0, part], sems.at[k]).wait()


def finish(*copies):
    for copy in copies:
        if isinstance(copy, (list, tuple)):
            finish(*copy)
        else:
            copy.wait()


def rows_of(i, step):
    return pl.ds(pl.multiple_of(i * step, math.gcd(step, 256)), step)


def loop(count, body):
    def step(i, carry):
        body(i)
        return carry

    lax.fori_loop(0, count, step, 0)


def column(row, width):
    return jnp.broadcast_to(row, (width, row.shape[1])).T


def is_region(types):
    return column((types == 1).astype(f32), 128)[:, 0:1] > 0.5


def allowed_keys(lengths, keys, s):
    slot = lax.broadcasted_iota(jnp.int32, (1, SPAN), 1)
    allowed = (slot < lengths[s]) & ((keys[:, rows_of(s, SPAN)] == 1) | (slot == 0))
    return jnp.where(allowed, 3e38, -1e30)


def embed(tokens, types, table):
    return tokens.astype(f32) + jnp.where(is_region(types), table[1:2, :], table[0:1, :])


def attend_kernel(
    place, lengths, a0, a1, a2, a3, b0, b1, b2, b3, tokens, types, keys, table,
    turned_out, context_out, spreads,
    weights, low, turned, context_turned, context, mask, sems,
):
    copies = ingest(place, 0, ((a0, a1, a2, a3), (b0, b1, b2, b3)), weights, sems)
    rows = tokens.shape[0]

    def prepare(i):
        here = rows_of(i, PART)
        low[here, :] = embed(tokens[here, :], types[:, here], table[...]).astype(bf16)
        mask[here, :] = column(allowed_keys(lengths, keys, i), SPAN)

    loop(rows // PART, prepare)
    finish(copies)
    step = 384

    def project(i):
        here = rows_of(i, step)
        half = rows_of(i % 2, step)
        bias = jnp.where(i // 2 == 0, table[4:5, half], jnp.where(i // 2 == 2, table[5:6, half], 0.0))
        made = contract(weights[here, :], low[...], 1, 1) + column(bias, 128)[:, 0:1]
        made = made * jnp.where(i < D // step, HD ** (-0.5), 1.0)
        turned[here, :] = made.astype(bf16)

    loop(Q // step, project)
    sent = begin(turned, turned_out, sems.at[8])

    together = 8

    def units(i):
        places = []
        for j in range(together):
            u = i * together + j
            places.append((u % H, pl.multiple_of((u % H) * HD, HD), rows_of(u // H, SPAN)))
        scores = [
            contract(turned[pl.ds(D + at, HD), cols], turned[pl.ds(at, HD), cols], 0, 0)
            for _, at, cols in places
        ]
        probs = []
        for (h, at, cols), score in zip(places, scores):
            score = jnp.minimum(score, mask[cols, :])
            peak = jnp.max(score, axis=0, keepdims=True)
            powers = jnp.exp(score - peak)
            total = jnp.sum(powers, axis=0, keepdims=True)
            probs.append((powers * (1.0 / total)).astype(bf16))
            spreads[pl.ds(h, 1), cols] = peak + jnp.log(total)
        for (h, at, cols), prob in zip(places, probs):
            context_turned[pl.ds(at, HD), cols] = contract(turned[pl.ds(2 * D + at, HD), cols], prob, 1, 0).astype(bf16)

    loop(H * (rows // SPAN) // together, units)

    def turn(i):
        here = rows_of(i, 128)
        context[here, :] = context_turned[:, here].T

    loop(rows // 128, turn)
    finish(begin(context, context_out, sems.at[9]), sent)


def attend(place, lengths, pieces, tokens, types, keys, table, after=()):
    rows = tokens.shape[0]
    return call(
        attend_kernel,
        [shape((Q, rows), bf16), shape((rows, D), bf16), shape((H, rows), f32)],
        [anywhere, anywhere, whole],
        [
            pltpu.VMEM((Q, D), bf16),
            pltpu.VMEM((rows, D), bf16),
            pltpu.VMEM((Q, rows), bf16),
            pltpu.VMEM((D, rows), bf16),
            pltpu.VMEM((rows, D), bf16),
            pltpu.VMEM((rows, SPAN), f32),
            pltpu.SemaphoreType.DMA((10,)),
        ],
        2 * rows * Q * D + 4 * rows * 256 * D,
        20 << 20,
        place, lengths, *pieces, tokens, types, keys, table,
        specs=[scalars] * 2 + [anywhere] * 8 + [whole] * 4,
        name="attend",
        after=after,
    )


def normalise(inputs):
    centre = jnp.mean(inputs, axis=-1, keepdims=True)
    offset = inputs - centre
    spread = lax.rsqrt(jnp.mean(offset * offset, axis=-1, keepdims=True) + norm_eps)
    return offset * spread, spread


def normalise_back(scaled, unit, spread):
    return spread * (
        scaled
        - jnp.mean(scaled, axis=-1, keepdims=True)
        - unit * jnp.mean(scaled * unit, axis=-1, keepdims=True)
    )


def gelu_both(v):
    cumulative = 0.5 * (1.0 + lax.erf(v * math.sqrt(0.5)))
    density = jnp.exp(-0.5 * v * v) * (1.0 / math.sqrt(2.0 * math.pi))
    return v * cumulative, cumulative + v * density


def weight_chunk(weights, offset, i):
    return weights[pl.ds(pl.multiple_of(offset + i * CHUNK, CHUNK), CHUNK), :]


def row_sums(count, body, sums, rows):
    zero = jnp.zeros((8, D), f32)

    def step(i, carry):
        made = body(i)
        return tuple(
            have + jnp.sum(more.reshape(-1, 8, D), axis=0) for have, more in zip(carry, made)
        )

    made = lax.fori_loop(0, count, step, (zero,) * len(rows))
    for have, row in zip(made, rows):
        sums[row : row + 1, 0:D] = jnp.sum(have, axis=0, keepdims=True)


STEP = 512


def middle_kernel(
    place, a0, a1, a2, a3, b0, b1, b2, b3, c0, c1, c2, c3, tokens_in, context_in, cotangent_in, types, table,
    layer_out_to, grad_first_to, grad_context_to, sums, keep_lo, keep_hi, give_lo, give_hi,
    weights, pre_a, pre_b, total, tokens, context, cotangent, layer_out, active, slope, unit_one, spread_one, normed_low,
    grad_context, down_made, sems, more,
):
    rows = tokens.shape[0]
    slots = ((a0, a1, a2, a3), (b0, b1, b2, b3), (c0, c1, c2, c3), (c0, c1, c2, c3))
    early = [begin(context_in, context, more.at[0]), begin(tokens_in, tokens, more.at[1])]
    batches = [ingest(place, 1, slots, weights.at[pl.ds(0, Q)], sems.at[0])]
    up, down = D, D + FF
    finish(early, batches[0])
    batches.append(ingest(place, 2, slots, weights.at[pl.ds(Q, Q)], sems.at[1]))
    batches.append(ingest(place, 3, slots, weights.at[pl.ds(2 * Q, Q)], sems.at[2]))
    late = begin(cotangent_in, cotangent, more.at[2])

    def branch(i):
        here = rows_of(i, SPAN)
        total[here, :] = contract(context[here, :], weights[0:D, :], 1, 1)

    loop(rows // SPAN, branch)

    def first(i):
        here = rows_of(i, PART)
        unit, spread = normalise(embed(tokens[here, :], types[:, here], table[...]) + (total[here, :] + table[6:7, :]))
        unit_one[here, :] = unit
        spread_one[here, :] = jnp.broadcast_to(spread, (PART, 128))
        normed_low[here, :] = (unit * table[2:3, :] + table[3:4, :]).astype(bf16)

    loop(rows // PART, first)
    sent = []
    targets = (keep_lo, keep_hi, give_lo, give_hi)
    finish(batches[1])

    def gelu(pre, i, here):
        bias = table[pl.ds(10 + i // (D // CHUNK), 1), rows_of(i % (D // CHUNK), CHUNK)]
        return gelu_both(pre[here, :] + bias)

    def keep_gelu(made, i, here):
        cols = rows_of(i, CHUNK)
        active[here, cols] = made[0].astype(bf16)
        slope[here, cols] = made[1]

    everything = slice(None)

    def forward(t):
        before = jnp.maximum(2 * t - 1, 0)
        both = gelu(pre_b, before, everything)
        pre_a[...] = contract(normed_low[...], weight_chunk(weights, up, 2 * t), 1, 1)
        keep_gelu(both, before, everything)
        both = gelu(pre_a, 2 * t, everything)
        pre_b[...] = contract(normed_low[...], weight_chunk(weights, up, 2 * t + 1), 1, 1)
        keep_gelu(both, 2 * t, everything)

    loop(CHUNKS // 2, forward)

    def forward_end(i):
        here = rows_of(i, PART)
        keep_gelu(gelu(pre_b, CHUNKS - 1, here), CHUNKS - 1, here)

    loop(rows // PART, forward_end)
    finish(batches[2])

    def add_down(i):
        here = rows_of(i, SPAN)
        total[here, :] = contract(active[here, :], weights[down : down + FF, :], 1, 0)

    loop(rows // SPAN, add_down)
    finish(late)

    def second(i):
        here = rows_of(i, PART)
        normed_one = unit_one[here, :] * table[2:3, :] + table[3:4, :]
        unit, spread = normalise(normed_one + (total[here, :] + table[9:10, :]))
        layer_out[here, :] = (unit * table[7:8, :] + table[8:9, :]).astype(bf16)
        upstream = cotangent[here, :].astype(f32)
        grad = normalise_back(upstream * table[7:8, :], unit, spread)
        total[here, :] = grad
        low = grad.astype(bf16)
        tokens[here, :] = low
        return upstream * unit, upstream, low.astype(f32)

    row_sums(rows // PART, second, sums, (7, 8, 9))
    sent.append(begin(layer_out, layer_out_to, more.at[5]))

    def weigh_down(i):
        here = rows_of(i, STEP)
        down_made[here, :] = contract(active[:, here], tokens[...], 0, 0).astype(bf16)

    loop(FF // STEP, weigh_down)
    third_quarter = down_made.at[pl.ds(D, Q)]
    loop(8, lambda p: hand_block(place, third_quarter, p, targets, 2, sems.at[2, p]))

    def through(pre, i, here):
        return (pre[here, :] * slope[here, rows_of(i, CHUNK)]).astype(bf16)

    def backward(t):
        before = jnp.maximum(2 * t - 1, 0)
        low = through(pre_b, before, everything)
        pre_a[...] = contract(tokens[...], weight_chunk(weights, down, 2 * t), 1, 1)
        active[:, rows_of(before, CHUNK)] = low
        low = through(pre_a, 2 * t, everything)
        pre_b[...] = contract(tokens[...], weight_chunk(weights, down, 2 * t + 1), 1, 1)
        active[:, rows_of(2 * t, CHUNK)] = low

    loop(CHUNKS // 2, backward)

    def backward_end(i):
        here = rows_of(i, PART)
        active[here, rows_of(CHUNKS - 1, CHUNK)] = through(pre_b, CHUNKS - 1, here)

    loop(rows // PART, backward_end)

    def add_up(i):
        here = rows_of(i, SPAN)
        total[here, :] += contract(active[here, :], weights[up : up + FF, :], 1, 0)

    loop(rows // SPAN, add_up)

    def third(i):
        here = rows_of(i, PART)
        upstream = total[here, :]
        unit = unit_one[here, :]
        grad = normalise_back(upstream * table[2:3, :], unit, spread_one[here, 0:1])
        total[here, :] = grad
        low = grad.astype(bf16)
        cotangent[here, :] = low
        of_one = is_region(types[:, here])
        return upstream * unit, upstream, low.astype(f32), jnp.where(of_one, 0.0, grad), jnp.where(of_one, grad, 0.0)

    row_sums(rows // PART, third, sums, (2, 3, 6, 0, 1))
    sent.append(begin(total, grad_first_to, more.at[8]))

    def through_out(i):
        here = rows_of(i, SPAN)
        grad_context[:, here] = contract(cotangent[here, :], weights[0:D, :], 1, 0).T.astype(bf16)

    loop(rows // SPAN, through_out)
    sent.append(begin(grad_context, grad_context_to, more.at[10]))
    moved = begin(down_made.at[pl.ds(0, D)], weights.at[pl.ds(D + FF, D)], more.at[9])

    def weigh_up(i):
        here = rows_of(i, STEP)
        rows_there = pl.ds(pl.multiple_of(D + i * STEP, 256), STEP)
        weights[rows_there, :] = contract(active[:, here], normed_low[...], 0, 0).astype(bf16)
        added = jnp.sum(active[:, here].astype(f32), 0, keepdims=True)
        sums[pl.ds(10, 1), here] = added

    half = FF // STEP // 2
    loop(half, lambda i: weigh_up(half + i))
    finish(moved)
    hand_wait(third_quarter, targets, 2, sems.at[2])
    quarters = weights.at[pl.ds(0, Q)], weights.at[pl.ds(Q, Q)]
    loop(8, lambda p: hand_block(place, quarters[1], p, targets, 1, sems.at[1, p]))

    def weigh_out(i):
        here = rows_of(i, 384)
        weights[here, :] = contract(cotangent[:, here], context[...], 0, 0).astype(bf16)

    loop(2, weigh_out)
    loop(half, weigh_up)
    loop(8, lambda p: hand_block(place, quarters[0], p, targets, 0, sems.at[0, p]))
    hand_wait(quarters[1], targets, 1, sems.at[1])
    hand_wait(quarters[0], targets, 0, sems.at[0])
    finish(sent)


def middle(place, pieces, tokens, types, context, cotangent, table, after=()):
    rows = tokens.shape[0]
    tall = pltpu.VMEM((rows, D), bf16)
    return call(
        middle_kernel,
        [shape((rows, D), bf16), shape((rows, D), f32), shape((D, rows), bf16), shape((11, FF), f32)]
        + [shape((2, 3, Q // 8, D), bf16)] * 4,
        [anywhere] * 3 + [whole] + [anywhere] * 4,
        [
            pltpu.VMEM((3 * Q, D), bf16),
            pltpu.VMEM((rows, CHUNK), f32),
            pltpu.VMEM((rows, CHUNK), f32),
            pltpu.VMEM((rows, D), f32),
            tall,
            tall,
            tall,
            tall,
            pltpu.VMEM((rows, FF), bf16),
            pltpu.VMEM((rows, FF), f32),
            pltpu.VMEM((rows, D), f32),
            pltpu.VMEM((rows, 128), f32),
            tall,
            pltpu.VMEM((D, rows), bf16),
            pltpu.VMEM((FF, D), bf16),
            pltpu.SemaphoreType.DMA((3, 8)),
            pltpu.SemaphoreType.DMA((11,)),
        ],
        6 * rows * 3 * Q * D,
        60 << 20,
        place, *pieces, tokens, context, cotangent, types, table,
        specs=[scalars] + [anywhere] * 15 + [whole] * 2,
        name="middle",
        after=after,
    )


def attend_back_kernel(
    place, lengths, turned, grad_context, spreads, keys,
    mixed_to,
    mixed, mask, sems,
):
    rows = turned.shape[1]

    def prepare(i):
        here = rows_of(i, PART)
        mask[here, :] = column(allowed_keys(lengths, keys, i), SPAN)

    loop(rows // PART, prepare)

    together = 6

    def units(i):
        places = []
        for j in range(together):
            u = i * together + j
            places.append((u % H, pl.multiple_of((u % H) * HD, HD), rows_of(u // H, SPAN)))
        query = [turned[pl.ds(at, HD), cols] for _, at, cols in places]
        key = [turned[pl.ds(D + at, HD), cols] for _, at, cols in places]
        grad = [grad_context[pl.ds(at, HD), cols] for _, at, cols in places]
        scores = [contract(k, q, 0, 0) for k, q in zip(key, query)]
        grad_probs = [
            contract(turned[pl.ds(2 * D + at, HD), cols], g, 0, 0) for (_, at, cols), g in zip(places, grad)
        ]
        made = []
        for (h, at, cols), score, grad_prob in zip(places, scores, grad_probs):
            probs = jnp.exp(jnp.minimum(score, mask[cols, :]) - spreads[pl.ds(h, 1), cols])
            inner = jnp.sum(probs * grad_prob, axis=0, keepdims=True)
            made.append(((probs * (grad_prob - inner)).astype(bf16), probs.astype(bf16)))
        for (h, at, cols), q, k, g, (grad_score, prob) in zip(places, query, key, grad, made):
            mixed[pl.ds(at, HD), cols] = (contract(k, grad_score, 1, 0) * HD ** (-0.5)).astype(bf16)
            mixed[pl.ds(D + at, HD), cols] = contract(q, grad_score, 1, 1).astype(bf16)
            mixed[pl.ds(2 * D + at, HD), cols] = contract(g, prob, 1, 1).astype(bf16)

    loop(H * (rows // SPAN) // together, units)
    finish(begin(mixed, mixed_to, sems.at[0]))


def attend_back(place, lengths, turned, grad_context, spreads, keys, after=()):
    rows = turned.shape[1]
    return call(
        attend_back_kernel,
        [shape((Q, rows), bf16)],
        [anywhere],
        [
            pltpu.VMEM((Q, rows), bf16),
            pltpu.VMEM((rows, SPAN), f32),
            pltpu.SemaphoreType.DMA((1,)),
        ],
        10 * rows * 256 * D,
        25 << 20,
        place, lengths, turned, grad_context, spreads, keys,
        specs=[scalars] * 2 + [whole] * 4,
        limit=36 * 1024 * 1024,
        name="attend_back",
        after=after,
    )[0]


def mixed_grad_kernel(
    place, a0, a1, a2, a3, b0, b1, b2, b3, mixed_in, tokens, types, table, middle_sums,
    keep_lo, keep_hi, give_lo, give_hi, sums,
    low, mixed, made, weights, by_type, sems, more,
):
    step = 384
    for i in range(Q // step):
        here = pl.ds(i * step, step)
        begin(mixed_in.at[here], mixed.at[here], more.at[i])
    copies = ingest(place, 0, ((a0, a1, a2, a3), (b0, b1, b2, b3)), weights, sems)
    rows = tokens.shape[0]
    targets = (keep_lo, keep_hi, give_lo, give_hi)

    def prepare(i):
        here = rows_of(i, PART)
        low[here, :] = embed(tokens[here, :], types[:, here], table[...]).astype(bf16)

    loop(rows // PART, prepare)
    type_row = lax.broadcasted_iota(jnp.int32, (8, rows), 0)
    one_hot = (type_row == types[...]).astype(f32).astype(bf16)

    def weigh(i):
        here = rows_of(i, step)
        pltpu.make_async_copy(mixed_in.at[here], mixed.at[here], more.at[i]).wait()
        made[here, :] = contract(mixed[here, :], low[...], 1, 0).astype(bf16)
        by_type[:, here] = contract(one_hot, mixed[here, :], 1, 1)

    loop(Q // step, weigh)
    finish(copies)
    loop(8, lambda p: hand_block(place, made, p, targets, 0, sems.at[p]))
    high, rest = twice(by_type[...])
    through = contract(high, weights[...], 1, 0) + contract(rest, weights[...], 1, 0)
    sums[0:10, :] = middle_sums[0:10, 0:D]
    sums[0:2, :] = middle_sums[0:2, 0:D] + through[0:2, :]
    for row, start in ((4, 0), (5, 2 * D)):
        sums[row : row + 1, :] = by_type[0:1, start : start + D] + by_type[1:2, start : start + D]
    for i in range(FF // D):
        sums[10 + i : 11 + i, :] = middle_sums[10:11, i * D : (i + 1) * D]
    hand_wait(made, targets, 0, sems)


def mixed_grad(place, pieces, mixed, tokens, types, table, middle_sums, after=()):
    rows = tokens.shape[0]
    return call(
        mixed_grad_kernel,
        [shape((2, 1, Q // 8, D), bf16)] * 4 + [shape((NVEC // D, D), f32)],
        [anywhere] * 4 + [whole],
        [
            pltpu.VMEM((rows, D), bf16),
            pltpu.VMEM((Q, rows), bf16),
            pltpu.VMEM((Q, D), bf16),
            pltpu.VMEM((Q, D), bf16),
            pltpu.VMEM((8, Q), f32),
            pltpu.SemaphoreType.DMA((8,)),
            pltpu.SemaphoreType.DMA((6,)),
        ],
        0,
        0,
        place, *pieces, mixed, tokens, types, table, middle_sums,
        specs=[scalars] + [anywhere] * 9 + [whole] * 4,
        name="mixed_grad",
        after=after,
    )


def input_kernel(place, a0, a1, a2, a3, b0, b1, b2, b3, mixed, grad_first, input_grad_to, weights, made, sems):
    finish(ingest(place, 0, ((a0, a1, a2, a3), (b0, b1, b2, b3)), weights, sems))
    rows = grad_first.shape[0]

    def through(i):
        here = rows_of(i, SPAN)
        made[here, :] = grad_first[here, :] + contract(mixed[:, here], weights[...], 0, 0)
        begin(made.at[here], input_grad_to.at[here], sems.at[i])

    loop(rows // SPAN, through)
    for i in range(rows // SPAN):
        here = pl.ds(i * SPAN, SPAN)
        pltpu.make_async_copy(made.at[here], input_grad_to.at[here], sems.at[i]).wait()


def input_back(place, pieces, mixed, grad_first, after=()):
    rows = grad_first.shape[0]
    return call(
        input_kernel,
        [shape((rows, D), f32)],
        [anywhere],
        [pltpu.VMEM((Q, D), bf16), pltpu.VMEM((rows, D), f32), pltpu.SemaphoreType.DMA((8,))],
        2 * rows * Q * D,
        15 << 20,
        place, *pieces, mixed, grad_first,
        specs=[scalars] + [anywhere] * 8 + [whole] * 2,
        name="input_back",
        after=after,
    )[0]


SMALL_LIMIT = 16 * 1024 * 1024


def small(kernel, outs, *args, name, after=(), scratch=(), specs=None, out_specs=None):
    specs = specs or [scalars if a.dtype == jnp.int32 else whole for a in args]
    many = isinstance(outs, (list, tuple))
    return call(
        kernel, outs, out_specs or ([whole] * len(outs) if many else whole), list(scratch), 0, 0, *args,
        specs=specs, name=name, after=after, limit=SMALL_LIMIT,
    )


def hold(values, *after):
    skip = len(after)
    return pl.pallas_call(
        lambda *refs: None,
        out_shape=shape(values.shape, values.dtype),
        in_specs=[anywhere] * (1 + skip),
        out_specs=anywhere,
        input_output_aliases={0: 0},
        name="hold",
    )(values, *after)


def prepare_kernel(place, turned, few, own, sem):
    rows = own.shape[0] - 16
    copy = begin(turned.at[pl.ds(pl.multiple_of(place[2] * rows, 16), rows)], own.at[pl.ds(0, rows)], sem)
    entries = few.shape[1] // 2
    row = few[...].astype(f32)
    row = jnp.where(place[2] == 0, row[:, :entries], row[:, entries:])
    here = lax.broadcasted_iota(jnp.int32, (16, entries), 0) == place[3]
    own[rows:, :] = jnp.zeros((16, D), bf16)
    own[rows:, 0:entries] = jnp.where(here, row, 0.0).astype(bf16)
    finish(copy)


def prepare_own(place, turned, few):
    return small(
        prepare_kernel, shape((turned.shape[0] // 2 + 16, D), bf16), place, turned, few,
        name="prepare_own", scratch=[pltpu.SemaphoreType.DMA], specs=[scalars, anywhere, whole],
    )


def by_plane(place, table, choices):
    out = choices[table[3]]
    for z in (2, 1, 0):
        out = jnp.where(place[3] == z, choices[table[z]], out)
    return out


def merge(old, new):
    old, new = old.astype(f32), new.astype(f32)
    return jnp.where(old == 0.0, new, old).astype(bf16)


def after_one_kernel(place, own, one, side, pass_on, slab, pair):
    rows = own.shape[0] - 16
    pass_on[:rows, :] = by_plane(place, (0, 1, 1, 0), (own[:rows, :], one[:rows, :]))
    merged = merge(own[rows:, :], one[rows:, :])
    pass_on[rows:, :] = merged
    slab[...] = merged
    pair[0] = own[...]
    pair[1] = side[...]


def after_one(place, own, one, side):
    outs = [shape(own.shape, bf16), shape((16, D), bf16), shape((2, *own.shape), bf16)]
    return small(after_one_kernel, outs, place, own, one, side, name="after_one")


def after_two_kernel(place, pass_on, one, two, far, block, slot):
    rows = one.shape[0] - 16
    block[:rows, :] = by_plane(place, (0, 1, 0, 1), (one[:rows, :], two[:rows, :]))
    block[rows:, :] = merge(merge(pass_on[rows:, :], two[rows:, :]), far[...])
    slot[...] = by_plane(place, (1, 0, 1, 0), (one[:rows, :], two[:rows, :]))


def after_two(place, pass_on, one, two, far, after):
    outs = [shape(one.shape, bf16), shape((one.shape[0] - 16, D), bf16)]
    return small(after_two_kernel, outs, place, pass_on, one, two, far, name="after_two", after=after)


def after_three_kernel(place, block, side, middle, three, pair, slot):
    rows = slot.shape[0]
    pair[0] = block[...]
    pair[1] = side[...]
    slot[...] = by_plane(place, (1, 0, 0, 1), (middle[:rows, :], three[:rows, :]))


def after_three(place, block, side, middle, three, after):
    outs = [shape((2, *block.shape), bf16), shape((block.shape[0] - 16, D), bf16)]
    return small(after_three_kernel, outs, place, block, side, middle, three, name="after_three", after=after)


def after_four_kernel(slot_c, side_c, slot_d, side_d, late):
    late[0, 0], late[0, 1] = slot_c[...], slot_d[...]
    late[1, 0], late[1, 1] = side_c[...], side_d[...]


def after_four(slot_c, side_c, slot_d, side_d, after):
    outs = shape((2, 2, *slot_c.shape), bf16)
    return small(after_four_kernel, outs, slot_c, side_c, slot_d, side_d, name="after_four", after=after)


def read_vectors_kernel(entries, place, a, b, c, d, out, got, sems):
    rows = a.shape[1] - 16
    refs = (a, b, c, d)
    finish([begin(refs[k // 2].at[k % 2, pl.ds(rows, 16)], got.at[k], sems.at[k]) for k in range(8)])
    for k in range(8):
        at = block_place(place, k // 4, k % 4)
        slab = got[k].astype(f32)
        for z in range(4):
            out[pl.ds(z * 8 + at, 1), :] = slab[z : z + 1, 0:entries]


def read_vectors(place, pieces, entries):
    return small(
        functools.partial(read_vectors_kernel, entries), shape((32, entries), f32), place, *pieces,
        name="read_vectors", specs=[scalars] + [anywhere] * 4,
        scratch=[pltpu.VMEM((8, 16, D), bf16), pltpu.SemaphoreType.DMA((8,))],
    )


def picked(kernel, outs, specs, args, name, after=()):
    count, skip = len(specs), len(after)

    def body(*refs):
        kernel(*refs[:count], *refs[count + skip :])

    return pl.pallas_call(
        body,
        grid=(1,),
        out_shape=outs,
        in_specs=[*specs, *[anywhere] * skip],
        out_specs=[pl.BlockSpec(o.shape, lambda i, n=len(o.shape): (0,) * n) for o in outs],
        compiler_params=pltpu.CompilerParams(vmem_limit_bytes=SMALL_LIMIT),
        cost_estimate=pl.CostEstimate(flops=0, bytes_accessed=0, transcendentals=0),
        name=name,
    )(*args, *after)


ADD_ROWS = 96


def add_pieces_kernel(*refs):
    _, n, rows, _ = refs[0].shape
    for a in range(refs[0].shape[0]):
        for b in range(n):

            def step(i):
                here = rows_of(i, ADD_ROWS)
                total = refs[0][a, b, here, :].astype(f32)
                for ref in refs[1:-1]:
                    total = total + ref[a, b, here, :].astype(f32)
                refs[-1][a, b, here, :] = total.astype(bf16)

            loop(rows // ADD_ROWS, step)


def add_pieces(parts, first, count, after=()):
    _, n, rows, width = parts[0].shape
    block = (count, n, rows, width)
    return picked(
        add_pieces_kernel,
        [shape(block, bf16)],
        [pl.BlockSpec(block, lambda i: (first // count, 0, 0, 0))] * len(parts),
        parts,
        "add_pieces",
        after,
    )[0]


def rows_spec(rows):
    return pl.BlockSpec((rows, D), lambda i: (0, 0))


def piece_spec(rows, j):
    return pl.BlockSpec((1, 1, rows, D), lambda i: (0, j, 0, 0))


def sum_of(refs, here):
    total = refs[0][0, 0, here, :].astype(f32)
    for ref in refs[1:]:
        total = total + ref[0, 0, here, :].astype(f32)
    return total


def two_sums_kernel(table, keep_table, place, *refs):
    def step(i):
        here = rows_of(i, ADD_ROWS)
        sums = sum_of(refs[:4], here), sum_of(refs[4:8], here)
        refs[8][here, :] = by_plane(place, keep_table, sums)
        refs[9][here, :] = by_plane(place, table, sums).astype(bf16)

    loop(refs[8].shape[0] // ADD_ROWS, step)


def two_sums(place, table, first, second, name, after):
    rows = first[0][0].shape[2]
    args = first + second
    return picked(
        functools.partial(two_sums_kernel, table, tuple(1 - k for k in table)),
        [shape((rows, D), f32), shape((rows, D), bf16)],
        [scalars] + [piece_spec(rows, j) for _, j in args],
        [place] + [a for a, _ in args],
        name,
        after,
    )


def far_sums(place, rest, after=()):
    return two_sums(place, (1, 1, 0, 0), [(p, 0) for p in rest], [(p, 1) for p in rest], "far_sums", after)


def near_sums(place, zero, rest, after=()):
    return two_sums(place, (1, 0, 1, 0), [(p, 0) for p in zero], [(p, 2) for p in rest], "near_sums", after)


def last_sums_kernel(place, kept_near, kept_far, near, far, base, give):
    def step(i):
        here = rows_of(i, ADD_ROWS)
        sums = (kept_near[here, :] + near[here, :].astype(f32), kept_far[here, :] + far[here, :].astype(f32))
        give[here, :] = by_plane(place, (1, 0, 0, 1), sums).astype(bf16)
        base[here, :] = by_plane(place, (0, 1, 1, 0), sums)

    loop(base.shape[0] // ADD_ROWS, step)


def last_sums(place, *args, after=()):
    rows = args[0].shape[0]
    return picked(
        last_sums_kernel,
        [shape((rows, D), f32), shape((rows, D), bf16)],
        [scalars] + [rows_spec(rows)] * 4,
        [place, *args],
        "last_sums",
        after,
    )


def twice(values):
    high = values.astype(bf16)
    return high, (values - high.astype(f32)).astype(bf16)


def owner_kernel(
    base, last, left, right, left_root, right_root, master, slow,
    grad_to, left_to, right_to, master_to, slow_to, low_to,
    grad_v, last_v, left_v, right_v, left_root_v, right_root_v, master_v, slow_v, low_v, sems,
):
    pairs = (
        (base, grad_v), (last, last_v), (left_root, left_root_v), (right_root, right_root_v),
        (left, left_v), (right, right_v), (master, master_v), (slow, slow_v),
    )
    loads = [begin(a, b, sems.at[i]) for i, (a, b) in enumerate(pairs)]
    finish(loads[:2])
    grad_v[...] = grad_v[...] + last_v[...].astype(f32)
    sent = [begin(grad_v, grad_to, sems.at[8])]
    high, low = twice(grad_v[...])
    wide = jnp.concatenate([high, high, low], axis=1)
    finish(loads[2:4])
    root_high, root_low = twice(left_root_v[...])
    turned = contract(wide, jnp.concatenate([root_high, root_low, root_high], axis=0), 1, 0)
    high_t, low_t = twice(turned)
    root_high, root_low = twice(right_root_v[...])
    steered = (
        contract(root_high, high_t, 1, 0) + contract(root_high, low_t, 1, 0) + contract(root_low, high_t, 1, 0)
    )
    finish(loads[6:])
    made = master_v[...] - learning_rate * steered
    master_v[...] = made
    slow_v[...] = slow_decay * slow_v[...] + (1.0 - slow_decay) * made
    low_v[...] = made.astype(bf16)
    sent += [
        begin(master_v, master_to, sems.at[9]), begin(slow_v, slow_to, sems.at[10]), begin(low_v, low_to, sems.at[11])
    ]
    finish(loads[4:6])
    tall_a = jnp.concatenate([high, high, low], axis=0)
    tall_b = jnp.concatenate([high, low, high], axis=0)
    left_v[...] = stat_decay * left_v[...] + (1.0 - stat_decay) * contract(tall_a, tall_b, 0, 0)
    sent.append(begin(left_v, left_to, sems.at[12]))
    other = jnp.concatenate([high, low, high], axis=1)
    right_v[...] = stat_decay * right_v[...] + (1.0 - stat_decay) * contract(wide, other, 1, 1)
    finish(sent, begin(right_v, right_to, sems.at[13]))


def owner_step(base, last, left, right, left_root, right_root, master, slow):
    rows = base.shape[0]
    flat, stats, small_stats = (rows, D), (D, D), (rows, rows)
    return call(
        owner_kernel,
        [shape(flat, f32), shape(stats, f32), shape(small_stats, f32), shape(flat, f32), shape(flat, f32), shape(flat, bf16)],
        [anywhere] * 6,
        [
            pltpu.VMEM(flat, f32), pltpu.VMEM(flat, bf16), pltpu.VMEM(stats, f32), pltpu.VMEM(small_stats, f32),
            pltpu.VMEM(stats, f32), pltpu.VMEM(small_stats, f32), pltpu.VMEM(flat, f32), pltpu.VMEM(flat, f32),
            pltpu.VMEM(flat, bf16), pltpu.SemaphoreType.DMA((14,)),
        ],
        6 * D * rows * (2 * D + 2 * rows), 15 << 20,
        base, last, left, right, left_root, right_root, master, slow,
        specs=[anywhere] * 8, name="owner_step",
    )


def per_device(
    ring,
    tokens,
    cotangent,
    lengths,
    key_mask,
    type_ids,
    weights,
    vectors,
    master,
    slow_weights,
    left_stats,
    right_stats,
    left_root,
    right_root,
    vector_master,
    vector_moment,
    slow_vectors,
):
    ring = ring()
    place = ring.place
    slot_a, slot_b, table = ring.gather_early(weights, vectors)
    early = [*slot_a, *slot_b]
    types, keys = type_ids[None, :], key_mask[None, :]

    turned, context, spreads = attend(place, lengths, early, tokens, types, keys, table, after=ring.gather_late())
    pieces = early + ring.gather_last(context)
    layer_out, grad_first, grad_context, middle_sums, *parts = middle(
        place, pieces, tokens, types, context, cotangent, table
    )
    rest = ring.reduction(parts)
    rest.across()
    mixed = attend_back(place, lengths, turned, grad_context, spreads, keys, after=rest.give)
    *parts, vector_sums = mixed_grad(place, early, mixed, tokens, types, table, middle_sums)
    zero = ring.reduction(parts)
    swapped = ring.vectors_begin(vector_sums)
    rest.side(after=[vector_sums])
    zero.across(after=rest.give + swapped)
    crossed = ring.vectors_next(PLANE_B)
    input_grad = input_back(place, early, mixed, grad_first, after=zero.give)
    zero.side(after=[input_grad, *rest.last(), *crossed])
    crossed = ring.vectors_next(PLANE_A)
    ring.reduce_far(rest, after=zero.give)
    ring.reduce_near(zero, rest, after=crossed)
    crossed = ring.vectors_next(Z_NEAR)
    base, last = ring.reduce_last(after=crossed)
    ring.vectors_next(Z_FAR)
    owned_vector = ring.vectors_end()
    grad_t, left_new, right_new, master_t, slow_t, low_t = owner_step(
        base, last, left_stats, right_stats, left_root, right_root, master.T, slow_weights.T
    )
    owned_grad, master_new, slow_new, weights_new = grad_t.T, master_t.T, slow_t.T, low_t.T
    moment_new = stat_decay * vector_moment + (1.0 - stat_decay) * owned_vector * owned_vector
    vector_master_new = vector_master - vector_rate * owned_vector / (jnp.sqrt(moment_new) + 1e-08)
    slow_vectors_new = slow_decay * slow_vectors + (1.0 - slow_decay) * vector_master_new
    vectors_new = vector_master_new.astype(bf16)
    return (
        layer_out,
        input_grad,
        owned_grad,
        left_new,
        right_new,
        master_new,
        slow_new,
        weights_new,
        owned_vector,
        moment_new,
        vector_master_new,
        slow_vectors_new,
        vectors_new,
    )


def solution(mesh):
    in_specs = (
        P(("dp", "opt"), None),
        P(("dp", "opt"), None),
        P(("dp", "opt")),
        P(("dp", "opt")),
        P(("dp", "opt")),
        P(None, "dp"),
        P("dp"),
        P(None, ("dp", "opt")),
        P(None, ("dp", "opt")),
        P(("dp", "opt"), None),
        P(("dp", "opt"), None),
        P(("dp", "opt"), None),
        P(("dp", "opt"), None),
        P(("dp", "opt")),
        P(("dp", "opt")),
        P(("dp", "opt")),
    )
    out_specs = (
        P(("dp", "opt"), None),
        P(("dp", "opt"), None),
        P(None, ("dp", "opt")),
        P(("dp", "opt"), None),
        P(("dp", "opt"), None),
        P(None, ("dp", "opt")),
        P(None, ("dp", "opt")),
        P(None, ("dp", "opt")),
        P(("dp", "opt")),
        P(("dp", "opt")),
        P(("dp", "opt")),
        P(("dp", "opt")),
        P(("dp", "opt")),
    )
    ring = Ring if dict(mesh.shape) == {"dp": 16, "opt": 2} else Plain
    return jax.shard_map(
        functools.partial(per_device, ring),
        mesh=mesh,
        in_specs=in_specs,
        out_specs=out_specs,
        check_vma=False,
    )
```

time: 353 us -> 305 us (0.86)
  other arithmetic: 42.2 us -> 3.58 us
  matrix products: 13.6 us -> 0 us
  Pallas kernels: 130 us -> 141 us
  waiting for transfers between devices: 108 us -> 104 us
    dot_general x4 -> x0, matrix products: 13.6 us -> none  [the longest x1 5.65 us: per_device(): jnp.dot(owned_grad, owned_grad.T, precision=highest)]
    convert_element_type x9 -> x0, other arithmetic: 12.2 us -> none  [the longest x3 5.88 us: side(): self.got.append(send(give.astype(bf16), PLANE_A))]
    pallas_call x6 -> x20, Pallas kernels: 130 us -> 141 us  [the longest x12 128 us: call(): pl.pallas_call(body, out_shape=outs, in_specs=[*specs, *[anywhere] * skip...]
    unnamed x66 -> x76, local copies, waits for them, and re-layouts: 4.45 us -> 15.2 us
    another operation x15 -> x7, other arithmetic: 10.3 us -> 0.2 us  [the longest x2 3.92 us: gather_early(): self.late = jnp.stack([own, send(own, PLANE_A)])]
    slice x12 -> x0, local copies, waits for them, and re-layouts: 6.96 us -> none  [the longest x4 4.08 us: unit_of(): return flag[0, 0]]
    concatenate x4 -> x0, other arithmetic: 4.87 us -> none  [the longest x1 2.66 us: gather_early(): half = jnp.concatenate([pair, across])]
    add x7 -> x2, other arithmetic: 4.96 us -> 0.16 us  [cross_vectors(): self.kept = self.kept + unpack(arrived, self.kept.shape[-1])]
  transfers between devices with their start and end apart: 35 -> 34, of which waited for: 16 -> 21; matrix products, arithmetic and copies ran while one was open for 14% -> 2% of each run, Pallas kernels for 15% -> 21%
where the time goes in v2:
time: 305 us; the launch traced here: 304 us
  Pallas kernels  141 us (46%)
  waiting for transfers between devices  104 us (34%)
  starting transfers between devices  36.7 us (12%)
  local copies, waits for them, and re-layouts  17.7 us (6%)
  other arithmetic  3.58 us (1%)
    pallas_call x12, Pallas kernels, call(): pl.pallas_call(body, out_shape=outs, in_specs=[*specs, *[anywhere] * skip...  128 us
    ppermute x34, waiting for transfers between devices, send(): return lax.ppermute(values, AXES, pairs)  104 us
    ppermute x34, starting transfers between devices, send(): return lax.ppermute(values, AXES, pairs)  36.7 us
    unnamed x76, local copies, waits for them, and re-layouts  15.2 us
    pallas_call x7, Pallas kernels, picked(): pl.pallas_call(body, grid=(1,), out_shape=outs, in_specs=[*specs, *[anywh...  12.5 us
  transfers between devices with their start and end apart: 34, of which 21 were waited for; matrix products, arithmetic and copies ran while one was open for 2% of the time, Pallas kernels for 21%

profile of v2, /device:TPU:0, one launch (start us, length us, event | category | flops | bytes accessed | tf_op | source)
XLA Modules:
  0.0 303.9 jit_solution(10363707391649065556)
XLA Ops:
  1.5 1.2 copy-done.17
  2.7 0.9 prepare_own.1.refs_1_
  3.5 3.0 collective-permute-start.1
  6.6 2.6 collective-permute-start
  9.2 4.0 %collective-permute-done.1.refs_3_ = bf16[304,768]{1,0:T(8,128)(2,1)S(1)} collective-permute-done((bf16[304,768]{1,0:T(8,128)(2,1)S(1)}, bf16[304,768]{1,0:T(8,128)(2,1)S(1)}, u32[]{:S(2)}, u32[]{:S(2)}) %collective-permute-start.1) | collective-permute-done | bytes 466976 | tf_op jit(solution)/shard_map/ppermute | solution.py:59
  13.1 5.7 %collective-permute-done.refs_2_ = bf16[304,768]{1,0:T(8,128)(2,1)S(1)} collective-permute-done((bf16[304,768]{1,0:T(8,128)(2,1)S(1)}, bf16[304,768]{1,0:T(8,128)(2,1)S(1)}, u32[]{:S(2)}, u32[]{:S(2)}) %collective-permute-start) | collective-permute-done | bytes 466976 | tf_op jit(solution)/shard_map/ppermute | solution.py:59
  21.5 5.0 %collective-permute-start.5 = (bf16[304,768]{1,0:T(8,128)(2,1)S(1)}, bf16[304,768]{1,0:T(8,128)(2,1)S(1)}, u32[]{:S(2)}, u32[]{:S(2)}) collective-permute-start(bf16[304,768]{1,0:T(8,128)(2,1)S(1)} %get-tuple-element.49.refs_1_), channel_id=1, source_target_pairs={{0,8},{1,9},{2,10},{3,11},{4,12},{5,13},{6,14},{7,15},{8,0},{9,1},... | collective-permute-start | bytes 1400840 | tf_op jit(solution)/shard_map/ppermute | solution.py:59
  26.5 6.7 %collective-permute-done.2.refs_5_.refs_3_.refs_2_ = bf16[2,304,768]{2,1,0:T(8,128)(2,1)S(1)} collective-permute-done((bf16[2,304,768]{2,1,0:T(8,128)(2,1)S(1)}, bf16[2,304,768]{2,1,0:T(8,128)(2,1)S(1)}, u32[]{:S(2)}, u32[]{:S(2)}) %collective-permute-start.2) | collective-permute-done | bytes 933920 | tf_op jit(solution)/shard_map/ppermute | solution.py:59
  33.1 3.4 %collective-permute-start.6 = (bf16[16,768]{1,0:T(8,128)(2,1)S(1)}, bf16[16,768]{1,0:T(8,128)(2,1)S(1)}, u32[]{:S(2)}, u32[]{:S(2)}) collective-permute-start(bf16[16,768]{1,0:T(8,128)(2,1)S(1)} %get-tuple-element.50), channel_id=1, source_target_pairs={{0,16},{1,17},{2,18},{3,19},{4,20},{5,21},{6,22},{7,23},{8,24},{9,... | collective-permute-start | bytes 73736 | tf_op jit(solution)/shard_map/ppermute | solution.py:59
  36.5 0.9 collective-permute-start.9
  37.5 0.9 collective-permute-done.6.refs_4_
  39.1 0.9 copy-done.6
  40.0 1.5 collective-permute-start.7
  42.1 7.3 %collective-permute-done.9.refs_4_ = bf16[304,768]{1,0:T(8,128)(2,1)S(1)} collective-permute-done((bf16[304,768]{1,0:T(8,128)(2,1)S(1)}, bf16[304,768]{1,0:T(8,128)(2,1)S(1)}, u32[]{:S(2)}, u32[]{:S(2)}) %collective-permute-start.9) | collective-permute-done | bytes 466976 | tf_op jit(solution)/shard_map/ppermute | solution.py:59
  49.3 4.0 %collective-permute-done.10.refs_5_.refs_1_ = bf16[288,768]{1,0:T(8,128)(2,1)S(1)} collective-permute-done((bf16[288,768]{1,0:T(8,128)(2,1)S(1)}, bf16[288,768]{1,0:T(8,128)(2,1)S(1)}, u32[]{:S(2)}, u32[]{:S(2)}) %collective-permute-start.10) | collective-permute-done | bytes 442400 | tf_op jit(solution)/shard_map/ppermute | solution.py:59
  54.1 0.8 collective-permute-start.11
  54.9 1.5 collective-permute-start.14
  56.4 11.6 %collective-permute-done.14.refs_3_ = bf16[288,768]{1,0:T(8,128)(2,1)S(1)} collective-permute-done((bf16[288,768]{1,0:T(8,128)(2,1)S(1)}, bf16[288,768]{1,0:T(8,128)(2,1)S(1)}, u32[]{:S(2)}, u32[]{:S(2)}) %collective-permute-start.14) | collective-permute-done | bytes 442400 | tf_op jit(solution)/shard_map/ppermute | solution.py:59
  68.0 4.5 %collective-permute-done.11.refs_4_.refs_2_.refs_7_.refs_6_ = bf16[2,304,768]{2,1,0:T(8,128)(2,1)S(1)} collective-permute-done((bf16[2,304,768]{2,1,0:T(8,128)(2,1)S(1)}, bf16[2,304,768]{2,1,0:T(8,128)(2,1)S(1)}, u32[]{:S(2)}, u32[]{:S(2)}) %collective-permute-start.11) | collective-permute-done | bytes 933920 | tf_op jit(solution)/shard_map/ppermute | solution.py:59
  72.5 1.4 after_four.1.refs_14_.refs_9_
  73.9 0.7 collective-permute-start.15
  75.1 2.3 collective-permute-done.13.refs_4_.refs_9_.refs_8_
  77.4 0.9 read_vectors.1
  78.4 0.7 reshape.141.refs_13_.refs_17_.refs_12_
  79.1 17.5 %attend.1 = (bf16[2304,1024]{1,0:T(8,128)(2,1)}, bf16[1024,768]{1,0:T(8,128)(2,1)}, f32[12,1024]{1,0:T(8,128)}) custom-call(s32[8]{0:T(128)} %copy-done.20, s32[4]{0:T(128)} %refs_1_.3, bf16[2,304,768]{2,1,0:T(8,128)(2,1)} %copy-done.11, bf16[2,304,768]{2,1,0:T(8,128)(2,1)} %copy-done.5, bf16[2,304,768]{2,1,0:T(8,128)(2,1)} %copy-done.6, ...), custom_call_target="tpu_custom_call" | custom-call | flops 4429185024 | bytes 20971520 | tf_op jit(solution)/shard_map/attend/pallas_call | solution.py:284
  96.8 3.8 %collective-permute-done.17.refs_12_ = bf16[2,2,288,768]{3,2,1,0:T(8,128)(2,1)S(1)} collective-permute-done((bf16[2,2,288,768]{3,2,1,0:T(8,128)(2,1)}, bf16[2,2,288,768]{3,2,1,0:T(8,128)(2,1)S(1)}, u32[]{:S(2)}, u32[]{:S(2)}) %collective-permute-start.17) | collective-permute-done | bytes 1769504 | tf_op jit(solution)/shard_map/ppermute | solution.py:59
  100.6 1.2 copy-done.36
  101.9 62.9 %middle.1 = (bf16[1024,768]{1,0:T(8,128)(2,1)}, f32[1024,768]{1,0:T(8,128)}, bf16[768,1024]{1,0:T(8,128)(2,1)}, f32[11,3072]{1,0:T(8,128)}, bf16[2,3,288,768]{3,...) custom-call(s32[8]{0:T(128)} %copy-done.20, ...), custom_call_target="tpu_custom_call" | custom-call | flops 32614907904 | bytes 62914560 | tf_op jit(solution)/shard_map/middle/pallas_call | solution.py:284
  165.3 6.9 %collective-permute-done.18.refs_1_ = bf16[2,3,288,768]{3,2,1,0:T(8,128)(2,1)S(1)} collective-permute-done((bf16[2,3,288,768]{3,2,1,0:T(8,128)(2,1)}, bf16[2,3,288,768]{3,2,1,0:T(8,128)(2,1)S(1)}, u32[]{:S(2)}, u32[]{:S(2)}) %collective-permute-start.18) | collective-permute-done | bytes 2654240 | tf_op jit(solution)/shard_map/ppermute | solution.py:59
  172.2 1.7 copy-done.15
  173.9 2.2 add_pieces.4.refs_6_
  176.2 2.6 collective-permute-start.21
  179.0 2.3 copy-done.10
  181.3 11.7 %attend_back.1.refs_9_ = bf16[2304,1024]{1,0:T(8,128)(2,1)S(1)} custom-call(s32[8]{0:T(128)S(1)} %copy-done.21, s32[4]{0:T(128)S(1)} %copy-done.29, bf16[2304,1024]{1,0:T(8,128)(2,1)S(1)} %copy-done.10, bf16[768,1024]{1,0:T(8,128)(2,1)S(1)} %copy-done.16, f32[12,1024]{1,0:T(8,128)S(1)} %copy-done.23, s32[1,1024]{1,0:T(1,128)S(1)} %bitcast.28, ...), custom_call_target="tpu_custom_call" | custom-call | flops 2013265920 | bytes 26214400 | tf_op jit(solution)/shard_map/attend_back/pallas_call | solution.py:284
  193.0 2.1 copy-done.1
  195.1 11.5 %mixed_grad.1 = (bf16[2,1,288,768]{3,2,1,0:T(8,128)(2,1)}, bf16[2,1,288,768]{3,2,1,0:T(8,128)(2,1)}, bf16[2,1,288,768]{3,2,1,0:T(8,128)(2,1)}, bf16[2,1,288,768]{3,2,1,0:T(8,128)(2,1)}, f32[14,768]{1,0:T(8,128)}) custom-call(s32[8]{0:T(128)} %copy-done.20, bf16[2,304,768]{2,1,0:T(8,128)(2,1)} %copy-done.11, bf16[2,304,768]{2,1,0:T(8,128)(2,1)} %copy-done.5, ...), custom_call_target="tpu_custom_call" | custom-call | tf_op jit(solution)/shard_map/mixed_grad/pallas_call | solution.py:284
  206.6 0.9 reshape.142
  207.9 1.3 collective-permute-done.22.refs_3_
  210.2 3.2 %collective-permute-done.26.refs_5_ = bf16[2,16,768]{2,1,0:T(8,128)(2,1)S(1)} collective-permute-done((bf16[2,16,768]{2,1,0:T(8,128)(2,1)S(1)}, bf16[2,16,768]{2,1,0:T(8,128)(2,1)S(1)}, u32[]{:S(2)}, u32[]{:S(2)}) %collective-permute-start.26) | collective-permute-done | bytes 49184 | tf_op jit(solution)/shard_map/ppermute | solution.py:59
  213.6 1.0 collective-permute-start.28
  214.7 0.8 copy-done.19
  215.5 3.4 %add_pieces.5.refs_2_ = bf16[1,3,288,768]{3,2,1,0:T(8,128)(2,1)} custom-call(bf16[2,3,288,768]{3,2,1,0:T(8,128)(2,1)S(1)} %copy-done, bf16[2,3,288,768]{3,2,1,0:T(8,128)(2,1)} %collective-permute-done.20.refs_1_.refs_6_.refs_2_, bf16[2,3,288,768]{3,2,1,0:T(8,128)(2,1)} %collective-permute-done.21.refs_2_.refs_7_.refs_3_, f32[14,768]{1,0:T(8,128)S(1)} %copy-done.19), custom_call_target="tpu_custom_call" | custom-call | tf_op jit(solution)/shard_map/add_pieces/pallas_call | solution.py:1014
  218.8 1.0 collective-permute-start.25
  220.9 1.7 collective-permute-start.31
  222.6 2.1 collective-permute-done.31.refs_5_
  224.7 10.9 %input_back.1.refs_3_ = f32[1024,768]{1,0:T(8,128)} custom-call(s32[8]{0:T(128)} %copy-done.20, bf16[2,304,768]{2,1,0:T(8,128)(2,1)} %copy-done.11, bf16[2,304,768]{2,1,0:T(8,128)(2,1)} %copy-done.5, bf16[2,304,768]{2,1,0:T(8,128)(2,1)} %copy-done.6, bf16[2,304,768]{2,1,0:T(8,128)(2,1)} %copy-done.7, bf16[2,304,768]{2,1,0:T(8,128)(2,1)} %copy-done.8, ...), custom_call_target="tpu_custom_call" | custom-call | flops 3623878656 | bytes 15728640 | tf_op jit(solution)/shard_map/input_back/pallas_call | solution.py:284
  235.7 7.3 %collective-permute-done.24.refs_2_.refs_3_ = bf16[2,1,288,768]{3,2,1,0:T(8,128)(2,1)} collective-permute-done((bf16[2,1,288,768]{3,2,1,0:T(8,128)(2,1)S(1)}, bf16[2,1,288,768]{3,2,1,0:T(8,128)(2,1)}, u32[]{:S(2)}, u32[]{:S(2)}) %collective-permute-start.24) | collective-permute-done | bytes 884768 | tf_op jit(solution)/shard_map/ppermute | solution.py:59
  243.0 3.4 %collective-permute-done.25.refs_4_.refs_8_ = bf16[1,3,288,768]{3,2,1,0:T(8,128)(2,1)} collective-permute-done((bf16[1,3,288,768]{3,2,1,0:T(8,128)(2,1)}, bf16[1,3,288,768]{3,2,1,0:T(8,128)(2,1)}, u32[]{:S(2)}, u32[]{:S(2)}) %collective-permute-start.25) | collective-permute-done | bytes 1327136 | tf_op jit(solution)/shard_map/ppermute | solution.py:59
  246.4 1.9 copy-done.4
  248.3 1.2 copy-done.13
  249.5 1.3 add_pieces.7.refs_9_
  250.8 1.1 collective-permute-start.27
  252.7 2.7 collective-permute-start.33
  255.3 2.3 far_sums.1
  258.0 1.2 collective-permute-done.27.refs_4_
  259.2 2.2 near_sums.1
  261.4 1.7 collective-permute-start.29
  263.9 15.2 %collective-permute-done.30.refs_4_ = bf16[288,768]{1,0:T(8,128)(2,1)S(1)} collective-permute-done((bf16[288,768]{1,0:T(8,128)(2,1)S(1)}, bf16[288,768]{1,0:T(8,128)(2,1)S(1)}, u32[]{:S(2)}, u32[]{:S(2)}) %collective-permute-start.30) | collective-permute-done | bytes 442400 | tf_op jit(solution)/shard_map/ppermute | solution.py:59
  279.1 2.6 collective-permute-done.29.refs_3_
  281.7 0.9 last_sums.1
  282.6 0.9 copy-done.30
  284.7 9.7 %collective-permute-done.32.refs_1_ = bf16[288,768]{1,0:T(8,128)(2,1)S(1)} collective-permute-done((bf16[288,768]{1,0:T(8,128)(2,1)S(1)}, bf16[288,768]{1,0:T(8,128)(2,1)S(1)}, u32[]{:S(2)}, u32[]{:S(2)}) %collective-permute-start.32) | collective-permute-done | bytes 442400 | tf_op jit(solution)/shard_map/ppermute | solution.py:59
  294.4 0.8 copy-done.37
  295.2 8.5 %owner_step.1 = (f32[288,768]{1,0:T(8,128)}, f32[768,768]{1,0:T(8,128)}, f32[288,288]{1,0:T(8,128)}, f32[288,768]{1,0:T(8,128)}, f32[288,768]{1,0:T(8,128)}, /*index=5*/bf16[288,768]{1,0:T(8,128)(2,1)}) custom-call(f32[288,768]{1,0:T(8,128)} %copy-done.30, bf16[288,768]{1,0:T(8,128)(2,1)} %copy-done.37, f32[768,768]{1,0:T(8,128)} %refs_2_.1, ...), custom_call_target="tpu_custom_call" | custom-call | flops 2802843648 | bytes 15728640 | tf_op jit(solution)/shard_map/owner_step/pallas_call | solution.py:284
  (130 shorter events, 12.6 us)
Async XLA Ops:
  1.5 75.9 %copy-start.20 = (s32[8]{0:T(128)}, s32[8]{0:T(128)S(1)}, u32[]{:S(2)}) copy-start(s32[8]{0:T(128)S(1)} %stack.62.refs_0_) | copy-start | bytes 100
  3.5 9.6 %collective-permute-start.1 = (bf16[304,768]{1,0:T(8,128)(2,1)S(1)}, bf16[304,768]{1,0:T(8,128)(2,1)S(1)}, u32[]{:S(2)}, u32[]{:S(2)}) collective-permute-start(bf16[304,768]{1,0:T(8,128)(2,1)S(1)} %prepare_own.1.refs_1_), channel_id=1, source_target_pairs={{0,4},{1,5},{2,3},{3,2},{4,0},{5,1},{6,7},{7,6},{8,12},{9,13},{10,... | collective-permute-start | bytes 1400840 | tf_op jit(solution)/shard_map/ppermute | solution.py:59
  6.6 12.2 %collective-permute-start = (bf16[304,768]{1,0:T(8,128)(2,1)S(1)}, bf16[304,768]{1,0:T(8,128)(2,1)S(1)}, u32[]{:S(2)}, u32[]{:S(2)}) collective-permute-start(bf16[304,768]{1,0:T(8,128)(2,1)S(1)} %prepare_own.1.refs_1_), channel_id=1, source_target_pairs={{0,16},{1,17},{2,18},{3,19},{4,20},{5,21},{6,22},{7,23},{8,0},{9,1... | collective-permute-start | bytes 1400840 | tf_op jit(solution)/shard_map/ppermute | solution.py:59
  19.5 34.5 %copy-start.11 = (bf16[2,304,768]{2,1,0:T(8,128)(2,1)}, bf16[2,304,768]{2,1,0:T(8,128)(2,1)S(1)}, u32[]{:S(2)}) copy-start(bf16[2,304,768]{2,1,0:T(8,128)(2,1)S(1)} %get-tuple-element.48.refs_2_.refs_1_) | copy-start | bytes 2801668
  19.5 13.6 %collective-permute-start.2 = (bf16[2,304,768]{2,1,0:T(8,128)(2,1)S(1)}, bf16[2,304,768]{2,1,0:T(8,128)(2,1)S(1)}, u32[]{:S(2)}, u32[]{:S(2)}) collective-permute-start(bf16[2,304,768]{2,1,0:T(8,128)(2,1)S(1)} %get-tuple-element.48.refs_2_.refs_1_), channel_id=1, source_target_pairs={{0,1},{1,0},{2,6},{3,7},{4,5},{5,4},{6,2},{7,3},{8,9},{9,8},{10,14... | collective-permute-start | bytes 2801672 | tf_op jit(solution)/shard_map/ppermute | solution.py:59
  20.1 18.3 %collective-permute-start.3 = (bf16[2,304,768]{2,1,0:T(8,128)(2,1)S(1)}, bf16[2,304,768]{2,1,0:T(8,128)(2,1)S(1)}, u32[]{:S(2)}, u32[]{:S(2)}) collective-permute-start(bf16[2,304,768]{2,1,0:T(8,128)(2,1)S(1)} %get-tuple-element.48.refs_2_.refs_1_), channel_id=1, source_target_pairs={{0,2},{1,3},{2,0},{3,1},{4,6},{5,7},{6,4},{7,5},{8,10},{9,11},{10,... | collective-permute-start | bytes 2801672 | tf_op jit(solution)/shard_map/ppermute | solution.py:59
  20.8 15.7 %collective-permute-start.8 = (bf16[304,768]{1,0:T(8,128)(2,1)S(1)}, bf16[304,768]{1,0:T(8,128)(2,1)S(1)}, u32[]{:S(2)}, u32[]{:S(2)}) collective-permute-start(bf16[304,768]{1,0:T(8,128)(2,1)S(1)} %prepare_own.1.refs_1_), channel_id=1, source_target_pairs={{0,0},{1,1},{2,2},{3,3},{4,4},{5,5},{6,6},{7,7},{8,16},{9,17},{10,... | collective-permute-start | bytes 1400840 | tf_op jit(solution)/shard_map/ppermute | solution.py:59
  21.5 16.9 %collective-permute-start.5 = (bf16[304,768]{1,0:T(8,128)(2,1)S(1)}, bf16[304,768]{1,0:T(8,128)(2,1)S(1)}, u32[]{:S(2)}, u32[]{:S(2)}) collective-permute-start(bf16[304,768]{1,0:T(8,128)(2,1)S(1)} %get-tuple-element.49.refs_1_), channel_id=1, source_target_pairs={{0,8},{1,9},{2,10},{3,11},{4,12},{5,13},{6,14},{7,15},{8,0},{9,1},... | collective-permute-start | bytes 1400840 | tf_op jit(solution)/shard_map/ppermute | solution.py:59
  33.1 20.9 %copy-start.5 = (bf16[2,304,768]{2,1,0:T(8,128)(2,1)}, bf16[2,304,768]{2,1,0:T(8,128)(2,1)S(1)}, u32[]{:S(2)}) copy-start(bf16[2,304,768]{2,1,0:T(8,128)(2,1)S(1)} %collective-permute-done.2.refs_5_.refs_3_.refs_2_) | copy-start | bytes 2801668
  33.1 20.2 %collective-permute-start.4 = (bf16[2,304,768]{2,1,0:T(8,128)(2,1)S(1)}, bf16[2,304,768]{2,1,0:T(8,128)(2,1)S(1)}, u32[]{:S(2)}, u32[]{:S(2)}) collective-permute-start(bf16[2,304,768]{2,1,0:T(8,128)(2,1)S(1)} %collective-permute-done.2.refs_5_.refs_3_.refs_2_), channel_id=1, source_target_pairs={{0,2},{1,3},{2,0},{3,1},{4,6},{5,7},{6,4},{7,5},{8,10},{9,11},{10,... | collective-permute-start | bytes 2801672 | tf_op jit(solution)/shard_map/ppermute | solution.py:59
  33.1 5.3 %collective-permute-start.6 = (bf16[16,768]{1,0:T(8,128)(2,1)S(1)}, bf16[16,768]{1,0:T(8,128)(2,1)S(1)}, u32[]{:S(2)}, u32[]{:S(2)}) collective-permute-start(bf16[16,768]{1,0:T(8,128)(2,1)S(1)} %get-tuple-element.50), channel_id=1, source_target_pairs={{0,16},{1,17},{2,18},{3,19},{4,20},{5,21},{6,22},{7,23},{8,24},{9,... | collective-permute-start | bytes 73736 | tf_op jit(solution)/shard_map/ppermute | solution.py:59
  36.5 12.8 %collective-permute-start.9 = (bf16[304,768]{1,0:T(8,128)(2,1)S(1)}, bf16[304,768]{1,0:T(8,128)(2,1)S(1)}, u32[]{:S(2)}, u32[]{:S(2)}) collective-permute-start(bf16[304,768]{1,0:T(8,128)(2,1)S(1)} %collective-permute-done.8.refs_3_), channel_id=1, source_target_pairs={{0,8},{1,9},{2,10},{3,11},{4,12},{5,13},{6,14},{7,15},{8,0},{9,1},... | collective-permute-start | bytes 1400840 | tf_op jit(solution)/shard_map/ppermute | solution.py:59
  40.0 13.3 %collective-permute-start.7 = (bf16[304,768]{1,0:T(8,128)(2,1)S(1)}, bf16[304,768]{1,0:T(8,128)(2,1)S(1)}, u32[]{:S(2)}, u32[]{:S(2)}) collective-permute-start(bf16[304,768]{1,0:T(8,128)(2,1)S(1)} %get-tuple-element.51.refs_1_), channel_id=1, source_target_pairs={{0,4},{1,5},{2,3},{3,2},{4,0},{5,1},{6,7},{7,6},{8,12},{9,13},{10,... | collective-permute-start | bytes 1400840 | tf_op jit(solution)/shard_map/ppermute | solution.py:59
  41.6 11.8 %collective-permute-start.10 = (bf16[288,768]{1,0:T(8,128)(2,1)S(1)}, bf16[288,768]{1,0:T(8,128)(2,1)S(1)}, u32[]{:S(2)}, u32[]{:S(2)}) collective-permute-start(bf16[288,768]{1,0:T(8,128)(2,1)S(1)} %get-tuple-element.52.refs_0_), channel_id=1, source_target_pairs={{0,4},{1,5},{2,3},{3,2},{4,0},{5,1},{6,7},{7,6},{8,12},{9,13},{10,... | collective-permute-start | bytes 1327112 | tf_op jit(solution)/shard_map/ppermute | solution.py:59
  53.4 14.6 %copy-start.7 = (bf16[2,304,768]{2,1,0:T(8,128)(2,1)}, bf16[2,304,768]{2,1,0:T(8,128)(2,1)S(1)}, u32[]{:S(2)}) copy-start(bf16[2,304,768]{2,1,0:T(8,128)(2,1)S(1)} %collective-permute-done.4.refs_6_.refs_5_.refs_4_) | copy-start | bytes 2801668
  54.0 23.4 %copy-start.8 = (bf16[2,304,768]{2,1,0:T(8,128)(2,1)}, bf16[2,304,768]{2,1,0:T(8,128)(2,1)S(1)}, u32[]{:S(2)}) copy-start(bf16[2,304,768]{2,1,0:T(8,128)(2,1)S(1)} %get-tuple-element.53.refs_1_.refs_6_.refs_5_) | copy-start | bytes 2801668
  54.0 13.9 %collective-permute-start.12 = (bf16[2,304,768]{2,1,0:T(8,128)(2,1)S(1)}, bf16[2,304,768]{2,1,0:T(8,128)(2,1)S(1)}, u32[]{:S(2)}, u32[]{:S(2)}) collective-permute-start(bf16[2,304,768]{2,1,0:T(8,128)(2,1)S(1)} %get-tuple-element.53.refs_1_.refs_6_.refs_5_), channel_id=1, source_target_pairs={{0,2},{1,3},{2,0},{3,1},{4,6},{5,7},{6,4},{7,5},{8,10},{9,11},{10,... | collective-permute-start | bytes 2801672 | tf_op jit(solution)/shard_map/ppermute | solution.py:59
  54.1 18.4 %collective-permute-start.11 = (bf16[2,304,768]{2,1,0:T(8,128)(2,1)S(1)}, bf16[2,304,768]{2,1,0:T(8,128)(2,1)S(1)}, u32[]{:S(2)}, u32[]{:S(2)}) collective-permute-start(bf16[2,304,768]{2,1,0:T(8,128)(2,1)S(1)} %get-tuple-element.53.refs_1_.refs_6_.refs_5_), channel_id=1, source_target_pairs={{0,1},{1,0},{2,6},{3,7},{4,5},{5,4},{6,2},{7,3},{8,9},{9,8},{10,14... | collective-permute-start | bytes 2801672 | tf_op jit(solution)/shard_map/ppermute | solution.py:59
  54.9 13.1 %collective-permute-start.14 = (bf16[288,768]{1,0:T(8,128)(2,1)S(1)}, bf16[288,768]{1,0:T(8,128)(2,1)S(1)}, u32[]{:S(2)}, u32[]{:S(2)}) collective-permute-start(bf16[288,768]{1,0:T(8,128)(2,1)S(1)} %get-tuple-element.54.refs_2_), channel_id=1, source_target_pairs={{0,4},{1,5},{2,3},{3,2},{4,0},{5,1},{6,7},{7,6},{8,12},{9,13},{10,... | collective-permute-start | bytes 1327112 | tf_op jit(solution)/shard_map/ppermute | solution.py:59
  68.0 9.4 %copy-start.2 = (bf16[2,304,768]{2,1,0:T(8,128)(2,1)}, bf16[2,304,768]{2,1,0:T(8,128)(2,1)S(1)}, u32[]{:S(2)}) copy-start(bf16[2,304,768]{2,1,0:T(8,128)(2,1)S(1)} %collective-permute-done.12.refs_5_.refs_3_.refs_8_.refs_7_) | copy-start | bytes 2801668
  72.5 4.9 %copy-start.3 = (bf16[2,304,768]{2,1,0:T(8,128)(2,1)}, bf16[2,304,768]{2,1,0:T(8,128)(2,1)S(1)}, u32[]{:S(2)}) copy-start(bf16[2,304,768]{2,1,0:T(8,128)(2,1)S(1)} %collective-permute-done.11.refs_4_.refs_2_.refs_7_.refs_6_) | copy-start | bytes 2801668
  73.9 22.8 %collective-permute-start.15 = (bf16[2,2,288,768]{3,2,1,0:T(8,128)(2,1)}, bf16[2,2,288,768]{3,2,1,0:T(8,128)(2,1)}, u32[]{:S(2)}, u32[]{:S(2)}) collective-permute-start(bf16[2,2,288,768]{3,2,1,0:T(8,128)(2,1)} %after_four.1.refs_14_.refs_9_), channel_id=1, source_target_pairs={{0,1},{1,0},{2,6},{3,7},{4,5},{5,4},{6,2},{7,3},{8,9},{9,8},{10,14... | collective-permute-start | bytes 5308424 | tf_op jit(solution)/shard_map/ppermute | solution.py:59
  74.6 2.8 collective-permute-start.13
  74.7 22.1 %collective-permute-start.16 = (bf16[2,2,288,768]{3,2,1,0:T(8,128)(2,1)}, bf16[2,2,288,768]{3,2,1,0:T(8,128)(2,1)}, u32[]{:S(2)}, u32[]{:S(2)}) collective-permute-start(bf16[2,2,288,768]{3,2,1,0:T(8,128)(2,1)} %after_four.1.refs_14_.refs_9_), channel_id=1, source_target_pairs={{0,2},{1,3},{2,0},{3,1},{4,6},{5,7},{6,4},{7,5},{8,10},{9,11},{10,... | collective-permute-start | bytes 5308424 | tf_op jit(solution)/shard_map/ppermute | solution.py:59
  96.7 3.9 %collective-permute-start.17 = (bf16[2,2,288,768]{3,2,1,0:T(8,128)(2,1)}, bf16[2,2,288,768]{3,2,1,0:T(8,128)(2,1)S(1)}, u32[]{:S(2)}, u32[]{:S(2)}) collective-permute-start(bf16[2,2,288,768]{3,2,1,0:T(8,128)(2,1)} %hold.1.refs_10_), channel_id=1, source_target_pairs={{0,2},{1,3},{2,0},{3,1},{4,6},{5,7},{6,4},{7,5},{8,10},{9,11},{10,... | collective-permute-start | bytes 5308424 | tf_op jit(solution)/shard_map/ppermute | solution.py:59
  164.7 7.5 %collective-permute-start.18 = (bf16[2,3,288,768]{3,2,1,0:T(8,128)(2,1)}, bf16[2,3,288,768]{3,2,1,0:T(8,128)(2,1)S(1)}, u32[]{:S(2)}, u32[]{:S(2)}) collective-permute-start(bf16[2,3,288,768]{3,2,1,0:T(8,128)(2,1)} %get-tuple-element.61), channel_id=1, source_target_pairs={{0,2},{1,3},{2,0},{3,1},{4,6},{5,7},{6,4},{7,5},{8,10},{9,11},{10,... | collective-permute-start | bytes 7962632 | tf_op jit(solution)/shard_map/ppermute | solution.py:59
  164.9 49.7 %collective-permute-start.20 = (bf16[2,3,288,768]{3,2,1,0:T(8,128)(2,1)}, bf16[2,3,288,768]{3,2,1,0:T(8,128)(2,1)}, u32[]{:S(2)}, u32[]{:S(2)}) collective-permute-start(bf16[2,3,288,768]{3,2,1,0:T(8,128)(2,1)} %get-tuple-element.67), channel_id=1, source_target_pairs={{0,2},{1,3},{2,0},{3,1},{4,6},{5,7},{6,4},{7,5},{8,10},{9,11},{10,... | collective-permute-start | bytes 7962632 | tf_op jit(solution)/shard_map/ppermute | solution.py:59
  172.2 1.8 copy-start.15
  173.9 5.0 %copy-start.16 = (bf16[768,1024]{1,0:T(8,128)(2,1)S(1)}, bf16[768,1024]{1,0:T(8,128)(2,1)}, u32[]{:S(2)}) copy-start(bf16[768,1024]{1,0:T(8,128)(2,1)} %get-tuple-element.58.refs_3_) | copy-start | bytes 4718596
  173.9 5.0 %copy-start.21 = (s32[8]{0:T(128)S(1)}, s32[8]{0:T(128)}, u32[]{:S(2)}) copy-start(s32[8]{0:T(128)} %copy-done.20) | copy-start | bytes 100
  173.9 5.0 %copy-start.23 = (f32[12,1024]{1,0:T(8,128)S(1)}, f32[12,1024]{1,0:T(8,128)}, u32[]{:S(2)}) copy-start(f32[12,1024]{1,0:T(8,128)} %get-tuple-element.59.refs_4_) | copy-start | bytes 147460
  173.9 5.0 %copy-start.28 = (s32[1024]{0:T(1024)S(1)}, s32[1024]{0:T(1024)}, u32[]{:S(2)}) copy-start(s32[1024]{0:T(1024)} %param.19) | copy-start | bytes 12292
  173.9 5.0 %copy-start.29 = (s32[4]{0:T(128)S(1)}, s32[4]{0:T(128)}, u32[]{:S(2)}) copy-start(s32[4]{0:T(128)} %refs_1_.3) | copy-start | bytes 52
  176.2 38.5 %collective-permute-start.21 = (bf16[2,3,288,768]{3,2,1,0:T(8,128)(2,1)}, bf16[2,3,288,768]{3,2,1,0:T(8,128)(2,1)}, u32[]{:S(2)}, u32[]{:S(2)}) collective-permute-start(bf16[2,3,288,768]{3,2,1,0:T(8,128)(2,1)} %add_pieces.4.refs_6_), channel_id=1, source_target_pairs={{0,1},{1,0},{2,6},{3,7},{4,5},{5,4},{6,2},{7,3},{8,9},{9,8},{10,14... | collective-permute-start | bytes 7962632 | tf_op jit(solution)/shard_map/ppermute | solution.py:59
  178.9 2.3 copy-start.10
  193.0 2.1 copy-start.1
  195.1 19.6 %copy-start = (bf16[2,3,288,768]{3,2,1,0:T(8,128)(2,1)S(1)}, bf16[2,3,288,768]{3,2,1,0:T(8,128)(2,1)}, u32[]{:S(2)}) copy-start(bf16[2,3,288,768]{3,2,1,0:T(8,128)(2,1)} %get-tuple-element.66.refs_0_.refs_5_.refs_1_) | copy-start | bytes 7962628
  207.8 1.4 collective-permute-start.22
  209.3 4.1 %collective-permute-start.26 = (bf16[2,16,768]{2,1,0:T(8,128)(2,1)S(1)}, bf16[2,16,768]{2,1,0:T(8,128)(2,1)S(1)}, u32[]{:S(2)}, u32[]{:S(2)}) collective-permute-start(bf16[2,16,768]{2,1,0:T(8,128)(2,1)S(1)} %fusion.11), channel_id=1, source_target_pairs={{0,1},{1,0},{2,6},{3,7},{4,5},{5,4},{6,2},{7,3},{8,9},{9,8},{10,14... | collective-permute-start | bytes 147464 | tf_op jit(solution)/shard_map/ppermute | solution.py:59
  209.9 10.1 %collective-permute-start.19 = (bf16[2,1,288,768]{3,2,1,0:T(8,128)(2,1)}, bf16[2,1,288,768]{3,2,1,0:T(8,128)(2,1)S(1)}, u32[]{:S(2)}, u32[]{:S(2)}) collective-permute-start(bf16[2,1,288,768]{3,2,1,0:T(8,128)(2,1)} %get-tuple-element.65), channel_id=1, source_target_pairs={{0,2},{1,3},{2,0},{3,1},{4,6},{5,7},{6,4},{7,5},{8,10},{9,11},{10,... | collective-permute-start | bytes 2654216 | tf_op jit(solution)/shard_map/ppermute | solution.py:59
  213.6 6.3 %collective-permute-start.28 = (bf16[1,16,768]{2,1,0:T(8,128)(2,1)S(1)}, bf16[1,16,768]{2,1,0:T(8,128)(2,1)S(1)}, u32[]{:S(2)}, u32[]{:S(2)}) collective-permute-start(bf16[1,16,768]{2,1,0:T(8,128)(2,1)S(1)} %fusion.21), channel_id=1, source_target_pairs={{0,4},{1,5},{2,3},{3,2},{4,0},{5,1},{6,7},{7,6},{8,12},{9,13},{10,... | collective-permute-start | bytes 73736 | tf_op jit(solution)/shard_map/ppermute | solution.py:59
  214.6 21.1 %collective-permute-start.23 = (bf16[2,1,288,768]{3,2,1,0:T(8,128)(2,1)}, bf16[2,1,288,768]{3,2,1,0:T(8,128)(2,1)}, u32[]{:S(2)}, u32[]{:S(2)}) collective-permute-start(bf16[2,1,288,768]{3,2,1,0:T(8,128)(2,1)} %get-tuple-element.70), channel_id=1, source_target_pairs={{0,2},{1,3},{2,0},{3,1},{4,6},{5,7},{6,4},{7,5},{8,10},{9,11},{10,... | collective-permute-start | bytes 2654216 | tf_op jit(solution)/shard_map/ppermute | solution.py:59
  215.5 4.5 %copy-start.18 = (bf16[2,1,288,768]{3,2,1,0:T(8,128)(2,1)S(1)}, bf16[2,1,288,768]{3,2,1,0:T(8,128)(2,1)}, u32[]{:S(2)}) copy-start(bf16[2,1,288,768]{3,2,1,0:T(8,128)(2,1)} %get-tuple-element.64.refs_0_) | copy-start | bytes 2654212
  218.8 27.6 %collective-permute-start.25 = (bf16[1,3,288,768]{3,2,1,0:T(8,128)(2,1)}, bf16[1,3,288,768]{3,2,1,0:T(8,128)(2,1)}, u32[]{:S(2)}, u32[]{:S(2)}) collective-permute-start(bf16[1,3,288,768]{3,2,1,0:T(8,128)(2,1)} %add_pieces.5.refs_2_), channel_id=1, source_target_pairs={{0,4},{1,5},{2,3},{3,2},{4,0},{5,1},{6,7},{7,6},{8,12},{9,13},{10,... | collective-permute-start | bytes 3981320 | tf_op jit(solution)/shard_map/ppermute | solution.py:59
  219.9 4.8 %copy-start.26 = (bf16[1,16,768]{2,1,0:T(8,128)(2,1)}, bf16[1,16,768]{2,1,0:T(8,128)(2,1)S(1)}, u32[]{:S(2)}) copy-start(bf16[1,16,768]{2,1,0:T(8,128)(2,1)S(1)} %collective-permute-done.28.refs_9_) | copy-start | bytes 73732
  220.2 4.5 %copy-start.12 = (bf16[2,1,288,768]{3,2,1,0:T(8,128)(2,1)}, bf16[2,1,288,768]{3,2,1,0:T(8,128)(2,1)S(1)}, u32[]{:S(2)}) copy-start(bf16[2,1,288,768]{3,2,1,0:T(8,128)(2,1)S(1)} %add_pieces.6.refs_11_) | copy-start | bytes 2654212
  220.2 22.8 %collective-permute-start.24 = (bf16[2,1,288,768]{3,2,1,0:T(8,128)(2,1)S(1)}, bf16[2,1,288,768]{3,2,1,0:T(8,128)(2,1)}, u32[]{:S(2)}, u32[]{:S(2)}) collective-permute-start(bf16[2,1,288,768]{3,2,1,0:T(8,128)(2,1)S(1)} %add_pieces.6.refs_11_), channel_id=1, source_target_pairs={{0,1},{1,0},{2,6},{3,7},{4,5},{5,4},{6,2},{7,3},{8,9},{9,8},{10,14... | collective-permute-start | bytes 2654216 | tf_op jit(solution)/shard_map/ppermute | solution.py:59
  220.9 3.8 %collective-permute-start.31 = (bf16[1,16,768]{2,1,0:T(8,128)(2,1)S(1)}, bf16[1,16,768]{2,1,0:T(8,128)(2,1)S(1)}, u32[]{:S(2)}, u32[]{:S(2)}) collective-permute-start(bf16[1,16,768]{2,1,0:T(8,128)(2,1)S(1)} %fusion.24), channel_id=1, source_target_pairs={{0,8},{1,9},{2,10},{3,11},{4,12},{5,13},{6,14},{7,15},{8,0},{9,1},... | collective-permute-start | bytes 73736 | tf_op jit(solution)/shard_map/ppermute | solution.py:59
  224.7 11.0 %copy-start.24 = (bf16[1,16,768]{2,1,0:T(8,128)(2,1)}, bf16[1,16,768]{2,1,0:T(8,128)(2,1)S(1)}, u32[]{:S(2)}) copy-start(bf16[1,16,768]{2,1,0:T(8,128)(2,1)S(1)} %collective-permute-done.31.refs_5_) | copy-start | bytes 73732
  246.4 1.9 copy-start.4
  249.5 5.9 %copy-start.22 = (s32[8]{0:T(128)S(1)}, s32[8]{0:T(128)}, u32[]{:S(2)}) copy-start(s32[8]{0:T(128)} %copy-done.20) | copy-start | bytes 100
  250.8 8.4 %collective-permute-start.27 = (bf16[1,1,288,768]{3,2,1,0:T(8,128)(2,1)S(1)}, bf16[1,1,288,768]{3,2,1,0:T(8,128)(2,1)S(1)}, u32[]{:S(2)}, u32[]{:S(2)}) collective-permute-start(bf16[1,1,288,768]{3,2,1,0:T(8,128)(2,1)S(1)} %add_pieces.7.refs_9_), channel_id=1, source_target_pairs={{0,4},{1,5},{2,3},{3,2},{4,0},{5,1},{6,7},{7,6},{8,12},{9,13},{10,... | collective-permute-start | bytes 1327112 | tf_op jit(solution)/shard_map/ppermute | solution.py:59
  252.7 10.4 %collective-permute-start.33 = (bf16[1,16,768]{2,1,0:T(8,128)(2,1)}, bf16[1,16,768]{2,1,0:T(8,128)(2,1)}, u32[]{:S(2)}, u32[]{:S(2)}) collective-permute-start(bf16[1,16,768]{2,1,0:T(8,128)(2,1)} %fusion.27), channel_id=1, source_target_pairs={{0,16},{1,17},{2,18},{3,19},{4,20},{5,21},{6,22},{7,23},{8,24},{9,... | collective-permute-start | bytes 73736 | tf_op jit(solution)/shard_map/ppermute | solution.py:59
  255.3 3.9 %copy-start.14 = (bf16[2,1,288,768]{3,2,1,0:T(8,128)(2,1)S(1)}, bf16[2,1,288,768]{3,2,1,0:T(8,128)(2,1)}, u32[]{:S(2)}) copy-start(bf16[2,1,288,768]{3,2,1,0:T(8,128)(2,1)} %get-tuple-element.69.refs_0_.refs_1_) | copy-start | bytes 2654212
  255.3 3.9 %copy-start.27 = (bf16[1,16,768]{2,1,0:T(8,128)(2,1)S(1)}, bf16[1,16,768]{2,1,0:T(8,128)(2,1)}, u32[]{:S(2)}) copy-start(bf16[1,16,768]{2,1,0:T(8,128)(2,1)} %copy-done.26) | copy-start | bytes 73732
  257.7 24.1 %copy-start.25 = (bf16[1,16,768]{2,1,0:T(8,128)(2,1)S(1)}, bf16[1,16,768]{2,1,0:T(8,128)(2,1)}, u32[]{:S(2)}) copy-start(bf16[1,16,768]{2,1,0:T(8,128)(2,1)} %copy-done.24) | copy-start | bytes 73732
  257.7 21.4 %collective-permute-start.30 = (bf16[288,768]{1,0:T(8,128)(2,1)S(1)}, bf16[288,768]{1,0:T(8,128)(2,1)S(1)}, u32[]{:S(2)}, u32[]{:S(2)}) collective-permute-start(bf16[288,768]{1,0:T(8,128)(2,1)S(1)} %get-tuple-element.74), channel_id=1, source_target_pairs={{0,16},{1,17},{2,18},{3,19},{4,20},{5,21},{6,22},{7,23},{8,24},{9,... | collective-permute-start | bytes 1327112 | tf_op jit(solution)/shard_map/ppermute | solution.py:59
  261.4 22.2 %copy-start.34 = (f32[336]{0:T(512)S(1)}, f32[336]{0:T(512)}, u32[]{:S(2)}) copy-start(f32[336]{0:T(512)} %param.29) | copy-start | bytes 4036
  261.4 22.2 %copy-start.35 = (f32[336]{0:T(512)S(1)}, f32[336]{0:T(512)}, u32[]{:S(2)}) copy-start(f32[336]{0:T(512)} %param.30) | copy-start | bytes 4036
  261.4 22.8 %copy-start.33 = (f32[336]{0:T(512)S(1)}, f32[336]{0:T(512)}, u32[]{:S(2)}) copy-start(f32[336]{0:T(512)} %param.31) | copy-start | bytes 4036
  261.4 20.3 %collective-permute-start.29 = (bf16[288,768]{1,0:T(8,128)(2,1)S(1)}, bf16[288,768]{1,0:T(8,128)(2,1)S(1)}, u32[]{:S(2)}, u32[]{:S(2)}) collective-permute-start(bf16[288,768]{1,0:T(8,128)(2,1)S(1)} %get-tuple-element.73), channel_id=1, source_target_pairs={{0,8},{1,9},{2,10},{3,11},{4,12},{5,13},{6,14},{7,15},{8,0},{9,1},... | collective-permute-start | bytes 1327112 | tf_op jit(solution)/shard_map/ppermute | solution.py:59
  263.9 39.8 %copy-start.31 = (f32[336]{0:T(512)}, f32[336]{0:T(512)S(1)}, u32[]{:S(2)}) copy-start(f32[336]{0:T(512)S(1)} %fusion.38) | copy-start | bytes 4036
  283.6 10.8 %collective-permute-start.32 = (bf16[288,768]{1,0:T(8,128)(2,1)S(1)}, bf16[288,768]{1,0:T(8,128)(2,1)S(1)}, u32[]{:S(2)}, u32[]{:S(2)}) collective-permute-start(bf16[288,768]{1,0:T(8,128)(2,1)S(1)} %get-tuple-element.76), channel_id=1, source_target_pairs={{0,8},{1,9},{2,10},{3,11},{4,12},{5,13},{6,14},{7,15},{8,24},{9,25... | collective-permute-start | bytes 1327112 | tf_op jit(solution)/shard_map/ppermute | solution.py:59
  284.2 19.5 %copy-start.32 = (f32[336]{0:T(512)}, f32[336]{0:T(512)S(1)}, u32[]{:S(2)}) copy-start(f32[336]{0:T(512)S(1)} %get-tuple-element.84) | copy-start | bytes 4036
  (8 other events, 8.7 us)

commit v3 on v2

--- a/solution.py
+++ b/solution.py
@@ -60,6 +60,9 @@
 
 
 QUARTER_SLOT = np.array([[0, 1, 3, 2], [1, 0, 3, 2], [1, 3, 0, 2], [1, 3, 2, 0]])
+
+
+FAR_COST = 40 * 10**9
 
 
 class Ring:
@@ -111,45 +114,28 @@
         across = hold(self.across, context)
         return [self.late, across, self.swapped, send(across, CORES)]
 
-    def disordered(self, blocks):
-        hits = jnp.stack([block_place((self.y, self.c, self.x), who, k) for who in (0, 1) for k in range(4)])
-        hit = (jnp.arange(8)[None, :] == hits[:, None]).reshape((8, 8) + (1,) * (blocks.ndim - 1))
-        return jnp.sum(jnp.where(hit, blocks[None], 0.0), axis=1)
-
     def reduction(self, pieces, after=()):
         return Reduction(pieces, after)
 
-    def vectors_begin(self, vector_sums):
-        pieces = self.disordered(jnp.swapaxes(vector_sums.reshape(4, 8, -1), 0, 1))
-        self.kept = pieces[:4]
-        return self.cross_vectors(pieces[4:], CORES)
-
-    def vectors_next(self, pairs):
-        if pairs in (PLANE_B, PLANE_A):
-            count = self.kept.shape[0] // 2
-            more, self.kept = self.kept[count:], self.kept[:count]
-            return self.cross_vectors(more, pairs)
-        return self.cross_vectors(self.kept, pairs)
-
-    def cross_vectors(self, more, pairs):
-        arrived = send(pack(more), pairs)
-        self.kept = self.kept + unpack(arrived, self.kept.shape[-1])
-        return [arrived]
-
-    def vectors_end(self):
-        return lax.dynamic_index_in_dim(self.kept[0], self.z, 0, False)
-
-    def reduce_far(self, rest, after=()):
-        self.kept_far, give = far_sums(self.place, rest.parts(), after)
-        self.far = send(give, Z_FAR)
-
-    def reduce_near(self, zero, rest, after=()):
-        self.kept_near, give = near_sums(self.place, zero.parts(), rest.parts(), after)
+    def reduce_far(self, both, after=()):
+        self.kept_far, give = far_sums(self.place, both.parts(), after)
+        self.far = hold(send(give, Z_FAR), cost=FAR_COST)
+        return [give]
+
+    def reduce_near(self, zero, three, after=()):
+        self.kept_near, give, self.kept_rows = near_sums(self.place, zero.parts(), three.parts(), after)
         self.near = send(give, Z_NEAR)
 
-    def reduce_last(self, after=()):
-        base, give = last_sums(self.place, self.kept_near, self.kept_far, self.near, self.far, after=after)
-        return base, send(give, Z_CYCLE_BACK)
+    def reduce_last(self):
+        base, give, rows, packed = last_sums(
+            self.place, self.kept_near, self.kept_far, self.kept_rows, self.near, self.far
+        )
+        last = send(give, Z_CYCLE_BACK)
+        arrived = send(packed, Z_FAR).astype(f32)
+        half = rows.shape[1]
+        rows = rows + (arrived[:, :half] + arrived[:, half:])
+        vector = lax.dynamic_index_in_dim(rows, self.z, 0, False)
+        return base, last, vector[: NVEC // 32]
 
 
 class Reduction:
@@ -161,9 +147,10 @@
         self.got_lo = send(give_lo, CORES)
         self.more = []
 
-    def across(self, after=()):
+    def across(self, after=(), cost=0):
         self.give = [add_pieces([self.keep_hi, self.got_hi], 0, 2, after)]
-        self.more.append(send(*self.give, PLANE_B))
+        got = send(*self.give, PLANE_B)
+        self.more.append(hold(got, cost=cost) if cost else got)
 
     def side(self, after=()):
         self.give = [add_pieces(self.parts(), 1, 1, after)]
@@ -207,26 +194,23 @@
     def reduction(self, pieces, after=()):
         return PlainReduction(pieces)
 
-    def vectors_begin(self, vector_sums):
-        self.vector_sums = vector_sums.reshape(-1)
+    def reduce_far(self, both, after=()):
+        self.both = both
         return []
 
-    def vectors_next(self, pairs):
-        return []
-
-    def vectors_end(self):
-        return lax.psum_scatter(self.vector_sums, AXES, scatter_dimension=0, tiled=True)
-
-    def reduce_far(self, rest, after=()):
-        self.rest = rest
-
-    def reduce_near(self, zero, rest, after=()):
-        self.zero = zero
-
-    def reduce_last(self, after=()):
-        sums = jnp.concatenate([self.zero.whole(), self.rest.whole()])
+    def reduce_near(self, zero, three, after=()):
+        self.zero, self.three = zero, three
+
+    def reduce_last(self):
+        zero = self.zero.whole()
+        block = Q // 8
+        packed = zero[0, :, block:, :].astype(f32)
+        rows = packed[..., : D // 2] + packed[..., D // 2 :]
+        vectors = jnp.swapaxes(rows[:, :4, : NVEC // 32], 0, 1).reshape(-1)
+        vectors = lax.psum_scatter(vectors, AXES, scatter_dimension=0, tiled=True)
+        sums = jnp.concatenate([zero[:, :, :block].reshape(-1, D), *(v.whole().reshape(-1, D) for v in (self.both, self.three))])
         owned = lax.psum_scatter(sums, AXES, scatter_dimension=0, tiled=True)
-        return owned.astype(f32), jnp.zeros_like(owned)
+        return owned.astype(f32), jnp.zeros_like(owned), vectors
 
 
 class PlainReduction:
@@ -234,7 +218,7 @@
         self.pieces = jnp.concatenate(pieces)
         self.give = []
 
-    def across(self, after=()):
+    def across(self, after=(), cost=0):
         pass
 
     def side(self, after=()):
@@ -248,19 +232,7 @@
 
     def whole(self):
         order = np.argsort(np.array([0, 4, 1, 5, 2, 3, 6, 7]))
-        return jnp.swapaxes(self.pieces[order], 0, 1).reshape(-1, D)
-
-
-def pack(values):
-    high = lax.reduce_precision(values, 8, 7)
-    both = jnp.concatenate([high, values - high], axis=-1).astype(bf16)
-    gaps = [(0, 0)] * (both.ndim - 2) + [(0, 12), (0, D - both.shape[-1])]
-    return jnp.pad(both, gaps)
-
-
-def unpack(packed, count):
-    wide = packed[..., :4, :].astype(f32)
-    return wide[..., :count] + wide[..., count : 2 * count]
+        return jnp.swapaxes(self.pieces[order], 0, 1)
 
 
 VMEM_LIMIT = 60 * 1024 * 1024
@@ -336,25 +308,50 @@
     ]
 
 
-def hand_block(place, source, at, targets, part, sem):
-    rows = source.shape[0] // 8
+def piece_of(place, at):
     y, c, x = place[0], place[1], place[2]
     core = (at >> 1) & 1
     flip_y, flip_x = (at >> 2) ^ y, (at & 1) ^ x
     first = jnp.where(core == 0, flip_y, flip_x)
     second = jnp.where(core == 0, flip_x, flip_y)
-    which = jnp.where(core == c, 0, 2) + second
+    return jnp.where(core == c, 0, 2) + second, first
+
+
+def hand_block(place, source, at, targets, part, sem):
+    rows = source.shape[0] // 8
+    which, first = piece_of(place, at)
     for k, target in enumerate(targets):
 
         @pl.when(which == k)
         def _():
-            pltpu.make_async_copy(source.at[rows_of(at, rows)], target.at[first, part], sem).start()
+            pltpu.make_async_copy(source.at[rows_of(at, rows)], target.at[first, part, pl.ds(0, rows)], sem).start()
+
+
+def hand_rows(place, source, at, targets, sem):
+    count = source.shape[1]
+    which, first = piece_of(place, at)
+    for k, target in enumerate(targets):
+
+        @pl.when(which == k)
+        def _():
+            there = target.at[first, 0, pl.ds(target.shape[2] - count, count)]
+            pltpu.make_async_copy(source.at[at], there, sem).start()
+
+
+def pack_rows(values):
+    return jnp.concatenate(twice(values), axis=1)
+
+
+def unpack_rows(packed):
+    half = packed.shape[1] // 2
+    wide = packed.astype(f32)
+    return wide[:, :half] + wide[:, half:]
 
 
 def hand_wait(source, targets, part, sems):
     rows = source.shape[0] // 8
     for k in range(8):
-        pltpu.make_async_copy(source.at[pl.ds(0, rows)], targets[0].at[0, part], sems.at[k]).wait()
+        pltpu.make_async_copy(source.at[pl.ds(0, rows)], targets[0].at[0, part, pl.ds(0, rows)], sems.at[k]).wait()
 
 
 def finish(*copies):
@@ -523,7 +520,8 @@
 
 def middle_kernel(
     place, a0, a1, a2, a3, b0, b1, b2, b3, c0, c1, c2, c3, tokens_in, context_in, cotangent_in, types, table,
-    layer_out_to, grad_first_to, grad_context_to, sums, keep_lo, keep_hi, give_lo, give_hi,
+    layer_out_to, grad_first_to, grad_context_to, sums,
+    keep_lo, keep_hi, give_lo, give_hi, keep_lo3, keep_hi3, give_lo3, give_hi3,
     weights, pre_a, pre_b, total, tokens, context, cotangent, layer_out, active, slope, unit_one, spread_one, normed_low,
     grad_context, down_made, sems, more,
 ):
@@ -553,6 +551,7 @@
     loop(rows // PART, first)
     sent = []
     targets = (keep_lo, keep_hi, give_lo, give_hi)
+    targets3 = (keep_lo3, keep_hi3, give_lo3, give_hi3)
     finish(batches[1])
 
     def gelu(pre, i, here):
@@ -612,7 +611,7 @@
 
     loop(FF // STEP, weigh_down)
     third_quarter = down_made.at[pl.ds(D, Q)]
-    loop(8, lambda p: hand_block(place, third_quarter, p, targets, 2, sems.at[2, p]))
+    loop(8, lambda p: hand_block(place, third_quarter, p, targets3, 0, sems.at[2, p]))
 
     def through(pre, i, here):
         return (pre[here, :] * slope[here, rows_of(i, CHUNK)]).astype(bf16)
@@ -672,7 +671,7 @@
     half = FF // STEP // 2
     loop(half, lambda i: weigh_up(half + i))
     finish(moved)
-    hand_wait(third_quarter, targets, 2, sems.at[2])
+    hand_wait(third_quarter, targets3, 0, sems.at[2])
     quarters = weights.at[pl.ds(0, Q)], weights.at[pl.ds(Q, Q)]
     loop(8, lambda p: hand_block(place, quarters[1], p, targets, 1, sems.at[1, p]))
 
@@ -694,8 +693,9 @@
     return call(
         middle_kernel,
         [shape((rows, D), bf16), shape((rows, D), f32), shape((D, rows), bf16), shape((11, FF), f32)]
-        + [shape((2, 3, Q // 8, D), bf16)] * 4,
-        [anywhere] * 3 + [whole] + [anywhere] * 4,
+        + [shape((2, 2, Q // 8, D), bf16)] * 4
+        + [shape((2, 1, Q // 8, D), bf16)] * 4,
+        [anywhere] * 3 + [whole] + [anywhere] * 8,
         [
             pltpu.VMEM((3 * Q, D), bf16),
             pltpu.VMEM((rows, CHUNK), f32),
@@ -788,8 +788,8 @@
 
 def mixed_grad_kernel(
     place, a0, a1, a2, a3, b0, b1, b2, b3, mixed_in, tokens, types, table, middle_sums,
-    keep_lo, keep_hi, give_lo, give_hi, sums,
-    low, mixed, made, weights, by_type, sems, more,
+    keep_lo, keep_hi, give_lo, give_hi,
+    low, mixed, made, weights, by_type, sums, wide, packed, sems, more, others,
 ):
     step = 384
     for i in range(Q // step):
@@ -824,26 +824,44 @@
         sums[row : row + 1, :] = by_type[0:1, start : start + D] + by_type[1:2, start : start + D]
     for i in range(FF // D):
         sums[10 + i : 11 + i, :] = middle_sums[10:11, i * D : (i + 1) * D]
+    wide[...] = jnp.zeros_like(wide)
+    entries = NVEC // 32
+    for block in range(8):
+        for z in range(4):
+            row, lane = divmod((z * 8 + block) * entries, D)
+            taken = min(entries, D - lane)
+            wide[block, z : z + 1, 0:taken] = sums[row : row + 1, lane : lane + taken]
+            if taken < entries:
+                wide[block, z : z + 1, taken:entries] = sums[row + 1 : row + 2, 0 : entries - taken]
+        packed[block] = pack_rows(wide[block])
+
+    loop(8, lambda p: hand_rows(place, packed, p, targets, others.at[p]))
     hand_wait(made, targets, 0, sems)
+    for p in range(8):
+        pltpu.make_async_copy(packed.at[p], keep_lo.at[0, 0, pl.ds(Q // 8, 16)], others.at[p]).wait()
 
 
 def mixed_grad(place, pieces, mixed, tokens, types, table, middle_sums, after=()):
     rows = tokens.shape[0]
     return call(
         mixed_grad_kernel,
-        [shape((2, 1, Q // 8, D), bf16)] * 4 + [shape((NVEC // D, D), f32)],
-        [anywhere] * 4 + [whole],
+        [shape((2, 1, Q // 8 + 16, D), bf16)] * 4,
+        [anywhere] * 4,
         [
             pltpu.VMEM((rows, D), bf16),
             pltpu.VMEM((Q, rows), bf16),
             pltpu.VMEM((Q, D), bf16),
             pltpu.VMEM((Q, D), bf16),
             pltpu.VMEM((8, Q), f32),
+            pltpu.VMEM((16, D), f32),
+            pltpu.VMEM((8, 16, D // 2), f32),
+            pltpu.VMEM((8, 16, D), bf16),
             pltpu.SemaphoreType.DMA((8,)),
             pltpu.SemaphoreType.DMA((6,)),
+            pltpu.SemaphoreType.DMA((8,)),
         ],
-        0,
-        0,
+        2 * rows * Q * D,
+        12 << 20,
         place, *pieces, mixed, tokens, types, table, middle_sums,
         specs=[scalars] + [anywhere] * 9 + [whole] * 4,
         name="mixed_grad",
@@ -873,8 +891,8 @@
         [shape((rows, D), f32)],
         [anywhere],
         [pltpu.VMEM((Q, D), bf16), pltpu.VMEM((rows, D), f32), pltpu.SemaphoreType.DMA((8,))],
-        2 * rows * Q * D,
-        15 << 20,
+        0,
+        0,
         place, *pieces, mixed, grad_first,
         specs=[scalars] + [anywhere] * 8 + [whole] * 2,
         name="input_back",
@@ -894,7 +912,7 @@
     )
 
 
-def hold(values, *after):
+def hold(values, *after, cost=0):
     skip = len(after)
     return pl.pallas_call(
         lambda *refs: None,
@@ -902,6 +920,7 @@
         in_specs=[anywhere] * (1 + skip),
         out_specs=anywhere,
         input_output_aliases={0: 0},
+        cost_estimate=pl.CostEstimate(flops=cost, bytes_accessed=0, transcendentals=0),
         name="hold",
     )(values, *after)
 
@@ -1027,8 +1046,9 @@
 
 
 def add_pieces_kernel(*refs):
-    _, n, rows, _ = refs[0].shape
-    for a in range(refs[0].shape[0]):
+    count, n, rows, _ = refs[0].shape
+    block = rows // ADD_ROWS * ADD_ROWS
+    for a in range(count):
         for b in range(n):
 
             def step(i):
@@ -1038,7 +1058,9 @@
                     total = total + ref[a, b, here, :].astype(f32)
                 refs[-1][a, b, here, :] = total.astype(bf16)
 
-            loop(rows // ADD_ROWS, step)
+            loop(block // ADD_ROWS, step)
+            if rows > block:
+                refs[-1][a, b, block:, :] = pack_rows(sum(unpack_rows(ref[a, b, block:, :]) for ref in refs[:-1]))
 
 
 def add_pieces(parts, first, count, after=()):
@@ -1054,12 +1076,8 @@
     )[0]
 
 
-def rows_spec(rows):
-    return pl.BlockSpec((rows, D), lambda i: (0, 0))
-
-
-def piece_spec(rows, j):
-    return pl.BlockSpec((1, 1, rows, D), lambda i: (0, j, 0, 0))
+def piece_spec(part, j):
+    return pl.BlockSpec((1, 1, *part.shape[2:]), lambda i: (0, j, 0, 0))
 
 
 def sum_of(refs, here):
@@ -1070,22 +1088,29 @@
 
 
 def two_sums_kernel(table, keep_table, place, *refs):
+    keep, give = refs[8], refs[9]
+    block = keep.shape[0]
+
     def step(i):
         here = rows_of(i, ADD_ROWS)
         sums = sum_of(refs[:4], here), sum_of(refs[4:8], here)
-        refs[8][here, :] = by_plane(place, keep_table, sums)
-        refs[9][here, :] = by_plane(place, table, sums).astype(bf16)
-
-    loop(refs[8].shape[0] // ADD_ROWS, step)
+        keep[here, :] = by_plane(place, keep_table, sums)
+        give[here, :] = by_plane(place, table, sums).astype(bf16)
+
+    loop(block // ADD_ROWS, step)
+    if len(refs) > 10:
+        total = sum(unpack_rows(ref[0, 0, block:, :]) for ref in refs[:4])
+        refs[10][...] = total
+        give[block:, :] = pack_rows(total)
 
 
 def two_sums(place, table, first, second, name, after):
-    rows = first[0][0].shape[2]
+    rows, more = second[0][0].shape[2], first[0][0].shape[2] - second[0][0].shape[2]
     args = first + second
     return picked(
         functools.partial(two_sums_kernel, table, tuple(1 - k for k in table)),
-        [shape((rows, D), f32), shape((rows, D), bf16)],
-        [scalars] + [piece_spec(rows, j) for _, j in args],
+        [shape((rows, D), f32), shape((rows + more, D), bf16)] + ([shape((more, D // 2), f32)] if more else []),
+        [scalars] + [piece_spec(p, j) for p, j in args],
         [place] + [a for a, _ in args],
         name,
         after,
@@ -1097,28 +1122,32 @@
 
 
 def near_sums(place, zero, rest, after=()):
-    return two_sums(place, (1, 0, 1, 0), [(p, 0) for p in zero], [(p, 2) for p in rest], "near_sums", after)
-
-
-def last_sums_kernel(place, kept_near, kept_far, near, far, base, give):
+    return two_sums(place, (1, 0, 1, 0), [(p, 0) for p in zero], [(p, 0) for p in rest], "near_sums", after)
+
+
+def last_sums_kernel(place, kept_near, kept_far, kept_rows, near, far, base, give, sums, packed):
+    block = base.shape[0]
+
     def step(i):
         here = rows_of(i, ADD_ROWS)
-        sums = (kept_near[here, :] + near[here, :].astype(f32), kept_far[here, :] + far[here, :].astype(f32))
-        give[here, :] = by_plane(place, (1, 0, 0, 1), sums).astype(bf16)
-        base[here, :] = by_plane(place, (0, 1, 1, 0), sums)
-
-    loop(base.shape[0] // ADD_ROWS, step)
-
-
-def last_sums(place, *args, after=()):
-    rows = args[0].shape[0]
+        both = (kept_near[here, :] + near[here, :].astype(f32), kept_far[here, :] + far[here, :].astype(f32))
+        give[here, :] = by_plane(place, (1, 0, 0, 1), both).astype(bf16)
+        base[here, :] = by_plane(place, (0, 1, 1, 0), both)
+
+    loop(block // ADD_ROWS, step)
+    total = kept_rows[...] + unpack_rows(near[block:, :])
+    sums[...] = total
+    packed[...] = pack_rows(total)
+
+
+def last_sums(place, *args):
+    rows, more = args[0].shape[0], args[2].shape
     return picked(
         last_sums_kernel,
-        [shape((rows, D), f32), shape((rows, D), bf16)],
-        [scalars] + [rows_spec(rows)] * 4,
+        [shape((rows, D), f32), shape((rows, D), bf16), shape(more, f32), shape((more[0], D), bf16)],
+        [scalars] + [pl.BlockSpec(a.shape, lambda i: (0, 0)) for a in args],
         [place, *args],
         "last_sums",
-        after,
     )
 
 
@@ -1216,24 +1245,20 @@
     layer_out, grad_first, grad_context, middle_sums, *parts = middle(
         place, pieces, tokens, types, context, cotangent, table
     )
-    rest = ring.reduction(parts)
-    rest.across()
-    mixed = attend_back(place, lengths, turned, grad_context, spreads, keys, after=rest.give)
-    *parts, vector_sums = mixed_grad(place, early, mixed, tokens, types, table, middle_sums)
-    zero = ring.reduction(parts)
-    swapped = ring.vectors_begin(vector_sums)
-    rest.side(after=[vector_sums])
-    zero.across(after=rest.give + swapped)
-    crossed = ring.vectors_next(PLANE_B)
-    input_grad = input_back(place, early, mixed, grad_first, after=zero.give)
-    zero.side(after=[input_grad, *rest.last(), *crossed])
-    crossed = ring.vectors_next(PLANE_A)
-    ring.reduce_far(rest, after=zero.give)
-    ring.reduce_near(zero, rest, after=crossed)
-    crossed = ring.vectors_next(Z_NEAR)
-    base, last = ring.reduce_last(after=crossed)
-    ring.vectors_next(Z_FAR)
-    owned_vector = ring.vectors_end()
+    both, three = ring.reduction(parts[:4]), ring.reduction(parts[4:])
+    three.across()
+    both.across(after=three.give, cost=FAR_COST)
+    mixed = attend_back(place, lengths, turned, grad_context, spreads, keys, after=both.give)
+    three.side(after=[mixed])
+    parts = mixed_grad(place, early, mixed, tokens, types, table, middle_sums, after=three.give)
+    zero = ring.reduction(parts, after=three.last())
+    zero.across()
+    both.side(after=zero.give)
+    input_grad = input_back(place, early, mixed, grad_first, after=both.give)
+    give = ring.reduce_far(both, after=[input_grad])
+    zero.side(after=[input_grad])
+    ring.reduce_near(zero, three)
+    base, last, owned_vector = ring.reduce_last()
     grad_t, left_new, right_new, master_t, slow_t, low_t = owner_step(
         base, last, left_stats, right_stats, left_root, right_root, master.T, slow_weights.T
     )

time: 305 us -> 287 us (0.941)
  waiting for transfers between devices: 104 us -> 84.4 us
    ppermute x34, waiting for transfers between devices: 104 us -> 84.4 us  [send(): return lax.ppermute(values, AXES, pairs)]
    unnamed x76 -> x102, local copies, waits for them, and re-layouts: 15.2 us -> 17.2 us
    pallas_call x7 -> x9, Pallas kernels: 12.5 us -> 13.4 us  [picked(): pl.pallas_call(body, grid=(1,), out_shape=outs, in_specs=[*specs, *[anywh...]
  transfers between devices with their start and end apart: 34 -> 34, of which waited for: 21 -> 21; matrix products, arithmetic and copies ran while one was open for 2% -> 1% of each run, Pallas kernels for 21% -> 23%
where the time goes in v3:
time: 287 us; the launch traced here: 286 us
  Pallas kernels  141 us (49%)
  waiting for transfers between devices  84.4 us (29%)
  starting transfers between devices  39.2 us (14%)
  local copies, waits for them, and re-layouts  18.7 us (7%)
    pallas_call x12, Pallas kernels, call(): pl.pallas_call(body, out_shape=outs, in_specs=[*specs, *[anywhere] * skip...  128 us
    ppermute x34, waiting for transfers between devices, send(): return lax.ppermute(values, AXES, pairs)  84.4 us
    ppermute x34, starting transfers between devices, send(): return lax.ppermute(values, AXES, pairs)  39.2 us
    unnamed x102, local copies, waits for them, and re-layouts  17.2 us
    pallas_call x9, Pallas kernels, picked(): pl.pallas_call(body, grid=(1,), out_shape=outs, in_specs=[*specs, *[anywh...  13.4 us
  transfers between devices with their start and end apart: 34, of which 21 were waited for; matrix products, arithmetic and copies ran while one was open for 1% of the time, Pallas kernels for 23%

profile of v3, /device:TPU:0, one launch (start us, length us, event | category | flops | bytes accessed | tf_op | source)
XLA Modules:
  0.0 285.9 jit_solution(5674246437320572913)
XLA Ops:
  1.5 1.2 copy-done.32
  2.7 0.9 prepare_own.1.refs_1_
  3.5 3.0 %collective-permute-start.1 = (bf16[304,768]{1,0:T(8,128)(2,1)S(1)}, bf16[304,768]{1,0:T(8,128)(2,1)S(1)}, u32[]{:S(2)}, u32[]{:S(2)}) collective-permute-start(bf16[304,768]{1,0:T(8,128)(2,1)S(1)} %prepare_own.1.refs_1_), channel_id=1, source_target_pairs={{0,4},{1,5},{2,3},{3,2},{4,0},{5,1},{6,7},{7,6},{8,12},{9,13},{10,... | collective-permute-start | bytes 1400840 | tf_op jit(solution)/shard_map/ppermute | solution.py:59
  6.6 2.6 collective-permute-start
  9.2 4.0 %collective-permute-done.1.refs_3_ = bf16[304,768]{1,0:T(8,128)(2,1)S(1)} collective-permute-done((bf16[304,768]{1,0:T(8,128)(2,1)S(1)}, bf16[304,768]{1,0:T(8,128)(2,1)S(1)}, u32[]{:S(2)}, u32[]{:S(2)}) %collective-permute-start.1) | collective-permute-done | bytes 466976 | tf_op jit(solution)/shard_map/ppermute | solution.py:59
  13.1 5.7 %collective-permute-done.refs_2_ = bf16[304,768]{1,0:T(8,128)(2,1)S(1)} collective-permute-done((bf16[304,768]{1,0:T(8,128)(2,1)S(1)}, bf16[304,768]{1,0:T(8,128)(2,1)S(1)}, u32[]{:S(2)}, u32[]{:S(2)}) %collective-permute-start) | collective-permute-done | bytes 466976 | tf_op jit(solution)/shard_map/ppermute | solution.py:59
  21.5 5.0 %collective-permute-start.5 = (bf16[304,768]{1,0:T(8,128)(2,1)S(1)}, bf16[304,768]{1,0:T(8,128)(2,1)S(1)}, u32[]{:S(2)}, u32[]{:S(2)}) collective-permute-start(bf16[304,768]{1,0:T(8,128)(2,1)S(1)} %get-tuple-element.55.refs_1_), channel_id=1, source_target_pairs={{0,8},{1,9},{2,10},{3,11},{4,12},{5,13},{6,14},{7,15},{8,0},{9,1},... | collective-permute-start | bytes 1400840 | tf_op jit(solution)/shard_map/ppermute | solution.py:59
  26.5 6.7 %collective-permute-done.2.refs_5_.refs_3_.refs_2_ = bf16[2,304,768]{2,1,0:T(8,128)(2,1)S(1)} collective-permute-done((bf16[2,304,768]{2,1,0:T(8,128)(2,1)S(1)}, bf16[2,304,768]{2,1,0:T(8,128)(2,1)S(1)}, u32[]{:S(2)}, u32[]{:S(2)}) %collective-permute-start.2) | collective-permute-done | bytes 933920 | tf_op jit(solution)/shard_map/ppermute | solution.py:59
  33.1 3.4 %collective-permute-start.6 = (bf16[16,768]{1,0:T(8,128)(2,1)S(1)}, bf16[16,768]{1,0:T(8,128)(2,1)S(1)}, u32[]{:S(2)}, u32[]{:S(2)}) collective-permute-start(bf16[16,768]{1,0:T(8,128)(2,1)S(1)} %get-tuple-element.56), channel_id=1, source_target_pairs={{0,16},{1,17},{2,18},{3,19},{4,20},{5,21},{6,22},{7,23},{8,24},{9,... | collective-permute-start | bytes 73736 | tf_op jit(solution)/shard_map/ppermute | solution.py:59
  36.5 0.9 collective-permute-start.9
  37.5 0.9 collective-permute-done.6.refs_4_
  39.1 1.0 copy-done.10
  40.1 1.5 collective-permute-start.7
  42.1 7.2 %collective-permute-done.9.refs_4_ = bf16[304,768]{1,0:T(8,128)(2,1)S(1)} collective-permute-done((bf16[304,768]{1,0:T(8,128)(2,1)S(1)}, bf16[304,768]{1,0:T(8,128)(2,1)S(1)}, u32[]{:S(2)}, u32[]{:S(2)}) %collective-permute-start.9) | collective-permute-done | bytes 466976 | tf_op jit(solution)/shard_map/ppermute | solution.py:59
  49.3 4.0 %collective-permute-done.10.refs_5_.refs_1_ = bf16[288,768]{1,0:T(8,128)(2,1)S(1)} collective-permute-done((bf16[288,768]{1,0:T(8,128)(2,1)S(1)}, bf16[288,768]{1,0:T(8,128)(2,1)S(1)}, u32[]{:S(2)}, u32[]{:S(2)}) %collective-permute-start.10) | collective-permute-done | bytes 442400 | tf_op jit(solution)/shard_map/ppermute | solution.py:59
  54.2 0.8 collective-permute-start.11
  54.9 1.5 collective-permute-start.14
  56.5 11.6 %collective-permute-done.14.refs_3_ = bf16[288,768]{1,0:T(8,128)(2,1)S(1)} collective-permute-done((bf16[288,768]{1,0:T(8,128)(2,1)S(1)}, bf16[288,768]{1,0:T(8,128)(2,1)S(1)}, u32[]{:S(2)}, u32[]{:S(2)}) %collective-permute-start.14) | collective-permute-done | bytes 442400 | tf_op jit(solution)/shard_map/ppermute | solution.py:59
  68.0 4.5 %collective-permute-done.11.refs_4_.refs_2_.refs_7_.refs_6_ = bf16[2,304,768]{2,1,0:T(8,128)(2,1)S(1)} collective-permute-done((bf16[2,304,768]{2,1,0:T(8,128)(2,1)S(1)}, bf16[2,304,768]{2,1,0:T(8,128)(2,1)S(1)}, u32[]{:S(2)}, u32[]{:S(2)}) %collective-permute-start.11) | collective-permute-done | bytes 933920 | tf_op jit(solution)/shard_map/ppermute | solution.py:59
  72.5 1.4 after_four.1.refs_14_.refs_9_
  75.2 2.3 collective-permute-done.13.refs_4_.refs_9_.refs_8_
  77.5 0.9 read_vectors.1
  79.2 17.5 %attend.1 = (bf16[2304,1024]{1,0:T(8,128)(2,1)}, bf16[1024,768]{1,0:T(8,128)(2,1)}, f32[12,1024]{1,0:T(8,128)}) custom-call(s32[8]{0:T(128)} %copy-done.36, s32[4]{0:T(128)} %refs_1_.3, bf16[2,304,768]{2,1,0:T(8,128)(2,1)} %copy-done.15, bf16[2,304,768]{2,1,0:T(8,128)(2,1)} %copy-done.9, bf16[2,304,768]{2,1,0:T(8,128)(2,1)} %copy-done.10, ...), custom_call_target="tpu_custom_call" | custom-call | flops 4429185024 | bytes 20971520 | tf_op jit(solution)/shard_map/attend/pallas_call | solution.py:256
  96.9 3.8 %collective-permute-done.17.refs_12_ = bf16[2,2,288,768]{3,2,1,0:T(8,128)(2,1)S(1)} collective-permute-done((bf16[2,2,288,768]{3,2,1,0:T(8,128)(2,1)}, bf16[2,2,288,768]{3,2,1,0:T(8,128)(2,1)S(1)}, u32[]{:S(2)}, u32[]{:S(2)}) %collective-permute-start.17) | collective-permute-done | bytes 1769504 | tf_op jit(solution)/shard_map/ppermute | solution.py:59
  100.7 1.2 copy-done.49
  101.9 62.8 %middle.1 = (bf16[1024,768]{1,0:T(8,128)(2,1)}, f32[1024,768]{1,0:T(8,128)}, bf16[768,1024]{1,0:T(8,128)(2,1)}, f32[11,3072]{1,0:T(8,128)}, bf16[2,2,288,768]{3,...) custom-call(s32[8]{0:T(128)} %copy-done.36, ...), custom_call_target="tpu_custom_call" | custom-call | flops 32614907904 | bytes 62914560 | tf_op jit(solution)/shard_map/middle/pallas_call | solution.py:256
  165.5 4.5 %collective-permute-done.19.refs_1_ = bf16[2,1,288,768]{3,2,1,0:T(8,128)(2,1)S(1)} collective-permute-done((bf16[2,1,288,768]{3,2,1,0:T(8,128)(2,1)}, bf16[2,1,288,768]{3,2,1,0:T(8,128)(2,1)S(1)}, u32[]{:S(2)}, u32[]{:S(2)}) %collective-permute-start.19) | collective-permute-done | bytes 884768 | tf_op jit(solution)/shard_map/ppermute | solution.py:59
  170.0 1.2 copy-done.33
  171.4 2.4 collective-permute-start.23
  173.8 1.7 add_pieces.7.refs_6_
  175.6 1.2 copy-done.14
  176.8 11.7 %attend_back.1.refs_3_.refs_9_ = bf16[2304,1024]{1,0:T(8,128)(2,1)S(1)} custom-call(s32[8]{0:T(128)S(1)} %copy-done.37, s32[4]{0:T(128)S(1)} %copy-done.41, bf16[2304,1024]{1,0:T(8,128)(2,1)S(1)} %copy-done.14, bf16[768,1024]{1,0:T(8,128)(2,1)S(1)} %copy-done.28, f32[12,1024]{1,0:T(8,128)S(1)} %copy-done.39, s32[1,1024]{1,0:T(1,128)S(1)} %bitcast.19, ...), custom_call_target="tpu_custom_call" | custom-call | flops 2013265920 | bytes 26214400 | tf_op jit(solution)/shard_map/attend_back/pallas_call | solution.py:256
  188.7 1.9 copy-done
  191.2 1.3 collective-permute-start.24
  192.5 11.0 %mixed_grad.1 = (bf16[2,1,304,768]{3,2,1,0:T(8,128)(2,1)}, bf16[2,1,304,768]{3,2,1,0:T(8,128)(2,1)}, bf16[2,1,304,768]{3,2,1,0:T(8,128)(2,1)}, bf16[2,1,304,768]{3,2,1,0:T(8,128)(2,1)}) custom-call(s32[8]{0:T(128)} %copy-done.36, bf16[2,304,768]{2,1,0:T(8,128)(2,1)} %copy-done.15, bf16[2,304,768]{2,1,0:T(8,128)(2,1)} %copy-done.9, ...), custom_call_target="tpu_custom_call" | custom-call | flops 3623878656 | bytes 12582912 | tf_op jit(solution)/shard_map/mixed_grad/pallas_call | solution.py:256
  203.5 0.8 collective-permute-done.24.refs_1_.refs_8_
  205.6 2.2 collective-permute-done.25.refs_1_
  207.8 1.2 add_pieces.9.refs_3_
  209.0 0.8 collective-permute-start.27
  209.8 1.9 collective-permute-done.20.refs_1_.refs_2_.refs_6_
  211.7 3.1 %add_pieces.10.refs_11_ = bf16[1,2,288,768]{3,2,1,0:T(8,128)(2,1)} custom-call(bf16[2,2,288,768]{3,2,1,0:T(8,128)(2,1)S(1)} %copy-done.3, bf16[2,2,288,768]{3,2,1,0:T(8,128)(2,1)S(1)} %collective-permute-done.20.refs_1_.refs_2_.refs_6_, bf16[2,2,288,768]{3,2,1,0:T(8,128)(2,1)} %hold.5.refs_2_.refs_3_.refs_7_, bf16[2,1,304,768]{3,2,1,0:T(8,128)(2,1)} %add_pieces.9.refs_3_), custom_call_target="tpu_custom_call" | custom-call | tf_op jit(solution)/shard_map/add_pieces/pallas_call | solution.py:1033
  214.8 1.3 collective-permute-start.29
  216.0 10.9 %input_back.1.refs_3_.refs_9_ = f32[1024,768]{1,0:T(8,128)} custom-call(s32[8]{0:T(128)} %copy-done.36, bf16[2,304,768]{2,1,0:T(8,128)(2,1)} %copy-done.15, bf16[2,304,768]{2,1,0:T(8,128)(2,1)} %copy-done.9, bf16[2,304,768]{2,1,0:T(8,128)(2,1)} %copy-done.10, bf16[2,304,768]{2,1,0:T(8,128)(2,1)} %copy-done.11, bf16[2,304,768]{2,1,0:T(8,128)(2,1)} %copy-done.12, ...), custom_call_target="tpu_custom_call" | custom-call | tf_op jit(solution)/shard_map/input_back/pallas_call | solution.py:256
  227.0 0.9 collective-permute-done.27.refs_2_.refs_3_
  227.9 1.9 copy-done.1
  229.8 1.2 copy-done.16
  231.0 1.5 add_pieces.11
  232.5 1.4 collective-permute-start.28
  233.9 1.5 copy-done.6
  235.4 2.1 far_sums.1
  237.5 3.1 %collective-permute-start.31 = (bf16[288,768]{1,0:T(8,128)(2,1)S(1)}, bf16[288,768]{1,0:T(8,128)(2,1)S(1)}, u32[]{:S(2)}, u32[]{:S(2)}) collective-permute-start(bf16[288,768]{1,0:T(8,128)(2,1)S(1)} %get-tuple-element.84), channel_id=1, source_target_pairs={{0,16},{1,17},{2,18},{3,19},{4,20},{5,21},{6,22},{7,23},{8,24},{9,... | collective-permute-start | bytes 1327112 | tf_op jit(solution)/shard_map/ppermute | solution.py:59
  241.2 2.6 near_sums.1
  243.7 1.8 collective-permute-start.30
  245.6 13.3 %collective-permute-done.31.refs_0_ = bf16[288,768]{1,0:T(8,128)(2,1)S(1)} collective-permute-done((bf16[288,768]{1,0:T(8,128)(2,1)S(1)}, bf16[288,768]{1,0:T(8,128)(2,1)S(1)}, u32[]{:S(2)}, u32[]{:S(2)}) %collective-permute-start.31) | collective-permute-done | bytes 442400 | tf_op jit(solution)/shard_map/ppermute | solution.py:59
  259.6 3.2 %collective-permute-done.30.refs_4_ = bf16[304,768]{1,0:T(8,128)(2,1)S(1)} collective-permute-done((bf16[304,768]{1,0:T(8,128)(2,1)}, bf16[304,768]{1,0:T(8,128)(2,1)S(1)}, u32[]{:S(2)}, u32[]{:S(2)}) %collective-permute-start.30) | collective-permute-done | bytes 466976 | tf_op jit(solution)/shard_map/ppermute | solution.py:59
  262.8 1.0 copy-done.35
  263.8 0.9 last_sums.1
  264.7 0.9 copy-done.42
  265.6 0.8 collective-permute-start.33
  266.5 2.4 collective-permute-start.32
  268.8 2.0 collective-permute-done.33
  272.1 4.4 %collective-permute-done.32.refs_1_ = bf16[288,768]{1,0:T(8,128)(2,1)S(1)} collective-permute-done((bf16[288,768]{1,0:T(8,128)(2,1)S(1)}, bf16[288,768]{1,0:T(8,128)(2,1)S(1)}, u32[]{:S(2)}, u32[]{:S(2)}) %collective-permute-start.32) | collective-permute-done | bytes 442400 | tf_op jit(solution)/shard_map/ppermute | solution.py:59
  276.5 0.8 copy-done.50
  277.2 8.5 %owner_step.1 = (f32[288,768]{1,0:T(8,128)}, f32[768,768]{1,0:T(8,128)}, f32[288,288]{1,0:T(8,128)}, f32[288,768]{1,0:T(8,128)}, f32[288,768]{1,0:T(8,128)}, /*index=5*/bf16[288,768]{1,0:T(8,128)(2,1)}) custom-call(f32[288,768]{1,0:T(8,128)} %copy-done.42, bf16[288,768]{1,0:T(8,128)(2,1)} %copy-done.50, f32[768,768]{1,0:T(8,128)} %refs_2_.1, ...), custom_call_target="tpu_custom_call" | custom-call | flops 2802843648 | bytes 15728640 | tf_op jit(solution)/shard_map/owner_step/pallas_call | solution.py:256
  (138 shorter events, 13.2 us)
Async XLA Ops:
  1.5 76.0 %copy-start.36 = (s32[8]{0:T(128)}, s32[8]{0:T(128)S(1)}, u32[]{:S(2)}) copy-start(s32[8]{0:T(128)S(1)} %stack.35.refs_0_) | copy-start | bytes 100
  3.5 9.6 %collective-permute-start.1 = (bf16[304,768]{1,0:T(8,128)(2,1)S(1)}, bf16[304,768]{1,0:T(8,128)(2,1)S(1)}, u32[]{:S(2)}, u32[]{:S(2)}) collective-permute-start(bf16[304,768]{1,0:T(8,128)(2,1)S(1)} %prepare_own.1.refs_1_), channel_id=1, source_target_pairs={{0,4},{1,5},{2,3},{3,2},{4,0},{5,1},{6,7},{7,6},{8,12},{9,13},{10,... | collective-permute-start | bytes 1400840 | tf_op jit(solution)/shard_map/ppermute | solution.py:59
  6.6 12.2 %collective-permute-start = (bf16[304,768]{1,0:T(8,128)(2,1)S(1)}, bf16[304,768]{1,0:T(8,128)(2,1)S(1)}, u32[]{:S(2)}, u32[]{:S(2)}) collective-permute-start(bf16[304,768]{1,0:T(8,128)(2,1)S(1)} %prepare_own.1.refs_1_), channel_id=1, source_target_pairs={{0,16},{1,17},{2,18},{3,19},{4,20},{5,21},{6,22},{7,23},{8,0},{9,1... | collective-permute-start | bytes 1400840 | tf_op jit(solution)/shard_map/ppermute | solution.py:59
  19.5 34.6 %copy-start.15 = (bf16[2,304,768]{2,1,0:T(8,128)(2,1)}, bf16[2,304,768]{2,1,0:T(8,128)(2,1)S(1)}, u32[]{:S(2)}) copy-start(bf16[2,304,768]{2,1,0:T(8,128)(2,1)S(1)} %get-tuple-element.54.refs_2_.refs_1_) | copy-start | bytes 2801668
  19.5 13.6 %collective-permute-start.2 = (bf16[2,304,768]{2,1,0:T(8,128)(2,1)S(1)}, bf16[2,304,768]{2,1,0:T(8,128)(2,1)S(1)}, u32[]{:S(2)}, u32[]{:S(2)}) collective-permute-start(bf16[2,304,768]{2,1,0:T(8,128)(2,1)S(1)} %get-tuple-element.54.refs_2_.refs_1_), channel_id=1, source_target_pairs={{0,1},{1,0},{2,6},{3,7},{4,5},{5,4},{6,2},{7,3},{8,9},{9,8},{10,14... | collective-permute-start | bytes 2801672 | tf_op jit(solution)/shard_map/ppermute | solution.py:59
  20.1 18.3 %collective-permute-start.3 = (bf16[2,304,768]{2,1,0:T(8,128)(2,1)S(1)}, bf16[2,304,768]{2,1,0:T(8,128)(2,1)S(1)}, u32[]{:S(2)}, u32[]{:S(2)}) collective-permute-start(bf16[2,304,768]{2,1,0:T(8,128)(2,1)S(1)} %get-tuple-element.54.refs_2_.refs_1_), channel_id=1, source_target_pairs={{0,2},{1,3},{2,0},{3,1},{4,6},{5,7},{6,4},{7,5},{8,10},{9,11},{10,... | collective-permute-start | bytes 2801672 | tf_op jit(solution)/shard_map/ppermute | solution.py:59
  20.8 15.7 %collective-permute-start.8 = (bf16[304,768]{1,0:T(8,128)(2,1)S(1)}, bf16[304,768]{1,0:T(8,128)(2,1)S(1)}, u32[]{:S(2)}, u32[]{:S(2)}) collective-permute-start(bf16[304,768]{1,0:T(8,128)(2,1)S(1)} %prepare_own.1.refs_1_), channel_id=1, source_target_pairs={{0,0},{1,1},{2,2},{3,3},{4,4},{5,5},{6,6},{7,7},{8,16},{9,17},{10,... | collective-permute-start | bytes 1400840 | tf_op jit(solution)/shard_map/ppermute | solution.py:59
  21.5 16.9 %collective-permute-start.5 = (bf16[304,768]{1,0:T(8,128)(2,1)S(1)}, bf16[304,768]{1,0:T(8,128)(2,1)S(1)}, u32[]{:S(2)}, u32[]{:S(2)}) collective-permute-start(bf16[304,768]{1,0:T(8,128)(2,1)S(1)} %get-tuple-element.55.refs_1_), channel_id=1, source_target_pairs={{0,8},{1,9},{2,10},{3,11},{4,12},{5,13},{6,14},{7,15},{8,0},{9,1},... | collective-permute-start | bytes 1400840 | tf_op jit(solution)/shard_map/ppermute | solution.py:59
  33.1 20.9 %copy-start.9 = (bf16[2,304,768]{2,1,0:T(8,128)(2,1)}, bf16[2,304,768]{2,1,0:T(8,128)(2,1)S(1)}, u32[]{:S(2)}) copy-start(bf16[2,304,768]{2,1,0:T(8,128)(2,1)S(1)} %collective-permute-done.2.refs_5_.refs_3_.refs_2_) | copy-start | bytes 2801668
  33.1 20.3 %collective-permute-start.4 = (bf16[2,304,768]{2,1,0:T(8,128)(2,1)S(1)}, bf16[2,304,768]{2,1,0:T(8,128)(2,1)S(1)}, u32[]{:S(2)}, u32[]{:S(2)}) collective-permute-start(bf16[2,304,768]{2,1,0:T(8,128)(2,1)S(1)} %collective-permute-done.2.refs_5_.refs_3_.refs_2_), channel_id=1, source_target_pairs={{0,2},{1,3},{2,0},{3,1},{4,6},{5,7},{6,4},{7,5},{8,10},{9,11},{10,... | collective-permute-start | bytes 2801672 | tf_op jit(solution)/shard_map/ppermute | solution.py:59
  33.1 5.3 %collective-permute-start.6 = (bf16[16,768]{1,0:T(8,128)(2,1)S(1)}, bf16[16,768]{1,0:T(8,128)(2,1)S(1)}, u32[]{:S(2)}, u32[]{:S(2)}) collective-permute-start(bf16[16,768]{1,0:T(8,128)(2,1)S(1)} %get-tuple-element.56), channel_id=1, source_target_pairs={{0,16},{1,17},{2,18},{3,19},{4,20},{5,21},{6,22},{7,23},{8,24},{9,... | collective-permute-start | bytes 73736 | tf_op jit(solution)/shard_map/ppermute | solution.py:59
  36.5 12.8 %collective-permute-start.9 = (bf16[304,768]{1,0:T(8,128)(2,1)S(1)}, bf16[304,768]{1,0:T(8,128)(2,1)S(1)}, u32[]{:S(2)}, u32[]{:S(2)}) collective-permute-start(bf16[304,768]{1,0:T(8,128)(2,1)S(1)} %collective-permute-done.8.refs_3_), channel_id=1, source_target_pairs={{0,8},{1,9},{2,10},{3,11},{4,12},{5,13},{6,14},{7,15},{8,0},{9,1},... | collective-permute-start | bytes 1400840 | tf_op jit(solution)/shard_map/ppermute | solution.py:59
  40.1 13.3 %collective-permute-start.7 = (bf16[304,768]{1,0:T(8,128)(2,1)S(1)}, bf16[304,768]{1,0:T(8,128)(2,1)S(1)}, u32[]{:S(2)}, u32[]{:S(2)}) collective-permute-start(bf16[304,768]{1,0:T(8,128)(2,1)S(1)} %get-tuple-element.57.refs_1_), channel_id=1, source_target_pairs={{0,4},{1,5},{2,3},{3,2},{4,0},{5,1},{6,7},{7,6},{8,12},{9,13},{10,... | collective-permute-start | bytes 1400840 | tf_op jit(solution)/shard_map/ppermute | solution.py:59
  41.6 11.8 %collective-permute-start.10 = (bf16[288,768]{1,0:T(8,128)(2,1)S(1)}, bf16[288,768]{1,0:T(8,128)(2,1)S(1)}, u32[]{:S(2)}, u32[]{:S(2)}) collective-permute-start(bf16[288,768]{1,0:T(8,128)(2,1)S(1)} %get-tuple-element.58.refs_0_), channel_id=1, source_target_pairs={{0,4},{1,5},{2,3},{3,2},{4,0},{5,1},{6,7},{7,6},{8,12},{9,13},{10,... | collective-permute-start | bytes 1327112 | tf_op jit(solution)/shard_map/ppermute | solution.py:59
  53.4 14.6 %copy-start.11 = (bf16[2,304,768]{2,1,0:T(8,128)(2,1)}, bf16[2,304,768]{2,1,0:T(8,128)(2,1)S(1)}, u32[]{:S(2)}) copy-start(bf16[2,304,768]{2,1,0:T(8,128)(2,1)S(1)} %collective-permute-done.4.refs_6_.refs_5_.refs_4_) | copy-start | bytes 2801668
  54.1 23.4 %copy-start.12 = (bf16[2,304,768]{2,1,0:T(8,128)(2,1)}, bf16[2,304,768]{2,1,0:T(8,128)(2,1)S(1)}, u32[]{:S(2)}) copy-start(bf16[2,304,768]{2,1,0:T(8,128)(2,1)S(1)} %get-tuple-element.59.refs_1_.refs_6_.refs_5_) | copy-start | bytes 2801668
  54.1 13.9 %collective-permute-start.12 = (bf16[2,304,768]{2,1,0:T(8,128)(2,1)S(1)}, bf16[2,304,768]{2,1,0:T(8,128)(2,1)S(1)}, u32[]{:S(2)}, u32[]{:S(2)}) collective-permute-start(bf16[2,304,768]{2,1,0:T(8,128)(2,1)S(1)} %get-tuple-element.59.refs_1_.refs_6_.refs_5_), channel_id=1, source_target_pairs={{0,2},{1,3},{2,0},{3,1},{4,6},{5,7},{6,4},{7,5},{8,10},{9,11},{10,... | collective-permute-start | bytes 2801672 | tf_op jit(solution)/shard_map/ppermute | solution.py:59
  54.2 18.4 %collective-permute-start.11 = (bf16[2,304,768]{2,1,0:T(8,128)(2,1)S(1)}, bf16[2,304,768]{2,1,0:T(8,128)(2,1)S(1)}, u32[]{:S(2)}, u32[]{:S(2)}) collective-permute-start(bf16[2,304,768]{2,1,0:T(8,128)(2,1)S(1)} %get-tuple-element.59.refs_1_.refs_6_.refs_5_), channel_id=1, source_target_pairs={{0,1},{1,0},{2,6},{3,7},{4,5},{5,4},{6,2},{7,3},{8,9},{9,8},{10,14... | collective-permute-start | bytes 2801672 | tf_op jit(solution)/shard_map/ppermute | solution.py:59
  54.9 13.1 %collective-permute-start.14 = (bf16[288,768]{1,0:T(8,128)(2,1)S(1)}, bf16[288,768]{1,0:T(8,128)(2,1)S(1)}, u32[]{:S(2)}, u32[]{:S(2)}) collective-permute-start(bf16[288,768]{1,0:T(8,128)(2,1)S(1)} %get-tuple-element.60.refs_2_), channel_id=1, source_target_pairs={{0,4},{1,5},{2,3},{3,2},{4,0},{5,1},{6,7},{7,6},{8,12},{9,13},{10,... | collective-permute-start | bytes 1327112 | tf_op jit(solution)/shard_map/ppermute | solution.py:59
  68.0 9.4 %copy-start.7 = (bf16[2,304,768]{2,1,0:T(8,128)(2,1)}, bf16[2,304,768]{2,1,0:T(8,128)(2,1)S(1)}, u32[]{:S(2)}) copy-start(bf16[2,304,768]{2,1,0:T(8,128)(2,1)S(1)} %collective-permute-done.12.refs_5_.refs_3_.refs_8_.refs_7_) | copy-start | bytes 2801668
  72.5 4.9 %copy-start.8 = (bf16[2,304,768]{2,1,0:T(8,128)(2,1)}, bf16[2,304,768]{2,1,0:T(8,128)(2,1)S(1)}, u32[]{:S(2)}) copy-start(bf16[2,304,768]{2,1,0:T(8,128)(2,1)S(1)} %collective-permute-done.11.refs_4_.refs_2_.refs_7_.refs_6_) | copy-start | bytes 2801668
  73.9 22.8 %collective-permute-start.15 = (bf16[2,2,288,768]{3,2,1,0:T(8,128)(2,1)}, bf16[2,2,288,768]{3,2,1,0:T(8,128)(2,1)}, u32[]{:S(2)}, u32[]{:S(2)}) collective-permute-start(bf16[2,2,288,768]{3,2,1,0:T(8,128)(2,1)} %after_four.1.refs_14_.refs_9_), channel_id=1, source_target_pairs={{0,1},{1,0},{2,6},{3,7},{4,5},{5,4},{6,2},{7,3},{8,9},{9,8},{10,14... | collective-permute-start | bytes 5308424 | tf_op jit(solution)/shard_map/ppermute | solution.py:59
  74.7 2.8 collective-permute-start.13
  74.8 22.2 %collective-permute-start.16 = (bf16[2,2,288,768]{3,2,1,0:T(8,128)(2,1)}, bf16[2,2,288,768]{3,2,1,0:T(8,128)(2,1)S(1)}, u32[]{:S(2)}, u32[]{:S(2)}) collective-permute-start(bf16[2,2,288,768]{3,2,1,0:T(8,128)(2,1)} %after_four.1.refs_14_.refs_9_), channel_id=1, source_target_pairs={{0,2},{1,3},{2,0},{3,1},{4,6},{5,7},{6,4},{7,5},{8,10},{9,11},{10,... | collective-permute-start | bytes 5308424 | tf_op jit(solution)/shard_map/ppermute | solution.py:59
  96.8 3.9 %collective-permute-start.17 = (bf16[2,2,288,768]{3,2,1,0:T(8,128)(2,1)}, bf16[2,2,288,768]{3,2,1,0:T(8,128)(2,1)S(1)}, u32[]{:S(2)}, u32[]{:S(2)}) collective-permute-start(bf16[2,2,288,768]{3,2,1,0:T(8,128)(2,1)} %hold.4.refs_10_), channel_id=1, source_target_pairs={{0,2},{1,3},{2,0},{3,1},{4,6},{5,7},{6,4},{7,5},{8,10},{9,11},{10,... | collective-permute-start | bytes 5308424 | tf_op jit(solution)/shard_map/ppermute | solution.py:59
  96.9 3.8 %copy-start.48 = (bf16[2,2,288,768]{3,2,1,0:T(8,128)(2,1)}, bf16[2,2,288,768]{3,2,1,0:T(8,128)(2,1)S(1)}, u32[]{:S(2)}) copy-start(bf16[2,2,288,768]{3,2,1,0:T(8,128)(2,1)S(1)} %collective-permute-done.16.refs_11_) | copy-start | bytes 5308420
  164.8 9.0 %copy-start.24 = (bf16[2,2,288,768]{3,2,1,0:T(8,128)(2,1)S(1)}, bf16[2,2,288,768]{3,2,1,0:T(8,128)(2,1)}, u32[]{:S(2)}) copy-start(bf16[2,2,288,768]{3,2,1,0:T(8,128)(2,1)} %get-tuple-element.66.refs_0_) | copy-start | bytes 5308420
  164.8 9.0 %collective-permute-start.18 = (bf16[2,2,288,768]{3,2,1,0:T(8,128)(2,1)}, bf16[2,2,288,768]{3,2,1,0:T(8,128)(2,1)S(1)}, u32[]{:S(2)}, u32[]{:S(2)}) collective-permute-start(bf16[2,2,288,768]{3,2,1,0:T(8,128)(2,1)} %get-tuple-element.67), channel_id=1, source_target_pairs={{0,2},{1,3},{2,0},{3,1},{4,6},{5,7},{6,4},{7,5},{8,10},{9,11},{10,... | collective-permute-start | bytes 5308424 | tf_op jit(solution)/shard_map/ppermute | solution.py:59
  165.0 5.0 %collective-permute-start.19 = (bf16[2,1,288,768]{3,2,1,0:T(8,128)(2,1)}, bf16[2,1,288,768]{3,2,1,0:T(8,128)(2,1)S(1)}, u32[]{:S(2)}, u32[]{:S(2)}) collective-permute-start(bf16[2,1,288,768]{3,2,1,0:T(8,128)(2,1)} %get-tuple-element.69), channel_id=1, source_target_pairs={{0,2},{1,3},{2,0},{3,1},{4,6},{5,7},{6,4},{7,5},{8,10},{9,11},{10,... | collective-permute-start | bytes 2654216 | tf_op jit(solution)/shard_map/ppermute | solution.py:59
  165.4 23.2 %collective-permute-start.22 = (bf16[2,1,288,768]{3,2,1,0:T(8,128)(2,1)}, bf16[2,1,288,768]{3,2,1,0:T(8,128)(2,1)S(1)}, u32[]{:S(2)}, u32[]{:S(2)}) collective-permute-start(bf16[2,1,288,768]{3,2,1,0:T(8,128)(2,1)} %get-tuple-element.75), channel_id=1, source_target_pairs={{0,2},{1,3},{2,0},{3,1},{4,6},{5,7},{6,4},{7,5},{8,10},{9,11},{10,... | collective-permute-start | bytes 2654216 | tf_op jit(solution)/shard_map/ppermute | solution.py:59
  171.2 4.4 %copy-start.28 = (bf16[768,1024]{1,0:T(8,128)(2,1)S(1)}, bf16[768,1024]{1,0:T(8,128)(2,1)}, u32[]{:S(2)}) copy-start(bf16[768,1024]{1,0:T(8,128)(2,1)} %get-tuple-element.64.refs_3_) | copy-start | bytes 4718596
  171.4 17.1 %collective-permute-start.23 = (bf16[2,1,288,768]{3,2,1,0:T(8,128)(2,1)S(1)}, bf16[2,1,288,768]{3,2,1,0:T(8,128)(2,1)S(1)}, u32[]{:S(2)}, u32[]{:S(2)}) collective-permute-start(bf16[2,1,288,768]{3,2,1,0:T(8,128)(2,1)S(1)} %add_pieces.6.refs_2_), channel_id=1, source_target_pairs={{0,1},{1,0},{2,6},{3,7},{4,5},{5,4},{6,2},{7,3},{8,9},{9,8},{10,14... | collective-permute-start | bytes 2654216 | tf_op jit(solution)/shard_map/ppermute | solution.py:59
  173.8 3.0 %copy-start.14 = (bf16[2304,1024]{1,0:T(8,128)(2,1)S(1)}, bf16[2304,1024]{1,0:T(8,128)(2,1)}, u32[]{:S(2)}) copy-start(bf16[2304,1024]{1,0:T(8,128)(2,1)} %get-tuple-element.63.refs_2_) | copy-start | bytes 14155780
  173.8 3.0 %copy-start.37 = (s32[8]{0:T(128)S(1)}, s32[8]{0:T(128)}, u32[]{:S(2)}) copy-start(s32[8]{0:T(128)} %copy-done.36) | copy-start | bytes 100
  173.8 3.0 %copy-start.39 = (f32[12,1024]{1,0:T(8,128)S(1)}, f32[12,1024]{1,0:T(8,128)}, u32[]{:S(2)}) copy-start(f32[12,1024]{1,0:T(8,128)} %get-tuple-element.65.refs_4_) | copy-start | bytes 147460
  173.8 3.0 %copy-start.40 = (s32[1024]{0:T(1024)S(1)}, s32[1024]{0:T(1024)}, u32[]{:S(2)}) copy-start(s32[1024]{0:T(1024)} %param.19) | copy-start | bytes 12292
  173.8 3.0 %copy-start.41 = (s32[4]{0:T(128)S(1)}, s32[4]{0:T(128)}, u32[]{:S(2)}) copy-start(s32[4]{0:T(128)} %refs_1_.3) | copy-start | bytes 52
  175.5 34.3 %collective-permute-start.21 = (bf16[2,2,288,768]{3,2,1,0:T(8,128)(2,1)}, bf16[2,2,288,768]{3,2,1,0:T(8,128)(2,1)}, u32[]{:S(2)}, u32[]{:S(2)}) collective-permute-start(bf16[2,2,288,768]{3,2,1,0:T(8,128)(2,1)} %add_pieces.7.refs_6_), channel_id=1, source_target_pairs={{0,1},{1,0},{2,6},{3,7},{4,5},{5,4},{6,2},{7,3},{8,9},{9,8},{10,14... | collective-permute-start | bytes 5308424 | tf_op jit(solution)/shard_map/ppermute | solution.py:59
  176.8 11.8 %copy-start.18 = (bf16[2,1,288,768]{3,2,1,0:T(8,128)(2,1)S(1)}, bf16[2,1,288,768]{3,2,1,0:T(8,128)(2,1)}, u32[]{:S(2)}) copy-start(bf16[2,1,288,768]{3,2,1,0:T(8,128)(2,1)} %get-tuple-element.74.refs_0_.refs_5_) | copy-start | bytes 2654212
  191.2 13.1 %collective-permute-start.24 = (bf16[1,1,288,768]{3,2,1,0:T(8,128)(2,1)S(1)}, bf16[1,1,288,768]{3,2,1,0:T(8,128)(2,1)S(1)}, u32[]{:S(2)}, u32[]{:S(2)}) collective-permute-start(bf16[1,1,288,768]{3,2,1,0:T(8,128)(2,1)S(1)} %add_pieces.8.refs_14_), channel_id=1, source_target_pairs={{0,4},{1,5},{2,3},{3,2},{4,0},{5,1},{6,7},{7,6},{8,12},{9,13},{10,... | collective-permute-start | bytes 1327112 | tf_op jit(solution)/shard_map/ppermute | solution.py:59
  203.5 4.3 %copy-start.29 = (bf16[2,1,304,768]{3,2,1,0:T(8,128)(2,1)S(1)}, bf16[2,1,304,768]{3,2,1,0:T(8,128)(2,1)}, u32[]{:S(2)}) copy-start(bf16[2,1,304,768]{3,2,1,0:T(8,128)(2,1)} %get-tuple-element.76.refs_0_) | copy-start | bytes 2801668
  205.1 2.7 collective-permute-start.25
  205.1 6.6 %collective-permute-start.20 = (bf16[2,2,288,768]{3,2,1,0:T(8,128)(2,1)}, bf16[2,2,288,768]{3,2,1,0:T(8,128)(2,1)S(1)}, u32[]{:S(2)}, u32[]{:S(2)}) collective-permute-start(bf16[2,2,288,768]{3,2,1,0:T(8,128)(2,1)} %get-tuple-element.72), channel_id=1, source_target_pairs={{0,2},{1,3},{2,0},{3,1},{4,6},{5,7},{6,4},{7,5},{8,10},{9,11},{10,... | collective-permute-start | bytes 5308424 | tf_op jit(solution)/shard_map/ppermute | solution.py:59
  205.6 21.4 %collective-permute-start.26 = (bf16[2,1,304,768]{3,2,1,0:T(8,128)(2,1)}, bf16[2,1,304,768]{3,2,1,0:T(8,128)(2,1)}, u32[]{:S(2)}, u32[]{:S(2)}) collective-permute-start(bf16[2,1,304,768]{3,2,1,0:T(8,128)(2,1)} %get-tuple-element.79), channel_id=1, source_target_pairs={{0,2},{1,3},{2,0},{3,1},{4,6},{5,7},{6,4},{7,5},{8,10},{9,11},{10,... | collective-permute-start | bytes 2801672 | tf_op jit(solution)/shard_map/ppermute | solution.py:59
  209.0 18.9 %collective-permute-start.27 = (bf16[2,1,304,768]{3,2,1,0:T(8,128)(2,1)}, bf16[2,1,304,768]{3,2,1,0:T(8,128)(2,1)}, u32[]{:S(2)}, u32[]{:S(2)}) collective-permute-start(bf16[2,1,304,768]{3,2,1,0:T(8,128)(2,1)} %add_pieces.9.refs_3_), channel_id=1, source_target_pairs={{0,1},{1,0},{2,6},{3,7},{4,5},{5,4},{6,2},{7,3},{8,9},{9,8},{10,14... | collective-permute-start | bytes 2801672 | tf_op jit(solution)/shard_map/ppermute | solution.py:59
  211.7 3.1 %copy-start.5 = (bf16[2,2,288,768]{3,2,1,0:T(8,128)(2,1)}, bf16[2,2,288,768]{3,2,1,0:T(8,128)(2,1)S(1)}, u32[]{:S(2)}) copy-start(bf16[2,2,288,768]{3,2,1,0:T(8,128)(2,1)S(1)} %collective-permute-done.20.refs_1_.refs_2_.refs_6_) | copy-start | bytes 5308420
  214.8 19.1 %collective-permute-start.29 = (bf16[1,2,288,768]{3,2,1,0:T(8,128)(2,1)}, bf16[1,2,288,768]{3,2,1,0:T(8,128)(2,1)}, u32[]{:S(2)}, u32[]{:S(2)}) collective-permute-start(bf16[1,2,288,768]{3,2,1,0:T(8,128)(2,1)} %add_pieces.10.refs_11_), channel_id=1, source_target_pairs={{0,4},{1,5},{2,3},{3,2},{4,0},{5,1},{6,7},{7,6},{8,12},{9,13},{10,... | collective-permute-start | bytes 2654216 | tf_op jit(solution)/shard_map/ppermute | solution.py:59
  231.0 10.2 %copy-start.17 = (bf16[2,1,304,768]{3,2,1,0:T(8,128)(2,1)S(1)}, bf16[2,1,304,768]{3,2,1,0:T(8,128)(2,1)}, u32[]{:S(2)}) copy-start(bf16[2,1,304,768]{3,2,1,0:T(8,128)(2,1)} %get-tuple-element.78.refs_0_.refs_1_) | copy-start | bytes 2801668
  231.0 10.2 %copy-start.26 = (bf16[1,1,288,768]{3,2,1,0:T(8,128)(2,1)S(1)}, bf16[1,1,288,768]{3,2,1,0:T(8,128)(2,1)}, u32[]{:S(2)}) copy-start(bf16[1,1,288,768]{3,2,1,0:T(8,128)(2,1)} %copy-done.25) | copy-start | bytes 1327108
  232.5 8.6 %collective-permute-start.28 = (bf16[1,1,304,768]{3,2,1,0:T(8,128)(2,1)S(1)}, bf16[1,1,304,768]{3,2,1,0:T(8,128)(2,1)S(1)}, u32[]{:S(2)}, u32[]{:S(2)}) collective-permute-start(bf16[1,1,304,768]{3,2,1,0:T(8,128)(2,1)S(1)} %add_pieces.11), channel_id=1, source_target_pairs={{0,4},{1,5},{2,3},{3,2},{4,0},{5,1},{6,7},{7,6},{8,12},{9,13},{10,... | collective-permute-start | bytes 1400840 | tf_op jit(solution)/shard_map/ppermute | solution.py:59
  235.4 5.8 %copy-start.19 = (bf16[2,1,288,768]{3,2,1,0:T(8,128)(2,1)S(1)}, bf16[2,1,288,768]{3,2,1,0:T(8,128)(2,1)}, u32[]{:S(2)}) copy-start(bf16[2,1,288,768]{3,2,1,0:T(8,128)(2,1)} %get-tuple-element.74.refs_0_.refs_5_) | copy-start | bytes 2654212
  235.4 5.8 %copy-start.21 = (bf16[2,1,288,768]{3,2,1,0:T(8,128)(2,1)S(1)}, bf16[2,1,288,768]{3,2,1,0:T(8,128)(2,1)}, u32[]{:S(2)}) copy-start(bf16[2,1,288,768]{3,2,1,0:T(8,128)(2,1)} %copy-done.20) | copy-start | bytes 2654212
  235.4 5.8 %copy-start.23 = (bf16[2,1,288,768]{3,2,1,0:T(8,128)(2,1)S(1)}, bf16[2,1,288,768]{3,2,1,0:T(8,128)(2,1)}, u32[]{:S(2)}) copy-start(bf16[2,1,288,768]{3,2,1,0:T(8,128)(2,1)} %copy-done.22) | copy-start | bytes 2654212
  237.5 6.2 %copy-start.30 = (f32[288,768]{1,0:T(8,128)}, f32[288,768]{1,0:T(8,128)S(1)}, u32[]{:S(2)}) copy-start(f32[288,768]{1,0:T(8,128)S(1)} %get-tuple-element.81.refs_2_) | copy-start | bytes 2654212
  237.5 21.3 %collective-permute-start.31 = (bf16[288,768]{1,0:T(8,128)(2,1)S(1)}, bf16[288,768]{1,0:T(8,128)(2,1)S(1)}, u32[]{:S(2)}, u32[]{:S(2)}) collective-permute-start(bf16[288,768]{1,0:T(8,128)(2,1)S(1)} %get-tuple-element.84), channel_id=1, source_target_pairs={{0,16},{1,17},{2,18},{3,19},{4,20},{5,21},{6,22},{7,23},{8,24},{9,... | collective-permute-start | bytes 1327112 | tf_op jit(solution)/shard_map/ppermute | solution.py:59
  243.7 19.1 %copy-start.31 = (f32[288,768]{1,0:T(8,128)S(1)}, f32[288,768]{1,0:T(8,128)}, u32[]{:S(2)}) copy-start(f32[288,768]{1,0:T(8,128)} %copy-done.30) | copy-start | bytes 2654212
  243.7 19.1 %collective-permute-start.30 = (bf16[304,768]{1,0:T(8,128)(2,1)}, bf16[304,768]{1,0:T(8,128)(2,1)S(1)}, u32[]{:S(2)}, u32[]{:S(2)}) collective-permute-start(bf16[304,768]{1,0:T(8,128)(2,1)} %get-tuple-element.83), channel_id=1, source_target_pairs={{0,8},{1,9},{2,10},{3,11},{4,12},{5,13},{6,14},{7,15},{8,0},{9,1},... | collective-permute-start | bytes 1400840 | tf_op jit(solution)/shard_map/ppermute | solution.py:59
  259.6 11.3 %copy-start.47 = (f32[336]{0:T(512)S(1)}, f32[336]{0:T(512)}, u32[]{:S(2)}) copy-start(f32[336]{0:T(512)} %param.30) | copy-start | bytes 4036
  259.6 11.3 %copy-start.46 = (f32[336]{0:T(512)S(1)}, f32[336]{0:T(512)}, u32[]{:S(2)}) copy-start(f32[336]{0:T(512)} %param.29) | copy-start | bytes 4036
  259.6 11.9 %copy-start.45 = (f32[336]{0:T(512)S(1)}, f32[336]{0:T(512)}, u32[]{:S(2)}) copy-start(f32[336]{0:T(512)} %param.31) | copy-start | bytes 4036
  265.6 5.2 %collective-permute-start.33 = (bf16[16,768]{1,0:T(8,128)(2,1)S(1)}, bf16[16,768]{1,0:T(8,128)(2,1)S(1)}, u32[]{:S(2)}, u32[]{:S(2)}) collective-permute-start(bf16[16,768]{1,0:T(8,128)(2,1)S(1)} %get-tuple-element.94), channel_id=1, source_target_pairs={{0,16},{1,17},{2,18},{3,19},{4,20},{5,21},{6,22},{7,23},{8,24},{9,... | collective-permute-start | bytes 73736 | tf_op jit(solution)/shard_map/ppermute | solution.py:59
  266.5 10.0 %collective-permute-start.32 = (bf16[288,768]{1,0:T(8,128)(2,1)S(1)}, bf16[288,768]{1,0:T(8,128)(2,1)S(1)}, u32[]{:S(2)}, u32[]{:S(2)}) collective-permute-start(bf16[288,768]{1,0:T(8,128)(2,1)S(1)} %get-tuple-element.86), channel_id=1, source_target_pairs={{0,8},{1,9},{2,10},{3,11},{4,12},{5,13},{6,14},{7,15},{8,24},{9,25... | collective-permute-start | bytes 1327112 | tf_op jit(solution)/shard_map/ppermute | solution.py:59
  270.9 14.9 %copy-start.43 = (f32[336]{0:T(512)}, f32[336]{0:T(512)S(1)}, u32[]{:S(2)}) copy-start(f32[336]{0:T(512)S(1)} %fusion.1) | copy-start | bytes 4036
  271.5 14.3 %copy-start.44 = (f32[336]{0:T(512)}, f32[336]{0:T(512)S(1)}, u32[]{:S(2)}) copy-start(f32[336]{0:T(512)S(1)} %get-tuple-element.96) | copy-start | bytes 4036
  (21 other events, 34.4 us)

commit v4 on v3

--- a/solution.py
+++ b/solution.py
@@ -99,7 +99,7 @@
         across_b = send(pair_b, PLANE_B)
         swap_b = send(pair_b, CORES)
         side_d = send(slot_d, PLANE_A)
-        self.late = after_four(slot_c, side_c, slot_d, side_d, after=[across_b, swap_b])
+        self.late = after_four(slot_c, side_c, slot_d, side_d, after=[swap_b])
         swap_bb = send(across_b, CORES)
         slot_b = [pair_b, across_b, swap_b, swap_bb]
         table = read_vectors(place, slot_b, vectors.shape[0] // 2)
@@ -244,6 +244,8 @@
 CHUNKS = FF // CHUNK
 Q = 3 * D
 SPAN = 256
+TALL = 512
+flag_shape = jax.ShapeDtypeStruct((8, 128), jnp.float32)
 PART = 256
 
 
@@ -393,10 +395,11 @@
 
 
 def attend_kernel(
-    place, lengths, a0, a1, a2, a3, b0, b1, b2, b3, tokens, types, keys, table,
+    place, lengths, a0, a1, a2, a3, b0, b1, b2, b3, tokens_in, types, keys, table,
     turned_out, context_out, spreads,
-    weights, low, turned, context_turned, context, mask, sems,
+    weights, low, turned, context_turned, context, mask, tokens, sems, more,
 ):
+    arrived = begin(tokens_in, tokens, sems.at[9])
     copies = ingest(place, 0, ((a0, a1, a2, a3), (b0, b1, b2, b3)), weights, sems)
     rows = tokens.shape[0]
 
@@ -405,6 +408,7 @@
         low[here, :] = embed(tokens[here, :], types[:, here], table[...]).astype(bf16)
         mask[here, :] = column(allowed_keys(lengths, keys, i), SPAN)
 
+    finish(arrived)
     loop(rows // PART, prepare)
     finish(copies)
     step = 384
@@ -420,36 +424,32 @@
     loop(Q // step, project)
     sent = begin(turned, turned_out, sems.at[8])
 
-    together = 8
-
-    def units(i):
-        places = []
-        for j in range(together):
-            u = i * together + j
-            places.append((u % H, pl.multiple_of((u % H) * HD, HD), rows_of(u // H, SPAN)))
+
+    def sequence(s):
+        cols = rows_of(s, SPAN)
         scores = [
-            contract(turned[pl.ds(D + at, HD), cols], turned[pl.ds(at, HD), cols], 0, 0)
-            for _, at, cols in places
+            contract(turned[D + h * HD : D + (h + 1) * HD, cols], turned[h * HD : (h + 1) * HD, cols], 0, 0)
+            for h in range(H)
         ]
         probs = []
-        for (h, at, cols), score in zip(places, scores):
+        for h, score in enumerate(scores):
             score = jnp.minimum(score, mask[cols, :])
             peak = jnp.max(score, axis=0, keepdims=True)
             powers = jnp.exp(score - peak)
             total = jnp.sum(powers, axis=0, keepdims=True)
             probs.append((powers * (1.0 / total)).astype(bf16))
-            spreads[pl.ds(h, 1), cols] = peak + jnp.log(total)
-        for (h, at, cols), prob in zip(places, probs):
-            context_turned[pl.ds(at, HD), cols] = contract(turned[pl.ds(2 * D + at, HD), cols], prob, 1, 0).astype(bf16)
-
-    loop(H * (rows // SPAN) // together, units)
-
-    def turn(i):
-        here = rows_of(i, 128)
-        context[here, :] = context_turned[:, here].T
-
-    loop(rows // 128, turn)
-    finish(begin(context, context_out, sems.at[9]), sent)
+            spreads[h : h + 1, cols] = peak + jnp.log(total)
+        for h, prob in enumerate(probs):
+            value = turned[2 * D + h * HD : 2 * D + (h + 1) * HD, cols]
+            context_turned[h * HD : (h + 1) * HD, :] = contract(value, prob, 1, 0).astype(bf16)
+        context[cols, :] = context_turned[...].T
+        pltpu.make_async_copy(context.at[cols], context_out.at[cols], more.at[s]).start()
+
+    loop(rows // SPAN, sequence)
+    for s in range(rows // SPAN):
+        cols = pl.ds(s * SPAN, SPAN)
+        pltpu.make_async_copy(context.at[cols], context_out.at[cols], more.at[s]).wait()
+    finish(sent)
 
 
 def attend(place, lengths, pieces, tokens, types, keys, table, after=()):
@@ -462,15 +462,17 @@
             pltpu.VMEM((Q, D), bf16),
             pltpu.VMEM((rows, D), bf16),
             pltpu.VMEM((Q, rows), bf16),
-            pltpu.VMEM((D, rows), bf16),
+            pltpu.VMEM((D, SPAN), bf16),
             pltpu.VMEM((rows, D), bf16),
             pltpu.VMEM((rows, SPAN), f32),
+            pltpu.VMEM((rows, D), bf16),
             pltpu.SemaphoreType.DMA((10,)),
+            pltpu.SemaphoreType.DMA((rows // SPAN,)),
         ],
         2 * rows * Q * D + 4 * rows * 256 * D,
         20 << 20,
         place, lengths, *pieces, tokens, types, keys, table,
-        specs=[scalars] * 2 + [anywhere] * 8 + [whole] * 4,
+        specs=[scalars] * 2 + [anywhere] * 9 + [whole] * 3,
         name="attend",
         after=after,
     )
@@ -515,7 +517,7 @@
         sums[row : row + 1, 0:D] = jnp.sum(have, axis=0, keepdims=True)
 
 
-STEP = 512
+STEP = 768
 
 
 def middle_kernel(
@@ -584,10 +586,10 @@
     finish(batches[2])
 
     def add_down(i):
-        here = rows_of(i, SPAN)
+        here = rows_of(i, TALL)
         total[here, :] = contract(active[here, :], weights[down : down + FF, :], 1, 0)
 
-    loop(rows // SPAN, add_down)
+    loop(rows // TALL, add_down)
     finish(late)
 
     def second(i):
@@ -634,10 +636,10 @@
     loop(rows // PART, backward_end)
 
     def add_up(i):
-        here = rows_of(i, SPAN)
+        here = rows_of(i, TALL)
         total[here, :] += contract(active[here, :], weights[up : up + FF, :], 1, 0)
 
-    loop(rows // SPAN, add_up)
+    loop(rows // TALL, add_up)
 
     def third(i):
         here = rows_of(i, PART)
@@ -679,9 +681,16 @@
         here = rows_of(i, 384)
         weights[here, :] = contract(cotangent[:, here], context[...], 0, 0).astype(bf16)
 
+    def hand_one(p):
+        hand_block(place, quarters[0], p, targets, 0, sems.at[0, p])
+
+    def weigh_and_hand(i):
+        weigh_up(i)
+        loop(3, lambda p: hand_one(2 + 3 * i + p))
+
     loop(2, weigh_out)
-    loop(half, weigh_up)
-    loop(8, lambda p: hand_block(place, quarters[0], p, targets, 0, sems.at[0, p]))
+    loop(2, hand_one)
+    loop(half, weigh_and_hand)
     hand_wait(quarters[1], targets, 1, sems.at[1])
     hand_wait(quarters[0], targets, 0, sems.at[0])
     finish(sent)
@@ -869,7 +878,8 @@
     )
 
 
-def input_kernel(place, a0, a1, a2, a3, b0, b1, b2, b3, mixed, grad_first, input_grad_to, weights, made, sems):
+def input_kernel(place, a0, a1, a2, a3, b0, b1, b2, b3, mixed, grad_first, input_grad_to, flag, weights, made, sems):
+    flag[...] = jnp.zeros_like(flag)
     finish(ingest(place, 0, ((a0, a1, a2, a3), (b0, b1, b2, b3)), weights, sems))
     rows = grad_first.shape[0]
 
@@ -888,8 +898,8 @@
     rows = grad_first.shape[0]
     return call(
         input_kernel,
-        [shape((rows, D), f32)],
-        [anywhere],
+        [shape((rows, D), f32), flag_shape],
+        [anywhere, whole],
         [pltpu.VMEM((Q, D), bf16), pltpu.VMEM((rows, D), f32), pltpu.SemaphoreType.DMA((8,))],
         0,
         0,
@@ -897,7 +907,7 @@
         specs=[scalars] + [anywhere] * 8 + [whole] * 2,
         name="input_back",
         after=after,
-    )[0]
+    )
 
 
 SMALL_LIMIT = 16 * 1024 * 1024
@@ -1254,9 +1264,9 @@
     zero = ring.reduction(parts, after=three.last())
     zero.across()
     both.side(after=zero.give)
-    input_grad = input_back(place, early, mixed, grad_first, after=both.give)
-    give = ring.reduce_far(both, after=[input_grad])
-    zero.side(after=[input_grad])
+    input_grad, flag = input_back(place, early, mixed, grad_first, after=both.give)
+    ring.reduce_far(both, after=[flag])
+    zero.side(after=[flag])
     ring.reduce_near(zero, three)
     base, last, owned_vector = ring.reduce_last()
     grad_t, left_new, right_new, master_t, slow_t, low_t = owner_step(

time: 287 us -> 277 us (0.965)
  Pallas kernels: 141 us -> 136 us
  local copies, waits for them, and re-layouts: 18.7 us -> 14.8 us
    unnamed x102 -> x94, local copies, waits for them, and re-layouts: 17.2 us -> 13.3 us
    pallas_call x12, Pallas kernels: 128 us -> 124 us  [call(): pl.pallas_call(body, out_shape=outs, in_specs=[*specs, *[anywhere] * skip...]
  transfers between devices with their start and end apart: 34 -> 34, of which waited for: 21 -> 20; matrix products, arithmetic and copies ran while one was open for 1% -> 1% of each run, Pallas kernels for 23% -> 23%
where the time goes in v4:
time: 277 us
  Pallas kernels  136 us (49%)
  waiting for transfers between devices  83.6 us (30%)
  starting transfers between devices  39.7 us (14%)
  local copies, waits for them, and re-layouts  14.8 us (5%)
    pallas_call x12, Pallas kernels, call(): pl.pallas_call(body, out_shape=outs, in_specs=[*specs, *[anywhere] * skip...  124 us
    ppermute x34, waiting for transfers between devices, send(): return lax.ppermute(values, AXES, pairs)  83.6 us
    ppermute x34, starting transfers between devices, send(): return lax.ppermute(values, AXES, pairs)  39.7 us
    unnamed x94, local copies, waits for them, and re-layouts  13.3 us
    pallas_call x9, Pallas kernels, picked(): pl.pallas_call(body, grid=(1,), out_shape=outs, in_specs=[*specs, *[anywh...  11.7 us
  transfers between devices with their start and end apart: 34, of which 20 were waited for; matrix products, arithmetic and copies ran while one was open for 1% of the time, Pallas kernels for 23%

profile of v4, /device:TPU:0, one launch (start us, length us, event | category | flops | bytes accessed | tf_op | source)
XLA Modules:
  0.0 276.7 jit_solution(15780170563302995856)
XLA Ops:
  1.5 1.2 copy-done.27
  2.7 0.9 prepare_own.1.refs_1_
  3.5 3.0 %collective-permute-start.1 = (bf16[304,768]{1,0:T(8,128)(2,1)S(1)}, bf16[304,768]{1,0:T(8,128)(2,1)S(1)}, u32[]{:S(2)}, u32[]{:S(2)}) collective-permute-start(bf16[304,768]{1,0:T(8,128)(2,1)S(1)} %prepare_own.1.refs_1_), channel_id=1, source_target_pairs={{0,4},{1,5},{2,3},{3,2},{4,0},{5,1},{6,7},{7,6},{8,12},{9,13},{10,... | collective-permute-start | bytes 1400840 | tf_op jit(solution)/shard_map/ppermute | solution.py:59
  6.6 2.6 collective-permute-start
  9.2 4.0 %collective-permute-done.1.refs_3_ = bf16[304,768]{1,0:T(8,128)(2,1)S(1)} collective-permute-done((bf16[304,768]{1,0:T(8,128)(2,1)S(1)}, bf16[304,768]{1,0:T(8,128)(2,1)S(1)}, u32[]{:S(2)}, u32[]{:S(2)}) %collective-permute-start.1) | collective-permute-done | bytes 466976 | tf_op jit(solution)/shard_map/ppermute | solution.py:59
  13.1 5.7 %collective-permute-done.refs_2_ = bf16[304,768]{1,0:T(8,128)(2,1)S(1)} collective-permute-done((bf16[304,768]{1,0:T(8,128)(2,1)S(1)}, bf16[304,768]{1,0:T(8,128)(2,1)S(1)}, u32[]{:S(2)}, u32[]{:S(2)}) %collective-permute-start) | collective-permute-done | bytes 466976 | tf_op jit(solution)/shard_map/ppermute | solution.py:59
  21.5 5.0 %collective-permute-start.5 = (bf16[304,768]{1,0:T(8,128)(2,1)S(1)}, bf16[304,768]{1,0:T(8,128)(2,1)S(1)}, u32[]{:S(2)}, u32[]{:S(2)}) collective-permute-start(bf16[304,768]{1,0:T(8,128)(2,1)S(1)} %get-tuple-element.57.refs_1_), channel_id=1, source_target_pairs={{0,8},{1,9},{2,10},{3,11},{4,12},{5,13},{6,14},{7,15},{8,0},{9,1},... | collective-permute-start | bytes 1400840 | tf_op jit(solution)/shard_map/ppermute | solution.py:59
  26.5 6.7 %collective-permute-done.2.refs_5_.refs_3_.refs_2_ = bf16[2,304,768]{2,1,0:T(8,128)(2,1)S(1)} collective-permute-done((bf16[2,304,768]{2,1,0:T(8,128)(2,1)S(1)}, bf16[2,304,768]{2,1,0:T(8,128)(2,1)S(1)}, u32[]{:S(2)}, u32[]{:S(2)}) %collective-permute-start.2) | collective-permute-done | bytes 933920 | tf_op jit(solution)/shard_map/ppermute | solution.py:59
  33.1 3.4 %collective-permute-start.6 = (bf16[16,768]{1,0:T(8,128)(2,1)S(1)}, bf16[16,768]{1,0:T(8,128)(2,1)S(1)}, u32[]{:S(2)}, u32[]{:S(2)}) collective-permute-start(bf16[16,768]{1,0:T(8,128)(2,1)S(1)} %get-tuple-element.58), channel_id=1, source_target_pairs={{0,16},{1,17},{2,18},{3,19},{4,20},{5,21},{6,22},{7,23},{8,24},{9,... | collective-permute-start | bytes 73736 | tf_op jit(solution)/shard_map/ppermute | solution.py:59
  36.5 0.9 collective-permute-start.9
  37.5 0.9 collective-permute-done.6.refs_4_
  39.1 1.6 collective-permute-start.7
  41.2 8.2 %collective-permute-done.9.refs_4_ = bf16[304,768]{1,0:T(8,128)(2,1)S(1)} collective-permute-done((bf16[304,768]{1,0:T(8,128)(2,1)S(1)}, bf16[304,768]{1,0:T(8,128)(2,1)S(1)}, u32[]{:S(2)}, u32[]{:S(2)}) %collective-permute-start.9) | collective-permute-done | bytes 466976 | tf_op jit(solution)/shard_map/ppermute | solution.py:59
  49.3 3.1 %collective-permute-done.10.refs_5_.refs_1_ = bf16[288,768]{1,0:T(8,128)(2,1)S(1)} collective-permute-done((bf16[288,768]{1,0:T(8,128)(2,1)S(1)}, bf16[288,768]{1,0:T(8,128)(2,1)S(1)}, u32[]{:S(2)}, u32[]{:S(2)}) %collective-permute-start.10) | collective-permute-done | bytes 442400 | tf_op jit(solution)/shard_map/ppermute | solution.py:59
  53.2 0.8 collective-permute-start.11
  54.0 1.5 collective-permute-start.14
  55.5 11.6 %collective-permute-done.14.refs_3_ = bf16[288,768]{1,0:T(8,128)(2,1)S(1)} collective-permute-done((bf16[288,768]{1,0:T(8,128)(2,1)S(1)}, bf16[288,768]{1,0:T(8,128)(2,1)S(1)}, u32[]{:S(2)}, u32[]{:S(2)}) %collective-permute-start.14) | collective-permute-done | bytes 442400 | tf_op jit(solution)/shard_map/ppermute | solution.py:59
  67.1 1.4 after_four.1.refs_14_.refs_9_
  68.5 1.4 collective-permute-start.15
  69.9 1.8 collective-permute-done.11.refs_2_.refs_7_.refs_6_
  72.1 3.3 %collective-permute-done.13.refs_4_.refs_9_.refs_8_ = bf16[2,304,768]{2,1,0:T(8,128)(2,1)S(1)} collective-permute-done((bf16[2,304,768]{2,1,0:T(8,128)(2,1)S(1)}, bf16[2,304,768]{2,1,0:T(8,128)(2,1)S(1)}, u32[]{:S(2)}, u32[]{:S(2)}) %collective-permute-start.13) | collective-permute-done | bytes 933920 | tf_op jit(solution)/shard_map/ppermute | solution.py:59
  75.4 0.9 read_vectors.1
  77.1 15.8 %attend.1 = (bf16[2304,1024]{1,0:T(8,128)(2,1)}, bf16[1024,768]{1,0:T(8,128)(2,1)}, f32[12,1024]{1,0:T(8,128)}) custom-call(s32[8]{0:T(128)} %copy-done.31, s32[4]{0:T(128)} %refs_1_.3, bf16[2,304,768]{2,1,0:T(8,128)(2,1)} %copy-done.10, bf16[2,304,768]{2,1,0:T(8,128)(2,1)} %copy-done.3, bf16[2,304,768]{2,1,0:T(8,128)(2,1)} %copy-done.4, ...), custom_call_target="tpu_custom_call" | custom-call | flops 4429185024 | bytes 20971520 | tf_op jit(solution)/shard_map/attend/pallas_call | solution.py:258
  93.2 3.7 %collective-permute-done.17.refs_12_ = bf16[2,2,288,768]{3,2,1,0:T(8,128)(2,1)S(1)} collective-permute-done((bf16[2,2,288,768]{3,2,1,0:T(8,128)(2,1)}, bf16[2,2,288,768]{3,2,1,0:T(8,128)(2,1)S(1)}, u32[]{:S(2)}, u32[]{:S(2)}) %collective-permute-start.17) | collective-permute-done | bytes 1769504 | tf_op jit(solution)/shard_map/ppermute | solution.py:59
  97.0 1.2 copy-done.45
  98.2 60.5 %middle.1 = (bf16[1024,768]{1,0:T(8,128)(2,1)}, f32[1024,768]{1,0:T(8,128)}, bf16[768,1024]{1,0:T(8,128)(2,1)}, f32[11,3072]{1,0:T(8,128)}, bf16[2,2,288,768]{3,...) custom-call(s32[8]{0:T(128)} %copy-done.31, ...), custom_call_target="tpu_custom_call" | custom-call | flops 32614907904 | bytes 62914560 | tf_op jit(solution)/shard_map/middle/pallas_call | solution.py:258
  159.4 4.5 %collective-permute-done.19.refs_1_ = bf16[2,1,288,768]{3,2,1,0:T(8,128)(2,1)S(1)} collective-permute-done((bf16[2,1,288,768]{3,2,1,0:T(8,128)(2,1)}, bf16[2,1,288,768]{3,2,1,0:T(8,128)(2,1)S(1)}, u32[]{:S(2)}, u32[]{:S(2)}) %collective-permute-start.19) | collective-permute-done | bytes 884768 | tf_op jit(solution)/shard_map/ppermute | solution.py:59
  163.9 1.2 copy-done.28
  165.3 0.8 collective-permute-start.23
  166.2 1.7 add_pieces.7.refs_6_
  167.9 1.3 collective-permute-start.21
  169.2 11.7 %attend_back.1.refs_3_.refs_9_ = bf16[2304,1024]{1,0:T(8,128)(2,1)S(1)} custom-call(s32[8]{0:T(128)S(1)} %copy-done.32, s32[4]{0:T(128)S(1)} %copy-done.38, bf16[2304,1024]{1,0:T(8,128)(2,1)S(1)} %copy-done.9, bf16[768,1024]{1,0:T(8,128)(2,1)S(1)} %copy-done.23, f32[12,1024]{1,0:T(8,128)S(1)} %copy-done.34, s32[1,1024]{1,0:T(1,128)S(1)} %bitcast.19, ...), custom_call_target="tpu_custom_call" | custom-call | flops 2013265920 | bytes 26214400 | tf_op jit(solution)/shard_map/attend_back/pallas_call | solution.py:258
  181.2 1.9 copy-done
  183.7 1.2 collective-permute-start.24
  184.9 11.0 %mixed_grad.1 = (bf16[2,1,304,768]{3,2,1,0:T(8,128)(2,1)}, bf16[2,1,304,768]{3,2,1,0:T(8,128)(2,1)}, bf16[2,1,304,768]{3,2,1,0:T(8,128)(2,1)}, bf16[2,1,304,768]{3,2,1,0:T(8,128)(2,1)}) custom-call(s32[8]{0:T(128)} %copy-done.31, bf16[2,304,768]{2,1,0:T(8,128)(2,1)} %copy-done.10, bf16[2,304,768]{2,1,0:T(8,128)(2,1)} %copy-done.3, ...), custom_call_target="tpu_custom_call" | custom-call | flops 3623878656 | bytes 12582912 | tf_op jit(solution)/shard_map/mixed_grad/pallas_call | solution.py:258
  195.9 0.9 collective-permute-done.24.refs_1_.refs_8_
  196.8 0.8 copy-done.20
  198.1 2.2 collective-permute-done.25.refs_1_
  200.3 1.2 add_pieces.9.refs_3_
  201.4 1.2 collective-permute-start.27
  202.6 1.5 collective-permute-done.20.refs_1_.refs_2_.refs_6_
  204.1 2.4 add_pieces.10.refs_11_
  206.6 1.2 collective-permute-start.29
  207.8 11.5 %input_back.1 = (f32[1024,768]{1,0:T(8,128)}, f32[8,128]{1,0:T(8,128)}) custom-call(s32[8]{0:T(128)} %copy-done.31, bf16[2,304,768]{2,1,0:T(8,128)(2,1)} %copy-done.10, bf16[2,304,768]{2,1,0:T(8,128)(2,1)} %copy-done.3, bf16[2,304,768]{2,1,0:T(8,128)(2,1)} %copy-done.4, bf16[2,304,768]{2,1,0:T(8,128)(2,1)} %copy-done.5, bf16[2,304,768]{2,1,0:T(8,128)(2,1)} %copy-done.6, ...), custom_call_target="tpu_custom_call" | custom-call | tf_op jit(solution)/shard_map/input_back/pallas_call | solution.py:258
  219.3 1.6 collective-permute-done.27.refs_2_.refs_3_
  221.0 1.2 copy-done.11
  222.9 1.4 add_pieces.11
  224.3 1.3 collective-permute-start.28
  225.6 2.0 far_sums.1
  227.6 0.9 copy-done.25
  228.5 3.0 %collective-permute-start.31 = (bf16[288,768]{1,0:T(8,128)(2,1)S(1)}, bf16[288,768]{1,0:T(8,128)(2,1)S(1)}, u32[]{:S(2)}, u32[]{:S(2)}) collective-permute-start(bf16[288,768]{1,0:T(8,128)(2,1)S(1)} %get-tuple-element.88), channel_id=1, source_target_pairs={{0,16},{1,17},{2,18},{3,19},{4,20},{5,21},{6,22},{7,23},{8,24},{9,... | collective-permute-start | bytes 1327112 | tf_op jit(solution)/shard_map/ppermute | solution.py:59
  231.5 1.4 collective-permute-done.28.refs_4_
  232.9 1.8 near_sums.1
  234.8 1.9 collective-permute-start.30
  236.6 13.8 %collective-permute-done.31.refs_0_ = bf16[288,768]{1,0:T(8,128)(2,1)S(1)} collective-permute-done((bf16[288,768]{1,0:T(8,128)(2,1)S(1)}, bf16[288,768]{1,0:T(8,128)(2,1)S(1)}, u32[]{:S(2)}, u32[]{:S(2)}) %collective-permute-start.31) | collective-permute-done | bytes 442400 | tf_op jit(solution)/shard_map/ppermute | solution.py:59
  251.2 2.2 collective-permute-done.30.refs_4_
  253.4 1.0 copy-done.30
  254.4 0.9 last_sums.1
  255.3 0.9 copy-done.39
  256.9 2.5 collective-permute-start.32
  259.4 2.0 collective-permute-done.33
  262.6 4.5 %collective-permute-done.32.refs_1_ = bf16[288,768]{1,0:T(8,128)(2,1)S(1)} collective-permute-done((bf16[288,768]{1,0:T(8,128)(2,1)S(1)}, bf16[288,768]{1,0:T(8,128)(2,1)S(1)}, u32[]{:S(2)}, u32[]{:S(2)}) %collective-permute-start.32) | collective-permute-done | bytes 442400 | tf_op jit(solution)/shard_map/ppermute | solution.py:59
  267.2 0.8 copy-done.46
  267.9 8.5 %owner_step.1 = (f32[288,768]{1,0:T(8,128)}, f32[768,768]{1,0:T(8,128)}, f32[288,288]{1,0:T(8,128)}, f32[288,768]{1,0:T(8,128)}, f32[288,768]{1,0:T(8,128)}, /*index=5*/bf16[288,768]{1,0:T(8,128)(2,1)}) custom-call(f32[288,768]{1,0:T(8,128)} %copy-done.39, bf16[288,768]{1,0:T(8,128)(2,1)} %copy-done.46, f32[768,768]{1,0:T(8,128)} %refs_2_.1, ...), custom_call_target="tpu_custom_call" | custom-call | flops 2802843648 | bytes 15728640 | tf_op jit(solution)/shard_map/owner_step/pallas_call | solution.py:258
  (130 shorter events, 12.6 us)
Async XLA Ops:
  1.5 73.9 %copy-start.31 = (s32[8]{0:T(128)}, s32[8]{0:T(128)S(1)}, u32[]{:S(2)}) copy-start(s32[8]{0:T(128)S(1)} %stack.35.refs_0_) | copy-start | bytes 100
  3.5 9.6 %collective-permute-start.1 = (bf16[304,768]{1,0:T(8,128)(2,1)S(1)}, bf16[304,768]{1,0:T(8,128)(2,1)S(1)}, u32[]{:S(2)}, u32[]{:S(2)}) collective-permute-start(bf16[304,768]{1,0:T(8,128)(2,1)S(1)} %prepare_own.1.refs_1_), channel_id=1, source_target_pairs={{0,4},{1,5},{2,3},{3,2},{4,0},{5,1},{6,7},{7,6},{8,12},{9,13},{10,... | collective-permute-start | bytes 1400840 | tf_op jit(solution)/shard_map/ppermute | solution.py:59
  6.6 12.2 %collective-permute-start = (bf16[304,768]{1,0:T(8,128)(2,1)S(1)}, bf16[304,768]{1,0:T(8,128)(2,1)S(1)}, u32[]{:S(2)}, u32[]{:S(2)}) collective-permute-start(bf16[304,768]{1,0:T(8,128)(2,1)S(1)} %prepare_own.1.refs_1_), channel_id=1, source_target_pairs={{0,16},{1,17},{2,18},{3,19},{4,20},{5,21},{6,22},{7,23},{8,0},{9,1... | collective-permute-start | bytes 1400840 | tf_op jit(solution)/shard_map/ppermute | solution.py:59
  19.5 33.0 %copy-start.10 = (bf16[2,304,768]{2,1,0:T(8,128)(2,1)}, bf16[2,304,768]{2,1,0:T(8,128)(2,1)S(1)}, u32[]{:S(2)}) copy-start(bf16[2,304,768]{2,1,0:T(8,128)(2,1)S(1)} %get-tuple-element.56.refs_2_.refs_1_) | copy-start | bytes 2801668
  19.5 13.6 %collective-permute-start.2 = (bf16[2,304,768]{2,1,0:T(8,128)(2,1)S(1)}, bf16[2,304,768]{2,1,0:T(8,128)(2,1)S(1)}, u32[]{:S(2)}, u32[]{:S(2)}) collective-permute-start(bf16[2,304,768]{2,1,0:T(8,128)(2,1)S(1)} %get-tuple-element.56.refs_2_.refs_1_), channel_id=1, source_target_pairs={{0,1},{1,0},{2,6},{3,7},{4,5},{5,4},{6,2},{7,3},{8,9},{9,8},{10,14... | collective-permute-start | bytes 2801672 | tf_op jit(solution)/shard_map/ppermute | solution.py:59
  20.1 18.3 %collective-permute-start.3 = (bf16[2,304,768]{2,1,0:T(8,128)(2,1)S(1)}, bf16[2,304,768]{2,1,0:T(8,128)(2,1)S(1)}, u32[]{:S(2)}, u32[]{:S(2)}) collective-permute-start(bf16[2,304,768]{2,1,0:T(8,128)(2,1)S(1)} %get-tuple-element.56.refs_2_.refs_1_), channel_id=1, source_target_pairs={{0,2},{1,3},{2,0},{3,1},{4,6},{5,7},{6,4},{7,5},{8,10},{9,11},{10,... | collective-permute-start | bytes 2801672 | tf_op jit(solution)/shard_map/ppermute | solution.py:59
  20.8 15.7 %collective-permute-start.8 = (bf16[304,768]{1,0:T(8,128)(2,1)S(1)}, bf16[304,768]{1,0:T(8,128)(2,1)S(1)}, u32[]{:S(2)}, u32[]{:S(2)}) collective-permute-start(bf16[304,768]{1,0:T(8,128)(2,1)S(1)} %prepare_own.1.refs_1_), channel_id=1, source_target_pairs={{0,0},{1,1},{2,2},{3,3},{4,4},{5,5},{6,6},{7,7},{8,16},{9,17},{10,... | collective-permute-start | bytes 1400840 | tf_op jit(solution)/shard_map/ppermute | solution.py:59
  21.5 16.9 %collective-permute-start.5 = (bf16[304,768]{1,0:T(8,128)(2,1)S(1)}, bf16[304,768]{1,0:T(8,128)(2,1)S(1)}, u32[]{:S(2)}, u32[]{:S(2)}) collective-permute-start(bf16[304,768]{1,0:T(8,128)(2,1)S(1)} %get-tuple-element.57.refs_1_), channel_id=1, source_target_pairs={{0,8},{1,9},{2,10},{3,11},{4,12},{5,13},{6,14},{7,15},{8,0},{9,1},... | collective-permute-start | bytes 1400840 | tf_op jit(solution)/shard_map/ppermute | solution.py:59
  33.1 20.0 %copy-start.3 = (bf16[2,304,768]{2,1,0:T(8,128)(2,1)}, bf16[2,304,768]{2,1,0:T(8,128)(2,1)S(1)}, u32[]{:S(2)}) copy-start(bf16[2,304,768]{2,1,0:T(8,128)(2,1)S(1)} %collective-permute-done.2.refs_5_.refs_3_.refs_2_) | copy-start | bytes 2801668
  33.1 19.3 %collective-permute-start.4 = (bf16[2,304,768]{2,1,0:T(8,128)(2,1)S(1)}, bf16[2,304,768]{2,1,0:T(8,128)(2,1)S(1)}, u32[]{:S(2)}, u32[]{:S(2)}) collective-permute-start(bf16[2,304,768]{2,1,0:T(8,128)(2,1)S(1)} %collective-permute-done.2.refs_5_.refs_3_.refs_2_), channel_id=1, source_target_pairs={{0,2},{1,3},{2,0},{3,1},{4,6},{5,7},{6,4},{7,5},{8,10},{9,11},{10,... | collective-permute-start | bytes 2801672 | tf_op jit(solution)/shard_map/ppermute | solution.py:59
  33.1 5.3 %collective-permute-start.6 = (bf16[16,768]{1,0:T(8,128)(2,1)S(1)}, bf16[16,768]{1,0:T(8,128)(2,1)S(1)}, u32[]{:S(2)}, u32[]{:S(2)}) collective-permute-start(bf16[16,768]{1,0:T(8,128)(2,1)S(1)} %get-tuple-element.58), channel_id=1, source_target_pairs={{0,16},{1,17},{2,18},{3,19},{4,20},{5,21},{6,22},{7,23},{8,24},{9,... | collective-permute-start | bytes 73736 | tf_op jit(solution)/shard_map/ppermute | solution.py:59
  36.5 12.8 %collective-permute-start.9 = (bf16[304,768]{1,0:T(8,128)(2,1)S(1)}, bf16[304,768]{1,0:T(8,128)(2,1)S(1)}, u32[]{:S(2)}, u32[]{:S(2)}) collective-permute-start(bf16[304,768]{1,0:T(8,128)(2,1)S(1)} %collective-permute-done.8.refs_3_), channel_id=1, source_target_pairs={{0,8},{1,9},{2,10},{3,11},{4,12},{5,13},{6,14},{7,15},{8,0},{9,1},... | collective-permute-start | bytes 1400840 | tf_op jit(solution)/shard_map/ppermute | solution.py:59
  38.4 14.7 %copy-start.4 = (bf16[2,304,768]{2,1,0:T(8,128)(2,1)}, bf16[2,304,768]{2,1,0:T(8,128)(2,1)S(1)}, u32[]{:S(2)}) copy-start(bf16[2,304,768]{2,1,0:T(8,128)(2,1)S(1)} %collective-permute-done.3.refs_6_.refs_4_.refs_3_) | copy-start | bytes 2801668
  39.1 13.4 %collective-permute-start.7 = (bf16[304,768]{1,0:T(8,128)(2,1)S(1)}, bf16[304,768]{1,0:T(8,128)(2,1)S(1)}, u32[]{:S(2)}, u32[]{:S(2)}) collective-permute-start(bf16[304,768]{1,0:T(8,128)(2,1)S(1)} %get-tuple-element.59.refs_1_), channel_id=1, source_target_pairs={{0,4},{1,5},{2,3},{3,2},{4,0},{5,1},{6,7},{7,6},{8,12},{9,13},{10,... | collective-permute-start | bytes 1400840 | tf_op jit(solution)/shard_map/ppermute | solution.py:59
  40.7 11.8 %collective-permute-start.10 = (bf16[288,768]{1,0:T(8,128)(2,1)S(1)}, bf16[288,768]{1,0:T(8,128)(2,1)S(1)}, u32[]{:S(2)}, u32[]{:S(2)}) collective-permute-start(bf16[288,768]{1,0:T(8,128)(2,1)S(1)} %get-tuple-element.60.refs_0_), channel_id=1, source_target_pairs={{0,4},{1,5},{2,3},{3,2},{4,0},{5,1},{6,7},{7,6},{8,12},{9,13},{10,... | collective-permute-start | bytes 1327112 | tf_op jit(solution)/shard_map/ppermute | solution.py:59
  52.5 16.0 %copy-start.5 = (bf16[2,304,768]{2,1,0:T(8,128)(2,1)}, bf16[2,304,768]{2,1,0:T(8,128)(2,1)S(1)}, u32[]{:S(2)}) copy-start(bf16[2,304,768]{2,1,0:T(8,128)(2,1)S(1)} %collective-permute-done.4.refs_6_.refs_5_.refs_4_) | copy-start | bytes 2801668
  53.2 22.3 %copy-start.6 = (bf16[2,304,768]{2,1,0:T(8,128)(2,1)}, bf16[2,304,768]{2,1,0:T(8,128)(2,1)S(1)}, u32[]{:S(2)}) copy-start(bf16[2,304,768]{2,1,0:T(8,128)(2,1)S(1)} %get-tuple-element.61.refs_1_.refs_6_.refs_5_) | copy-start | bytes 2801668
  53.2 13.9 %collective-permute-start.12 = (bf16[2,304,768]{2,1,0:T(8,128)(2,1)S(1)}, bf16[2,304,768]{2,1,0:T(8,128)(2,1)S(1)}, u32[]{:S(2)}, u32[]{:S(2)}) collective-permute-start(bf16[2,304,768]{2,1,0:T(8,128)(2,1)S(1)} %get-tuple-element.61.refs_1_.refs_6_.refs_5_), channel_id=1, source_target_pairs={{0,2},{1,3},{2,0},{3,1},{4,6},{5,7},{6,4},{7,5},{8,10},{9,11},{10,... | collective-permute-start | bytes 2801672 | tf_op jit(solution)/shard_map/ppermute | solution.py:59
  53.2 18.4 %collective-permute-start.11 = (bf16[2,304,768]{2,1,0:T(8,128)(2,1)S(1)}, bf16[2,304,768]{2,1,0:T(8,128)(2,1)S(1)}, u32[]{:S(2)}, u32[]{:S(2)}) collective-permute-start(bf16[2,304,768]{2,1,0:T(8,128)(2,1)S(1)} %get-tuple-element.61.refs_1_.refs_6_.refs_5_), channel_id=1, source_target_pairs={{0,1},{1,0},{2,6},{3,7},{4,5},{5,4},{6,2},{7,3},{8,9},{9,8},{10,14... | collective-permute-start | bytes 2801672 | tf_op jit(solution)/shard_map/ppermute | solution.py:59
  54.0 13.1 %collective-permute-start.14 = (bf16[288,768]{1,0:T(8,128)(2,1)S(1)}, bf16[288,768]{1,0:T(8,128)(2,1)S(1)}, u32[]{:S(2)}, u32[]{:S(2)}) collective-permute-start(bf16[288,768]{1,0:T(8,128)(2,1)S(1)} %get-tuple-element.62.refs_2_), channel_id=1, source_target_pairs={{0,4},{1,5},{2,3},{3,2},{4,0},{5,1},{6,7},{7,6},{8,12},{9,13},{10,... | collective-permute-start | bytes 1327112 | tf_op jit(solution)/shard_map/ppermute | solution.py:59
  67.1 8.3 %copy-start.2 = (bf16[2,304,768]{2,1,0:T(8,128)(2,1)}, bf16[2,304,768]{2,1,0:T(8,128)(2,1)S(1)}, u32[]{:S(2)}) copy-start(bf16[2,304,768]{2,1,0:T(8,128)(2,1)S(1)} %collective-permute-done.12.refs_4_.refs_3_.refs_8_.refs_7_) | copy-start | bytes 2801668
  68.5 24.5 %collective-permute-start.15 = (bf16[2,2,288,768]{3,2,1,0:T(8,128)(2,1)}, bf16[2,2,288,768]{3,2,1,0:T(8,128)(2,1)}, u32[]{:S(2)}, u32[]{:S(2)}) collective-permute-start(bf16[2,2,288,768]{3,2,1,0:T(8,128)(2,1)} %after_four.1.refs_14_.refs_9_), channel_id=1, source_target_pairs={{0,1},{1,0},{2,6},{3,7},{4,5},{5,4},{6,2},{7,3},{8,9},{9,8},{10,14... | collective-permute-start | bytes 5308424 | tf_op jit(solution)/shard_map/ppermute | solution.py:59
  71.6 4.8 %copy-start.7 = (bf16[2,304,768]{2,1,0:T(8,128)(2,1)}, bf16[2,304,768]{2,1,0:T(8,128)(2,1)S(1)}, u32[]{:S(2)}) copy-start(bf16[2,304,768]{2,1,0:T(8,128)(2,1)S(1)} %collective-permute-done.11.refs_2_.refs_7_.refs_6_) | copy-start | bytes 2801668
  71.6 3.8 %collective-permute-start.13 = (bf16[2,304,768]{2,1,0:T(8,128)(2,1)S(1)}, bf16[2,304,768]{2,1,0:T(8,128)(2,1)S(1)}, u32[]{:S(2)}, u32[]{:S(2)}) collective-permute-start(bf16[2,304,768]{2,1,0:T(8,128)(2,1)S(1)} %collective-permute-done.11.refs_2_.refs_7_.refs_6_), channel_id=1, source_target_pairs={{0,2},{1,3},{2,0},{3,1},{4,6},{5,7},{6,4},{7,5},{8,10},{9,11},{10,... | collective-permute-start | bytes 2801672 | tf_op jit(solution)/shard_map/ppermute | solution.py:59
  71.6 21.6 %collective-permute-start.16 = (bf16[2,2,288,768]{3,2,1,0:T(8,128)(2,1)}, bf16[2,2,288,768]{3,2,1,0:T(8,128)(2,1)}, u32[]{:S(2)}, u32[]{:S(2)}) collective-permute-start(bf16[2,2,288,768]{3,2,1,0:T(8,128)(2,1)} %after_four.1.refs_14_.refs_9_), channel_id=1, source_target_pairs={{0,2},{1,3},{2,0},{3,1},{4,6},{5,7},{6,4},{7,5},{8,10},{9,11},{10,... | collective-permute-start | bytes 5308424 | tf_op jit(solution)/shard_map/ppermute | solution.py:59
  93.0 4.0 %collective-permute-start.17 = (bf16[2,2,288,768]{3,2,1,0:T(8,128)(2,1)}, bf16[2,2,288,768]{3,2,1,0:T(8,128)(2,1)S(1)}, u32[]{:S(2)}, u32[]{:S(2)}) collective-permute-start(bf16[2,2,288,768]{3,2,1,0:T(8,128)(2,1)} %hold.4.refs_10_), channel_id=1, source_target_pairs={{0,2},{1,3},{2,0},{3,1},{4,6},{5,7},{6,4},{7,5},{8,10},{9,11},{10,... | collective-permute-start | bytes 5308424 | tf_op jit(solution)/shard_map/ppermute | solution.py:59
  158.7 7.5 %copy-start.19 = (bf16[2,2,288,768]{3,2,1,0:T(8,128)(2,1)S(1)}, bf16[2,2,288,768]{3,2,1,0:T(8,128)(2,1)}, u32[]{:S(2)}) copy-start(bf16[2,2,288,768]{3,2,1,0:T(8,128)(2,1)} %get-tuple-element.68.refs_0_) | copy-start | bytes 5308420
  158.7 7.4 %collective-permute-start.18 = (bf16[2,2,288,768]{3,2,1,0:T(8,128)(2,1)}, bf16[2,2,288,768]{3,2,1,0:T(8,128)(2,1)S(1)}, u32[]{:S(2)}, u32[]{:S(2)}) collective-permute-start(bf16[2,2,288,768]{3,2,1,0:T(8,128)(2,1)} %get-tuple-element.69), channel_id=1, source_target_pairs={{0,2},{1,3},{2,0},{3,1},{4,6},{5,7},{6,4},{7,5},{8,10},{9,11},{10,... | collective-permute-start | bytes 5308424 | tf_op jit(solution)/shard_map/ppermute | solution.py:59
  158.9 5.0 %collective-permute-start.19 = (bf16[2,1,288,768]{3,2,1,0:T(8,128)(2,1)}, bf16[2,1,288,768]{3,2,1,0:T(8,128)(2,1)S(1)}, u32[]{:S(2)}, u32[]{:S(2)}) collective-permute-start(bf16[2,1,288,768]{3,2,1,0:T(8,128)(2,1)} %get-tuple-element.71), channel_id=1, source_target_pairs={{0,2},{1,3},{2,0},{3,1},{4,6},{5,7},{6,4},{7,5},{8,10},{9,11},{10,... | collective-permute-start | bytes 2654216 | tf_op jit(solution)/shard_map/ppermute | solution.py:59
  159.3 21.7 %collective-permute-start.22 = (bf16[2,1,288,768]{3,2,1,0:T(8,128)(2,1)}, bf16[2,1,288,768]{3,2,1,0:T(8,128)(2,1)S(1)}, u32[]{:S(2)}, u32[]{:S(2)}) collective-permute-start(bf16[2,1,288,768]{3,2,1,0:T(8,128)(2,1)} %get-tuple-element.77), channel_id=1, source_target_pairs={{0,2},{1,3},{2,0},{3,1},{4,6},{5,7},{6,4},{7,5},{8,10},{9,11},{10,... | collective-permute-start | bytes 2654216 | tf_op jit(solution)/shard_map/ppermute | solution.py:59
  165.1 4.1 %copy-start.23 = (bf16[768,1024]{1,0:T(8,128)(2,1)S(1)}, bf16[768,1024]{1,0:T(8,128)(2,1)}, u32[]{:S(2)}) copy-start(bf16[768,1024]{1,0:T(8,128)(2,1)} %get-tuple-element.66.refs_3_) | copy-start | bytes 4718596
  165.3 15.6 %collective-permute-start.23 = (bf16[2,1,288,768]{3,2,1,0:T(8,128)(2,1)S(1)}, bf16[2,1,288,768]{3,2,1,0:T(8,128)(2,1)S(1)}, u32[]{:S(2)}, u32[]{:S(2)}) collective-permute-start(bf16[2,1,288,768]{3,2,1,0:T(8,128)(2,1)S(1)} %add_pieces.6.refs_2_), channel_id=1, source_target_pairs={{0,1},{1,0},{2,6},{3,7},{4,5},{5,4},{6,2},{7,3},{8,9},{9,8},{10,14... | collective-permute-start | bytes 2654216 | tf_op jit(solution)/shard_map/ppermute | solution.py:59
  166.2 3.1 %copy-start.9 = (bf16[2304,1024]{1,0:T(8,128)(2,1)S(1)}, bf16[2304,1024]{1,0:T(8,128)(2,1)}, u32[]{:S(2)}) copy-start(bf16[2304,1024]{1,0:T(8,128)(2,1)} %get-tuple-element.65.refs_2_) | copy-start | bytes 14155780
  166.2 3.1 %copy-start.32 = (s32[8]{0:T(128)S(1)}, s32[8]{0:T(128)}, u32[]{:S(2)}) copy-start(s32[8]{0:T(128)} %copy-done.31) | copy-start | bytes 100
  166.2 3.1 %copy-start.34 = (f32[12,1024]{1,0:T(8,128)S(1)}, f32[12,1024]{1,0:T(8,128)}, u32[]{:S(2)}) copy-start(f32[12,1024]{1,0:T(8,128)} %get-tuple-element.67.refs_4_) | copy-start | bytes 147460
  166.2 3.1 %copy-start.37 = (s32[1024]{0:T(1024)S(1)}, s32[1024]{0:T(1024)}, u32[]{:S(2)}) copy-start(s32[1024]{0:T(1024)} %param.19) | copy-start | bytes 12292
  166.2 3.0 %copy-start.38 = (s32[4]{0:T(128)S(1)}, s32[4]{0:T(128)}, u32[]{:S(2)}) copy-start(s32[4]{0:T(128)} %refs_1_.3) | copy-start | bytes 52
  167.9 34.8 %collective-permute-start.21 = (bf16[2,2,288,768]{3,2,1,0:T(8,128)(2,1)}, bf16[2,2,288,768]{3,2,1,0:T(8,128)(2,1)}, u32[]{:S(2)}, u32[]{:S(2)}) collective-permute-start(bf16[2,2,288,768]{3,2,1,0:T(8,128)(2,1)} %add_pieces.7.refs_6_), channel_id=1, source_target_pairs={{0,1},{1,0},{2,6},{3,7},{4,5},{5,4},{6,2},{7,3},{8,9},{9,8},{10,14... | collective-permute-start | bytes 5308424 | tf_op jit(solution)/shard_map/ppermute | solution.py:59
  169.2 11.8 %copy-start.13 = (bf16[2,1,288,768]{3,2,1,0:T(8,128)(2,1)S(1)}, bf16[2,1,288,768]{3,2,1,0:T(8,128)(2,1)}, u32[]{:S(2)}) copy-start(bf16[2,1,288,768]{3,2,1,0:T(8,128)(2,1)} %get-tuple-element.76.refs_0_.refs_5_) | copy-start | bytes 2654212
  183.7 13.1 %collective-permute-start.24 = (bf16[1,1,288,768]{3,2,1,0:T(8,128)(2,1)S(1)}, bf16[1,1,288,768]{3,2,1,0:T(8,128)(2,1)S(1)}, u32[]{:S(2)}, u32[]{:S(2)}) collective-permute-start(bf16[1,1,288,768]{3,2,1,0:T(8,128)(2,1)S(1)} %add_pieces.8.refs_14_), channel_id=1, source_target_pairs={{0,4},{1,5},{2,3},{3,2},{4,0},{5,1},{6,7},{7,6},{8,12},{9,13},{10,... | collective-permute-start | bytes 1327112 | tf_op jit(solution)/shard_map/ppermute | solution.py:59
  195.9 4.4 %copy-start.24 = (bf16[2,1,304,768]{3,2,1,0:T(8,128)(2,1)S(1)}, bf16[2,1,304,768]{3,2,1,0:T(8,128)(2,1)}, u32[]{:S(2)}) copy-start(bf16[2,1,304,768]{3,2,1,0:T(8,128)(2,1)} %get-tuple-element.78.refs_0_) | copy-start | bytes 2801668
  197.6 2.7 collective-permute-start.25
  197.6 6.6 %collective-permute-start.20 = (bf16[2,2,288,768]{3,2,1,0:T(8,128)(2,1)}, bf16[2,2,288,768]{3,2,1,0:T(8,128)(2,1)S(1)}, u32[]{:S(2)}, u32[]{:S(2)}) collective-permute-start(bf16[2,2,288,768]{3,2,1,0:T(8,128)(2,1)} %get-tuple-element.74), channel_id=1, source_target_pairs={{0,2},{1,3},{2,0},{3,1},{4,6},{5,7},{6,4},{7,5},{8,10},{9,11},{10,... | collective-permute-start | bytes 5308424 | tf_op jit(solution)/shard_map/ppermute | solution.py:59
  198.1 21.3 %collective-permute-start.26 = (bf16[2,1,304,768]{3,2,1,0:T(8,128)(2,1)}, bf16[2,1,304,768]{3,2,1,0:T(8,128)(2,1)}, u32[]{:S(2)}, u32[]{:S(2)}) collective-permute-start(bf16[2,1,304,768]{3,2,1,0:T(8,128)(2,1)} %get-tuple-element.82), channel_id=1, source_target_pairs={{0,2},{1,3},{2,0},{3,1},{4,6},{5,7},{6,4},{7,5},{8,10},{9,11},{10,... | collective-permute-start | bytes 2801672 | tf_op jit(solution)/shard_map/ppermute | solution.py:59
  201.4 19.5 %collective-permute-start.27 = (bf16[2,1,304,768]{3,2,1,0:T(8,128)(2,1)}, bf16[2,1,304,768]{3,2,1,0:T(8,128)(2,1)}, u32[]{:S(2)}, u32[]{:S(2)}) collective-permute-start(bf16[2,1,304,768]{3,2,1,0:T(8,128)(2,1)} %add_pieces.9.refs_3_), channel_id=1, source_target_pairs={{0,1},{1,0},{2,6},{3,7},{4,5},{5,4},{6,2},{7,3},{8,9},{9,8},{10,14... | collective-permute-start | bytes 2801672 | tf_op jit(solution)/shard_map/ppermute | solution.py:59
  206.6 19.0 %collective-permute-start.29 = (bf16[1,2,288,768]{3,2,1,0:T(8,128)(2,1)}, bf16[1,2,288,768]{3,2,1,0:T(8,128)(2,1)}, u32[]{:S(2)}, u32[]{:S(2)}) collective-permute-start(bf16[1,2,288,768]{3,2,1,0:T(8,128)(2,1)} %add_pieces.10.refs_11_), channel_id=1, source_target_pairs={{0,4},{1,5},{2,3},{3,2},{4,0},{5,1},{6,7},{7,6},{8,12},{9,13},{10,... | collective-permute-start | bytes 2654216 | tf_op jit(solution)/shard_map/ppermute | solution.py:59
  219.3 6.2 %copy-start.33 = (s32[8]{0:T(128)S(1)}, s32[8]{0:T(128)}, u32[]{:S(2)}) copy-start(s32[8]{0:T(128)} %copy-done.31) | copy-start | bytes 100
  222.9 2.7 copy-start.36
  224.2 8.7 %copy-start.12 = (bf16[2,1,304,768]{3,2,1,0:T(8,128)(2,1)S(1)}, bf16[2,1,304,768]{3,2,1,0:T(8,128)(2,1)}, u32[]{:S(2)}) copy-start(bf16[2,1,304,768]{3,2,1,0:T(8,128)(2,1)} %get-tuple-element.81.refs_0_.refs_1_) | copy-start | bytes 2801668
  224.2 8.7 %copy-start.14 = (bf16[2,1,288,768]{3,2,1,0:T(8,128)(2,1)S(1)}, bf16[2,1,288,768]{3,2,1,0:T(8,128)(2,1)}, u32[]{:S(2)}) copy-start(bf16[2,1,288,768]{3,2,1,0:T(8,128)(2,1)} %get-tuple-element.76.refs_0_.refs_5_) | copy-start | bytes 2654212
  224.2 8.7 %copy-start.16 = (bf16[2,1,288,768]{3,2,1,0:T(8,128)(2,1)S(1)}, bf16[2,1,288,768]{3,2,1,0:T(8,128)(2,1)}, u32[]{:S(2)}) copy-start(bf16[2,1,288,768]{3,2,1,0:T(8,128)(2,1)} %copy-done.15) | copy-start | bytes 2654212
  224.3 8.7 %copy-start.18 = (bf16[2,1,288,768]{3,2,1,0:T(8,128)(2,1)S(1)}, bf16[2,1,288,768]{3,2,1,0:T(8,128)(2,1)}, u32[]{:S(2)}) copy-start(bf16[2,1,288,768]{3,2,1,0:T(8,128)(2,1)} %copy-done.17) | copy-start | bytes 2654212
  224.3 8.7 %copy-start.21 = (bf16[1,1,288,768]{3,2,1,0:T(8,128)(2,1)S(1)}, bf16[1,1,288,768]{3,2,1,0:T(8,128)(2,1)}, u32[]{:S(2)}) copy-start(bf16[1,1,288,768]{3,2,1,0:T(8,128)(2,1)} %copy-done.20) | copy-start | bytes 1327108
  224.3 8.6 %collective-permute-start.28 = (bf16[1,1,304,768]{3,2,1,0:T(8,128)(2,1)S(1)}, bf16[1,1,304,768]{3,2,1,0:T(8,128)(2,1)S(1)}, u32[]{:S(2)}, u32[]{:S(2)}) collective-permute-start(bf16[1,1,304,768]{3,2,1,0:T(8,128)(2,1)S(1)} %add_pieces.11), channel_id=1, source_target_pairs={{0,4},{1,5},{2,3},{3,2},{4,0},{5,1},{6,7},{7,6},{8,12},{9,13},{10,... | collective-permute-start | bytes 1400840 | tf_op jit(solution)/shard_map/ppermute | solution.py:59
  228.5 22.0 %collective-permute-start.31 = (bf16[288,768]{1,0:T(8,128)(2,1)S(1)}, bf16[288,768]{1,0:T(8,128)(2,1)S(1)}, u32[]{:S(2)}, u32[]{:S(2)}) collective-permute-start(bf16[288,768]{1,0:T(8,128)(2,1)S(1)} %get-tuple-element.88), channel_id=1, source_target_pairs={{0,16},{1,17},{2,18},{3,19},{4,20},{5,21},{6,22},{7,23},{8,24},{9,... | collective-permute-start | bytes 1327112 | tf_op jit(solution)/shard_map/ppermute | solution.py:59
  234.7 18.7 %copy-start.26 = (f32[288,768]{1,0:T(8,128)S(1)}, f32[288,768]{1,0:T(8,128)}, u32[]{:S(2)}) copy-start(f32[288,768]{1,0:T(8,128)} %copy-done.25) | copy-start | bytes 2654212
  234.8 18.6 %collective-permute-start.30 = (bf16[304,768]{1,0:T(8,128)(2,1)S(1)}, bf16[304,768]{1,0:T(8,128)(2,1)S(1)}, u32[]{:S(2)}, u32[]{:S(2)}) collective-permute-start(bf16[304,768]{1,0:T(8,128)(2,1)S(1)} %get-tuple-element.87), channel_id=1, source_target_pairs={{0,8},{1,9},{2,10},{3,11},{4,12},{5,13},{6,14},{7,15},{8,0},{9,1},... | collective-permute-start | bytes 1400840 | tf_op jit(solution)/shard_map/ppermute | solution.py:59
  251.2 10.2 %copy-start.44 = (f32[336]{0:T(512)S(1)}, f32[336]{0:T(512)}, u32[]{:S(2)}) copy-start(f32[336]{0:T(512)} %param.30) | copy-start | bytes 4036
  251.2 10.2 %copy-start.43 = (f32[336]{0:T(512)S(1)}, f32[336]{0:T(512)}, u32[]{:S(2)}) copy-start(f32[336]{0:T(512)} %param.29) | copy-start | bytes 4036
  251.2 10.8 %copy-start.42 = (f32[336]{0:T(512)S(1)}, f32[336]{0:T(512)}, u32[]{:S(2)}) copy-start(f32[336]{0:T(512)} %param.31) | copy-start | bytes 4036
  256.2 5.2 %collective-permute-start.33 = (bf16[16,768]{1,0:T(8,128)(2,1)S(1)}, bf16[16,768]{1,0:T(8,128)(2,1)S(1)}, u32[]{:S(2)}, u32[]{:S(2)}) collective-permute-start(bf16[16,768]{1,0:T(8,128)(2,1)S(1)} %get-tuple-element.98), channel_id=1, source_target_pairs={{0,16},{1,17},{2,18},{3,19},{4,20},{5,21},{6,22},{7,23},{8,24},{9,... | collective-permute-start | bytes 73736 | tf_op jit(solution)/shard_map/ppermute | solution.py:59
  256.9 10.3 %collective-permute-start.32 = (bf16[288,768]{1,0:T(8,128)(2,1)S(1)}, bf16[288,768]{1,0:T(8,128)(2,1)S(1)}, u32[]{:S(2)}, u32[]{:S(2)}) collective-permute-start(bf16[288,768]{1,0:T(8,128)(2,1)S(1)} %get-tuple-element.90), channel_id=1, source_target_pairs={{0,8},{1,9},{2,10},{3,11},{4,12},{5,13},{6,14},{7,15},{8,24},{9,25... | collective-permute-start | bytes 1327112 | tf_op jit(solution)/shard_map/ppermute | solution.py:59
  261.5 15.0 %copy-start.40 = (f32[336]{0:T(512)}, f32[336]{0:T(512)S(1)}, u32[]{:S(2)}) copy-start(f32[336]{0:T(512)S(1)} %fusion.1) | copy-start | bytes 4036
  262.1 14.4 %copy-start.41 = (f32[336]{0:T(512)}, f32[336]{0:T(512)S(1)}, u32[]{:S(2)}) copy-start(f32[336]{0:T(512)S(1)} %get-tuple-element.100) | copy-start | bytes 4036
  (17 other events, 22.8 us)

commit v5 on v4

--- a/solution.py
+++ b/solution.py
@@ -538,10 +538,10 @@
     late = begin(cotangent_in, cotangent, more.at[2])
 
     def branch(i):
-        here = rows_of(i, SPAN)
+        here = rows_of(i, TALL)
         total[here, :] = contract(context[here, :], weights[0:D, :], 1, 1)
 
-    loop(rows // SPAN, branch)
+    loop(rows // TALL, branch)
 
     def first(i):
         here = rows_of(i, PART)
@@ -656,10 +656,10 @@
     sent.append(begin(total, grad_first_to, more.at[8]))
 
     def through_out(i):
-        here = rows_of(i, SPAN)
+        here = rows_of(i, TALL)
         grad_context[:, here] = contract(cotangent[here, :], weights[0:D, :], 1, 0).T.astype(bf16)
 
-    loop(rows // SPAN, through_out)
+    loop(rows // TALL, through_out)
     sent.append(begin(grad_context, grad_context_to, more.at[10]))
     moved = begin(down_made.at[pl.ds(0, D)], weights.at[pl.ds(D + FF, D)], more.at[9])
 
@@ -1198,12 +1198,9 @@
         begin(master_v, master_to, sems.at[9]), begin(slow_v, slow_to, sems.at[10]), begin(low_v, low_to, sems.at[11])
     ]
     finish(loads[4:6])
-    tall_a = jnp.concatenate([high, high, low], axis=0)
-    tall_b = jnp.concatenate([high, low, high], axis=0)
-    left_v[...] = stat_decay * left_v[...] + (1.0 - stat_decay) * contract(tall_a, tall_b, 0, 0)
+    left_v[...] = stat_decay * left_v[...] + (1.0 - stat_decay) * contract(high, high, 0, 0)
     sent.append(begin(left_v, left_to, sems.at[12]))
-    other = jnp.concatenate([high, low, high], axis=1)
-    right_v[...] = stat_decay * right_v[...] + (1.0 - stat_decay) * contract(wide, other, 1, 1)
+    right_v[...] = stat_decay * right_v[...] + (1.0 - stat_decay) * contract(high, high, 1, 1)
     finish(sent, begin(right_v, right_to, sems.at[13]))
 
 

time: 277 us -> 276 us (level)
  no operation moved by 1% of the time
where the time goes in v5:
time: 276 us; the launch traced here: 275 us
  Pallas kernels  134 us (49%)
  waiting for transfers between devices  83.6 us (30%)
  starting transfers between devices  39.7 us (14%)
  local copies, waits for them, and re-layouts  14.8 us (5%)
    pallas_call x12, Pallas kernels, call(): pl.pallas_call(body, out_shape=outs, in_specs=[*specs, *[anywhere] * skip...  123 us
    ppermute x34, waiting for transfers between devices, send(): return lax.ppermute(values, AXES, pairs)  83.6 us
    ppermute x34, starting transfers between devices, send(): return lax.ppermute(values, AXES, pairs)  39.7 us
    unnamed x94, local copies, waits for them, and re-layouts  13.3 us
    pallas_call x9, Pallas kernels, picked(): pl.pallas_call(body, grid=(1,), out_shape=outs, in_specs=[*specs, *[anywh...  11.7 us
  transfers between devices with their start and end apart: 34, of which 20 were waited for; matrix products, arithmetic and copies ran while one was open for 1% of the time, Pallas kernels for 23%

profile of v5, /device:TPU:0, one launch (start us, length us, event | category | flops | bytes accessed | tf_op | source)
XLA Modules:
  0.0 274.9 jit_solution(3783843158694281653)
XLA Ops:
  1.5 1.2 copy-done.27
  2.7 0.9 prepare_own.1.refs_1_
  3.5 3.0 %collective-permute-start.1 = (bf16[304,768]{1,0:T(8,128)(2,1)S(1)}, bf16[304,768]{1,0:T(8,128)(2,1)S(1)}, u32[]{:S(2)}, u32[]{:S(2)}) collective-permute-start(bf16[304,768]{1,0:T(8,128)(2,1)S(1)} %prepare_own.1.refs_1_), channel_id=1, source_target_pairs={{0,4},{1,5},{2,3},{3,2},{4,0},{5,1},{6,7},{7,6},{8,12},{9,13},{10,... | collective-permute-start | bytes 1400840 | tf_op jit(solution)/shard_map/ppermute | solution.py:59
  6.6 2.6 collective-permute-start
  9.2 4.0 %collective-permute-done.1.refs_3_ = bf16[304,768]{1,0:T(8,128)(2,1)S(1)} collective-permute-done((bf16[304,768]{1,0:T(8,128)(2,1)S(1)}, bf16[304,768]{1,0:T(8,128)(2,1)S(1)}, u32[]{:S(2)}, u32[]{:S(2)}) %collective-permute-start.1) | collective-permute-done | bytes 466976 | tf_op jit(solution)/shard_map/ppermute | solution.py:59
  13.1 5.7 %collective-permute-done.refs_2_ = bf16[304,768]{1,0:T(8,128)(2,1)S(1)} collective-permute-done((bf16[304,768]{1,0:T(8,128)(2,1)S(1)}, bf16[304,768]{1,0:T(8,128)(2,1)S(1)}, u32[]{:S(2)}, u32[]{:S(2)}) %collective-permute-start) | collective-permute-done | bytes 466976 | tf_op jit(solution)/shard_map/ppermute | solution.py:59
  21.5 5.0 %collective-permute-start.5 = (bf16[304,768]{1,0:T(8,128)(2,1)S(1)}, bf16[304,768]{1,0:T(8,128)(2,1)S(1)}, u32[]{:S(2)}, u32[]{:S(2)}) collective-permute-start(bf16[304,768]{1,0:T(8,128)(2,1)S(1)} %get-tuple-element.57.refs_1_), channel_id=1, source_target_pairs={{0,8},{1,9},{2,10},{3,11},{4,12},{5,13},{6,14},{7,15},{8,0},{9,1},... | collective-permute-start | bytes 1400840 | tf_op jit(solution)/shard_map/ppermute | solution.py:59
  26.5 6.7 %collective-permute-done.2.refs_5_.refs_3_.refs_2_ = bf16[2,304,768]{2,1,0:T(8,128)(2,1)S(1)} collective-permute-done((bf16[2,304,768]{2,1,0:T(8,128)(2,1)S(1)}, bf16[2,304,768]{2,1,0:T(8,128)(2,1)S(1)}, u32[]{:S(2)}, u32[]{:S(2)}) %collective-permute-start.2) | collective-permute-done | bytes 933920 | tf_op jit(solution)/shard_map/ppermute | solution.py:59
  33.1 3.4 %collective-permute-start.6 = (bf16[16,768]{1,0:T(8,128)(2,1)S(1)}, bf16[16,768]{1,0:T(8,128)(2,1)S(1)}, u32[]{:S(2)}, u32[]{:S(2)}) collective-permute-start(bf16[16,768]{1,0:T(8,128)(2,1)S(1)} %get-tuple-element.58), channel_id=1, source_target_pairs={{0,16},{1,17},{2,18},{3,19},{4,20},{5,21},{6,22},{7,23},{8,24},{9,... | collective-permute-start | bytes 73736 | tf_op jit(solution)/shard_map/ppermute | solution.py:59
  36.5 0.9 collective-permute-start.9
  37.5 0.9 collective-permute-done.6.refs_4_
  39.1 1.6 collective-permute-start.7
  41.2 8.2 %collective-permute-done.9.refs_4_ = bf16[304,768]{1,0:T(8,128)(2,1)S(1)} collective-permute-done((bf16[304,768]{1,0:T(8,128)(2,1)S(1)}, bf16[304,768]{1,0:T(8,128)(2,1)S(1)}, u32[]{:S(2)}, u32[]{:S(2)}) %collective-permute-start.9) | collective-permute-done | bytes 466976 | tf_op jit(solution)/shard_map/ppermute | solution.py:59
  49.3 3.1 %collective-permute-done.10.refs_5_.refs_1_ = bf16[288,768]{1,0:T(8,128)(2,1)S(1)} collective-permute-done((bf16[288,768]{1,0:T(8,128)(2,1)S(1)}, bf16[288,768]{1,0:T(8,128)(2,1)S(1)}, u32[]{:S(2)}, u32[]{:S(2)}) %collective-permute-start.10) | collective-permute-done | bytes 442400 | tf_op jit(solution)/shard_map/ppermute | solution.py:59
  53.2 0.8 collective-permute-start.11
  54.0 1.5 collective-permute-start.14
  55.5 11.6 %collective-permute-done.14.refs_3_ = bf16[288,768]{1,0:T(8,128)(2,1)S(1)} collective-permute-done((bf16[288,768]{1,0:T(8,128)(2,1)S(1)}, bf16[288,768]{1,0:T(8,128)(2,1)S(1)}, u32[]{:S(2)}, u32[]{:S(2)}) %collective-permute-start.14) | collective-permute-done | bytes 442400 | tf_op jit(solution)/shard_map/ppermute | solution.py:59
  67.1 1.4 after_four.1.refs_14_.refs_9_
  68.5 1.4 collective-permute-start.15
  69.9 1.8 collective-permute-done.11.refs_2_.refs_7_.refs_6_
  72.1 3.3 %collective-permute-done.13.refs_4_.refs_9_.refs_8_ = bf16[2,304,768]{2,1,0:T(8,128)(2,1)S(1)} collective-permute-done((bf16[2,304,768]{2,1,0:T(8,128)(2,1)S(1)}, bf16[2,304,768]{2,1,0:T(8,128)(2,1)S(1)}, u32[]{:S(2)}, u32[]{:S(2)}) %collective-permute-start.13) | collective-permute-done | bytes 933920 | tf_op jit(solution)/shard_map/ppermute | solution.py:59
  75.4 0.9 read_vectors.1
  77.1 15.8 %attend.1 = (bf16[2304,1024]{1,0:T(8,128)(2,1)}, bf16[1024,768]{1,0:T(8,128)(2,1)}, f32[12,1024]{1,0:T(8,128)}) custom-call(s32[8]{0:T(128)} %copy-done.31, s32[4]{0:T(128)} %refs_1_.3, bf16[2,304,768]{2,1,0:T(8,128)(2,1)} %copy-done.10, bf16[2,304,768]{2,1,0:T(8,128)(2,1)} %copy-done.3, bf16[2,304,768]{2,1,0:T(8,128)(2,1)} %copy-done.4, ...), custom_call_target="tpu_custom_call" | custom-call | flops 4429185024 | bytes 20971520 | tf_op jit(solution)/shard_map/attend/pallas_call | solution.py:258
  93.2 3.7 %collective-permute-done.17.refs_12_ = bf16[2,2,288,768]{3,2,1,0:T(8,128)(2,1)S(1)} collective-permute-done((bf16[2,2,288,768]{3,2,1,0:T(8,128)(2,1)}, bf16[2,2,288,768]{3,2,1,0:T(8,128)(2,1)S(1)}, u32[]{:S(2)}, u32[]{:S(2)}) %collective-permute-start.17) | collective-permute-done | bytes 1769504 | tf_op jit(solution)/shard_map/ppermute | solution.py:59
  97.0 1.2 copy-done.45
  98.2 59.6 %middle.1 = (bf16[1024,768]{1,0:T(8,128)(2,1)}, f32[1024,768]{1,0:T(8,128)}, bf16[768,1024]{1,0:T(8,128)(2,1)}, f32[11,3072]{1,0:T(8,128)}, bf16[2,2,288,768]{3,...) custom-call(s32[8]{0:T(128)} %copy-done.31, ...), custom_call_target="tpu_custom_call" | custom-call | flops 32614907904 | bytes 62914560 | tf_op jit(solution)/shard_map/middle/pallas_call | solution.py:258
  158.5 4.5 %collective-permute-done.19.refs_1_ = bf16[2,1,288,768]{3,2,1,0:T(8,128)(2,1)S(1)} collective-permute-done((bf16[2,1,288,768]{3,2,1,0:T(8,128)(2,1)}, bf16[2,1,288,768]{3,2,1,0:T(8,128)(2,1)S(1)}, u32[]{:S(2)}, u32[]{:S(2)}) %collective-permute-start.19) | collective-permute-done | bytes 884768 | tf_op jit(solution)/shard_map/ppermute | solution.py:59
  163.0 1.2 copy-done.28
  164.4 0.8 collective-permute-start.23
  165.3 1.7 add_pieces.7.refs_6_
  167.0 1.3 collective-permute-start.21
  168.3 11.7 %attend_back.1.refs_3_.refs_9_ = bf16[2304,1024]{1,0:T(8,128)(2,1)S(1)} custom-call(s32[8]{0:T(128)S(1)} %copy-done.32, s32[4]{0:T(128)S(1)} %copy-done.38, bf16[2304,1024]{1,0:T(8,128)(2,1)S(1)} %copy-done.9, bf16[768,1024]{1,0:T(8,128)(2,1)S(1)} %copy-done.23, f32[12,1024]{1,0:T(8,128)S(1)} %copy-done.34, s32[1,1024]{1,0:T(1,128)S(1)} %bitcast.19, ...), custom_call_target="tpu_custom_call" | custom-call | flops 2013265920 | bytes 26214400 | tf_op jit(solution)/shard_map/attend_back/pallas_call | solution.py:258
  180.3 1.9 copy-done
  182.8 1.2 collective-permute-start.24
  184.0 11.0 %mixed_grad.1 = (bf16[2,1,304,768]{3,2,1,0:T(8,128)(2,1)}, bf16[2,1,304,768]{3,2,1,0:T(8,128)(2,1)}, bf16[2,1,304,768]{3,2,1,0:T(8,128)(2,1)}, bf16[2,1,304,768]{3,2,1,0:T(8,128)(2,1)}) custom-call(s32[8]{0:T(128)} %copy-done.31, bf16[2,304,768]{2,1,0:T(8,128)(2,1)} %copy-done.10, bf16[2,304,768]{2,1,0:T(8,128)(2,1)} %copy-done.3, ...), custom_call_target="tpu_custom_call" | custom-call | flops 3623878656 | bytes 12582912 | tf_op jit(solution)/shard_map/mixed_grad/pallas_call | solution.py:258
  195.0 0.9 collective-permute-done.24.refs_1_.refs_8_
  195.9 0.8 copy-done.20
  197.2 2.2 collective-permute-done.25.refs_1_
  199.4 1.2 add_pieces.9.refs_3_
  200.5 1.2 collective-permute-start.27
  201.8 1.5 collective-permute-done.20.refs_1_.refs_2_.refs_6_
  203.2 2.4 add_pieces.10.refs_11_
  205.7 1.2 collective-permute-start.29
  206.9 11.5 %input_back.1 = (f32[1024,768]{1,0:T(8,128)}, f32[8,128]{1,0:T(8,128)}) custom-call(s32[8]{0:T(128)} %copy-done.31, bf16[2,304,768]{2,1,0:T(8,128)(2,1)} %copy-done.10, bf16[2,304,768]{2,1,0:T(8,128)(2,1)} %copy-done.3, bf16[2,304,768]{2,1,0:T(8,128)(2,1)} %copy-done.4, bf16[2,304,768]{2,1,0:T(8,128)(2,1)} %copy-done.5, bf16[2,304,768]{2,1,0:T(8,128)(2,1)} %copy-done.6, ...), custom_call_target="tpu_custom_call" | custom-call | tf_op jit(solution)/shard_map/input_back/pallas_call | solution.py:258
  218.4 1.6 collective-permute-done.27.refs_2_.refs_3_
  220.1 1.2 copy-done.11
  222.0 1.4 add_pieces.11
  223.4 1.3 collective-permute-start.28
  224.7 2.0 far_sums.1
  226.7 0.9 copy-done.25
  227.6 3.0 %collective-permute-start.31 = (bf16[288,768]{1,0:T(8,128)(2,1)S(1)}, bf16[288,768]{1,0:T(8,128)(2,1)S(1)}, u32[]{:S(2)}, u32[]{:S(2)}) collective-permute-start(bf16[288,768]{1,0:T(8,128)(2,1)S(1)} %get-tuple-element.88), channel_id=1, source_target_pairs={{0,16},{1,17},{2,18},{3,19},{4,20},{5,21},{6,22},{7,23},{8,24},{9,... | collective-permute-start | bytes 1327112 | tf_op jit(solution)/shard_map/ppermute | solution.py:59
  230.6 1.4 collective-permute-done.28.refs_4_
  232.0 1.8 near_sums.1
  233.9 1.9 collective-permute-start.30
  235.7 13.8 %collective-permute-done.31.refs_0_ = bf16[288,768]{1,0:T(8,128)(2,1)S(1)} collective-permute-done((bf16[288,768]{1,0:T(8,128)(2,1)S(1)}, bf16[288,768]{1,0:T(8,128)(2,1)S(1)}, u32[]{:S(2)}, u32[]{:S(2)}) %collective-permute-start.31) | collective-permute-done | bytes 442400 | tf_op jit(solution)/shard_map/ppermute | solution.py:59
  250.4 2.2 collective-permute-done.30.refs_4_
  252.5 1.0 copy-done.30
  253.6 0.9 last_sums.1
  254.4 0.9 copy-done.39
  256.0 2.5 collective-permute-start.32
  258.5 2.1 collective-permute-done.33
  261.8 4.5 %collective-permute-done.32.refs_1_ = bf16[288,768]{1,0:T(8,128)(2,1)S(1)} collective-permute-done((bf16[288,768]{1,0:T(8,128)(2,1)S(1)}, bf16[288,768]{1,0:T(8,128)(2,1)S(1)}, u32[]{:S(2)}, u32[]{:S(2)}) %collective-permute-start.32) | collective-permute-done | bytes 442400 | tf_op jit(solution)/shard_map/ppermute | solution.py:59
  266.3 0.8 copy-done.46
  267.1 7.7 %owner_step.1 = (f32[288,768]{1,0:T(8,128)}, f32[768,768]{1,0:T(8,128)}, f32[288,288]{1,0:T(8,128)}, f32[288,768]{1,0:T(8,128)}, f32[288,768]{1,0:T(8,128)}, /*index=5*/bf16[288,768]{1,0:T(8,128)(2,1)}) custom-call(f32[288,768]{1,0:T(8,128)} %copy-done.39, bf16[288,768]{1,0:T(8,128)(2,1)} %copy-done.46, f32[768,768]{1,0:T(8,128)} %refs_2_.1, ...), custom_call_target="tpu_custom_call" | custom-call | flops 2802843648 | bytes 15728640 | tf_op jit(solution)/shard_map/owner_step/pallas_call | solution.py:258
  (130 shorter events, 12.5 us)
Async XLA Ops:
  1.5 73.9 %copy-start.31 = (s32[8]{0:T(128)}, s32[8]{0:T(128)S(1)}, u32[]{:S(2)}) copy-start(s32[8]{0:T(128)S(1)} %stack.35.refs_0_) | copy-start | bytes 100
  3.5 9.6 %collective-permute-start.1 = (bf16[304,768]{1,0:T(8,128)(2,1)S(1)}, bf16[304,768]{1,0:T(8,128)(2,1)S(1)}, u32[]{:S(2)}, u32[]{:S(2)}) collective-permute-start(bf16[304,768]{1,0:T(8,128)(2,1)S(1)} %prepare_own.1.refs_1_), channel_id=1, source_target_pairs={{0,4},{1,5},{2,3},{3,2},{4,0},{5,1},{6,7},{7,6},{8,12},{9,13},{10,... | collective-permute-start | bytes 1400840 | tf_op jit(solution)/shard_map/ppermute | solution.py:59
  6.6 12.2 %collective-permute-start = (bf16[304,768]{1,0:T(8,128)(2,1)S(1)}, bf16[304,768]{1,0:T(8,128)(2,1)S(1)}, u32[]{:S(2)}, u32[]{:S(2)}) collective-permute-start(bf16[304,768]{1,0:T(8,128)(2,1)S(1)} %prepare_own.1.refs_1_), channel_id=1, source_target_pairs={{0,16},{1,17},{2,18},{3,19},{4,20},{5,21},{6,22},{7,23},{8,0},{9,1... | collective-permute-start | bytes 1400840 | tf_op jit(solution)/shard_map/ppermute | solution.py:59
  19.5 33.0 %copy-start.10 = (bf16[2,304,768]{2,1,0:T(8,128)(2,1)}, bf16[2,304,768]{2,1,0:T(8,128)(2,1)S(1)}, u32[]{:S(2)}) copy-start(bf16[2,304,768]{2,1,0:T(8,128)(2,1)S(1)} %get-tuple-element.56.refs_2_.refs_1_) | copy-start | bytes 2801668
  19.5 13.6 %collective-permute-start.2 = (bf16[2,304,768]{2,1,0:T(8,128)(2,1)S(1)}, bf16[2,304,768]{2,1,0:T(8,128)(2,1)S(1)}, u32[]{:S(2)}, u32[]{:S(2)}) collective-permute-start(bf16[2,304,768]{2,1,0:T(8,128)(2,1)S(1)} %get-tuple-element.56.refs_2_.refs_1_), channel_id=1, source_target_pairs={{0,1},{1,0},{2,6},{3,7},{4,5},{5,4},{6,2},{7,3},{8,9},{9,8},{10,14... | collective-permute-start | bytes 2801672 | tf_op jit(solution)/shard_map/ppermute | solution.py:59
  20.1 18.3 %collective-permute-start.3 = (bf16[2,304,768]{2,1,0:T(8,128)(2,1)S(1)}, bf16[2,304,768]{2,1,0:T(8,128)(2,1)S(1)}, u32[]{:S(2)}, u32[]{:S(2)}) collective-permute-start(bf16[2,304,768]{2,1,0:T(8,128)(2,1)S(1)} %get-tuple-element.56.refs_2_.refs_1_), channel_id=1, source_target_pairs={{0,2},{1,3},{2,0},{3,1},{4,6},{5,7},{6,4},{7,5},{8,10},{9,11},{10,... | collective-permute-start | bytes 2801672 | tf_op jit(solution)/shard_map/ppermute | solution.py:59
  20.8 15.7 %collective-permute-start.8 = (bf16[304,768]{1,0:T(8,128)(2,1)S(1)}, bf16[304,768]{1,0:T(8,128)(2,1)S(1)}, u32[]{:S(2)}, u32[]{:S(2)}) collective-permute-start(bf16[304,768]{1,0:T(8,128)(2,1)S(1)} %prepare_own.1.refs_1_), channel_id=1, source_target_pairs={{0,0},{1,1},{2,2},{3,3},{4,4},{5,5},{6,6},{7,7},{8,16},{9,17},{10,... | collective-permute-start | bytes 1400840 | tf_op jit(solution)/shard_map/ppermute | solution.py:59
  21.5 16.9 %collective-permute-start.5 = (bf16[304,768]{1,0:T(8,128)(2,1)S(1)}, bf16[304,768]{1,0:T(8,128)(2,1)S(1)}, u32[]{:S(2)}, u32[]{:S(2)}) collective-permute-start(bf16[304,768]{1,0:T(8,128)(2,1)S(1)} %get-tuple-element.57.refs_1_), channel_id=1, source_target_pairs={{0,8},{1,9},{2,10},{3,11},{4,12},{5,13},{6,14},{7,15},{8,0},{9,1},... | collective-permute-start | bytes 1400840 | tf_op jit(solution)/shard_map/ppermute | solution.py:59
  33.1 20.0 %copy-start.3 = (bf16[2,304,768]{2,1,0:T(8,128)(2,1)}, bf16[2,304,768]{2,1,0:T(8,128)(2,1)S(1)}, u32[]{:S(2)}) copy-start(bf16[2,304,768]{2,1,0:T(8,128)(2,1)S(1)} %collective-permute-done.2.refs_5_.refs_3_.refs_2_) | copy-start | bytes 2801668
  33.1 19.3 %collective-permute-start.4 = (bf16[2,304,768]{2,1,0:T(8,128)(2,1)S(1)}, bf16[2,304,768]{2,1,0:T(8,128)(2,1)S(1)}, u32[]{:S(2)}, u32[]{:S(2)}) collective-permute-start(bf16[2,304,768]{2,1,0:T(8,128)(2,1)S(1)} %collective-permute-done.2.refs_5_.refs_3_.refs_2_), channel_id=1, source_target_pairs={{0,2},{1,3},{2,0},{3,1},{4,6},{5,7},{6,4},{7,5},{8,10},{9,11},{10,... | collective-permute-start | bytes 2801672 | tf_op jit(solution)/shard_map/ppermute | solution.py:59
  33.1 5.3 %collective-permute-start.6 = (bf16[16,768]{1,0:T(8,128)(2,1)S(1)}, bf16[16,768]{1,0:T(8,128)(2,1)S(1)}, u32[]{:S(2)}, u32[]{:S(2)}) collective-permute-start(bf16[16,768]{1,0:T(8,128)(2,1)S(1)} %get-tuple-element.58), channel_id=1, source_target_pairs={{0,16},{1,17},{2,18},{3,19},{4,20},{5,21},{6,22},{7,23},{8,24},{9,... | collective-permute-start | bytes 73736 | tf_op jit(solution)/shard_map/ppermute | solution.py:59
  36.5 12.8 %collective-permute-start.9 = (bf16[304,768]{1,0:T(8,128)(2,1)S(1)}, bf16[304,768]{1,0:T(8,128)(2,1)S(1)}, u32[]{:S(2)}, u32[]{:S(2)}) collective-permute-start(bf16[304,768]{1,0:T(8,128)(2,1)S(1)} %collective-permute-done.8.refs_3_), channel_id=1, source_target_pairs={{0,8},{1,9},{2,10},{3,11},{4,12},{5,13},{6,14},{7,15},{8,0},{9,1},... | collective-permute-start | bytes 1400840 | tf_op jit(solution)/shard_map/ppermute | solution.py:59
  38.4 14.7 %copy-start.4 = (bf16[2,304,768]{2,1,0:T(8,128)(2,1)}, bf16[2,304,768]{2,1,0:T(8,128)(2,1)S(1)}, u32[]{:S(2)}) copy-start(bf16[2,304,768]{2,1,0:T(8,128)(2,1)S(1)} %collective-permute-done.3.refs_6_.refs_4_.refs_3_) | copy-start | bytes 2801668
  39.1 13.4 %collective-permute-start.7 = (bf16[304,768]{1,0:T(8,128)(2,1)S(1)}, bf16[304,768]{1,0:T(8,128)(2,1)S(1)}, u32[]{:S(2)}, u32[]{:S(2)}) collective-permute-start(bf16[304,768]{1,0:T(8,128)(2,1)S(1)} %get-tuple-element.59.refs_1_), channel_id=1, source_target_pairs={{0,4},{1,5},{2,3},{3,2},{4,0},{5,1},{6,7},{7,6},{8,12},{9,13},{10,... | collective-permute-start | bytes 1400840 | tf_op jit(solution)/shard_map/ppermute | solution.py:59
  40.7 11.8 %collective-permute-start.10 = (bf16[288,768]{1,0:T(8,128)(2,1)S(1)}, bf16[288,768]{1,0:T(8,128)(2,1)S(1)}, u32[]{:S(2)}, u32[]{:S(2)}) collective-permute-start(bf16[288,768]{1,0:T(8,128)(2,1)S(1)} %get-tuple-element.60.refs_0_), channel_id=1, source_target_pairs={{0,4},{1,5},{2,3},{3,2},{4,0},{5,1},{6,7},{7,6},{8,12},{9,13},{10,... | collective-permute-start | bytes 1327112 | tf_op jit(solution)/shard_map/ppermute | solution.py:59
  52.5 16.0 %copy-start.5 = (bf16[2,304,768]{2,1,0:T(8,128)(2,1)}, bf16[2,304,768]{2,1,0:T(8,128)(2,1)S(1)}, u32[]{:S(2)}) copy-start(bf16[2,304,768]{2,1,0:T(8,128)(2,1)S(1)} %collective-permute-done.4.refs_6_.refs_5_.refs_4_) | copy-start | bytes 2801668
  53.2 22.3 %copy-start.6 = (bf16[2,304,768]{2,1,0:T(8,128)(2,1)}, bf16[2,304,768]{2,1,0:T(8,128)(2,1)S(1)}, u32[]{:S(2)}) copy-start(bf16[2,304,768]{2,1,0:T(8,128)(2,1)S(1)} %get-tuple-element.61.refs_1_.refs_6_.refs_5_) | copy-start | bytes 2801668
  53.2 13.9 %collective-permute-start.12 = (bf16[2,304,768]{2,1,0:T(8,128)(2,1)S(1)}, bf16[2,304,768]{2,1,0:T(8,128)(2,1)S(1)}, u32[]{:S(2)}, u32[]{:S(2)}) collective-permute-start(bf16[2,304,768]{2,1,0:T(8,128)(2,1)S(1)} %get-tuple-element.61.refs_1_.refs_6_.refs_5_), channel_id=1, source_target_pairs={{0,2},{1,3},{2,0},{3,1},{4,6},{5,7},{6,4},{7,5},{8,10},{9,11},{10,... | collective-permute-start | bytes 2801672 | tf_op jit(solution)/shard_map/ppermute | solution.py:59
  53.2 18.4 %collective-permute-start.11 = (bf16[2,304,768]{2,1,0:T(8,128)(2,1)S(1)}, bf16[2,304,768]{2,1,0:T(8,128)(2,1)S(1)}, u32[]{:S(2)}, u32[]{:S(2)}) collective-permute-start(bf16[2,304,768]{2,1,0:T(8,128)(2,1)S(1)} %get-tuple-element.61.refs_1_.refs_6_.refs_5_), channel_id=1, source_target_pairs={{0,1},{1,0},{2,6},{3,7},{4,5},{5,4},{6,2},{7,3},{8,9},{9,8},{10,14... | collective-permute-start | bytes 2801672 | tf_op jit(solution)/shard_map/ppermute | solution.py:59
  54.0 13.1 %collective-permute-start.14 = (bf16[288,768]{1,0:T(8,128)(2,1)S(1)}, bf16[288,768]{1,0:T(8,128)(2,1)S(1)}, u32[]{:S(2)}, u32[]{:S(2)}) collective-permute-start(bf16[288,768]{1,0:T(8,128)(2,1)S(1)} %get-tuple-element.62.refs_2_), channel_id=1, source_target_pairs={{0,4},{1,5},{2,3},{3,2},{4,0},{5,1},{6,7},{7,6},{8,12},{9,13},{10,... | collective-permute-start | bytes 1327112 | tf_op jit(solution)/shard_map/ppermute | solution.py:59
  67.1 8.3 %copy-start.2 = (bf16[2,304,768]{2,1,0:T(8,128)(2,1)}, bf16[2,304,768]{2,1,0:T(8,128)(2,1)S(1)}, u32[]{:S(2)}) copy-start(bf16[2,304,768]{2,1,0:T(8,128)(2,1)S(1)} %collective-permute-done.12.refs_4_.refs_3_.refs_8_.refs_7_) | copy-start | bytes 2801668
  68.5 24.5 %collective-permute-start.15 = (bf16[2,2,288,768]{3,2,1,0:T(8,128)(2,1)}, bf16[2,2,288,768]{3,2,1,0:T(8,128)(2,1)}, u32[]{:S(2)}, u32[]{:S(2)}) collective-permute-start(bf16[2,2,288,768]{3,2,1,0:T(8,128)(2,1)} %after_four.1.refs_14_.refs_9_), channel_id=1, source_target_pairs={{0,1},{1,0},{2,6},{3,7},{4,5},{5,4},{6,2},{7,3},{8,9},{9,8},{10,14... | collective-permute-start | bytes 5308424 | tf_op jit(solution)/shard_map/ppermute | solution.py:59
  71.6 4.8 %copy-start.7 = (bf16[2,304,768]{2,1,0:T(8,128)(2,1)}, bf16[2,304,768]{2,1,0:T(8,128)(2,1)S(1)}, u32[]{:S(2)}) copy-start(bf16[2,304,768]{2,1,0:T(8,128)(2,1)S(1)} %collective-permute-done.11.refs_2_.refs_7_.refs_6_) | copy-start | bytes 2801668
  71.6 3.8 %collective-permute-start.13 = (bf16[2,304,768]{2,1,0:T(8,128)(2,1)S(1)}, bf16[2,304,768]{2,1,0:T(8,128)(2,1)S(1)}, u32[]{:S(2)}, u32[]{:S(2)}) collective-permute-start(bf16[2,304,768]{2,1,0:T(8,128)(2,1)S(1)} %collective-permute-done.11.refs_2_.refs_7_.refs_6_), channel_id=1, source_target_pairs={{0,2},{1,3},{2,0},{3,1},{4,6},{5,7},{6,4},{7,5},{8,10},{9,11},{10,... | collective-permute-start | bytes 2801672 | tf_op jit(solution)/shard_map/ppermute | solution.py:59
  71.6 21.6 %collective-permute-start.16 = (bf16[2,2,288,768]{3,2,1,0:T(8,128)(2,1)}, bf16[2,2,288,768]{3,2,1,0:T(8,128)(2,1)}, u32[]{:S(2)}, u32[]{:S(2)}) collective-permute-start(bf16[2,2,288,768]{3,2,1,0:T(8,128)(2,1)} %after_four.1.refs_14_.refs_9_), channel_id=1, source_target_pairs={{0,2},{1,3},{2,0},{3,1},{4,6},{5,7},{6,4},{7,5},{8,10},{9,11},{10,... | collective-permute-start | bytes 5308424 | tf_op jit(solution)/shard_map/ppermute | solution.py:59
  93.0 4.0 %collective-permute-start.17 = (bf16[2,2,288,768]{3,2,1,0:T(8,128)(2,1)}, bf16[2,2,288,768]{3,2,1,0:T(8,128)(2,1)S(1)}, u32[]{:S(2)}, u32[]{:S(2)}) collective-permute-start(bf16[2,2,288,768]{3,2,1,0:T(8,128)(2,1)} %hold.4.refs_10_), channel_id=1, source_target_pairs={{0,2},{1,3},{2,0},{3,1},{4,6},{5,7},{6,4},{7,5},{8,10},{9,11},{10,... | collective-permute-start | bytes 5308424 | tf_op jit(solution)/shard_map/ppermute | solution.py:59
  157.8 7.5 %copy-start.19 = (bf16[2,2,288,768]{3,2,1,0:T(8,128)(2,1)S(1)}, bf16[2,2,288,768]{3,2,1,0:T(8,128)(2,1)}, u32[]{:S(2)}) copy-start(bf16[2,2,288,768]{3,2,1,0:T(8,128)(2,1)} %get-tuple-element.68.refs_0_) | copy-start | bytes 5308420
  157.8 7.4 %collective-permute-start.18 = (bf16[2,2,288,768]{3,2,1,0:T(8,128)(2,1)}, bf16[2,2,288,768]{3,2,1,0:T(8,128)(2,1)S(1)}, u32[]{:S(2)}, u32[]{:S(2)}) collective-permute-start(bf16[2,2,288,768]{3,2,1,0:T(8,128)(2,1)} %get-tuple-element.69), channel_id=1, source_target_pairs={{0,2},{1,3},{2,0},{3,1},{4,6},{5,7},{6,4},{7,5},{8,10},{9,11},{10,... | collective-permute-start | bytes 5308424 | tf_op jit(solution)/shard_map/ppermute | solution.py:59
  158.0 5.0 %collective-permute-start.19 = (bf16[2,1,288,768]{3,2,1,0:T(8,128)(2,1)}, bf16[2,1,288,768]{3,2,1,0:T(8,128)(2,1)S(1)}, u32[]{:S(2)}, u32[]{:S(2)}) collective-permute-start(bf16[2,1,288,768]{3,2,1,0:T(8,128)(2,1)} %get-tuple-element.71), channel_id=1, source_target_pairs={{0,2},{1,3},{2,0},{3,1},{4,6},{5,7},{6,4},{7,5},{8,10},{9,11},{10,... | collective-permute-start | bytes 2654216 | tf_op jit(solution)/shard_map/ppermute | solution.py:59
  158.4 21.7 %collective-permute-start.22 = (bf16[2,1,288,768]{3,2,1,0:T(8,128)(2,1)}, bf16[2,1,288,768]{3,2,1,0:T(8,128)(2,1)S(1)}, u32[]{:S(2)}, u32[]{:S(2)}) collective-permute-start(bf16[2,1,288,768]{3,2,1,0:T(8,128)(2,1)} %get-tuple-element.77), channel_id=1, source_target_pairs={{0,2},{1,3},{2,0},{3,1},{4,6},{5,7},{6,4},{7,5},{8,10},{9,11},{10,... | collective-permute-start | bytes 2654216 | tf_op jit(solution)/shard_map/ppermute | solution.py:59
  164.2 4.1 %copy-start.23 = (bf16[768,1024]{1,0:T(8,128)(2,1)S(1)}, bf16[768,1024]{1,0:T(8,128)(2,1)}, u32[]{:S(2)}) copy-start(bf16[768,1024]{1,0:T(8,128)(2,1)} %get-tuple-element.66.refs_3_) | copy-start | bytes 4718596
  164.4 15.6 %collective-permute-start.23 = (bf16[2,1,288,768]{3,2,1,0:T(8,128)(2,1)S(1)}, bf16[2,1,288,768]{3,2,1,0:T(8,128)(2,1)S(1)}, u32[]{:S(2)}, u32[]{:S(2)}) collective-permute-start(bf16[2,1,288,768]{3,2,1,0:T(8,128)(2,1)S(1)} %add_pieces.6.refs_2_), channel_id=1, source_target_pairs={{0,1},{1,0},{2,6},{3,7},{4,5},{5,4},{6,2},{7,3},{8,9},{9,8},{10,14... | collective-permute-start | bytes 2654216 | tf_op jit(solution)/shard_map/ppermute | solution.py:59
  165.3 3.1 %copy-start.9 = (bf16[2304,1024]{1,0:T(8,128)(2,1)S(1)}, bf16[2304,1024]{1,0:T(8,128)(2,1)}, u32[]{:S(2)}) copy-start(bf16[2304,1024]{1,0:T(8,128)(2,1)} %get-tuple-element.65.refs_2_) | copy-start | bytes 14155780
  165.3 3.1 %copy-start.32 = (s32[8]{0:T(128)S(1)}, s32[8]{0:T(128)}, u32[]{:S(2)}) copy-start(s32[8]{0:T(128)} %copy-done.31) | copy-start | bytes 100
  165.3 3.1 %copy-start.34 = (f32[12,1024]{1,0:T(8,128)S(1)}, f32[12,1024]{1,0:T(8,128)}, u32[]{:S(2)}) copy-start(f32[12,1024]{1,0:T(8,128)} %get-tuple-element.67.refs_4_) | copy-start | bytes 147460
  165.3 3.1 %copy-start.37 = (s32[1024]{0:T(1024)S(1)}, s32[1024]{0:T(1024)}, u32[]{:S(2)}) copy-start(s32[1024]{0:T(1024)} %param.19) | copy-start | bytes 12292
  165.3 3.0 %copy-start.38 = (s32[4]{0:T(128)S(1)}, s32[4]{0:T(128)}, u32[]{:S(2)}) copy-start(s32[4]{0:T(128)} %refs_1_.3) | copy-start | bytes 52
  167.0 34.8 %collective-permute-start.21 = (bf16[2,2,288,768]{3,2,1,0:T(8,128)(2,1)}, bf16[2,2,288,768]{3,2,1,0:T(8,128)(2,1)}, u32[]{:S(2)}, u32[]{:S(2)}) collective-permute-start(bf16[2,2,288,768]{3,2,1,0:T(8,128)(2,1)} %add_pieces.7.refs_6_), channel_id=1, source_target_pairs={{0,1},{1,0},{2,6},{3,7},{4,5},{5,4},{6,2},{7,3},{8,9},{9,8},{10,14... | collective-permute-start | bytes 5308424 | tf_op jit(solution)/shard_map/ppermute | solution.py:59
  168.3 11.8 %copy-start.13 = (bf16[2,1,288,768]{3,2,1,0:T(8,128)(2,1)S(1)}, bf16[2,1,288,768]{3,2,1,0:T(8,128)(2,1)}, u32[]{:S(2)}) copy-start(bf16[2,1,288,768]{3,2,1,0:T(8,128)(2,1)} %get-tuple-element.76.refs_0_.refs_5_) | copy-start | bytes 2654212
  182.8 13.1 %collective-permute-start.24 = (bf16[1,1,288,768]{3,2,1,0:T(8,128)(2,1)S(1)}, bf16[1,1,288,768]{3,2,1,0:T(8,128)(2,1)S(1)}, u32[]{:S(2)}, u32[]{:S(2)}) collective-permute-start(bf16[1,1,288,768]{3,2,1,0:T(8,128)(2,1)S(1)} %add_pieces.8.refs_14_), channel_id=1, source_target_pairs={{0,4},{1,5},{2,3},{3,2},{4,0},{5,1},{6,7},{7,6},{8,12},{9,13},{10,... | collective-permute-start | bytes 1327112 | tf_op jit(solution)/shard_map/ppermute | solution.py:59
  195.0 4.4 %copy-start.24 = (bf16[2,1,304,768]{3,2,1,0:T(8,128)(2,1)S(1)}, bf16[2,1,304,768]{3,2,1,0:T(8,128)(2,1)}, u32[]{:S(2)}) copy-start(bf16[2,1,304,768]{3,2,1,0:T(8,128)(2,1)} %get-tuple-element.78.refs_0_) | copy-start | bytes 2801668
  196.7 2.7 collective-permute-start.25
  196.7 6.6 %collective-permute-start.20 = (bf16[2,2,288,768]{3,2,1,0:T(8,128)(2,1)}, bf16[2,2,288,768]{3,2,1,0:T(8,128)(2,1)S(1)}, u32[]{:S(2)}, u32[]{:S(2)}) collective-permute-start(bf16[2,2,288,768]{3,2,1,0:T(8,128)(2,1)} %get-tuple-element.74), channel_id=1, source_target_pairs={{0,2},{1,3},{2,0},{3,1},{4,6},{5,7},{6,4},{7,5},{8,10},{9,11},{10,... | collective-permute-start | bytes 5308424 | tf_op jit(solution)/shard_map/ppermute | solution.py:59
  197.2 21.3 %collective-permute-start.26 = (bf16[2,1,304,768]{3,2,1,0:T(8,128)(2,1)}, bf16[2,1,304,768]{3,2,1,0:T(8,128)(2,1)}, u32[]{:S(2)}, u32[]{:S(2)}) collective-permute-start(bf16[2,1,304,768]{3,2,1,0:T(8,128)(2,1)} %get-tuple-element.82), channel_id=1, source_target_pairs={{0,2},{1,3},{2,0},{3,1},{4,6},{5,7},{6,4},{7,5},{8,10},{9,11},{10,... | collective-permute-start | bytes 2801672 | tf_op jit(solution)/shard_map/ppermute | solution.py:59
  200.5 19.5 %collective-permute-start.27 = (bf16[2,1,304,768]{3,2,1,0:T(8,128)(2,1)}, bf16[2,1,304,768]{3,2,1,0:T(8,128)(2,1)}, u32[]{:S(2)}, u32[]{:S(2)}) collective-permute-start(bf16[2,1,304,768]{3,2,1,0:T(8,128)(2,1)} %add_pieces.9.refs_3_), channel_id=1, source_target_pairs={{0,1},{1,0},{2,6},{3,7},{4,5},{5,4},{6,2},{7,3},{8,9},{9,8},{10,14... | collective-permute-start | bytes 2801672 | tf_op jit(solution)/shard_map/ppermute | solution.py:59
  205.7 19.0 %collective-permute-start.29 = (bf16[1,2,288,768]{3,2,1,0:T(8,128)(2,1)}, bf16[1,2,288,768]{3,2,1,0:T(8,128)(2,1)}, u32[]{:S(2)}, u32[]{:S(2)}) collective-permute-start(bf16[1,2,288,768]{3,2,1,0:T(8,128)(2,1)} %add_pieces.10.refs_11_), channel_id=1, source_target_pairs={{0,4},{1,5},{2,3},{3,2},{4,0},{5,1},{6,7},{7,6},{8,12},{9,13},{10,... | collective-permute-start | bytes 2654216 | tf_op jit(solution)/shard_map/ppermute | solution.py:59
  218.4 6.2 %copy-start.33 = (s32[8]{0:T(128)S(1)}, s32[8]{0:T(128)}, u32[]{:S(2)}) copy-start(s32[8]{0:T(128)} %copy-done.31) | copy-start | bytes 100
  222.0 2.7 copy-start.36
  223.3 8.7 %copy-start.12 = (bf16[2,1,304,768]{3,2,1,0:T(8,128)(2,1)S(1)}, bf16[2,1,304,768]{3,2,1,0:T(8,128)(2,1)}, u32[]{:S(2)}) copy-start(bf16[2,1,304,768]{3,2,1,0:T(8,128)(2,1)} %get-tuple-element.81.refs_0_.refs_1_) | copy-start | bytes 2801668
  223.3 8.7 %copy-start.14 = (bf16[2,1,288,768]{3,2,1,0:T(8,128)(2,1)S(1)}, bf16[2,1,288,768]{3,2,1,0:T(8,128)(2,1)}, u32[]{:S(2)}) copy-start(bf16[2,1,288,768]{3,2,1,0:T(8,128)(2,1)} %get-tuple-element.76.refs_0_.refs_5_) | copy-start | bytes 2654212
  223.3 8.7 %copy-start.16 = (bf16[2,1,288,768]{3,2,1,0:T(8,128)(2,1)S(1)}, bf16[2,1,288,768]{3,2,1,0:T(8,128)(2,1)}, u32[]{:S(2)}) copy-start(bf16[2,1,288,768]{3,2,1,0:T(8,128)(2,1)} %copy-done.15) | copy-start | bytes 2654212
  223.4 8.7 %copy-start.18 = (bf16[2,1,288,768]{3,2,1,0:T(8,128)(2,1)S(1)}, bf16[2,1,288,768]{3,2,1,0:T(8,128)(2,1)}, u32[]{:S(2)}) copy-start(bf16[2,1,288,768]{3,2,1,0:T(8,128)(2,1)} %copy-done.17) | copy-start | bytes 2654212
  223.4 8.7 %copy-start.21 = (bf16[1,1,288,768]{3,2,1,0:T(8,128)(2,1)S(1)}, bf16[1,1,288,768]{3,2,1,0:T(8,128)(2,1)}, u32[]{:S(2)}) copy-start(bf16[1,1,288,768]{3,2,1,0:T(8,128)(2,1)} %copy-done.20) | copy-start | bytes 1327108
  223.4 8.6 %collective-permute-start.28 = (bf16[1,1,304,768]{3,2,1,0:T(8,128)(2,1)S(1)}, bf16[1,1,304,768]{3,2,1,0:T(8,128)(2,1)S(1)}, u32[]{:S(2)}, u32[]{:S(2)}) collective-permute-start(bf16[1,1,304,768]{3,2,1,0:T(8,128)(2,1)S(1)} %add_pieces.11), channel_id=1, source_target_pairs={{0,4},{1,5},{2,3},{3,2},{4,0},{5,1},{6,7},{7,6},{8,12},{9,13},{10,... | collective-permute-start | bytes 1400840 | tf_op jit(solution)/shard_map/ppermute | solution.py:59
  227.6 22.0 %collective-permute-start.31 = (bf16[288,768]{1,0:T(8,128)(2,1)S(1)}, bf16[288,768]{1,0:T(8,128)(2,1)S(1)}, u32[]{:S(2)}, u32[]{:S(2)}) collective-permute-start(bf16[288,768]{1,0:T(8,128)(2,1)S(1)} %get-tuple-element.88), channel_id=1, source_target_pairs={{0,16},{1,17},{2,18},{3,19},{4,20},{5,21},{6,22},{7,23},{8,24},{9,... | collective-permute-start | bytes 1327112 | tf_op jit(solution)/shard_map/ppermute | solution.py:59
  233.8 18.7 %copy-start.26 = (f32[288,768]{1,0:T(8,128)S(1)}, f32[288,768]{1,0:T(8,128)}, u32[]{:S(2)}) copy-start(f32[288,768]{1,0:T(8,128)} %copy-done.25) | copy-start | bytes 2654212
  233.9 18.7 %collective-permute-start.30 = (bf16[304,768]{1,0:T(8,128)(2,1)S(1)}, bf16[304,768]{1,0:T(8,128)(2,1)S(1)}, u32[]{:S(2)}, u32[]{:S(2)}) collective-permute-start(bf16[304,768]{1,0:T(8,128)(2,1)S(1)} %get-tuple-element.87), channel_id=1, source_target_pairs={{0,8},{1,9},{2,10},{3,11},{4,12},{5,13},{6,14},{7,15},{8,0},{9,1},... | collective-permute-start | bytes 1400840 | tf_op jit(solution)/shard_map/ppermute | solution.py:59
  250.3 10.2 %copy-start.44 = (f32[336]{0:T(512)S(1)}, f32[336]{0:T(512)}, u32[]{:S(2)}) copy-start(f32[336]{0:T(512)} %param.30) | copy-start | bytes 4036
  250.3 10.2 %copy-start.43 = (f32[336]{0:T(512)S(1)}, f32[336]{0:T(512)}, u32[]{:S(2)}) copy-start(f32[336]{0:T(512)} %param.29) | copy-start | bytes 4036
  250.4 10.8 %copy-start.42 = (f32[336]{0:T(512)S(1)}, f32[336]{0:T(512)}, u32[]{:S(2)}) copy-start(f32[336]{0:T(512)} %param.31) | copy-start | bytes 4036
  255.4 5.2 %collective-permute-start.33 = (bf16[16,768]{1,0:T(8,128)(2,1)S(1)}, bf16[16,768]{1,0:T(8,128)(2,1)S(1)}, u32[]{:S(2)}, u32[]{:S(2)}) collective-permute-start(bf16[16,768]{1,0:T(8,128)(2,1)S(1)} %get-tuple-element.98), channel_id=1, source_target_pairs={{0,16},{1,17},{2,18},{3,19},{4,20},{5,21},{6,22},{7,23},{8,24},{9,... | collective-permute-start | bytes 73736 | tf_op jit(solution)/shard_map/ppermute | solution.py:59
  256.0 10.3 %collective-permute-start.32 = (bf16[288,768]{1,0:T(8,128)(2,1)S(1)}, bf16[288,768]{1,0:T(8,128)(2,1)S(1)}, u32[]{:S(2)}, u32[]{:S(2)}) collective-permute-start(bf16[288,768]{1,0:T(8,128)(2,1)S(1)} %get-tuple-element.90), channel_id=1, source_target_pairs={{0,8},{1,9},{2,10},{3,11},{4,12},{5,13},{6,14},{7,15},{8,24},{9,25... | collective-permute-start | bytes 1327112 | tf_op jit(solution)/shard_map/ppermute | solution.py:59
  260.6 14.2 %copy-start.40 = (f32[336]{0:T(512)}, f32[336]{0:T(512)S(1)}, u32[]{:S(2)}) copy-start(f32[336]{0:T(512)S(1)} %fusion.1) | copy-start | bytes 4036
  261.2 13.6 %copy-start.41 = (f32[336]{0:T(512)}, f32[336]{0:T(512)S(1)}, u32[]{:S(2)}) copy-start(f32[336]{0:T(512)S(1)} %get-tuple-element.100) | copy-start | bytes 4036
  (17 other events, 22.8 us)
